TPU v7x, 32 devices: a whole 2x2x4 slice. The times are simulated.
32 devices in a mesh: gx: 4 (over z), gy: 4 (over x, core), gz: 2 (over y).
Axes of the slice: x: 2, y: 2, z: 4, core: 2. Of those that a mesh axis runs over, the one named last changes fastest.
Arguments:
- pops: float32 [19, 16, 32, 512], P(None, 'gz', 'gy', 'gx'), may hold values from 0.4 to 1.6
- coarse_pops: bfloat16 [19, 16, 32, 512], P(None, 'gz', 'gy', 'gx'), may hold values from 0.3984375 to 1.59375
- interface: int32 [16, 32, 512], P('gz', 'gy', 'gx'), may hold values 0 or 1
- drop_vel: float32 [3, 512, 128], P(None, ('gx', 'gy', 'gz')), may hold values from -1 to 1
- drop_frac: float32 [3, 512, 128], P(None, ('gx', 'gy', 'gz')), may hold values from 0 to 1
- home: int32 [512, 128], P(('gx', 'gy', 'gz')), may hold values from 0 to 8191, as said below
- counts: int32 [512], P(('gx', 'gy', 'gz')), may hold values from 1 to 128, 49152 in all
- dest: int32 [512], P(('gx', 'gy', 'gz')), may hold values from 0 to 26, as said below
Outputs:
- pops_out: float32 [19, 16, 32, 512], P(None, 'gz', 'gy', 'gx')
- force: float32 [3, 16, 32, 512], P(None, 'gz', 'gy', 'gx')
- arrived: float32 [6, 2176, 128], P(None, ('gx', 'gy', 'gz'))
Inputs may be any that keep to these rules, and one draw needn't show every extreme that they name: All droplets of a block lie in one tile of 8 x 8 x 8 cells at tile-aligned offsets; home = (8 * z + y) * 128 + x in the device's brick. `counts`: live droplets fill the first slots of their block. `dest`: no block crosses a wall along z; apart from code 13, at most 2 blocks of one device share a code, and every device has exactly 2 blocks of some code other than 13.
All inputs are finite; a program needn't handle non-finite values. No bound on the sum of `interface` on one device may be relied on, other than what follows from the above.
Results may differ from a plain program's by a relative error of at most 0.0003.
Values sent between devices are 32-bit elements; how exact they have to be, the bound alone decides.
No kernel may reach another device: no remote copies, remote signals or barrier semaphores. Data moves between devices by JAX's collectives and lax.ppermute only.
A program may use at most 64 MiB of HBM per device.

v0:
```python
import math

import jax
import jax.numpy as jnp
import numpy as np
from jax import lax
from jax.sharding import PartitionSpec as P

TILE = 8
CAP = 2


lattice = np.array(
    [
        [0, 0, 0],
        [1, 0, 0],
        [-1, 0, 0],
        [0, 1, 0],
        [0, -1, 0],
        [0, 0, 1],
        [0, 0, -1],
        [1, 1, 0],
        [-1, -1, 0],
        [1, -1, 0],
        [-1, 1, 0],
        [1, 0, 1],
        [-1, 0, -1],
        [1, 0, -1],
        [-1, 0, 1],
        [0, 1, 1],
        [0, -1, -1],
        [0, 1, -1],
        [0, -1, 1],
    ]
)
weights_table = np.array([1.0 / 3.0] + [1.0 / 18.0] * 6 + [1.0 / 36.0] * 12)
opposite = [0, 2, 1, 4, 3, 6, 5, 8, 7, 10, 9, 12, 11, 14, 13, 16, 15, 18, 17]
inverse_tau = 0.8
relax = 0.5
couple = 8.0
highest = lax.Precision.HIGHEST


def with_halo(cells, sides, width, closed):
    for axis, dim in sides:
        count = lax.axis_size(axis)
        ends = count if closed else count - 1
        head = lax.slice_in_dim(cells, 0, width, axis=dim)
        tail = lax.slice_in_dim(cells, cells.shape[dim] - width, cells.shape[dim], axis=dim)
        cells = jnp.concatenate(
            [
                lax.ppermute(tail, axis, [(i, (i + 1) % count) for i in range(ends)]),
                cells,
                lax.ppermute(head, axis, [((i + 1) % count, i) for i in range(ends)]),
            ],
            axis=dim,
        )
    return cells


def kernel(distance):
    return 0.25 * (1.0 + jnp.cos(math.pi * 0.5 * distance))


def macroscopic(pops):
    density = pops[0] * float(weights_table[0])
    moment = [jnp.zeros_like(density), jnp.zeros_like(density), jnp.zeros_like(density)]
    for index in range(1, 19):
        term = pops[index] * float(weights_table[index])
        density = density + term
        for axis in range(3):
            if int(lattice[index][axis]) != 0:
                moment[axis] = moment[axis] + float(lattice[index][axis]) * term
    return (density, [moment[axis] / density for axis in range(3)])


def collide(pops, coarse, interface):
    density, flow = macroscopic(pops)
    square = flow[0] * flow[0] + flow[1] * flow[1] + flow[2] * flow[2]
    inside = interface == 1
    posts = []
    for index in range(19):
        along = jnp.zeros_like(density)
        for axis in range(3):
            if int(lattice[index][axis]) != 0:
                along = along + float(lattice[index][axis]) * flow[axis]
        balance = density * (1.0 + 3.0 * along + 4.5 * along * along - 1.5 * square)
        relaxed = pops[index] - (pops[index] - balance) * inverse_tau
        posts.append(jnp.where(inside, coarse[index].astype(jnp.float32), relaxed))
    return jnp.stack(posts)


def window(source, index, grown, shape):
    starts = [
        grown[0] * (1 - int(lattice[index][2])),
        grown[1] * (1 - int(lattice[index][1])),
        grown[2] * (1 - int(lattice[index][0])),
    ]
    return source[
        starts[0] : starts[0] + shape[0],
        starts[1] : starts[1] + shape[1],
        starts[2] : starts[2] + shape[2],
    ]


def axis_pull(posts):
    shape = posts.shape[1:]
    cross_z = [index for index in range(19) if int(lattice[index][2]) != 0]
    cross_y = [index for index in range(19) if int(lattice[index][1]) != 0]
    cross_x = [index for index in range(19) if int(lattice[index][0]) != 0]
    part_z = with_halo(jnp.stack([posts[index] for index in cross_z]), (("gz", 1),), 1, False)
    into_y = []
    for index in cross_y:
        if index in cross_z:
            into_y.append(part_z[cross_z.index(index)])
        else:
            into_y.append(jnp.pad(posts[index], ((1, 1), (0, 0), (0, 0))))
    part_y = with_halo(jnp.stack(into_y), (("gy", 2),), 1, True)
    into_x = []
    for index in cross_x:
        if index in cross_y:
            into_x.append(part_y[cross_y.index(index)])
        elif index in cross_z:
            into_x.append(jnp.pad(part_z[cross_z.index(index)], ((0, 0), (1, 1), (0, 0))))
        else:
            into_x.append(jnp.pad(posts[index], ((1, 1), (1, 1), (0, 0))))
    part_x = with_halo(jnp.stack(into_x), (("gx", 3),), 1, True)
    pulled = []
    for index in range(19):
        if index in cross_x:
            pulled.append(window(part_x[cross_x.index(index)], index, (1, 1, 1), shape))
        elif index in cross_y:
            pulled.append(window(part_y[cross_y.index(index)], index, (1, 1, 0), shape))
        elif index in cross_z:
            pulled.append(window(part_z[cross_z.index(index)], index, (1, 0, 0), shape))
        else:
            pulled.append(posts[index])
    return pulled


def wall_fix(pulled, posts, bottom, top):
    fixed = []
    for index in range(19):
        value = pulled[index]
        if int(lattice[index][2]) == 1:
            value = jnp.where(bottom, posts[opposite[index]], value)
        if int(lattice[index][2]) == -1:
            value = jnp.where(top, posts[opposite[index]], value)
        fixed.append(value)
    return jnp.stack(fixed)


def row_weights(offset, frac):
    span = lax.broadcasted_iota(jnp.int32, (1, TILE + 4), 1)
    distance = span - 2 - offset[:, None] - frac[:, None]
    return jnp.where(jnp.abs(distance) < 2.0, kernel(distance), 0.0)


def fold(array, dim, inner):
    core = lax.slice_in_dim(array, 4, inner + 4, axis=dim)
    lower = lax.slice_in_dim(array, 0, 2, axis=dim)
    upper = lax.slice_in_dim(array, inner + 6, inner + 8, axis=dim)
    low_pad = [(0, 0)] * array.ndim
    high_pad = [(0, 0)] * array.ndim
    low_pad[dim] = (0, inner - 2)
    high_pad[dim] = (inner - 2, 0)
    return core + jnp.pad(lower, low_pad) + jnp.pad(upper, high_pad)


def local(pops, coarse_pops, interface, drop_vel, drop_frac, home, counts, dest):
    level = lax.axis_index("gz")
    levels = lax.axis_size("gz")
    depth, height, width = interface.shape
    rows = lax.broadcasted_iota(jnp.int32, (depth, 1, 1), 0)
    bottom = (level == 0) & (rows == 0)
    top = (level == levels - 1) & (rows == depth - 1)
    state = pops
    for substep in range(2):
        posts = collide(state, coarse_pops, interface)
        pulled = axis_pull(posts)
        state = wall_fix(pulled, posts, bottom, top)
    density, flow = macroscopic(state)
    velocity = jnp.stack(flow)
    velocity_ext = with_halo(velocity, (("gx", 3), ("gy", 2), ("gz", 1)), 2, True)
    rim_rows = lax.broadcasted_iota(jnp.int32, (1, depth + 4, 1, 1), 1)
    keep = jnp.logical_not(
        (level == 0) & (rim_rows < 2) | (level == levels - 1) & (rim_rows >= depth + 2)
    )
    velocity_ext = jnp.where(keep, velocity_ext, 0.0)
    blocks = home.shape[0]
    groups = blocks // 4
    edge = TILE + 4
    homes = home.reshape(groups, 4, 128)
    speeds = jnp.moveaxis(drop_vel, 1, 0).reshape(groups, 4, 3, 128)
    fracs = jnp.moveaxis(drop_frac, 1, 0).reshape(groups, 4, 3, 128)
    slots = lax.broadcasted_iota(jnp.int32, (blocks, 128), 1)
    lives = (slots < counts[:, None]).reshape(groups, 4, 128)

    def droplet_group(spread, group):
        group_homes, group_speeds, group_fracs, group_lives = group
        results = []
        for member in range(4):
            cells = group_homes[member]
            speed = group_speeds[member]
            frac = group_fracs[member]
            alive = group_lives[member][None, :]
            first = cells[0]
            start_x = first % width // TILE * TILE
            start_y = first // width % height // TILE * TILE
            start_z = first // (width * height) // TILE * TILE
            weight_x = row_weights(cells % width - start_x, frac[0])
            weight_y = row_weights(cells // width % height - start_y, frac[1])
            weight_z = row_weights(cells // (width * height) - start_z, frac[2])
            corner = (jnp.zeros((), jnp.int32), start_z, start_y, start_x)
            tile = lax.dynamic_slice(velocity_ext, corner, (3, edge, edge, edge))
            partial_value = jnp.dot(
                tile.reshape(3 * edge * edge, edge), weight_x.T, precision=highest
            )
            partial_value = jnp.sum(
                partial_value.reshape(3, edge, edge, 128) * weight_y.T[None, None, :, :], axis=2
            )
            sampled = jnp.sum(partial_value * weight_z.T[None, :, :], axis=1)
            moved = speed + relax * (sampled - speed)
            push = jnp.where(alive, couple * (moved - sampled), 0.0)
            source = (
                push[:, None, None, :] * weight_z.T[None, :, None, :] * weight_y.T[None, None, :, :]
            )
            patch = jnp.dot(source.reshape(3 * edge * edge, 128), weight_x, precision=highest)
            patch = patch.reshape(3, edge, edge, edge)
            spread = lax.dynamic_update_slice(
                spread, lax.dynamic_slice(spread, corner, (3, edge, edge, edge)) + patch, corner
            )
            results.append(jnp.where(alive, jnp.concatenate([moved, frac + moved], axis=0), 0.0))
        return (spread, jnp.stack(results))

    spread, states = lax.scan(
        droplet_group, jnp.zeros_like(velocity_ext), (homes, speeds, fracs, lives)
    )
    states = jnp.moveaxis(states.reshape(blocks, 6, 128), 0, 1)
    spread = jnp.where(keep, spread, 0.0)
    force_ext = with_halo(spread, (("gx", 3), ("gy", 2), ("gz", 1)), 2, True)
    force = fold(fold(fold(force_ext, 1, depth), 2, height), 3, width)
    order = lax.broadcasted_iota(jnp.int32, (blocks,), 0)
    earlier = (dest[:, None] == dest[None, :]) & (order[None, :] < order[:, None])
    rank = jnp.sum(earlier.astype(jnp.int32), axis=1)
    moving = dest != 13
    slot = jnp.where(moving, dest * CAP + rank, 27 * CAP)
    outbox = jnp.zeros((6, 27 * CAP, 128), jnp.float32).at[:, slot].set(states, mode="drop")
    outbox = outbox.reshape(6, 3, 3, 3, CAP, 128)
    arrived_box = with_halo(outbox, (("gx", 3), ("gy", 2), ("gz", 1)), 1, True)
    inbox = arrived_box[:, 4::-2, 4::-2, 4::-2].reshape(6, 27 * CAP, 128)
    incoming = jnp.concatenate([inbox[:, : 13 * CAP], inbox[:, 14 * CAP :]], axis=1)
    staying = jnp.where(moving[None, :, None], 0.0, states)
    arrived = jnp.concatenate([staying, incoming], axis=1)
    return (state, force, arrived)


def solution(mesh):
    return jax.shard_map(
        local,
        mesh=mesh,
        in_specs=(
            P(None, "gz", "gy", "gx"),
            P(None, "gz", "gy", "gx"),
            P("gz", "gy", "gx"),
            P(None, ("gx", "gy", "gz"), None),
            P(None, ("gx", "gy", "gz"), None),
            P(("gx", "gy", "gz"), None),
            P(("gx", "gy", "gz")),
            P(("gx", "gy", "gz")),
        ),
        out_specs=(
            P(None, "gz", "gy", "gx"),
            P(None, "gz", "gy", "gx"),
            P(None, ("gx", "gy", "gz"), None),
        ),
        check_vma=False,
    )
```

profile of v0, /device:TPU:0, one launch (start us, length us, event | category | flops | bytes accessed | tf_op | source)
XLA Modules:
  0.0 292.8 jit_solution(6845195197376977074)
XLA Ops:
  10.7 4.9 %collective-permute-start = (f32[10,1,8,128]{3,2,1,0:T(8,128)S(1)}, f32[10,1,8,128]{3,2,1,0:T(8,128)S(1)}, u32[]{:S(2)}, u32[]{:S(2)}) collective-permute-start(f32[10,1,8,128]{3,2,1,0:T(8,128)S(1)} %get-tuple-element.412), channel_id=1, source_target_pairs={{0,1},{2,3},{4,5},{6,7},{8,9},{10,11},{12,13},{14,15},{16,17},{18,... | collective-permute-start | bytes 122888 | tf_op jit(solution)/shard_map/ppermute | solution.py:52
  48.6 4.2 %collective-permute-done.7 = f32[10,1,8,128]{3,2,1,0:T(8,128)S(1)} collective-permute-done((f32[10,1,8,128]{3,2,1,0:T(8,128)S(1)}, f32[10,1,8,128]{3,2,1,0:T(8,128)S(1)}, u32[]{:S(2)}, u32[]{:S(2)}) %collective-permute-start.7) | collective-permute-done | bytes 40992 | tf_op jit(solution)/shard_map/ppermute | solution.py:54
  90.1 161.5 %while.15 = (s32[]{:T(128)}, f32[3,12,12,132]{3,2,1,0:T(8,128)S(1)}, f32[4,4,6,128]{3,1,0,2:T(4,128)S(1)}, s32[4,4,128]{2,1,0:T(4,128)}, pred[4,4,128]{2,1,0:T(4...) while((s32[]{:T(128)}, ...), condition=%wide.region_9.10_spmd, body=%wide.region_0.9_spmd.sunk | while | flops 64692984 | bytes 2140945 | solution.py:236
  106.6 5.5 %dynamic_update_slice.47 = f32[3,12,12,132]{3,2,1,0:T(8,128)S(1)} dynamic-update-slice(f32[3,12,12,132]{3,2,1,0:T(8,128)S(1)} %get-tuple-element.609, f32[3,12,12,12]{3,2,1,0:T(8,128)S(1)} %convolution_add_fusion.8, s32[]{:T(128)} %constant.667.clone.1..sunk, s32[]{:T(128)} %constant.667.clone.1..sunk, s32[]{:T(128)} %constant.667.clone.1..sunk, s32[]{:T(128)S(6)} %select_n.1233) | dynamic-update-slice | bytes 41476 | tf_op jit(solution)/shard_map/while/body/eval_jaxpr/dynamic_update_slice | solution.py:230
  112.7 5.5 %dynamic_update_slice.48 = f32[3,12,12,132]{3,2,1,0:T(8,128)S(1)} dynamic-update-slice(f32[3,12,12,132]{3,2,1,0:T(8,128)S(1)} %dynamic_update_slice.47, f32[3,12,12,12]{3,2,1,0:T(8,128)S(1)} %convolution_add_fusion.9, s32[]{:T(128)} %constant.667.clone.1..sunk, s32[]{:T(128)} %constant.667.clone.1..sunk, s32[]{:T(128)} %constant.667.clone.1..sunk, s32[]{:T(128)S(6)} %select_n.1236) | dynamic-update-slice | bytes 41476 | tf_op jit(solution)/shard_map/while/body/eval_jaxpr/dynamic_update_slice | solution.py:230
  118.8 5.5 %dynamic_update_slice.49 = f32[3,12,12,132]{3,2,1,0:T(8,128)S(1)} dynamic-update-slice(f32[3,12,12,132]{3,2,1,0:T(8,128)S(1)} %dynamic_update_slice.48, f32[3,12,12,12]{3,2,1,0:T(8,128)S(1)} %convolution_add_fusion.10, s32[]{:T(128)} %constant.667.clone.1..sunk, s32[]{:T(128)} %constant.667.clone.1..sunk, s32[]{:T(128)} %constant.667.clone.1..sunk, s32[]{:T(128)S(6)} %select_n.1262) | dynamic-update-slice | bytes 41476 | tf_op jit(solution)/shard_map/while/body/eval_jaxpr/dynamic_update_slice | solution.py:230
  124.8 5.5 %dynamic_update_slice.50 = f32[3,12,12,132]{3,2,1,0:T(8,128)S(1)} dynamic-update-slice(f32[3,12,12,132]{3,2,1,0:T(8,128)S(1)} %dynamic_update_slice.49, f32[3,12,12,12]{3,2,1,0:T(8,128)S(1)} %convolution_add_fusion.11, s32[]{:T(128)} %constant.667.clone.1..sunk, s32[]{:T(128)} %constant.667.clone.1..sunk, s32[]{:T(128)} %constant.667.clone.1..sunk, s32[]{:T(128)S(6)} %select_n.1261) | dynamic-update-slice | bytes 41476 | tf_op jit(solution)/shard_map/while/body/eval_jaxpr/dynamic_update_slice | solution.py:230
  147.0 5.5 %dynamic_update_slice.47 = f32[3,12,12,132]{3,2,1,0:T(8,128)S(1)} dynamic-update-slice(f32[3,12,12,132]{3,2,1,0:T(8,128)S(1)} %get-tuple-element.609, f32[3,12,12,12]{3,2,1,0:T(8,128)S(1)} %convolution_add_fusion.8, s32[]{:T(128)} %constant.667.clone.1..sunk, s32[]{:T(128)} %constant.667.clone.1..sunk, s32[]{:T(128)} %constant.667.clone.1..sunk, s32[]{:T(128)S(6)} %select_n.1233) | dynamic-update-slice | bytes 41476 | tf_op jit(solution)/shard_map/while/body/eval_jaxpr/dynamic_update_slice | solution.py:230
  153.1 5.5 %dynamic_update_slice.48 = f32[3,12,12,132]{3,2,1,0:T(8,128)S(1)} dynamic-update-slice(f32[3,12,12,132]{3,2,1,0:T(8,128)S(1)} %dynamic_update_slice.47, f32[3,12,12,12]{3,2,1,0:T(8,128)S(1)} %convolution_add_fusion.9, s32[]{:T(128)} %constant.667.clone.1..sunk, s32[]{:T(128)} %constant.667.clone.1..sunk, s32[]{:T(128)} %constant.667.clone.1..sunk, s32[]{:T(128)S(6)} %select_n.1236) | dynamic-update-slice | bytes 41476 | tf_op jit(solution)/shard_map/while/body/eval_jaxpr/dynamic_update_slice | solution.py:230
  159.1 5.5 %dynamic_update_slice.49 = f32[3,12,12,132]{3,2,1,0:T(8,128)S(1)} dynamic-update-slice(f32[3,12,12,132]{3,2,1,0:T(8,128)S(1)} %dynamic_update_slice.48, f32[3,12,12,12]{3,2,1,0:T(8,128)S(1)} %convolution_add_fusion.10, s32[]{:T(128)} %constant.667.clone.1..sunk, s32[]{:T(128)} %constant.667.clone.1..sunk, s32[]{:T(128)} %constant.667.clone.1..sunk, s32[]{:T(128)S(6)} %select_n.1262) | dynamic-update-slice | bytes 41476 | tf_op jit(solution)/shard_map/while/body/eval_jaxpr/dynamic_update_slice | solution.py:230
  165.2 5.5 %dynamic_update_slice.50 = f32[3,12,12,132]{3,2,1,0:T(8,128)S(1)} dynamic-update-slice(f32[3,12,12,132]{3,2,1,0:T(8,128)S(1)} %dynamic_update_slice.49, f32[3,12,12,12]{3,2,1,0:T(8,128)S(1)} %convolution_add_fusion.11, s32[]{:T(128)} %constant.667.clone.1..sunk, s32[]{:T(128)} %constant.667.clone.1..sunk, s32[]{:T(128)} %constant.667.clone.1..sunk, s32[]{:T(128)S(6)} %select_n.1261) | dynamic-update-slice | bytes 41476 | tf_op jit(solution)/shard_map/while/body/eval_jaxpr/dynamic_update_slice | solution.py:230
  187.4 5.5 %dynamic_update_slice.47 = f32[3,12,12,132]{3,2,1,0:T(8,128)S(1)} dynamic-update-slice(f32[3,12,12,132]{3,2,1,0:T(8,128)S(1)} %get-tuple-element.609, f32[3,12,12,12]{3,2,1,0:T(8,128)S(1)} %convolution_add_fusion.8, s32[]{:T(128)} %constant.667.clone.1..sunk, s32[]{:T(128)} %constant.667.clone.1..sunk, s32[]{:T(128)} %constant.667.clone.1..sunk, s32[]{:T(128)S(6)} %select_n.1233) | dynamic-update-slice | bytes 41476 | tf_op jit(solution)/shard_map/while/body/eval_jaxpr/dynamic_update_slice | solution.py:230
  193.5 5.5 %dynamic_update_slice.48 = f32[3,12,12,132]{3,2,1,0:T(8,128)S(1)} dynamic-update-slice(f32[3,12,12,132]{3,2,1,0:T(8,128)S(1)} %dynamic_update_slice.47, f32[3,12,12,12]{3,2,1,0:T(8,128)S(1)} %convolution_add_fusion.9, s32[]{:T(128)} %constant.667.clone.1..sunk, s32[]{:T(128)} %constant.667.clone.1..sunk, s32[]{:T(128)} %constant.667.clone.1..sunk, s32[]{:T(128)S(6)} %select_n.1236) | dynamic-update-slice | bytes 41476 | tf_op jit(solution)/shard_map/while/body/eval_jaxpr/dynamic_update_slice | solution.py:230
  199.5 5.5 %dynamic_update_slice.49 = f32[3,12,12,132]{3,2,1,0:T(8,128)S(1)} dynamic-update-slice(f32[3,12,12,132]{3,2,1,0:T(8,128)S(1)} %dynamic_update_slice.48, f32[3,12,12,12]{3,2,1,0:T(8,128)S(1)} %convolution_add_fusion.10, s32[]{:T(128)} %constant.667.clone.1..sunk, s32[]{:T(128)} %constant.667.clone.1..sunk, s32[]{:T(128)} %constant.667.clone.1..sunk, s32[]{:T(128)S(6)} %select_n.1262) | dynamic-update-slice | bytes 41476 | tf_op jit(solution)/shard_map/while/body/eval_jaxpr/dynamic_update_slice | solution.py:230
  205.6 5.5 %dynamic_update_slice.50 = f32[3,12,12,132]{3,2,1,0:T(8,128)S(1)} dynamic-update-slice(f32[3,12,12,132]{3,2,1,0:T(8,128)S(1)} %dynamic_update_slice.49, f32[3,12,12,12]{3,2,1,0:T(8,128)S(1)} %convolution_add_fusion.11, s32[]{:T(128)} %constant.667.clone.1..sunk, s32[]{:T(128)} %constant.667.clone.1..sunk, s32[]{:T(128)} %constant.667.clone.1..sunk, s32[]{:T(128)S(6)} %select_n.1261) | dynamic-update-slice | bytes 41476 | tf_op jit(solution)/shard_map/while/body/eval_jaxpr/dynamic_update_slice | solution.py:230
  227.8 5.5 %dynamic_update_slice.47 = f32[3,12,12,132]{3,2,1,0:T(8,128)S(1)} dynamic-update-slice(f32[3,12,12,132]{3,2,1,0:T(8,128)S(1)} %get-tuple-element.609, f32[3,12,12,12]{3,2,1,0:T(8,128)S(1)} %convolution_add_fusion.8, s32[]{:T(128)} %constant.667.clone.1..sunk, s32[]{:T(128)} %constant.667.clone.1..sunk, s32[]{:T(128)} %constant.667.clone.1..sunk, s32[]{:T(128)S(6)} %select_n.1233) | dynamic-update-slice | bytes 41476 | tf_op jit(solution)/shard_map/while/body/eval_jaxpr/dynamic_update_slice | solution.py:230
  233.8 5.5 %dynamic_update_slice.48 = f32[3,12,12,132]{3,2,1,0:T(8,128)S(1)} dynamic-update-slice(f32[3,12,12,132]{3,2,1,0:T(8,128)S(1)} %dynamic_update_slice.47, f32[3,12,12,12]{3,2,1,0:T(8,128)S(1)} %convolution_add_fusion.9, s32[]{:T(128)} %constant.667.clone.1..sunk, s32[]{:T(128)} %constant.667.clone.1..sunk, s32[]{:T(128)} %constant.667.clone.1..sunk, s32[]{:T(128)S(6)} %select_n.1236) | dynamic-update-slice | bytes 41476 | tf_op jit(solution)/shard_map/while/body/eval_jaxpr/dynamic_update_slice | solution.py:230
  239.9 5.5 %dynamic_update_slice.49 = f32[3,12,12,132]{3,2,1,0:T(8,128)S(1)} dynamic-update-slice(f32[3,12,12,132]{3,2,1,0:T(8,128)S(1)} %dynamic_update_slice.48, f32[3,12,12,12]{3,2,1,0:T(8,128)S(1)} %convolution_add_fusion.10, s32[]{:T(128)} %constant.667.clone.1..sunk, s32[]{:T(128)} %constant.667.clone.1..sunk, s32[]{:T(128)} %constant.667.clone.1..sunk, s32[]{:T(128)S(6)} %select_n.1262) | dynamic-update-slice | bytes 41476 | tf_op jit(solution)/shard_map/while/body/eval_jaxpr/dynamic_update_slice | solution.py:230
  246.0 5.5 %dynamic_update_slice.50 = f32[3,12,12,132]{3,2,1,0:T(8,128)S(1)} dynamic-update-slice(f32[3,12,12,132]{3,2,1,0:T(8,128)S(1)} %dynamic_update_slice.49, f32[3,12,12,12]{3,2,1,0:T(8,128)S(1)} %convolution_add_fusion.11, s32[]{:T(128)} %constant.667.clone.1..sunk, s32[]{:T(128)} %constant.667.clone.1..sunk, s32[]{:T(128)} %constant.667.clone.1..sunk, s32[]{:T(128)S(6)} %select_n.1261) | dynamic-update-slice | bytes 41476 | tf_op jit(solution)/shard_map/while/body/eval_jaxpr/dynamic_update_slice | solution.py:230
  252.0 3.8 %collective-permute-start.19 = (f32[3,12,12,2]{3,2,1,0:T(8,128)S(1)}, f32[3,12,12,2]{3,2,1,0:T(8,128)S(1)}, u32[]{:S(2)}, u32[]{:S(2)}) collective-permute-start(f32[3,12,12,2]{3,2,1,0:T(8,128)S(1)} %get-tuple-element.373), channel_id=1, source_target_pairs={{8,0},{16,8},{24,16},{0,24},{9,1},{17,9},{25,17},{1,25},{10,2},{18... | collective-permute-start | bytes 10376 | tf_op jit(solution)/shard_map/ppermute | solution.py:54
  257.0 3.8 %collective-permute-start.25 = (f32[6,3,3,1,2,128]{5,0,4,3,2,1:T(8,128)S(1)}, f32[6,3,3,1,2,128]{5,0,4,3,2,1:T(8,128)S(1)}, u32[]{:S(2)}, u32[]{:S(2)}) collective-permute-start(f32[6,3,3,1,2,128]{5,0,4,3,2,1:T(8,128)S(1)} %get-tuple-element.418), channel_id=1, source_target_pairs={{8,0},{16,8},{24,16},{0,24},{9,1},{17,9},{25,17},{1,25},{10,2},{18... | collective-permute-start | bytes 165896 | tf_op jit(solution)/shard_map/ppermute | solution.py:54
  263.7 4.2 %collective-permute-done.19 = f32[3,12,12,2]{3,2,1,0:T(8,128)S(1)} collective-permute-done((f32[3,12,12,2]{3,2,1,0:T(8,128)S(1)}, f32[3,12,12,2]{3,2,1,0:T(8,128)S(1)}, u32[]{:S(2)}, u32[]{:S(2)}) %collective-permute-start.19) | collective-permute-done | bytes 3488 | tf_op jit(solution)/shard_map/ppermute | solution.py:54
  282.6 4.8 %collective-permute-done.28 = f32[6,1,5,5,2,128]{5,0,4,3,2,1:T(8,128)S(1)} collective-permute-done((f32[6,1,5,5,2,128]{5,0,4,3,2,1:T(8,128)S(1)}, f32[6,1,5,5,2,128]{5,0,4,3,2,1:T(8,128)S(1)}, u32[]{:S(2)}, u32[]{:S(2)}) %collective-permute-start.28) | collective-permute-done | bytes 153632 | tf_op jit(solution)/shard_map/ppermute | solution.py:52
  287.4 4.4 %collective-permute-done.29 = f32[6,1,5,5,2,128]{5,0,4,3,2,1:T(8,128)S(1)} collective-permute-done((f32[6,1,5,5,2,128]{5,0,4,3,2,1:T(8,128)S(1)}, f32[6,1,5,5,2,128]{5,0,4,3,2,1:T(8,128)S(1)}, u32[]{:S(2)}, u32[]{:S(2)}) %collective-permute-start.29) | collective-permute-done | bytes 153632 | tf_op jit(solution)/shard_map/ppermute | solution.py:54
  (388 shorter events, 129.0 us)
Async XLA Ops:
  10.7 9.1 %collective-permute-start = (f32[10,1,8,128]{3,2,1,0:T(8,128)S(1)}, f32[10,1,8,128]{3,2,1,0:T(8,128)S(1)}, u32[]{:S(2)}, u32[]{:S(2)}) collective-permute-start(f32[10,1,8,128]{3,2,1,0:T(8,128)S(1)} %get-tuple-element.412), channel_id=1, source_target_pairs={{0,1},{2,3},{4,5},{6,7},{8,9},{10,11},{12,13},{14,15},{16,17},{18,... | collective-permute-start | bytes 122888 | tf_op jit(solution)/shard_map/ppermute | solution.py:52
  15.6 5.9 %collective-permute-start.1 = (f32[10,1,8,128]{3,2,1,0:T(8,128)S(1)}, f32[10,1,8,128]{3,2,1,0:T(8,128)S(1)}, u32[]{:S(2)}, u32[]{:S(2)}) collective-permute-start(f32[10,1,8,128]{3,2,1,0:T(8,128)S(1)} %get-tuple-element.411), channel_id=1, source_target_pairs={{1,0},{3,2},{5,4},{7,6},{9,8},{11,10},{13,12},{15,14},{17,16},{19,... | collective-permute-start | bytes 122888 | tf_op jit(solution)/shard_map/ppermute | solution.py:54
  21.6 3.6 %collective-permute-start.2 = (f32[10,10,1,128]{3,2,1,0:T(1,128)S(1)}, f32[10,10,1,128]{3,2,1,0:T(1,128)S(1)}, u32[]{:S(2)}, u32[]{:S(2)}) collective-permute-start(f32[10,10,1,128]{3,2,1,0:T(1,128)S(1)} %get-tuple-element.403), channel_id=1, source_target_pairs={{0,2},{2,4},{4,6},{6,0},{1,3},{3,5},{5,7},{7,1},{8,10},{10,12},{12... | collective-permute-start | bytes 153608 | tf_op jit(solution)/shard_map/ppermute | solution.py:52
  26.5 6.2 %collective-permute-start.4 = (f32[10,10,10,1]{2,3,1,0:T(1,128)S(1)}, f32[10,10,10,1]{2,3,1,0:T(1,128)S(1)}, u32[]{:S(2)}, u32[]{:S(2)}) collective-permute-start(f32[10,10,10,1]{2,3,1,0:T(1,128)S(1)} %copy.108), channel_id=1, source_target_pairs={{0,8},{8,16},{16,24},{24,0},{1,9},{9,17},{17,25},{25,1},{2,10},{10... | collective-permute-start | bytes 12008 | tf_op jit(solution)/shard_map/ppermute | solution.py:52
  28.8 5.1 %collective-permute-start.5 = (f32[10,10,10,1]{2,3,1,0:T(1,128)S(1)}, f32[10,10,10,1]{2,3,1,0:T(1,128)S(1)}, u32[]{:S(2)}, u32[]{:S(2)}) collective-permute-start(f32[10,10,10,1]{2,3,1,0:T(1,128)S(1)} %copy.109), channel_id=1, source_target_pairs={{8,0},{16,8},{24,16},{0,24},{9,1},{17,9},{25,17},{1,25},{10,2},{18... | collective-permute-start | bytes 12008 | tf_op jit(solution)/shard_map/ppermute | solution.py:54
  44.0 4.6 %collective-permute-start.6 = (f32[10,1,8,128]{3,2,1,0:T(8,128)S(1)}, f32[10,1,8,128]{3,2,1,0:T(8,128)S(1)}, u32[]{:S(2)}, u32[]{:S(2)}) collective-permute-start(f32[10,1,8,128]{3,2,1,0:T(8,128)S(1)} %get-tuple-element.409), channel_id=1, source_target_pairs={{0,1},{2,3},{4,5},{6,7},{8,9},{10,11},{12,13},{14,15},{16,17},{18,... | collective-permute-start | bytes 122888 | tf_op jit(solution)/shard_map/ppermute | solution.py:52
  47.0 5.9 %collective-permute-start.7 = (f32[10,1,8,128]{3,2,1,0:T(8,128)S(1)}, f32[10,1,8,128]{3,2,1,0:T(8,128)S(1)}, u32[]{:S(2)}, u32[]{:S(2)}) collective-permute-start(f32[10,1,8,128]{3,2,1,0:T(8,128)S(1)} %get-tuple-element.410), channel_id=1, source_target_pairs={{1,0},{3,2},{5,4},{7,6},{9,8},{11,10},{13,12},{15,14},{17,16},{19,... | collective-permute-start | bytes 122888 | tf_op jit(solution)/shard_map/ppermute | solution.py:54
  58.4 6.3 %collective-permute-start.10 = (f32[10,10,10,1]{2,3,1,0:T(1,128)}, f32[10,10,10,1]{2,3,1,0:T(1,128)S(1)}, u32[]{:S(2)}, u32[]{:S(2)}) collective-permute-start(f32[10,10,10,1]{2,3,1,0:T(1,128)} %copy.110), channel_id=1, source_target_pairs={{0,8},{8,16},{16,24},{24,0},{1,9},{9,17},{17,25},{25,1},{2,10},{10... | collective-permute-start | bytes 12008 | tf_op jit(solution)/shard_map/ppermute | solution.py:52
  60.0 5.8 %collective-permute-start.11 = (f32[10,10,10,1]{2,3,1,0:T(1,128)S(1)}, f32[10,10,10,1]{2,3,1,0:T(1,128)}, u32[]{:S(2)}, u32[]{:S(2)}) collective-permute-start(f32[10,10,10,1]{2,3,1,0:T(1,128)S(1)} %copy.111), channel_id=1, source_target_pairs={{8,0},{16,8},{24,16},{0,24},{9,1},{17,9},{25,17},{1,25},{10,2},{18... | collective-permute-start | bytes 12008 | tf_op jit(solution)/shard_map/ppermute | solution.py:54
  70.4 7.5 %collective-permute-start.12 = (f32[3,8,8,2]{3,2,1,0:T(8,128)S(1)}, f32[3,8,8,2]{3,2,1,0:T(8,128)S(1)}, u32[]{:S(2)}, u32[]{:S(2)}) collective-permute-start(f32[3,8,8,2]{3,2,1,0:T(8,128)S(1)} %get-tuple-element.421), channel_id=1, source_target_pairs={{0,8},{8,16},{16,24},{24,0},{1,9},{9,17},{17,25},{25,1},{2,10},{10... | collective-permute-start | bytes 4616 | tf_op jit(solution)/shard_map/ppermute | solution.py:52
  71.4 6.7 %collective-permute-start.13 = (f32[3,8,8,2]{3,2,1,0:T(8,128)S(1)}, f32[3,8,8,2]{3,2,1,0:T(8,128)S(1)}, u32[]{:S(2)}, u32[]{:S(2)}) collective-permute-start(f32[3,8,8,2]{3,2,1,0:T(8,128)S(1)} %get-tuple-element.422), channel_id=1, source_target_pairs={{8,0},{16,8},{24,16},{0,24},{9,1},{17,9},{25,17},{1,25},{10,2},{18... | collective-permute-start | bytes 4616 | tf_op jit(solution)/shard_map/ppermute | solution.py:54
  82.2 5.5 %collective-permute-start.16 = (f32[3,2,12,132]{3,2,1,0:T(8,128)S(1)}, f32[3,2,12,132]{3,2,1,0:T(8,128)S(1)}, u32[]{:S(2)}, u32[]{:S(2)}) collective-permute-start(f32[3,2,12,132]{3,2,1,0:T(8,128)S(1)} %get-tuple-element.405), channel_id=1, source_target_pairs={{0,1},{1,0},{2,3},{3,2},{4,5},{5,4},{6,7},{7,6},{8,9},{9,8},{10,11... | collective-permute-start | bytes 114056 | tf_op jit(solution)/shard_map/ppermute | solution.py:52
  82.2 7.5 %collective-permute-start.17 = (f32[3,2,12,132]{3,2,1,0:T(8,128)S(1)}, f32[3,2,12,132]{3,2,1,0:T(8,128)S(1)}, u32[]{:S(2)}, u32[]{:S(2)}) collective-permute-start(f32[3,2,12,132]{3,2,1,0:T(8,128)S(1)} %get-tuple-element.406), channel_id=1, source_target_pairs={{1,0},{0,1},{3,2},{2,3},{5,4},{4,5},{7,6},{6,7},{9,8},{8,9},{11,10... | collective-permute-start | bytes 114056 | tf_op jit(solution)/shard_map/ppermute | solution.py:54
  251.9 11.8 %collective-permute-start.18 = (f32[3,12,12,2]{3,2,1,0:T(8,128)S(1)}, f32[3,12,12,2]{3,2,1,0:T(8,128)S(1)}, u32[]{:S(2)}, u32[]{:S(2)}) collective-permute-start(f32[3,12,12,2]{3,2,1,0:T(8,128)S(1)} %get-tuple-element.372), channel_id=1, source_target_pairs={{0,8},{8,16},{16,24},{24,0},{1,9},{9,17},{17,25},{25,1},{2,10},{10... | collective-permute-start | bytes 10376 | tf_op jit(solution)/shard_map/ppermute | solution.py:52
  252.0 15.9 %collective-permute-start.19 = (f32[3,12,12,2]{3,2,1,0:T(8,128)S(1)}, f32[3,12,12,2]{3,2,1,0:T(8,128)S(1)}, u32[]{:S(2)}, u32[]{:S(2)}) collective-permute-start(f32[3,12,12,2]{3,2,1,0:T(8,128)S(1)} %get-tuple-element.373), channel_id=1, source_target_pairs={{8,0},{16,8},{24,16},{0,24},{9,1},{17,9},{25,17},{1,25},{10,2},{18... | collective-permute-start | bytes 10376 | tf_op jit(solution)/shard_map/ppermute | solution.py:54
  256.9 17.7 %collective-permute-start.24 = (f32[6,3,3,1,2,128]{5,0,4,3,2,1:T(8,128)S(1)}, f32[6,3,3,1,2,128]{5,0,4,3,2,1:T(8,128)S(1)}, u32[]{:S(2)}, u32[]{:S(2)}) collective-permute-start(f32[6,3,3,1,2,128]{5,0,4,3,2,1:T(8,128)S(1)} %get-tuple-element.417), channel_id=1, source_target_pairs={{0,8},{8,16},{16,24},{24,0},{1,9},{9,17},{17,25},{25,1},{2,10},{10... | collective-permute-start | bytes 165896 | tf_op jit(solution)/shard_map/ppermute | solution.py:52
  257.0 17.7 %collective-permute-start.25 = (f32[6,3,3,1,2,128]{5,0,4,3,2,1:T(8,128)S(1)}, f32[6,3,3,1,2,128]{5,0,4,3,2,1:T(8,128)S(1)}, u32[]{:S(2)}, u32[]{:S(2)}) collective-permute-start(f32[6,3,3,1,2,128]{5,0,4,3,2,1:T(8,128)S(1)} %get-tuple-element.418), channel_id=1, source_target_pairs={{8,0},{16,8},{24,16},{0,24},{9,1},{17,9},{25,17},{1,25},{10,2},{18... | collective-permute-start | bytes 165896 | tf_op jit(solution)/shard_map/ppermute | solution.py:54
  268.2 3.8 %collective-permute-start.20 = (f32[3,12,2,136]{3,2,1,0:T(2,128)S(1)}, f32[3,12,2,136]{3,2,1,0:T(2,128)S(1)}, u32[]{:S(2)}, u32[]{:S(2)}) collective-permute-start(f32[3,12,2,136]{3,2,1,0:T(2,128)S(1)} %get-tuple-element.357), channel_id=1, source_target_pairs={{0,2},{2,4},{4,6},{6,0},{1,3},{3,5},{5,7},{7,1},{8,10},{10,12},{12... | collective-permute-start | bytes 117512 | tf_op jit(solution)/shard_map/ppermute | solution.py:52
  272.2 5.0 %collective-permute-start.22 = (f32[3,2,16,136]{3,2,1,0:T(8,128)S(1)}, f32[3,2,16,136]{3,2,1,0:T(8,128)S(1)}, u32[]{:S(2)}, u32[]{:S(2)}) collective-permute-start(f32[3,2,16,136]{3,2,1,0:T(8,128)S(1)} %get-tuple-element.355), channel_id=1, source_target_pairs={{0,1},{1,0},{2,3},{3,2},{4,5},{5,4},{6,7},{7,6},{8,9},{9,8},{10,11... | collective-permute-start | bytes 156680 | tf_op jit(solution)/shard_map/ppermute | solution.py:52
  272.3 7.0 %collective-permute-start.23 = (f32[3,2,16,136]{3,2,1,0:T(8,128)S(1)}, f32[3,2,16,136]{3,2,1,0:T(8,128)S(1)}, u32[]{:S(2)}, u32[]{:S(2)}) collective-permute-start(f32[3,2,16,136]{3,2,1,0:T(8,128)S(1)} %get-tuple-element.356), channel_id=1, source_target_pairs={{1,0},{0,1},{3,2},{2,3},{5,4},{4,5},{7,6},{6,7},{9,8},{8,9},{11,10... | collective-permute-start | bytes 156680 | tf_op jit(solution)/shard_map/ppermute | solution.py:54
  274.7 4.9 %collective-permute-start.26 = (f32[6,3,1,5,2,128]{5,0,4,3,2,1:T(8,128)S(1)}, f32[6,3,1,5,2,128]{5,0,4,3,2,1:T(8,128)S(1)}, u32[]{:S(2)}, u32[]{:S(2)}) collective-permute-start(f32[6,3,1,5,2,128]{5,0,4,3,2,1:T(8,128)S(1)} %get-tuple-element.407), channel_id=1, source_target_pairs={{0,2},{2,4},{4,6},{6,0},{1,3},{3,5},{5,7},{7,1},{8,10},{10,12},{12... | collective-permute-start | bytes 276488 | tf_op jit(solution)/shard_map/ppermute | solution.py:52
  275.9 3.7 %collective-permute-start.27 = (f32[6,3,1,5,2,128]{5,0,4,3,2,1:T(8,128)S(1)}, f32[6,3,1,5,2,128]{5,0,4,3,2,1:T(8,128)S(1)}, u32[]{:S(2)}, u32[]{:S(2)}) collective-permute-start(f32[6,3,1,5,2,128]{5,0,4,3,2,1:T(8,128)S(1)} %get-tuple-element.408), channel_id=1, source_target_pairs={{2,0},{4,2},{6,4},{0,6},{3,1},{5,3},{7,5},{1,7},{10,8},{12,10},{14... | collective-permute-start | bytes 276488 | tf_op jit(solution)/shard_map/ppermute | solution.py:54
  279.7 7.7 %collective-permute-start.28 = (f32[6,1,5,5,2,128]{5,0,4,3,2,1:T(8,128)S(1)}, f32[6,1,5,5,2,128]{5,0,4,3,2,1:T(8,128)S(1)}, u32[]{:S(2)}, u32[]{:S(2)}) collective-permute-start(f32[6,1,5,5,2,128]{5,0,4,3,2,1:T(8,128)S(1)} %get-tuple-element.370), channel_id=1, source_target_pairs={{0,1},{1,0},{2,3},{3,2},{4,5},{5,4},{6,7},{7,6},{8,9},{9,8},{10,11... | collective-permute-start | bytes 460808 | tf_op jit(solution)/shard_map/ppermute | solution.py:52
  280.1 11.7 %collective-permute-start.29 = (f32[6,1,5,5,2,128]{5,0,4,3,2,1:T(8,128)S(1)}, f32[6,1,5,5,2,128]{5,0,4,3,2,1:T(8,128)S(1)}, u32[]{:S(2)}, u32[]{:S(2)}) collective-permute-start(f32[6,1,5,5,2,128]{5,0,4,3,2,1:T(8,128)S(1)} %get-tuple-element.371), channel_id=1, source_target_pairs={{1,0},{0,1},{3,2},{2,3},{5,4},{4,5},{7,6},{6,7},{9,8},{8,9},{11,10... | collective-permute-start | bytes 460808 | tf_op jit(solution)/shard_map/ppermute | solution.py:54
  (42 other events, 175.6 us)
where the time goes:
time: 293 us
  local copies, waits for them, and re-layouts  110 us (38%)
  starting transfers between devices  44.9 us (15%)
  loops' own time  43.1 us (15%)
  waiting for transfers between devices  42.6 us (15%)
  other arithmetic  33.8 us (12%)
  matrix products  16.3 us (6%)
    dynamic_update_slice x16, local copies, waits for them, and re-layouts, droplet_group(): lax.dynamic_update_slice(spread, lax.dynamic_slice(spread, corner, (3, ed...  88.7 us
    another operation x1, loops' own time, local(): lax.scan(droplet_group, jnp.zeros_like(velocity_ext), (homes, speeds, fra...  43.1 us
    ppermute x15, starting transfers between devices, with_halo(): lax.ppermute(head, axis, [((i + 1) % count, i) for i in range(ends)])  30.4 us
    ppermute x15, waiting for transfers between devices, with_halo(): lax.ppermute(tail, axis, [(i, (i + 1) % count) for i in range(ends)])  22.7 us
    ppermute x15, waiting for transfers between devices, with_halo(): lax.ppermute(head, axis, [((i + 1) % count, i) for i in range(ends)])  19.9 us
    unnamed x18, other arithmetic  15 us
    ppermute x15, starting transfers between devices, with_halo(): lax.ppermute(tail, axis, [(i, (i + 1) % count) for i in range(ends)])  14.5 us
    dot_general x16, matrix products, droplet_group(): jnp.dot(tile.reshape(3 * edge * edge, edge), weight_x.T, precision=highest)  8.3 us
  transfers between devices with their start and end apart: 30, of which 21 were waited for; matrix products, arithmetic and copies ran while one was open for 4% of the time, Pallas kernels for 0%

commit v1 on v0

--- a/solution.py
+++ b/solution.py
@@ -1,9 +1,12 @@
+import functools
 import math
 
 import jax
 import jax.numpy as jnp
 import numpy as np
 from jax import lax
+from jax.experimental import pallas as pl
+from jax.experimental.pallas import tpu as pltpu
 from jax.sharding import PartitionSpec as P
 
 TILE = 8
@@ -167,6 +170,137 @@
     return core + jnp.pad(lower, low_pad) + jnp.pad(upper, high_pad)
 
 
+def phis(frac):
+    angle = frac * (0.5 * math.pi)
+    sine = 0.25 * jnp.sin(angle)
+    cosine = 0.25 * jnp.cos(angle)
+    return (0.25 - sine, 0.25 + cosine, 0.25 + sine, 0.25 - cosine)
+
+
+def split(value):
+    high = value.astype(jnp.bfloat16)
+    return high, (value - high.astype(jnp.float32)).astype(jnp.bfloat16)
+
+
+def pick(step, parts):
+    value = jnp.where(step == 0, parts[0], 0.0)
+    for index in range(1, 4):
+        value = jnp.where(step == index, parts[index], value)
+    return value
+
+
+def dots(left, right, dims):
+    return lax.dot_general(left, right, (dims, ((), ())), preferred_element_type=jnp.float32)
+
+
+def droplet_body(size, counts_ref, vel_ref, speed_ref, frac_ref, home_ref, spread_ref, state_ref,
+                 vel_high, vel_low, row_high, row_low, push_high, push_low, plane_ref):
+    depth, height, width = size
+    blocks = home_ref.shape[0]
+    layers, rows, lanes = depth + 3, height + 8, width + 128
+    high, low = split(vel_ref[...].reshape(3 * layers * rows, lanes))
+    vel_high[...] = high
+    vel_low[...] = low
+    row_high[...] = jnp.zeros_like(row_high)
+    row_low[...] = jnp.zeros_like(row_low)
+    used = width + 16
+    span_x = lax.broadcasted_iota(jnp.int32, (used, 128), 0) + 1
+    span_y = lax.broadcasted_iota(jnp.int32, (rows, 128), 0)
+    span_y = jnp.where(span_y >= height + 4, span_y - rows, span_y) + 1
+    span_z = lax.broadcasted_iota(jnp.int32, (layers, 128), 0)
+    last = lax.broadcasted_iota(jnp.int32, (16, 128), 0) == 15
+    slots = lax.broadcasted_iota(jnp.int32, (1, 128), 1)
+
+    def pair(number):
+        for half in range(2):
+            block = 2 * number + half
+            side = pl.ds(half * 128, 128)
+            cell = home_ref[pl.ds(block, 1), :]
+            cell_x = cell & (width - 1) if width & (width - 1) == 0 else cell % width
+            cell_y = cell // width % height
+            cell_z = cell // (width * height)
+            part_x = phis(frac_ref[0, pl.ds(block, 1), :])
+            part_y = phis(frac_ref[1, pl.ds(block, 1), :])
+            part_z = phis(frac_ref[2, pl.ds(block, 1), :])
+            high, low = split(pick(span_x - cell_x, part_x))
+            row_high[0:used, side] = high
+            row_low[0:used, side] = low
+            high, low = split(jnp.where(last & (cell_x == 0), part_x[0], 0.0))
+            row_high[lanes - 16 : lanes, side] = high
+            row_low[lanes - 16 : lanes, side] = low
+            weight_y = pick(span_y - cell_y, part_y)
+            weight_z = pick(span_z - cell_z, part_z)
+            for layer in range(layers):
+                plane_ref[layer, :, side] = weight_y * weight_z[layer : layer + 1, :]
+        along_high = row_high[...]
+        along_low = row_low[...]
+        sums = (
+            dots(vel_high[...], along_high, ((1,), (0,)))
+            + dots(vel_low[...], along_high, ((1,), (0,)))
+            + dots(vel_high[...], along_low, ((1,), (0,)))
+        ).reshape(3, layers, rows, 256)
+        plane = plane_ref[...]
+        sampled = jnp.sum(jnp.sum(sums * plane[None], axis=1), axis=1)
+        for half in range(2):
+            block = 2 * number + half
+            live = slots < counts_ref[block]
+            for axis in range(3):
+                sample = sampled[axis : axis + 1, half * 128 : half * 128 + 128]
+                speed = speed_ref[axis, pl.ds(block, 1), :]
+                frac = frac_ref[axis, pl.ds(block, 1), :]
+                moved = speed + relax * (sample - speed)
+                push = jnp.where(live, couple * (moved - sample), 0.0)
+                state_ref[axis, pl.ds(block, 1), :] = jnp.where(live, moved, 0.0)
+                state_ref[3 + axis, pl.ds(block, 1), :] = jnp.where(live, frac + moved, 0.0)
+                high, low = split(
+                    (plane[:, :, half * 128 : half * 128 + 128] * push[None]).reshape(layers * rows, 128)
+                )
+                where = pl.ds(axis * layers * rows, layers * rows)
+                push_high[where, half * 128 : half * 128 + 128] = high
+                push_low[where, half * 128 : half * 128 + 128] = low
+        patch = (
+            dots(push_high[...], along_high, ((1,), (1,)))
+            + dots(push_low[...], along_high, ((1,), (1,)))
+            + dots(push_high[...], along_low, ((1,), (1,)))
+        ).reshape(3, layers, rows, lanes)
+        return patch
+
+    spread_ref[...] = pair(0)
+
+    def step(number, carry):
+        spread_ref[...] += pair(number)
+        return carry
+
+    lax.fori_loop(1, blocks // 2, step, 0)
+
+
+def droplets(velocity, drop_vel, drop_frac, home, counts, size):
+    depth, height, width = size
+    blocks = home.shape[0]
+    layers, rows, lanes = depth + 3, height + 8, width + 128
+    flat = 3 * layers * rows
+    vmem = pl.BlockSpec(memory_space=pltpu.VMEM)
+    return pl.pallas_call(
+        functools.partial(droplet_body, size),
+        out_shape=(
+            jax.ShapeDtypeStruct((3, layers, rows, lanes), jnp.float32),
+            jax.ShapeDtypeStruct((6, blocks, 128), jnp.float32),
+        ),
+        in_specs=[pl.BlockSpec(memory_space=pltpu.SMEM), vmem, vmem, vmem, vmem],
+        out_specs=(vmem, vmem),
+        scratch_shapes=[
+            pltpu.VMEM((flat, lanes), jnp.bfloat16),
+            pltpu.VMEM((flat, lanes), jnp.bfloat16),
+            pltpu.VMEM((lanes, 256), jnp.bfloat16),
+            pltpu.VMEM((lanes, 256), jnp.bfloat16),
+            pltpu.VMEM((flat, 256), jnp.bfloat16),
+            pltpu.VMEM((flat, 256), jnp.bfloat16),
+            pltpu.VMEM((layers, rows, 256), jnp.float32),
+        ],
+        compiler_params=pltpu.CompilerParams(vmem_limit_bytes=48 * 1024 * 1024),
+    )(counts, velocity, drop_vel, drop_frac, home)
+
+
 def local(pops, coarse_pops, interface, drop_vel, drop_frac, home, counts, dest):
     level = lax.axis_index("gz")
     levels = lax.axis_size("gz")
@@ -188,55 +322,23 @@
     )
     velocity_ext = jnp.where(keep, velocity_ext, 0.0)
     blocks = home.shape[0]
-    groups = blocks // 4
-    edge = TILE + 4
-    homes = home.reshape(groups, 4, 128)
-    speeds = jnp.moveaxis(drop_vel, 1, 0).reshape(groups, 4, 3, 128)
-    fracs = jnp.moveaxis(drop_frac, 1, 0).reshape(groups, 4, 3, 128)
-    slots = lax.broadcasted_iota(jnp.int32, (blocks, 128), 1)
-    lives = (slots < counts[:, None]).reshape(groups, 4, 128)
-
-    def droplet_group(spread, group):
-        group_homes, group_speeds, group_fracs, group_lives = group
-        results = []
-        for member in range(4):
-            cells = group_homes[member]
-            speed = group_speeds[member]
-            frac = group_fracs[member]
-            alive = group_lives[member][None, :]
-            first = cells[0]
-            start_x = first % width // TILE * TILE
-            start_y = first // width % height // TILE * TILE
-            start_z = first // (width * height) // TILE * TILE
-            weight_x = row_weights(cells % width - start_x, frac[0])
-            weight_y = row_weights(cells // width % height - start_y, frac[1])
-            weight_z = row_weights(cells // (width * height) - start_z, frac[2])
-            corner = (jnp.zeros((), jnp.int32), start_z, start_y, start_x)
-            tile = lax.dynamic_slice(velocity_ext, corner, (3, edge, edge, edge))
-            partial_value = jnp.dot(
-                tile.reshape(3 * edge * edge, edge), weight_x.T, precision=highest
-            )
-            partial_value = jnp.sum(
-                partial_value.reshape(3, edge, edge, 128) * weight_y.T[None, None, :, :], axis=2
-            )
-            sampled = jnp.sum(partial_value * weight_z.T[None, :, :], axis=1)
-            moved = speed + relax * (sampled - speed)
-            push = jnp.where(alive, couple * (moved - sampled), 0.0)
-            source = (
-                push[:, None, None, :] * weight_z.T[None, :, None, :] * weight_y.T[None, None, :, :]
-            )
-            patch = jnp.dot(source.reshape(3 * edge * edge, 128), weight_x, precision=highest)
-            patch = patch.reshape(3, edge, edge, edge)
-            spread = lax.dynamic_update_slice(
-                spread, lax.dynamic_slice(spread, corner, (3, edge, edge, edge)) + patch, corner
-            )
-            results.append(jnp.where(alive, jnp.concatenate([moved, frac + moved], axis=0), 0.0))
-        return (spread, jnp.stack(results))
-
-    spread, states = lax.scan(
-        droplet_group, jnp.zeros_like(velocity_ext), (homes, speeds, fracs, lives)
-    )
-    states = jnp.moveaxis(states.reshape(blocks, 6, 128), 0, 1)
+    circle = velocity_ext[:, 1:]
+    circle = jnp.pad(
+        jnp.concatenate([circle[:, :, 2:], jnp.zeros_like(circle[:, :, :5]), circle[:, :, 1:2]], axis=2),
+        ((0, 0), (0, 0), (0, 0), (0, 0)),
+    )
+    lanes = jnp.zeros(circle.shape[:3] + (125,), jnp.float32)
+    circle = jnp.concatenate([circle[..., 2:], lanes, circle[..., 1:2]], axis=3)
+    spread, states = droplets(
+        circle, drop_vel, drop_frac, home, counts, (depth, height, width)
+    )
+    spread = jnp.concatenate(
+        [jnp.zeros_like(spread[..., :1]), spread[..., -1:], spread[..., : width + 2]], axis=3
+    )
+    spread = jnp.concatenate(
+        [jnp.zeros_like(spread[:, :, :1]), spread[:, :, -1:], spread[:, :, : height + 2]], axis=2
+    )
+    spread = jnp.concatenate([jnp.zeros_like(spread[:, :1]), spread], axis=1)
     spread = jnp.where(keep, spread, 0.0)
     force_ext = with_halo(spread, (("gx", 3), ("gy", 2), ("gz", 1)), 2, True)
     force = fold(fold(fold(force_ext, 1, depth), 2, height), 3, width)

time: 293 us -> 147 us (0.50)
  local copies, waits for them, and re-layouts: 110 us -> 14.4 us
  loops' own time: 43.1 us -> 0 us
  matrix products: 16.3 us -> 0 us
  Pallas kernels: 0 us -> 9.85 us
  other arithmetic: 33.8 us -> 29.1 us
    dynamic_update_slice x20 -> x0, local copies, waits for them, and re-layouts: 88.8 us -> none  [the longest x16 88.7 us: droplet_group(): lax.dynamic_update_slice(spread, lax.dynamic_slice(spread, corner, (3, ed...]
    another operation x1 -> x0, loops' own time: 43.1 us -> none  [local(): lax.scan(droplet_group, jnp.zeros_like(velocity_ext), (homes, speeds, fra...]
    dot_general x32 -> x0, matrix products: 16.3 us -> none  [the longest x16 8.3 us: droplet_group(): jnp.dot(tile.reshape(3 * edge * edge, edge), weight_x.T, precision=highest)]
    pallas_call x0 -> x1, Pallas kernels: none -> 9.85 us  [droplets(): pl.pallas_call(functools.partial(droplet_body, size), out_shape=(jax.Shap...]
    sub x4 -> x0, local copies, waits for them, and re-layouts: 3.3 us -> none  [row_weights(): distance = span - 2 - offset[:, None] - frac[:, None]]
    unnamed x122 -> x118, local copies, waits for them, and re-layouts: 5.46 us -> 2.23 us
  transfers between devices with their start and end apart: 30 -> 30, of which waited for: 21 -> 20; matrix products, arithmetic and copies ran while one was open for 4% -> 8% of each run, Pallas kernels for 0% -> 0%
where the time goes in v1:
time: 147 us; the launch traced here: 146 us
  starting transfers between devices  45.5 us (31%)
  waiting for transfers between devices  45.4 us (31%)
  other arithmetic  29.1 us (20%)
  local copies, waits for them, and re-layouts  14.4 us (10%)
  Pallas kernels  9.85 us (7%)
  between operations  1.78 us (1%)
    ppermute x15, starting transfers between devices, with_halo(): lax.ppermute(head, axis, [((i + 1) % count, i) for i in range(ends)])  30 us
    ppermute x15, waiting for transfers between devices, with_halo(): lax.ppermute(tail, axis, [(i, (i + 1) % count) for i in range(ends)])  24.5 us
    ppermute x15, waiting for transfers between devices, with_halo(): lax.ppermute(head, axis, [((i + 1) % count, i) for i in range(ends)])  21 us
    ppermute x15, starting transfers between devices, with_halo(): lax.ppermute(tail, axis, [(i, (i + 1) % count) for i in range(ends)])  15.5 us
    unnamed x18, other arithmetic  14.8 us
    pallas_call x1, Pallas kernels, droplets(): pl.pallas_call(functools.partial(droplet_body, size), out_shape=(jax.Shap...  9.85 us
    slice x10, local copies, waits for them, and re-layouts, with_halo(): lax.slice_in_dim(cells, cells.shape[dim] - width, cells.shape[dim], axis=...  3.57 us
  transfers between devices with their start and end apart: 30, of which 20 were waited for; matrix products, arithmetic and copies ran while one was open for 8% of the time, Pallas kernels for 0%

profile of v1, /device:TPU:0, one launch (start us, length us, event | category | flops | bytes accessed | tf_op | source)
XLA Modules:
  0.0 146.0 jit_solution(17236227466103968345)
XLA Ops:
  11.3 4.9 %collective-permute-start = (f32[10,1,8,128]{3,2,1,0:T(8,128)S(1)}, f32[10,1,8,128]{3,2,1,0:T(8,128)S(1)}, u32[]{:S(2)}, u32[]{:S(2)}) collective-permute-start(f32[10,1,8,128]{3,2,1,0:T(8,128)S(1)} %get-tuple-element.159), channel_id=1, source_target_pairs={{0,1},{2,3},{4,5},{6,7},{8,9},{10,11},{12,13},{14,15},{16,17},{18,... | collective-permute-start | bytes 122888 | tf_op jit(solution)/shard_map/ppermute | solution.py:55
  24.0 1.8 %collective-permute-done.2 = f32[10,10,1,128]{3,2,1,0:T(1,128)S(1)} collective-permute-done((f32[10,10,1,128]{3,2,1,0:T(1,128)S(1)}, f32[10,10,1,128]{3,2,1,0:T(1,128)S(1)}, u32[]{:S(2)}, u32[]{:S(2)}) %collective-permute-start.2) | collective-permute-done | bytes 51232 | tf_op jit(solution)/shard_map/ppermute | solution.py:55
  29.9 2.3 %collective-permute-start.5 = (f32[10,10,10,1]{2,3,1,0:T(1,128)S(1)}, f32[10,10,10,1]{2,3,1,0:T(1,128)S(1)}, u32[]{:S(2)}, u32[]{:S(2)}) collective-permute-start(f32[10,10,10,1]{2,3,1,0:T(1,128)S(1)} %copy.24), channel_id=1, source_target_pairs={{8,0},{16,8},{24,16},{0,24},{9,1},{17,9},{25,17},{1,25},{10,2},{18... | collective-permute-start | bytes 12008 | tf_op jit(solution)/shard_map/ppermute | solution.py:57
  44.7 3.4 %collective-permute-start.6 = (f32[10,1,8,128]{3,2,1,0:T(8,128)S(1)}, f32[10,1,8,128]{3,2,1,0:T(8,128)S(1)}, u32[]{:S(2)}, u32[]{:S(2)}) collective-permute-start(f32[10,1,8,128]{3,2,1,0:T(8,128)S(1)} %get-tuple-element.156), channel_id=1, source_target_pairs={{0,1},{2,3},{4,5},{6,7},{8,9},{10,11},{12,13},{14,15},{16,17},{18,... | collective-permute-start | bytes 122888 | tf_op jit(solution)/shard_map/ppermute | solution.py:55
  49.8 4.2 %collective-permute-done.7 = f32[10,1,8,128]{3,2,1,0:T(8,128)S(1)} collective-permute-done((f32[10,1,8,128]{3,2,1,0:T(8,128)S(1)}, f32[10,1,8,128]{3,2,1,0:T(8,128)S(1)}, u32[]{:S(2)}, u32[]{:S(2)}) %collective-permute-start.7) | collective-permute-done | bytes 40992 | tf_op jit(solution)/shard_map/ppermute | solution.py:57
  55.9 1.8 %collective-permute-done.8 = f32[10,10,1,128]{3,2,1,0:T(1,128)S(1)} collective-permute-done((f32[10,10,1,128]{3,2,1,0:T(1,128)S(1)}, f32[10,10,1,128]{3,2,1,0:T(1,128)S(1)}, u32[]{:S(2)}, u32[]{:S(2)}) %collective-permute-start.8) | collective-permute-done | bytes 51232 | tf_op jit(solution)/shard_map/ppermute | solution.py:55
  60.9 3.2 %collective-permute-start.11 = (f32[10,10,10,1]{2,3,1,0:T(1,128)S(1)}, f32[10,10,10,1]{2,3,1,0:T(1,128)}, u32[]{:S(2)}, u32[]{:S(2)}) collective-permute-start(f32[10,10,10,1]{2,3,1,0:T(1,128)S(1)} %copy.28), channel_id=1, source_target_pairs={{8,0},{16,8},{24,16},{0,24},{9,1},{17,9},{25,17},{1,25},{10,2},{18... | collective-permute-start | bytes 12008 | tf_op jit(solution)/shard_map/ppermute | solution.py:57
  72.5 2.6 %collective-permute-start.13 = (f32[3,8,8,2]{3,2,1,0:T(8,128)S(1)}, f32[3,8,8,2]{3,2,1,0:T(8,128)S(1)}, u32[]{:S(2)}, u32[]{:S(2)}) collective-permute-start(f32[3,8,8,2]{3,2,1,0:T(8,128)S(1)} %get-tuple-element.169), channel_id=1, source_target_pairs={{8,0},{16,8},{24,16},{0,24},{9,1},{17,9},{25,17},{1,25},{10,2},{18... | collective-permute-start | bytes 4616 | tf_op jit(solution)/shard_map/ppermute | solution.py:57
  75.5 3.1 %collective-permute-done.12 = f32[3,8,8,2]{3,2,1,0:T(8,128)S(1)} collective-permute-done((f32[3,8,8,2]{3,2,1,0:T(8,128)S(1)}, f32[3,8,8,2]{3,2,1,0:T(8,128)S(1)}, u32[]{:S(2)}, u32[]{:S(2)}) %collective-permute-start.12) | collective-permute-done | bytes 1568 | tf_op jit(solution)/shard_map/ppermute | solution.py:55
  81.2 1.8 %collective-permute-done.14 = f32[3,8,2,132]{3,2,1,0:T(2,128)S(1)} collective-permute-done((f32[3,8,2,132]{3,2,1,0:T(2,128)S(1)}, f32[3,8,2,132]{3,2,1,0:T(2,128)S(1)}, u32[]{:S(2)}, u32[]{:S(2)}) %collective-permute-start.14) | collective-permute-done | bytes 25376 | tf_op jit(solution)/shard_map/ppermute | solution.py:55
  83.2 2.0 %collective-permute-start.17 = (f32[3,2,12,132]{3,2,1,0:T(8,128)S(1)}, f32[3,2,12,132]{3,2,1,0:T(8,128)S(1)}, u32[]{:S(2)}, u32[]{:S(2)}) collective-permute-start(f32[3,2,12,132]{3,2,1,0:T(8,128)S(1)} %get-tuple-element.153), channel_id=1, source_target_pairs={{1,0},{0,1},{3,2},{2,3},{5,4},{4,5},{7,6},{6,7},{9,8},{8,9},{11,10... | collective-permute-start | bytes 114056 | tf_op jit(solution)/shard_map/ppermute | solution.py:57
  85.3 3.4 %collective-permute-done.16 = f32[3,2,12,132]{3,2,1,0:T(8,128)S(1)} collective-permute-done((f32[3,2,12,132]{3,2,1,0:T(8,128)S(1)}, f32[3,2,12,132]{3,2,1,0:T(8,128)S(1)}, u32[]{:S(2)}, u32[]{:S(2)}) %collective-permute-start.16) | collective-permute-done | bytes 38048 | tf_op jit(solution)/shard_map/ppermute | solution.py:55
  88.6 2.1 %collective-permute-done.17 = f32[3,2,12,132]{3,2,1,0:T(8,128)S(1)} collective-permute-done((f32[3,2,12,132]{3,2,1,0:T(8,128)S(1)}, f32[3,2,12,132]{3,2,1,0:T(8,128)S(1)}, u32[]{:S(2)}, u32[]{:S(2)}) %collective-permute-start.17) | collective-permute-done | bytes 38048 | tf_op jit(solution)/shard_map/ppermute | solution.py:57
  92.0 9.8 %shard_map.103 = (f32[3,11,16,256]{3,2,1,0:T(8,128)S(1)}, f32[6,16,128]{2,1,0:T(8,128)S(1)}) custom-call(s32[16]{0:T(128)S(1)} %copy-done.3, f32[3,11,16,256]{3,2,1,0:T(8,128)S(1)} %pad_maximum_fusion.7.vel_ref, f32[3,16,128]{2,1,0:T(8,128)S(1)} %copy-done, f32[3,16,128]{2,1,0:T(8,128)S(1)} %copy-done.1, s32[16,128]{1,0:T(8,128)S(1)} %copy-done.2), custom_call_target="tpu_custom_call" | custom-call | tf_op jit(solution)/shard_map/pallas_call | solution.py:283
  102.9 2.0 %collective-permute-start.18 = (f32[3,12,12,2]{3,2,1,0:T(8,128)S(1)}, f32[3,12,12,2]{3,2,1,0:T(8,128)S(1)}, u32[]{:S(2)}, u32[]{:S(2)}) collective-permute-start(f32[3,12,12,2]{3,2,1,0:T(8,128)S(1)} %get-tuple-element.119), channel_id=1, source_target_pairs={{0,8},{8,16},{16,24},{24,0},{1,9},{9,17},{17,25},{25,1},{2,10},{10... | collective-permute-start | bytes 10376 | tf_op jit(solution)/shard_map/ppermute | solution.py:55
  105.0 1.9 %collective-permute-start.19 = (f32[3,12,12,2]{3,2,1,0:T(8,128)S(1)}, f32[3,12,12,2]{3,2,1,0:T(8,128)S(1)}, u32[]{:S(2)}, u32[]{:S(2)}) collective-permute-start(f32[3,12,12,2]{3,2,1,0:T(8,128)S(1)} %get-tuple-element.120), channel_id=1, source_target_pairs={{8,0},{16,8},{24,16},{0,24},{9,1},{17,9},{25,17},{1,25},{10,2},{18... | collective-permute-start | bytes 10376 | tf_op jit(solution)/shard_map/ppermute | solution.py:57
  108.1 3.7 %collective-permute-start.25 = (f32[6,3,3,1,2,128]{5,0,4,3,2,1:T(8,128)S(1)}, f32[6,3,3,1,2,128]{5,0,4,3,2,1:T(8,128)S(1)}, u32[]{:S(2)}, u32[]{:S(2)}) collective-permute-start(f32[6,3,3,1,2,128]{5,0,4,3,2,1:T(8,128)S(1)} %get-tuple-element.165), channel_id=1, source_target_pairs={{8,0},{16,8},{24,16},{0,24},{9,1},{17,9},{25,17},{1,25},{10,2},{18... | collective-permute-start | bytes 165896 | tf_op jit(solution)/shard_map/ppermute | solution.py:57
  111.8 2.9 %collective-permute-done.18 = f32[3,12,12,2]{3,2,1,0:T(8,128)S(1)} collective-permute-done((f32[3,12,12,2]{3,2,1,0:T(8,128)S(1)}, f32[3,12,12,2]{3,2,1,0:T(8,128)S(1)}, u32[]{:S(2)}, u32[]{:S(2)}) %collective-permute-start.18) | collective-permute-done | bytes 3488 | tf_op jit(solution)/shard_map/ppermute | solution.py:55
  114.7 6.4 %collective-permute-done.19 = f32[3,12,12,2]{3,2,1,0:T(8,128)S(1)} collective-permute-done((f32[3,12,12,2]{3,2,1,0:T(8,128)S(1)}, f32[3,12,12,2]{3,2,1,0:T(8,128)S(1)}, u32[]{:S(2)}, u32[]{:S(2)}) %collective-permute-start.19) | collective-permute-done | bytes 3488 | tf_op jit(solution)/shard_map/ppermute | solution.py:57
  123.3 2.0 %collective-permute-done.20 = f32[3,12,2,136]{3,2,1,0:T(2,128)S(1)} collective-permute-done((f32[3,12,2,136]{3,2,1,0:T(2,128)S(1)}, f32[3,12,2,136]{3,2,1,0:T(2,128)S(1)}, u32[]{:S(2)}, u32[]{:S(2)}) %collective-permute-start.20) | collective-permute-done | bytes 39200 | tf_op jit(solution)/shard_map/ppermute | solution.py:55
  131.1 2.1 %collective-permute-done.23 = f32[3,2,16,136]{3,2,1,0:T(8,128)S(1)} collective-permute-done((f32[3,2,16,136]{3,2,1,0:T(8,128)S(1)}, f32[3,2,16,136]{3,2,1,0:T(8,128)S(1)}, u32[]{:S(2)}, u32[]{:S(2)}) %collective-permute-start.23) | collective-permute-done | bytes 52256 | tf_op jit(solution)/shard_map/ppermute | solution.py:57
  133.7 1.9 %collective-permute-start.29 = (f32[6,1,5,5,2,128]{5,0,4,3,2,1:T(8,128)S(1)}, f32[6,1,5,5,2,128]{5,0,4,3,2,1:T(8,128)S(1)}, u32[]{:S(2)}, u32[]{:S(2)}) collective-permute-start(f32[6,1,5,5,2,128]{5,0,4,3,2,1:T(8,128)S(1)} %get-tuple-element.118), channel_id=1, source_target_pairs={{1,0},{0,1},{3,2},{2,3},{5,4},{4,5},{7,6},{6,7},{9,8},{8,9},{11,10... | collective-permute-start | bytes 460808 | tf_op jit(solution)/shard_map/ppermute | solution.py:57
  136.4 5.1 %collective-permute-done.28 = f32[6,1,5,5,2,128]{5,0,4,3,2,1:T(8,128)S(1)} collective-permute-done((f32[6,1,5,5,2,128]{5,0,4,3,2,1:T(8,128)S(1)}, f32[6,1,5,5,2,128]{5,0,4,3,2,1:T(8,128)S(1)}, u32[]{:S(2)}, u32[]{:S(2)}) %collective-permute-start.28) | collective-permute-done | bytes 153632 | tf_op jit(solution)/shard_map/ppermute | solution.py:55
  141.5 3.6 %collective-permute-done.29 = f32[6,1,5,5,2,128]{5,0,4,3,2,1:T(8,128)S(1)} collective-permute-done((f32[6,1,5,5,2,128]{5,0,4,3,2,1:T(8,128)S(1)}, f32[6,1,5,5,2,128]{5,0,4,3,2,1:T(8,128)S(1)}, u32[]{:S(2)}, u32[]{:S(2)}) %collective-permute-start.29) | collective-permute-done | bytes 153632 | tf_op jit(solution)/shard_map/ppermute | solution.py:57
  (260 shorter events, 66.3 us)
Async XLA Ops:
  11.3 9.6 %collective-permute-start = (f32[10,1,8,128]{3,2,1,0:T(8,128)S(1)}, f32[10,1,8,128]{3,2,1,0:T(8,128)S(1)}, u32[]{:S(2)}, u32[]{:S(2)}) collective-permute-start(f32[10,1,8,128]{3,2,1,0:T(8,128)S(1)} %get-tuple-element.159), channel_id=1, source_target_pairs={{0,1},{2,3},{4,5},{6,7},{8,9},{10,11},{12,13},{14,15},{16,17},{18,... | collective-permute-start | bytes 122888 | tf_op jit(solution)/shard_map/ppermute | solution.py:55
  16.1 5.9 %collective-permute-start.1 = (f32[10,1,8,128]{3,2,1,0:T(8,128)S(1)}, f32[10,1,8,128]{3,2,1,0:T(8,128)S(1)}, u32[]{:S(2)}, u32[]{:S(2)}) collective-permute-start(f32[10,1,8,128]{3,2,1,0:T(8,128)S(1)} %get-tuple-element.158), channel_id=1, source_target_pairs={{1,0},{3,2},{5,4},{7,6},{9,8},{11,10},{13,12},{15,14},{17,16},{19,... | collective-permute-start | bytes 122888 | tf_op jit(solution)/shard_map/ppermute | solution.py:57
  27.6 6.1 %collective-permute-start.4 = (f32[10,10,10,1]{2,3,1,0:T(1,128)}, f32[10,10,10,1]{2,3,1,0:T(1,128)S(1)}, u32[]{:S(2)}, u32[]{:S(2)}) collective-permute-start(f32[10,10,10,1]{2,3,1,0:T(1,128)} %copy.23), channel_id=1, source_target_pairs={{0,8},{8,16},{16,24},{24,0},{1,9},{9,17},{17,25},{25,1},{2,10},{10... | collective-permute-start | bytes 12008 | tf_op jit(solution)/shard_map/ppermute | solution.py:55
  29.9 5.4 %collective-permute-start.5 = (f32[10,10,10,1]{2,3,1,0:T(1,128)S(1)}, f32[10,10,10,1]{2,3,1,0:T(1,128)S(1)}, u32[]{:S(2)}, u32[]{:S(2)}) collective-permute-start(f32[10,10,10,1]{2,3,1,0:T(1,128)S(1)} %copy.24), channel_id=1, source_target_pairs={{8,0},{16,8},{24,16},{0,24},{9,1},{17,9},{25,17},{1,25},{10,2},{18... | collective-permute-start | bytes 12008 | tf_op jit(solution)/shard_map/ppermute | solution.py:57
  44.7 5.1 %collective-permute-start.6 = (f32[10,1,8,128]{3,2,1,0:T(8,128)S(1)}, f32[10,1,8,128]{3,2,1,0:T(8,128)S(1)}, u32[]{:S(2)}, u32[]{:S(2)}) collective-permute-start(f32[10,1,8,128]{3,2,1,0:T(8,128)S(1)} %get-tuple-element.156), channel_id=1, source_target_pairs={{0,1},{2,3},{4,5},{6,7},{8,9},{10,11},{12,13},{14,15},{16,17},{18,... | collective-permute-start | bytes 122888 | tf_op jit(solution)/shard_map/ppermute | solution.py:55
  48.1 5.9 %collective-permute-start.7 = (f32[10,1,8,128]{3,2,1,0:T(8,128)S(1)}, f32[10,1,8,128]{3,2,1,0:T(8,128)S(1)}, u32[]{:S(2)}, u32[]{:S(2)}) collective-permute-start(f32[10,1,8,128]{3,2,1,0:T(8,128)S(1)} %get-tuple-element.157), channel_id=1, source_target_pairs={{1,0},{3,2},{5,4},{7,6},{9,8},{11,10},{13,12},{15,14},{17,16},{19,... | collective-permute-start | bytes 122888 | tf_op jit(solution)/shard_map/ppermute | solution.py:57
  59.6 6.4 %collective-permute-start.10 = (f32[10,10,10,1]{2,3,1,0:T(1,128)}, f32[10,10,10,1]{2,3,1,0:T(1,128)S(1)}, u32[]{:S(2)}, u32[]{:S(2)}) collective-permute-start(f32[10,10,10,1]{2,3,1,0:T(1,128)} %copy.27), channel_id=1, source_target_pairs={{0,8},{8,16},{16,24},{24,0},{1,9},{9,17},{17,25},{25,1},{2,10},{10... | collective-permute-start | bytes 12008 | tf_op jit(solution)/shard_map/ppermute | solution.py:55
  60.9 5.8 %collective-permute-start.11 = (f32[10,10,10,1]{2,3,1,0:T(1,128)S(1)}, f32[10,10,10,1]{2,3,1,0:T(1,128)}, u32[]{:S(2)}, u32[]{:S(2)}) collective-permute-start(f32[10,10,10,1]{2,3,1,0:T(1,128)S(1)} %copy.28), channel_id=1, source_target_pairs={{8,0},{16,8},{24,16},{0,24},{9,1},{17,9},{25,17},{1,25},{10,2},{18... | collective-permute-start | bytes 12008 | tf_op jit(solution)/shard_map/ppermute | solution.py:57
  71.2 7.5 %collective-permute-start.12 = (f32[3,8,8,2]{3,2,1,0:T(8,128)S(1)}, f32[3,8,8,2]{3,2,1,0:T(8,128)S(1)}, u32[]{:S(2)}, u32[]{:S(2)}) collective-permute-start(f32[3,8,8,2]{3,2,1,0:T(8,128)S(1)} %get-tuple-element.168), channel_id=1, source_target_pairs={{0,8},{8,16},{16,24},{24,0},{1,9},{9,17},{17,25},{25,1},{2,10},{10... | collective-permute-start | bytes 4616 | tf_op jit(solution)/shard_map/ppermute | solution.py:55
  72.5 6.7 %collective-permute-start.13 = (f32[3,8,8,2]{3,2,1,0:T(8,128)S(1)}, f32[3,8,8,2]{3,2,1,0:T(8,128)S(1)}, u32[]{:S(2)}, u32[]{:S(2)}) collective-permute-start(f32[3,8,8,2]{3,2,1,0:T(8,128)S(1)} %get-tuple-element.169), channel_id=1, source_target_pairs={{8,0},{16,8},{24,16},{0,24},{9,1},{17,9},{25,17},{1,25},{10,2},{18... | collective-permute-start | bytes 4616 | tf_op jit(solution)/shard_map/ppermute | solution.py:57
  83.2 5.5 %collective-permute-start.16 = (f32[3,2,12,132]{3,2,1,0:T(8,128)S(1)}, f32[3,2,12,132]{3,2,1,0:T(8,128)S(1)}, u32[]{:S(2)}, u32[]{:S(2)}) collective-permute-start(f32[3,2,12,132]{3,2,1,0:T(8,128)S(1)} %get-tuple-element.152), channel_id=1, source_target_pairs={{0,1},{1,0},{2,3},{3,2},{4,5},{5,4},{6,7},{7,6},{8,9},{9,8},{10,11... | collective-permute-start | bytes 114056 | tf_op jit(solution)/shard_map/ppermute | solution.py:55
  83.2 7.5 %collective-permute-start.17 = (f32[3,2,12,132]{3,2,1,0:T(8,128)S(1)}, f32[3,2,12,132]{3,2,1,0:T(8,128)S(1)}, u32[]{:S(2)}, u32[]{:S(2)}) collective-permute-start(f32[3,2,12,132]{3,2,1,0:T(8,128)S(1)} %get-tuple-element.153), channel_id=1, source_target_pairs={{1,0},{0,1},{3,2},{2,3},{5,4},{4,5},{7,6},{6,7},{9,8},{8,9},{11,10... | collective-permute-start | bytes 114056 | tf_op jit(solution)/shard_map/ppermute | solution.py:57
  102.9 11.8 %collective-permute-start.18 = (f32[3,12,12,2]{3,2,1,0:T(8,128)S(1)}, f32[3,12,12,2]{3,2,1,0:T(8,128)S(1)}, u32[]{:S(2)}, u32[]{:S(2)}) collective-permute-start(f32[3,12,12,2]{3,2,1,0:T(8,128)S(1)} %get-tuple-element.119), channel_id=1, source_target_pairs={{0,8},{8,16},{16,24},{24,0},{1,9},{9,17},{17,25},{25,1},{2,10},{10... | collective-permute-start | bytes 10376 | tf_op jit(solution)/shard_map/ppermute | solution.py:55
  105.0 16.2 %collective-permute-start.19 = (f32[3,12,12,2]{3,2,1,0:T(8,128)S(1)}, f32[3,12,12,2]{3,2,1,0:T(8,128)S(1)}, u32[]{:S(2)}, u32[]{:S(2)}) collective-permute-start(f32[3,12,12,2]{3,2,1,0:T(8,128)S(1)} %get-tuple-element.120), channel_id=1, source_target_pairs={{8,0},{16,8},{24,16},{0,24},{9,1},{17,9},{25,17},{1,25},{10,2},{18... | collective-permute-start | bytes 10376 | tf_op jit(solution)/shard_map/ppermute | solution.py:57
  107.9 20.0 %collective-permute-start.24 = (f32[6,3,3,1,2,128]{5,0,4,3,2,1:T(8,128)S(1)}, f32[6,3,3,1,2,128]{5,0,4,3,2,1:T(8,128)S(1)}, u32[]{:S(2)}, u32[]{:S(2)}) collective-permute-start(f32[6,3,3,1,2,128]{5,0,4,3,2,1:T(8,128)S(1)} %get-tuple-element.164), channel_id=1, source_target_pairs={{0,8},{8,16},{16,24},{24,0},{1,9},{9,17},{17,25},{25,1},{2,10},{10... | collective-permute-start | bytes 165896 | tf_op jit(solution)/shard_map/ppermute | solution.py:55
  108.1 19.8 %collective-permute-start.25 = (f32[6,3,3,1,2,128]{5,0,4,3,2,1:T(8,128)S(1)}, f32[6,3,3,1,2,128]{5,0,4,3,2,1:T(8,128)S(1)}, u32[]{:S(2)}, u32[]{:S(2)}) collective-permute-start(f32[6,3,3,1,2,128]{5,0,4,3,2,1:T(8,128)S(1)} %get-tuple-element.165), channel_id=1, source_target_pairs={{8,0},{16,8},{24,16},{0,24},{9,1},{17,9},{25,17},{1,25},{10,2},{18... | collective-permute-start | bytes 165896 | tf_op jit(solution)/shard_map/ppermute | solution.py:57
  121.4 3.8 %collective-permute-start.20 = (f32[3,12,2,136]{3,2,1,0:T(2,128)S(1)}, f32[3,12,2,136]{3,2,1,0:T(2,128)S(1)}, u32[]{:S(2)}, u32[]{:S(2)}) collective-permute-start(f32[3,12,2,136]{3,2,1,0:T(2,128)S(1)} %get-tuple-element.104), channel_id=1, source_target_pairs={{0,2},{2,4},{4,6},{6,0},{1,3},{3,5},{5,7},{7,1},{8,10},{10,12},{12... | collective-permute-start | bytes 117512 | tf_op jit(solution)/shard_map/ppermute | solution.py:55
  121.5 3.8 %collective-permute-start.21 = (f32[3,12,2,136]{3,2,1,0:T(2,128)S(1)}, f32[3,12,2,136]{3,2,1,0:T(2,128)S(1)}, u32[]{:S(2)}, u32[]{:S(2)}) collective-permute-start(f32[3,12,2,136]{3,2,1,0:T(2,128)S(1)} %get-tuple-element.105), channel_id=1, source_target_pairs={{2,0},{4,2},{6,4},{0,6},{3,1},{5,3},{7,5},{1,7},{10,8},{12,10},{14... | collective-permute-start | bytes 117512 | tf_op jit(solution)/shard_map/ppermute | solution.py:57
  125.4 5.6 %collective-permute-start.22 = (f32[3,2,16,136]{3,2,1,0:T(8,128)S(1)}, f32[3,2,16,136]{3,2,1,0:T(8,128)S(1)}, u32[]{:S(2)}, u32[]{:S(2)}) collective-permute-start(f32[3,2,16,136]{3,2,1,0:T(8,128)S(1)} %get-tuple-element.102), channel_id=1, source_target_pairs={{0,1},{1,0},{2,3},{3,2},{4,5},{5,4},{6,7},{7,6},{8,9},{9,8},{10,11... | collective-permute-start | bytes 156680 | tf_op jit(solution)/shard_map/ppermute | solution.py:55
  125.8 7.4 %collective-permute-start.23 = (f32[3,2,16,136]{3,2,1,0:T(8,128)S(1)}, f32[3,2,16,136]{3,2,1,0:T(8,128)S(1)}, u32[]{:S(2)}, u32[]{:S(2)}) collective-permute-start(f32[3,2,16,136]{3,2,1,0:T(8,128)S(1)} %get-tuple-element.103), channel_id=1, source_target_pairs={{1,0},{0,1},{3,2},{2,3},{5,4},{4,5},{7,6},{6,7},{9,8},{8,9},{11,10... | collective-permute-start | bytes 156680 | tf_op jit(solution)/shard_map/ppermute | solution.py:57
  127.9 5.5 %collective-permute-start.26 = (f32[6,3,1,5,2,128]{5,0,4,3,2,1:T(8,128)S(1)}, f32[6,3,1,5,2,128]{5,0,4,3,2,1:T(8,128)S(1)}, u32[]{:S(2)}, u32[]{:S(2)}) collective-permute-start(f32[6,3,1,5,2,128]{5,0,4,3,2,1:T(8,128)S(1)} %get-tuple-element.154), channel_id=1, source_target_pairs={{0,2},{2,4},{4,6},{6,0},{1,3},{3,5},{5,7},{7,1},{8,10},{10,12},{12... | collective-permute-start | bytes 276488 | tf_op jit(solution)/shard_map/ppermute | solution.py:55
  128.5 5.0 %collective-permute-start.27 = (f32[6,3,1,5,2,128]{5,0,4,3,2,1:T(8,128)S(1)}, f32[6,3,1,5,2,128]{5,0,4,3,2,1:T(8,128)S(1)}, u32[]{:S(2)}, u32[]{:S(2)}) collective-permute-start(f32[6,3,1,5,2,128]{5,0,4,3,2,1:T(8,128)S(1)} %get-tuple-element.155), channel_id=1, source_target_pairs={{2,0},{4,2},{6,4},{0,6},{3,1},{5,3},{7,5},{1,7},{10,8},{12,10},{14... | collective-permute-start | bytes 276488 | tf_op jit(solution)/shard_map/ppermute | solution.py:57
  133.5 8.0 %collective-permute-start.28 = (f32[6,1,5,5,2,128]{5,0,4,3,2,1:T(8,128)S(1)}, f32[6,1,5,5,2,128]{5,0,4,3,2,1:T(8,128)S(1)}, u32[]{:S(2)}, u32[]{:S(2)}) collective-permute-start(f32[6,1,5,5,2,128]{5,0,4,3,2,1:T(8,128)S(1)} %get-tuple-element.117), channel_id=1, source_target_pairs={{0,1},{1,0},{2,3},{3,2},{4,5},{5,4},{6,7},{7,6},{8,9},{9,8},{10,11... | collective-permute-start | bytes 460808 | tf_op jit(solution)/shard_map/ppermute | solution.py:55
  133.7 11.3 %collective-permute-start.29 = (f32[6,1,5,5,2,128]{5,0,4,3,2,1:T(8,128)S(1)}, f32[6,1,5,5,2,128]{5,0,4,3,2,1:T(8,128)S(1)}, u32[]{:S(2)}, u32[]{:S(2)}) collective-permute-start(f32[6,1,5,5,2,128]{5,0,4,3,2,1:T(8,128)S(1)} %get-tuple-element.118), channel_id=1, source_target_pairs={{1,0},{0,1},{3,2},{2,3},{5,4},{4,5},{7,6},{6,7},{9,8},{8,9},{11,10... | collective-permute-start | bytes 460808 | tf_op jit(solution)/shard_map/ppermute | solution.py:57
  (43 other events, 167.7 us)

commit v2 on v1

--- a/solution.py
+++ b/solution.py
@@ -61,104 +61,6 @@
     return cells
 
 
-def kernel(distance):
-    return 0.25 * (1.0 + jnp.cos(math.pi * 0.5 * distance))
-
-
-def macroscopic(pops):
-    density = pops[0] * float(weights_table[0])
-    moment = [jnp.zeros_like(density), jnp.zeros_like(density), jnp.zeros_like(density)]
-    for index in range(1, 19):
-        term = pops[index] * float(weights_table[index])
-        density = density + term
-        for axis in range(3):
-            if int(lattice[index][axis]) != 0:
-                moment[axis] = moment[axis] + float(lattice[index][axis]) * term
-    return (density, [moment[axis] / density for axis in range(3)])
-
-
-def collide(pops, coarse, interface):
-    density, flow = macroscopic(pops)
-    square = flow[0] * flow[0] + flow[1] * flow[1] + flow[2] * flow[2]
-    inside = interface == 1
-    posts = []
-    for index in range(19):
-        along = jnp.zeros_like(density)
-        for axis in range(3):
-            if int(lattice[index][axis]) != 0:
-                along = along + float(lattice[index][axis]) * flow[axis]
-        balance = density * (1.0 + 3.0 * along + 4.5 * along * along - 1.5 * square)
-        relaxed = pops[index] - (pops[index] - balance) * inverse_tau
-        posts.append(jnp.where(inside, coarse[index].astype(jnp.float32), relaxed))
-    return jnp.stack(posts)
-
-
-def window(source, index, grown, shape):
-    starts = [
-        grown[0] * (1 - int(lattice[index][2])),
-        grown[1] * (1 - int(lattice[index][1])),
-        grown[2] * (1 - int(lattice[index][0])),
-    ]
-    return source[
-        starts[0] : starts[0] + shape[0],
-        starts[1] : starts[1] + shape[1],
-        starts[2] : starts[2] + shape[2],
-    ]
-
-
-def axis_pull(posts):
-    shape = posts.shape[1:]
-    cross_z = [index for index in range(19) if int(lattice[index][2]) != 0]
-    cross_y = [index for index in range(19) if int(lattice[index][1]) != 0]
-    cross_x = [index for index in range(19) if int(lattice[index][0]) != 0]
-    part_z = with_halo(jnp.stack([posts[index] for index in cross_z]), (("gz", 1),), 1, False)
-    into_y = []
-    for index in cross_y:
-        if index in cross_z:
-            into_y.append(part_z[cross_z.index(index)])
-        else:
-            into_y.append(jnp.pad(posts[index], ((1, 1), (0, 0), (0, 0))))
-    part_y = with_halo(jnp.stack(into_y), (("gy", 2),), 1, True)
-    into_x = []
-    for index in cross_x:
-        if index in cross_y:
-            into_x.append(part_y[cross_y.index(index)])
-        elif index in cross_z:
-            into_x.append(jnp.pad(part_z[cross_z.index(index)], ((0, 0), (1, 1), (0, 0))))
-        else:
-            into_x.append(jnp.pad(posts[index], ((1, 1), (1, 1), (0, 0))))
-    part_x = with_halo(jnp.stack(into_x), (("gx", 3),), 1, True)
-    pulled = []
-    for index in range(19):
-        if index in cross_x:
-            pulled.append(window(part_x[cross_x.index(index)], index, (1, 1, 1), shape))
-        elif index in cross_y:
-            pulled.append(window(part_y[cross_y.index(index)], index, (1, 1, 0), shape))
-        elif index in cross_z:
-            pulled.append(window(part_z[cross_z.index(index)], index, (1, 0, 0), shape))
-        else:
-            pulled.append(posts[index])
-    return pulled
-
-
-def wall_fix(pulled, posts, bottom, top):
-    fixed = []
-    for index in range(19):
-        value = pulled[index]
-        if int(lattice[index][2]) == 1:
-            value = jnp.where(bottom, posts[opposite[index]], value)
-        if int(lattice[index][2]) == -1:
-            value = jnp.where(top, posts[opposite[index]], value)
-        fixed.append(value)
-    return jnp.stack(fixed)
-
-
-def row_weights(offset, frac):
-    span = lax.broadcasted_iota(jnp.int32, (1, TILE + 4), 1)
-    distance = span - 2 - offset[:, None] - frac[:, None]
-    return jnp.where(jnp.abs(distance) < 2.0, kernel(distance), 0.0)
-
-
 def fold(array, dim, inner):
     core = lax.slice_in_dim(array, 4, inner + 4, axis=dim)
     lower = lax.slice_in_dim(array, 0, 2, axis=dim)
@@ -168,6 +70,419 @@
     low_pad[dim] = (0, inner - 2)
     high_pad[dim] = (inner - 2, 0)
     return core + jnp.pad(lower, low_pad) + jnp.pad(upper, high_pad)
+
+
+ways = [tuple(int(part) for part in lattice[index][::-1]) for index in range(19)] + [(0, 0, 0)]
+channels = len(ways)
+LOW = 3
+HIGH = 4
+
+
+def low_reach(way):
+    return 2 + way
+
+
+def high_reach(way):
+    return 3 - way
+
+
+def rim(kind):
+    count, reach = (LOW, low_reach) if kind == "low" else (HIGH, high_reach)
+    return [
+        (step, channel)
+        for step in range(1, count + 1)
+        for channel in range(channels)
+        if step <= reach(ways[channel][0])
+    ]
+
+
+def rim_count(kind):
+    return LOW if kind == "low" else HIGH
+
+
+def rim_sides(levels):
+    if levels == 2:
+        return [("low", 1, 0, 0), ("high", 0, 1, 0)]
+    return [("low", None, None, 0), ("high", None, None, 1)]
+
+
+def rim_sizes(levels):
+    sides = [(len(rim(kind)), rim_count(kind)) for kind, _, _, _ in rim_sides(levels)]
+    return [max(sides)] if levels == 2 else sides
+
+
+def guarded(level, guard, action):
+    if guard is None:
+        action()
+    else:
+        pl.when(level == guard)(action)
+
+
+def row_table(depth, levels):
+    high_at, low_at = 0, 0
+    own, own_strips, rims, strips = [], [], {}, {}
+
+    def entry(channel, bounces=False):
+        nonlocal high_at, low_at
+        way_z, way, _ = ways[channel]
+        above, below = high_reach(way), low_reach(way)
+        if bounces and way_z != 0:
+            above, below = max(above, HIGH - 1), max(below, LOW - 1)
+        place = (high_at, low_at, above, below)
+        high_at, low_at = high_at + place[2], low_at + place[3]
+        return place
+
+    def strip():
+        nonlocal high_at, low_at
+        place = (high_at, low_at, HIGH, LOW)
+        high_at, low_at = high_at + HIGH, low_at + LOW
+        return place
+
+    for layer in range(depth):
+        for channel in range(channels):
+            own.append((layer, channel, entry(channel, layer in (0, depth - 1))))
+        own_strips.append((strip(), strip()))
+    start = (high_at, low_at)
+    most = start
+    for kind, _, _, _ in rim_sides(levels):
+        if levels == 2:
+            high_at, low_at = start
+        rims[kind] = [(step, channel, entry(channel)) for step, channel in rim(kind)]
+        strips[kind] = [(strip(), strip()) for _ in range(rim_count(kind))]
+        most = (max(most[0], high_at), max(most[1], low_at))
+    return own, own_strips, rims, strips, [-(-count // 8) * 8 for count in most]
+
+
+def moments(cells):
+    density = cells[0] * float(weights_table[0])
+    moment = [None, None, None]
+    face, edge = float(weights_table[1]), float(weights_table[7])
+    edge_sum = cells[7]
+    for index in range(8, 19):
+        edge_sum = edge_sum + cells[index]
+    face_sum = cells[1]
+    for index in range(2, 7):
+        face_sum = face_sum + cells[index]
+    density = density + face * face_sum + edge * edge_sum
+    for axis in range(3):
+        total = {}
+        for group, indices in ((face, range(1, 7)), (edge, range(7, 19))):
+            plus, minus = None, None
+            for index in indices:
+                way = int(lattice[index][axis])
+                if way == 1:
+                    plus = cells[index] if plus is None else plus + cells[index]
+                if way == -1:
+                    minus = cells[index] if minus is None else minus + cells[index]
+            total[group] = plus - minus
+        moment[axis] = face * total[face] + edge * total[edge]
+    return density, moment
+
+
+def relaxed(cells):
+    density, moment = moments(cells)
+    inverse = 1.0 / density
+    flow = [part * inverse for part in moment]
+    square = flow[0] * flow[0] + flow[1] * flow[1] + flow[2] * flow[2]
+    scale = density * inverse_tau
+    base = scale * (1.0 - 1.5 * square)
+    keep = 1.0 - inverse_tau
+    posts = [None] * 19
+    posts[0] = keep * cells[0] + base
+    for index in range(1, 19, 2):
+        along = None
+        for axis in range(3):
+            way = int(lattice[index][axis])
+            if way != 0:
+                part = flow[axis] if way == 1 else -flow[axis]
+                along = part if along is None else along + part
+        odd = 3.0 * scale * along
+        even = base + (4.5 * scale) * (along * along)
+        posts[index] = keep * cells[index] + (even + odd)
+        posts[index + 1] = keep * cells[index + 1] + (even - odd)
+    return posts
+
+
+def lane_roll(value, shift):
+    shift = shift % value.shape[-1]
+    return value if shift == 0 else pltpu.roll(value, shift, value.ndim - 1)
+
+
+def first_body(levels, level_ref, pops_ref, coarse_ref, interface_ref, posts_ref, *outs):
+    depth, height, width = interface_ref.shape
+    sides = rim_sides(levels)
+    slots = len(rim_sizes(levels))
+    rims = outs[:slots]
+    right_ref, left_ref = outs[slots : slots + 2]
+    right_rims = outs[slots + 2 : 2 * slots + 2]
+    left_rims = outs[2 * slots + 2 :]
+    level = level_ref[0]
+    lane = lax.broadcasted_iota(jnp.int32, (height, 128), 1)
+
+    def layer_step(layer, carry):
+        mask = interface_ref[layer]
+        inside = mask == 1
+        posts = relaxed([pops_ref[index, layer] for index in range(19)])
+        posts = [
+            jnp.where(inside, coarse_ref[index, layer].astype(jnp.float32), posts[index])
+            for index in range(19)
+        ] + [mask.astype(jnp.float32)]
+        right, left = jnp.zeros((height, 128), jnp.float32), jnp.zeros((height, 128), jnp.float32)
+        for channel in range(channels):
+            posts_ref[channel, layer] = posts[channel]
+            here = (lane >= 4 * channel) & (lane < 4 * channel + 4)
+            right = jnp.where(here, lane_roll(posts[channel][:, width - 128 :], 4 * channel + 4), right)
+            left = jnp.where(here, lane_roll(posts[channel][:, :128], 4 * channel), left)
+        right_ref[layer] = right
+        left_ref[layer] = left
+        return carry
+
+    lax.fori_loop(0, depth, layer_step, 0)
+    for kind, _, sender, slot in sides:
+
+        def pack(kind=kind, slot=slot):
+            for place, (step, channel) in enumerate(rim(kind)):
+                rims[slot][place] = posts_ref[channel, depth - step if kind == "low" else step - 1]
+            for step in range(1, rim_count(kind) + 1):
+                layer = depth - step if kind == "low" else step - 1
+                right_rims[slot][step - 1] = right_ref[layer]
+                left_rims[slot][step - 1] = left_ref[layer]
+
+        guarded(level, sender, pack)
+
+
+def rows_body(levels, level_ref, posts_ref, low_ref, high_ref, *rest):
+    depth, height = posts_ref.shape[1:3]
+    slots = len(rim_sizes(levels))
+    rims, low_rims, high_rims = rest[:slots], rest[slots : 2 * slots], rest[2 * slots : 3 * slots]
+    down_ref, up_ref = rest[3 * slots :]
+    own, own_strips, rim_rows, rim_strips, _ = row_table(depth, levels)
+
+    def put(place, source, *index):
+        down_at, up_at, down_rows, up_rows = place
+        down_ref[down_at : down_at + down_rows, :] = source[(*index, slice(0, down_rows))]
+        up_ref[up_at : up_at + up_rows, :] = source[(*index, slice(height - up_rows, height))]
+
+    for layer, channel, place in own:
+        put(place, posts_ref, channel, layer)
+    for layer in range(depth):
+        put(own_strips[layer][0], low_ref, layer)
+        put(own_strips[layer][1], high_ref, layer)
+    for kind, receiver, _, slot in rim_sides(levels):
+
+        def pack(kind=kind, slot=slot):
+            for at, (_, _, place) in enumerate(rim_rows[kind]):
+                put(place, rims[slot], at)
+            for step, (low, high) in enumerate(rim_strips[kind]):
+                put(low, low_rims[slot], step)
+                put(high, high_rims[slot], step)
+
+        guarded(level_ref[0], receiver, pack)
+
+
+def steps_body(levels, level_ref, posts_ref, low_ref, high_ref, *rest):
+    depth, height, width = posts_ref.shape[1:]
+    slots = len(rim_sizes(levels))
+    rims, low_rims, high_rims = rest[:slots], rest[slots : 2 * slots], rest[2 * slots : 3 * slots]
+    above_ref, below_ref, pops_ref, vel_ref, ext, strip_low, strip_high, pulled, second = rest[3 * slots :]
+    own, own_strips, rim_rows, rim_strips, _ = row_table(depth, levels)
+    level = level_ref[0]
+    rows, lanes = height + 8, width + 128
+    main = slice(0, width)
+
+    def place_rows(target, index, place, cols):
+        above_at, below_at, above_rows, below_rows = place
+        target[(*index, slice(height, height + above_rows), cols)] = above_ref[
+            above_at : above_at + above_rows, :
+        ]
+        target[(*index, slice(rows - below_rows, rows), cols)] = below_ref[
+            below_at : below_at + below_rows, :
+        ]
+
+    whole = slice(None)
+    for layer, channel, place in own:
+        ext[channel, LOW + layer, :height, main] = posts_ref[channel, layer]
+        place_rows(ext, (channel, LOW + layer), place, main)
+    for layer in range(depth):
+        for strip, source, place in (
+            (strip_low, low_ref, own_strips[layer][0]),
+            (strip_high, high_ref, own_strips[layer][1]),
+        ):
+            strip[LOW + layer, :height, :] = source[layer]
+            place_rows(strip, (LOW + layer,), place, whole)
+    for kind, receiver, _, slot in rim_sides(levels):
+
+        def unpack(kind=kind, slot=slot):
+            def at_layer(step):
+                return LOW - step if kind == "low" else LOW + depth + step - 1
+
+            for at, (step, channel, place) in enumerate(rim_rows[kind]):
+                ext[channel, at_layer(step), :height, main] = rims[slot][at]
+                place_rows(ext, (channel, at_layer(step)), place, main)
+            for step in range(1, rim_count(kind) + 1):
+                for strip, source, place in (
+                    (strip_low, low_rims[slot], rim_strips[kind][step - 1][0]),
+                    (strip_high, high_rims[slot], rim_strips[kind][step - 1][1]),
+                ):
+                    strip[at_layer(step), :height, :] = source[step - 1]
+                    place_rows(strip, (at_layer(step),), place, whole)
+
+        guarded(level, receiver, unpack)
+
+    lane = lax.broadcasted_iota(jnp.int32, (rows, 128), 1)
+
+    def strip_step(layer, carry):
+        low, high = strip_low[layer], strip_high[layer]
+        for channel in range(channels):
+            ext[channel, layer, :, width:] = jnp.where(
+                lane < 64, lane_roll(high, -4 * channel), lane_roll(low, 124 - 4 * channel)
+            )
+        return carry
+
+    lax.fori_loop(0, LOW + depth + HIGH, strip_step, 0)
+
+    def pull(source, layer, at):
+        bottom = (level == 0) & (layer == 0)
+        top = (level == levels - 1) & (layer == depth - 1)
+        for index in range(19):
+            way_z, way_y, way_x = ways[index]
+            value = source[index, at - way_z]
+            if way_x != 0:
+                value = pltpu.roll(value, way_x % lanes, 1)
+            if way_y != 0:
+                value = pltpu.roll(value, way_y % rows, 0)
+            if way_z != 0:
+                wall = bottom if way_z == 1 else top
+                value = jnp.where(wall, source[opposite[index], at], value)
+            pulled[index] = value
+
+    tiles = [
+        (slice(row, row + 8), slice(col, col + 128))
+        for row in range(0, rows, 8)
+        for col in range(0, lanes, 128)
+    ]
+
+    def first_step(number, carry):
+        at = number + 1
+        pull(ext, at - LOW, at)
+        for tile in tiles:
+            posts = relaxed([pulled[(index, *tile)] for index in range(19)])
+            inside = ext[(19, at, *tile)] > 0.5
+            for index in range(19):
+                second[(index, number, *tile)] = jnp.where(inside, ext[(index, at, *tile)], posts[index])
+        return carry
+
+    lax.fori_loop(0, depth + LOW + HIGH - 2, first_step, 0)
+
+    row_at = lax.broadcasted_iota(jnp.int32, (8, 128), 0)
+    lane_at = lax.broadcasted_iota(jnp.int32, (8, 128), 1)
+
+    def second_step(number, carry):
+        layer = number - 1
+        pull(second, layer, number + 1)
+        keep = jnp.logical_not((level == 0) & (layer < 0) | (level == levels - 1) & (layer >= depth))
+        for tile in tiles:
+            density, moment = moments([pulled[(index, *tile)] for index in range(19)])
+            inverse = 1.0 / density
+            row = row_at + tile[0].start
+            col = lane_at + tile[1].start
+            valid = ((row < height + 2) | (row == rows - 1)) & ((col < width + 2) | (col == lanes - 1))
+            for axis in range(3):
+                vel_ref[(axis, number, *tile)] = jnp.where(valid & keep, moment[axis] * inverse, 0.0)
+        return carry
+
+    lax.fori_loop(0, 1, second_step, 0)
+
+    def second_inner(number, carry):
+        second_step(number, carry)
+        for index in range(19):
+            pops_ref[index, number - 1] = pulled[index, :height, main]
+        return carry
+
+    lax.fori_loop(1, depth + 1, second_inner, 0)
+    lax.fori_loop(depth + 1, depth + 3, second_step, 0)
+
+
+def call(body, outs, ins, scratch=()):
+    vmem = pl.BlockSpec(memory_space=pltpu.VMEM)
+    return pl.pallas_call(
+        body,
+        out_shape=[jax.ShapeDtypeStruct(shape, jnp.float32) for shape in outs],
+        in_specs=[pl.BlockSpec(memory_space=pltpu.SMEM)] + [vmem] * (len(ins) - 1),
+        out_specs=[vmem] * len(outs),
+        scratch_shapes=list(scratch),
+        compiler_params=pltpu.CompilerParams(vmem_limit_bytes=56 * 1024 * 1024),
+    )(*ins)
+
+
+def shifted(value, axis, step):
+    count = lax.axis_size(axis)
+    return lax.ppermute(value, axis, [(i, (i + step) % count) for i in range(count)])
+
+
+def to_level(value, kind, levels, step=0):
+    count = lax.axis_size("gx")
+    pairs = []
+    for at in range(levels):
+        other = 1 - at if levels == 2 else at + 1 if kind == "low" else at - 1
+        if 0 <= other < levels:
+            pairs.append((at, other))
+    if step == 0:
+        return lax.ppermute(value, "gz", pairs)
+    return lax.ppermute(
+        value,
+        ("gx", "gz"),
+        [
+            (x * levels + at, (x + step) % count * levels + other)
+            for x in range(count)
+            for at, other in pairs
+        ],
+    )
+
+
+def two_substeps(pops, coarse_pops, interface):
+    level = lax.axis_index("gz").astype(jnp.int32).reshape(1)
+    levels = lax.axis_size("gz")
+    depth, height, width = interface.shape
+    sizes = rim_sizes(levels)
+    slots = len(sizes)
+    kinds = ["low", "high"][:slots]
+    rims_of = [(size, height, width) for size, _ in sizes]
+    strips_of = [(count, height, 128) for _, count in sizes]
+    outs = call(
+        functools.partial(first_body, levels),
+        [(channels, depth, height, width)] + rims_of + [(depth, height, 128)] * 2 + strips_of * 2,
+        [level, pops, coarse_pops, interface],
+    )
+    posts, rims = outs[0], outs[1 : slots + 1]
+    right, left = outs[slots + 1 : slots + 3]
+    right_rims, left_rims = outs[slots + 3 : 2 * slots + 3], outs[2 * slots + 3 :]
+    low = shifted(right, "gx", 1)
+    high = shifted(left, "gx", -1)
+    low_rims = [to_level(value, kind, levels, 1) for value, kind in zip(right_rims, kinds)]
+    high_rims = [to_level(value, kind, levels, -1) for value, kind in zip(left_rims, kinds)]
+    rims = [to_level(value, kind, levels) for value, kind in zip(rims, kinds)]
+    given = [level, posts, low, high, *rims, *low_rims, *high_rims]
+    counts = row_table(depth, levels)[-1]
+    down, up = call(
+        functools.partial(rows_body, levels), [(count, width) for count in counts], given
+    )
+    above = shifted(down, "gy", -1)
+    below = shifted(up, "gy", 1)
+    rows, lanes = height + 8, width + 128
+    layers = depth + LOW + HIGH
+    return call(
+        functools.partial(steps_body, levels),
+        [pops.shape, (3, depth + 3, rows, lanes)],
+        given + [above, below],
+        [
+            pltpu.VMEM((channels, layers, rows, lanes), jnp.float32),
+            pltpu.VMEM((layers, rows, 128), jnp.float32),
+            pltpu.VMEM((layers, rows, 128), jnp.float32),
+            pltpu.VMEM((19, rows, lanes), jnp.float32),
+            pltpu.VMEM((19, layers - 2, rows, lanes), jnp.float32),
+        ],
+    )
 
 
 def phis(frac):
@@ -305,30 +620,12 @@
     level = lax.axis_index("gz")
     levels = lax.axis_size("gz")
     depth, height, width = interface.shape
-    rows = lax.broadcasted_iota(jnp.int32, (depth, 1, 1), 0)
-    bottom = (level == 0) & (rows == 0)
-    top = (level == levels - 1) & (rows == depth - 1)
-    state = pops
-    for substep in range(2):
-        posts = collide(state, coarse_pops, interface)
-        pulled = axis_pull(posts)
-        state = wall_fix(pulled, posts, bottom, top)
-    density, flow = macroscopic(state)
-    velocity = jnp.stack(flow)
-    velocity_ext = with_halo(velocity, (("gx", 3), ("gy", 2), ("gz", 1)), 2, True)
+    state, circle = two_substeps(pops, coarse_pops, interface)
     rim_rows = lax.broadcasted_iota(jnp.int32, (1, depth + 4, 1, 1), 1)
     keep = jnp.logical_not(
         (level == 0) & (rim_rows < 2) | (level == levels - 1) & (rim_rows >= depth + 2)
     )
-    velocity_ext = jnp.where(keep, velocity_ext, 0.0)
     blocks = home.shape[0]
-    circle = velocity_ext[:, 1:]
-    circle = jnp.pad(
-        jnp.concatenate([circle[:, :, 2:], jnp.zeros_like(circle[:, :, :5]), circle[:, :, 1:2]], axis=2),
-        ((0, 0), (0, 0), (0, 0), (0, 0)),
-    )
-    lanes = jnp.zeros(circle.shape[:3] + (125,), jnp.float32)
-    circle = jnp.concatenate([circle[..., 2:], lanes, circle[..., 1:2]], axis=3)
     spread, states = droplets(
         circle, drop_vel, drop_frac, home, counts, (depth, height, width)
     )

time: 147 us -> 95.9 us (0.65)
  other arithmetic: 29.1 us -> 3.55 us
  starting transfers between devices: 45.5 us -> 24.9 us
  Pallas kernels: 9.85 us -> 24.5 us
  waiting for transfers between devices: 45.4 us -> 35.7 us
  local copies, waits for them, and re-layouts: 14.4 us -> 6.05 us
    ppermute x15 -> x6, starting transfers between devices: 30 us -> 10.9 us  [with_halo(): lax.ppermute(head, axis, [((i + 1) % count, i) for i in range(ends)])]
    unnamed x18 -> x0, other arithmetic: 14.8 us -> none
    pallas_call x0 -> x3, Pallas kernels: none -> 14.6 us  [call(): pl.pallas_call(body, out_shape=[jax.ShapeDtypeStruct(shape, jnp.float32)...]
    ppermute x15 -> x6, starting transfers between devices: 15.5 us -> 1.93 us  [with_halo(): lax.ppermute(tail, axis, [(i, (i + 1) % count) for i in range(ends)])]
    ppermute x0 -> x7, starting transfers between devices: none -> 12.1 us  [the longest x2 4.72 us: to_level(): lax.ppermute(value, ('gx', 'gz'), [(x * levels + at, (x + step) % count *...]
    ppermute x15 -> x6, waiting for transfers between devices: 24.5 us -> 13.8 us  [with_halo(): lax.ppermute(tail, axis, [(i, (i + 1) % count) for i in range(ends)])]
    ppermute x0 -> x7, waiting for transfers between devices: none -> 10.2 us  [the longest x4 8.33 us: shifted(): lax.ppermute(value, axis, [(i, (i + step) % count) for i in range(count)])]
    ppermute x15 -> x6, waiting for transfers between devices: 21 us -> 11.6 us  [with_halo(): lax.ppermute(head, axis, [((i + 1) % count, i) for i in range(ends)])]
  transfers between devices with their start and end apart: 30 -> 19, of which waited for: 20 -> 10; matrix products, arithmetic and copies ran while one was open for 8% -> 3% of each run, Pallas kernels for 0% -> 0%
where the time goes in v2:
time: 95.9 us; the launch traced here: 95.6 us
  waiting for transfers between devices  35.7 us (37%)
  starting transfers between devices  24.9 us (26%)
  Pallas kernels  24.5 us (26%)
  local copies, waits for them, and re-layouts  6.05 us (6%)
  other arithmetic  3.55 us (4%)
  between operations  0.96 us (1%)
    pallas_call x3, Pallas kernels, call(): pl.pallas_call(body, out_shape=[jax.ShapeDtypeStruct(shape, jnp.float32)...  14.6 us
    ppermute x6, waiting for transfers between devices, with_halo(): lax.ppermute(tail, axis, [(i, (i + 1) % count) for i in range(ends)])  13.8 us
    ppermute x6, waiting for transfers between devices, with_halo(): lax.ppermute(head, axis, [((i + 1) % count, i) for i in range(ends)])  11.6 us
    ppermute x6, starting transfers between devices, with_halo(): lax.ppermute(head, axis, [((i + 1) % count, i) for i in range(ends)])  10.9 us
    pallas_call x1, Pallas kernels, droplets(): pl.pallas_call(functools.partial(droplet_body, size), out_shape=(jax.Shap...  9.85 us
    ppermute x4, waiting for transfers between devices, shifted(): lax.ppermute(value, axis, [(i, (i + step) % count) for i in range(count)])  8.33 us
    ppermute x2, starting transfers between devices, to_level(): lax.ppermute(value, ('gx', 'gz'), [(x * levels + at, (x + step) % count *...  4.72 us
    unnamed x32, local copies, waits for them, and re-layouts  4.51 us
  transfers between devices with their start and end apart: 19, of which 10 were waited for; matrix products, arithmetic and copies ran while one was open for 3% of the time, Pallas kernels for 0%

profile of v2, /device:TPU:0, one launch (start us, length us, event | category | flops | bytes accessed | tf_op | source)
XLA Modules:
  0.0 95.6 jit_solution(17516798593802468156)
XLA Ops:
  0.6 3.3 %shard_map.103 = (f32[20,8,8,128]{3,2,1,0:T(8,128)}, f32[60,8,128]{2,1,0:T(8,128)}, f32[8,8,128]{2,1,0:T(8,128)}, f32[8,8,128]{2,1,0:T(8,128)}, f32[4,8,128]{2,1,0:T(8,128)}, /*index=5*/f32[4,8,128]{2,1,0:T(8,128)}) custom-call(s32[1]{0:T(128)} %bitcast.level_ref, f32[19,8,8,128]{3,2,1,0:T(8,128)} %pops_ref.1, bf16[19,8,8,128]{3,2,1,0:T(8,128)(2,1)} %coarse_ref.1, ...), custom_call_target="tpu_custom_call" | custom-call | tf_op jit(solution)/shard_map/pallas_call | solution.py:408
  3.9 3.0 %collective-permute-start.2 = (f32[60,8,128]{2,1,0:T(8,128)}, f32[60,8,128]{2,1,0:T(8,128)S(1)}, u32[]{:S(2)}, u32[]{:S(2)}) collective-permute-start(f32[60,8,128]{2,1,0:T(8,128)} %get-tuple-element.18), channel_id=1, source_target_pairs={{0,1},{1,0},{2,3},{3,2},{4,5},{5,4},{6,7},{7,6},{8,9},{9,8},{10,11... | collective-permute-start | bytes 737288 | tf_op jit(solution)/shard_map/ppermute | solution.py:431
  6.9 1.6 %collective-permute-start = (f32[8,8,128]{2,1,0:T(8,128)}, f32[8,8,128]{2,1,0:T(8,128)S(1)}, u32[]{:S(2)}, u32[]{:S(2)}) collective-permute-start(f32[8,8,128]{2,1,0:T(8,128)} %get-tuple-element.16), channel_id=1, source_target_pairs={{0,8},{8,16},{16,24},{24,0},{1,9},{9,17},{17,25},{25,1},{2,10},{10... | collective-permute-start | bytes 98312 | tf_op jit(solution)/shard_map/ppermute | solution.py:420
  8.5 2.2 %collective-permute-start.1 = (f32[8,8,128]{2,1,0:T(8,128)}, f32[8,8,128]{2,1,0:T(8,128)S(1)}, u32[]{:S(2)}, u32[]{:S(2)}) collective-permute-start(f32[8,8,128]{2,1,0:T(8,128)} %get-tuple-element.17), channel_id=1, source_target_pairs={{0,24},{8,0},{16,8},{24,16},{1,25},{9,1},{17,9},{25,17},{2,26},{10... | collective-permute-start | bytes 98312 | tf_op jit(solution)/shard_map/ppermute | solution.py:420
  10.7 4.7 %collective-permute-start.4 = (f32[4,8,128]{2,1,0:T(8,128)}, f32[4,8,128]{2,1,0:T(8,128)S(1)}, u32[]{:S(2)}, u32[]{:S(2)}) collective-permute-start(f32[4,8,128]{2,1,0:T(8,128)} %get-tuple-element.20), channel_id=1, source_target_pairs={{0,25},{1,24},{8,1},{9,0},{16,9},{17,8},{24,17},{25,16},{2,27},{3,... | collective-permute-start | bytes 49160 | tf_op jit(solution)/shard_map/ppermute | solution.py:432
  15.5 1.9 %collective-permute-done.3.rest_1_ = f32[4,8,128]{2,1,0:T(8,128)S(1)} collective-permute-done((f32[4,8,128]{2,1,0:T(8,128)}, f32[4,8,128]{2,1,0:T(8,128)S(1)}, u32[]{:S(2)}, u32[]{:S(2)}) %collective-permute-start.3) | collective-permute-done | bytes 16416 | tf_op jit(solution)/shard_map/ppermute | solution.py:432
  18.1 2.3 %shard_map.104 = (f32[760,128]{1,0:T(8,128)}, f32[520,128]{1,0:T(8,128)}) custom-call(s32[1]{0:T(128)} %bitcast.level_ref, f32[20,8,8,128]{3,2,1,0:T(8,128)} %get-tuple-element.15.posts_ref, f32[8,8,128]{2,1,0:T(8,128)} %copy-done.8, f32[8,8,128]{2,1,0:T(8,128)} %copy-done.9, f32[60,8,128]{2,1,0:T(8,128)} %copy-done.5, f32[4,8,128]{2,1,0:T(8,128)} %copy-done.10, ...), custom_call_target="tpu_custom_call" | custom-call | tf_op jit(solution)/shard_map/pallas_call | solution.py:408
  21.2 8.3 %collective-permute-done.6.rest_4_ = f32[520,128]{1,0:T(8,128)S(1)} collective-permute-done((f32[520,128]{1,0:T(8,128)}, f32[520,128]{1,0:T(8,128)S(1)}, u32[]{:S(2)}, u32[]{:S(2)}) %collective-permute-start.6) | collective-permute-done | bytes 266272 | tf_op jit(solution)/shard_map/ppermute | solution.py:420
  31.0 9.0 %shard_map.105 = (f32[19,8,8,128]{3,2,1,0:T(8,128)}, f32[3,11,16,256]{3,2,1,0:T(8,128)}) custom-call(s32[1]{0:T(128)} %bitcast.level_ref, f32[20,8,8,128]{3,2,1,0:T(8,128)} %get-tuple-element.15.posts_ref, f32[8,8,128]{2,1,0:T(8,128)} %copy-done.8, f32[8,8,128]{2,1,0:T(8,128)} %copy-done.9, f32[60,8,128]{2,1,0:T(8,128)} %copy-done.5, ...), custom_call_target="tpu_custom_call" | custom-call | tf_op jit(solution)/shard_map/pallas_call | solution.py:408
  40.7 1.0 %copy-done = f32[3,11,16,256]{3,2,1,0:T(8,128)S(1)} copy-done((f32[3,11,16,256]{3,2,1,0:T(8,128)S(1)}, f32[3,11,16,256]{3,2,1,0:T(8,128)}, u32[]{:S(2)}) %copy-start) | copy-done | bytes 540696
  41.7 9.8 %shard_map.106 = (f32[3,11,16,256]{3,2,1,0:T(8,128)S(1)}, f32[6,16,128]{2,1,0:T(8,128)S(1)}) custom-call(s32[16]{0:T(128)S(1)} %copy-done.4, f32[3,11,16,256]{3,2,1,0:T(8,128)S(1)} %copy-done, f32[3,16,128]{2,1,0:T(8,128)S(1)} %copy-done.1, f32[3,16,128]{2,1,0:T(8,128)S(1)} %copy-done.2, s32[16,128]{1,0:T(8,128)S(1)} %copy-done.3), custom_call_target="tpu_custom_call" | custom-call | tf_op jit(solution)/shard_map/pallas_call | solution.py:598
  52.6 3.7 %collective-permute-start.8 = (f32[3,12,12,2]{3,2,1,0:T(8,128)S(1)}, f32[3,12,12,2]{3,2,1,0:T(8,128)S(1)}, u32[]{:S(2)}, u32[]{:S(2)}) collective-permute-start(f32[3,12,12,2]{3,2,1,0:T(8,128)S(1)} %get-tuple-element.34), channel_id=1, source_target_pairs={{8,0},{16,8},{24,16},{0,24},{9,1},{17,9},{25,17},{1,25},{10,2},{18... | collective-permute-start | bytes 10376 | tf_op jit(solution)/shard_map/ppermute | solution.py:57
  56.3 1.0 %scatter_fusion = f32[6,54,128]{2,0,1:T(8,128)S(1)} fusion(f32[6,54,128]{2,0,1:T(8,128)S(1)} %broadcast_in_dim.52, s32[16]{0:T(128)S(1)} %compare_select_fusion, f32[16,6,128]{2,1,0:T(8,128)S(1)} %copy.13), kind=kCustom, calls=%fused_computation | custom fusion | bytes 147520 | tf_op jit(solution)/shard_map/scatter | solution.py:647
  57.4 3.9 %collective-permute-start.14 = (f32[6,3,3,1,2,128]{5,0,4,3,2,1:T(8,128)S(1)}, f32[6,3,3,1,2,128]{5,0,4,3,2,1:T(8,128)S(1)}, u32[]{:S(2)}, u32[]{:S(2)}) collective-permute-start(f32[6,3,3,1,2,128]{5,0,4,3,2,1:T(8,128)S(1)} %get-tuple-element.40), channel_id=1, source_target_pairs={{8,0},{16,8},{24,16},{0,24},{9,1},{17,9},{25,17},{1,25},{10,2},{18... | collective-permute-start | bytes 165896 | tf_op jit(solution)/shard_map/ppermute | solution.py:57
  61.3 2.4 %collective-permute-done.8 = f32[3,12,12,2]{3,2,1,0:T(8,128)S(1)} collective-permute-done((f32[3,12,12,2]{3,2,1,0:T(8,128)S(1)}, f32[3,12,12,2]{3,2,1,0:T(8,128)S(1)}, u32[]{:S(2)}, u32[]{:S(2)}) %collective-permute-start.8) | collective-permute-done | bytes 3488 | tf_op jit(solution)/shard_map/ppermute | solution.py:57
  63.7 6.8 %collective-permute-done.7 = f32[3,12,12,2]{3,2,1,0:T(8,128)S(1)} collective-permute-done((f32[3,12,12,2]{3,2,1,0:T(8,128)S(1)}, f32[3,12,12,2]{3,2,1,0:T(8,128)S(1)}, u32[]{:S(2)}, u32[]{:S(2)}) %collective-permute-start.7) | collective-permute-done | bytes 3488 | tf_op jit(solution)/shard_map/ppermute | solution.py:55
  71.4 1.4 %collective-permute-done.10 = f32[3,12,2,136]{3,2,1,0:T(2,128)S(1)} collective-permute-done((f32[3,12,2,136]{3,2,1,0:T(2,128)S(1)}, f32[3,12,2,136]{3,2,1,0:T(2,128)S(1)}, u32[]{:S(2)}, u32[]{:S(2)}) %collective-permute-start.10) | collective-permute-done | bytes 39200 | tf_op jit(solution)/shard_map/ppermute | solution.py:57
  72.8 2.5 %collective-permute-done.9 = f32[3,12,2,136]{3,2,1,0:T(2,128)S(1)} collective-permute-done((f32[3,12,2,136]{3,2,1,0:T(2,128)S(1)}, f32[3,12,2,136]{3,2,1,0:T(2,128)S(1)}, u32[]{:S(2)}, u32[]{:S(2)}) %collective-permute-start.9) | collective-permute-done | bytes 39200 | tf_op jit(solution)/shard_map/ppermute | solution.py:55
  75.4 1.6 %collective-permute-start.12 = (f32[3,2,16,136]{3,2,1,0:T(8,128)S(1)}, f32[3,2,16,136]{3,2,1,0:T(8,128)S(1)}, u32[]{:S(2)}, u32[]{:S(2)}) collective-permute-start(f32[3,2,16,136]{3,2,1,0:T(8,128)S(1)} %get-tuple-element.28), channel_id=1, source_target_pairs={{1,0},{0,1},{3,2},{2,3},{5,4},{4,5},{7,6},{6,7},{9,8},{8,9},{11,10... | collective-permute-start | bytes 156680 | tf_op jit(solution)/shard_map/ppermute | solution.py:57
  78.5 2.6 %collective-permute-done.12 = f32[3,2,16,136]{3,2,1,0:T(8,128)S(1)} collective-permute-done((f32[3,2,16,136]{3,2,1,0:T(8,128)S(1)}, f32[3,2,16,136]{3,2,1,0:T(8,128)S(1)}, u32[]{:S(2)}, u32[]{:S(2)}) %collective-permute-start.12) | collective-permute-done | bytes 52256 | tf_op jit(solution)/shard_map/ppermute | solution.py:57
  81.2 1.3 %collective-permute-done.11 = f32[3,2,16,136]{3,2,1,0:T(8,128)S(1)} collective-permute-done((f32[3,2,16,136]{3,2,1,0:T(8,128)S(1)}, f32[3,2,16,136]{3,2,1,0:T(8,128)S(1)}, u32[]{:S(2)}, u32[]{:S(2)}) %collective-permute-start.11) | collective-permute-done | bytes 52256 | tf_op jit(solution)/shard_map/ppermute | solution.py:55
  83.4 1.6 %collective-permute-start.18 = (f32[6,1,5,5,2,128]{5,0,4,3,2,1:T(8,128)S(1)}, f32[6,1,5,5,2,128]{5,0,4,3,2,1:T(8,128)S(1)}, u32[]{:S(2)}, u32[]{:S(2)}) collective-permute-start(f32[6,1,5,5,2,128]{5,0,4,3,2,1:T(8,128)S(1)} %get-tuple-element.32), channel_id=1, source_target_pairs={{1,0},{0,1},{3,2},{2,3},{5,4},{4,5},{7,6},{6,7},{9,8},{8,9},{11,10... | collective-permute-start | bytes 460808 | tf_op jit(solution)/shard_map/ppermute | solution.py:57
  86.3 5.2 %collective-permute-done.18 = f32[6,1,5,5,2,128]{5,0,4,3,2,1:T(8,128)S(1)} collective-permute-done((f32[6,1,5,5,2,128]{5,0,4,3,2,1:T(8,128)S(1)}, f32[6,1,5,5,2,128]{5,0,4,3,2,1:T(8,128)S(1)}, u32[]{:S(2)}, u32[]{:S(2)}) %collective-permute-start.18) | collective-permute-done | bytes 153632 | tf_op jit(solution)/shard_map/ppermute | solution.py:57
  91.5 3.2 %collective-permute-done.17 = f32[6,1,5,5,2,128]{5,0,4,3,2,1:T(8,128)S(1)} collective-permute-done((f32[6,1,5,5,2,128]{5,0,4,3,2,1:T(8,128)S(1)}, f32[6,1,5,5,2,128]{5,0,4,3,2,1:T(8,128)S(1)}, u32[]{:S(2)}, u32[]{:S(2)}) %collective-permute-start.17) | collective-permute-done | bytes 153632 | tf_op jit(solution)/shard_map/ppermute | solution.py:55
  (82 shorter events, 10.2 us)
Async XLA Ops:
  3.9 13.5 %collective-permute-start.2 = (f32[60,8,128]{2,1,0:T(8,128)}, f32[60,8,128]{2,1,0:T(8,128)S(1)}, u32[]{:S(2)}, u32[]{:S(2)}) collective-permute-start(f32[60,8,128]{2,1,0:T(8,128)} %get-tuple-element.18), channel_id=1, source_target_pairs={{0,1},{1,0},{2,3},{3,2},{4,5},{5,4},{6,7},{7,6},{8,9},{9,8},{10,11... | collective-permute-start | bytes 737288 | tf_op jit(solution)/shard_map/ppermute | solution.py:431
  6.9 10.5 %collective-permute-start = (f32[8,8,128]{2,1,0:T(8,128)}, f32[8,8,128]{2,1,0:T(8,128)S(1)}, u32[]{:S(2)}, u32[]{:S(2)}) collective-permute-start(f32[8,8,128]{2,1,0:T(8,128)} %get-tuple-element.16), channel_id=1, source_target_pairs={{0,8},{8,16},{16,24},{24,0},{1,9},{9,17},{17,25},{25,1},{2,10},{10... | collective-permute-start | bytes 98312 | tf_op jit(solution)/shard_map/ppermute | solution.py:420
  8.5 8.9 %collective-permute-start.1 = (f32[8,8,128]{2,1,0:T(8,128)}, f32[8,8,128]{2,1,0:T(8,128)S(1)}, u32[]{:S(2)}, u32[]{:S(2)}) collective-permute-start(f32[8,8,128]{2,1,0:T(8,128)} %get-tuple-element.17), channel_id=1, source_target_pairs={{0,24},{8,0},{16,8},{24,16},{1,25},{9,1},{17,9},{25,17},{2,26},{10... | collective-permute-start | bytes 98312 | tf_op jit(solution)/shard_map/ppermute | solution.py:420
  10.7 4.7 %copy-start.14 = (s32[16]{0:T(128)S(1)}, s32[16]{0:T(128)}, u32[]{:S(2)}) copy-start(s32[16]{0:T(128)} %param.15) | copy-start | bytes 196
  10.7 6.6 %collective-permute-start.3 = (f32[4,8,128]{2,1,0:T(8,128)}, f32[4,8,128]{2,1,0:T(8,128)S(1)}, u32[]{:S(2)}, u32[]{:S(2)}) collective-permute-start(f32[4,8,128]{2,1,0:T(8,128)} %get-tuple-element.19), channel_id=1, source_target_pairs={{0,9},{1,8},{8,17},{9,16},{16,25},{17,24},{24,1},{25,0},{2,11},{3,... | collective-permute-start | bytes 49160 | tf_op jit(solution)/shard_map/ppermute | solution.py:432
  10.7 6.6 %collective-permute-start.4 = (f32[4,8,128]{2,1,0:T(8,128)}, f32[4,8,128]{2,1,0:T(8,128)S(1)}, u32[]{:S(2)}, u32[]{:S(2)}) collective-permute-start(f32[4,8,128]{2,1,0:T(8,128)} %get-tuple-element.20), channel_id=1, source_target_pairs={{0,25},{1,24},{8,1},{9,0},{16,9},{17,8},{24,17},{25,16},{2,27},{3,... | collective-permute-start | bytes 49160 | tf_op jit(solution)/shard_map/ppermute | solution.py:432
  20.4 9.1 %collective-permute-start.5 = (f32[760,128]{1,0:T(8,128)}, f32[760,128]{1,0:T(8,128)S(1)}, u32[]{:S(2)}, u32[]{:S(2)}) collective-permute-start(f32[760,128]{1,0:T(8,128)} %get-tuple-element.21), channel_id=1, source_target_pairs={{0,6},{2,0},{4,2},{6,4},{1,7},{3,1},{5,3},{7,5},{8,14},{10,8},{12,... | collective-permute-start | bytes 1167368 | tf_op jit(solution)/shard_map/ppermute | solution.py:420
  20.6 8.9 %collective-permute-start.6 = (f32[520,128]{1,0:T(8,128)}, f32[520,128]{1,0:T(8,128)S(1)}, u32[]{:S(2)}, u32[]{:S(2)}) collective-permute-start(f32[520,128]{1,0:T(8,128)} %get-tuple-element.22), channel_id=1, source_target_pairs={{0,2},{2,4},{4,6},{6,0},{1,3},{3,5},{5,7},{7,1},{8,10},{10,12},{12... | collective-permute-start | bytes 798728 | tf_op jit(solution)/shard_map/ppermute | solution.py:420
  21.2 18.9 %copy-start.1 = (f32[3,16,128]{2,1,0:T(8,128)S(1)}, f32[3,16,128]{2,1,0:T(8,128)}, u32[]{:S(2)}) copy-start(f32[3,16,128]{2,1,0:T(8,128)} %speed_ref.1) | copy-start | bytes 73732
  21.2 18.8 %copy-start.2 = (f32[3,16,128]{2,1,0:T(8,128)S(1)}, f32[3,16,128]{2,1,0:T(8,128)}, u32[]{:S(2)}) copy-start(f32[3,16,128]{2,1,0:T(8,128)} %frac_ref.1) | copy-start | bytes 73732
  21.2 18.8 %copy-start.3 = (s32[16,128]{1,0:T(8,128)S(1)}, s32[16,128]{1,0:T(8,128)}, u32[]{:S(2)}) copy-start(s32[16,128]{1,0:T(8,128)} %home_ref.1) | copy-start | bytes 24580
  52.6 11.1 %collective-permute-start.8 = (f32[3,12,12,2]{3,2,1,0:T(8,128)S(1)}, f32[3,12,12,2]{3,2,1,0:T(8,128)S(1)}, u32[]{:S(2)}, u32[]{:S(2)}) collective-permute-start(f32[3,12,12,2]{3,2,1,0:T(8,128)S(1)} %get-tuple-element.34), channel_id=1, source_target_pairs={{8,0},{16,8},{24,16},{0,24},{9,1},{17,9},{25,17},{1,25},{10,2},{18... | collective-permute-start | bytes 10376 | tf_op jit(solution)/shard_map/ppermute | solution.py:57
  56.3 14.2 %collective-permute-start.7 = (f32[3,12,12,2]{3,2,1,0:T(8,128)S(1)}, f32[3,12,12,2]{3,2,1,0:T(8,128)S(1)}, u32[]{:S(2)}, u32[]{:S(2)}) collective-permute-start(f32[3,12,12,2]{3,2,1,0:T(8,128)S(1)} %get-tuple-element.33), channel_id=1, source_target_pairs={{0,8},{8,16},{16,24},{24,0},{1,9},{9,17},{17,25},{25,1},{2,10},{10... | collective-permute-start | bytes 10376 | tf_op jit(solution)/shard_map/ppermute | solution.py:55
  57.4 20.5 %collective-permute-start.14 = (f32[6,3,3,1,2,128]{5,0,4,3,2,1:T(8,128)S(1)}, f32[6,3,3,1,2,128]{5,0,4,3,2,1:T(8,128)S(1)}, u32[]{:S(2)}, u32[]{:S(2)}) collective-permute-start(f32[6,3,3,1,2,128]{5,0,4,3,2,1:T(8,128)S(1)} %get-tuple-element.40), channel_id=1, source_target_pairs={{8,0},{16,8},{24,16},{0,24},{9,1},{17,9},{25,17},{1,25},{10,2},{18... | collective-permute-start | bytes 165896 | tf_op jit(solution)/shard_map/ppermute | solution.py:57
  61.3 16.7 %collective-permute-start.13 = (f32[6,3,3,1,2,128]{5,0,4,3,2,1:T(8,128)S(1)}, f32[6,3,3,1,2,128]{5,0,4,3,2,1:T(8,128)S(1)}, u32[]{:S(2)}, u32[]{:S(2)}) collective-permute-start(f32[6,3,3,1,2,128]{5,0,4,3,2,1:T(8,128)S(1)} %get-tuple-element.39), channel_id=1, source_target_pairs={{0,8},{8,16},{16,24},{24,0},{1,9},{9,17},{17,25},{25,1},{2,10},{10... | collective-permute-start | bytes 165896 | tf_op jit(solution)/shard_map/ppermute | solution.py:55
  70.7 2.0 %collective-permute-start.10 = (f32[3,12,2,136]{3,2,1,0:T(2,128)S(1)}, f32[3,12,2,136]{3,2,1,0:T(2,128)S(1)}, u32[]{:S(2)}, u32[]{:S(2)}) collective-permute-start(f32[3,12,2,136]{3,2,1,0:T(2,128)S(1)} %get-tuple-element.30), channel_id=1, source_target_pairs={{2,0},{4,2},{6,4},{0,6},{3,1},{5,3},{7,5},{1,7},{10,8},{12,10},{14... | collective-permute-start | bytes 117512 | tf_op jit(solution)/shard_map/ppermute | solution.py:57
  70.8 4.5 %collective-permute-start.9 = (f32[3,12,2,136]{3,2,1,0:T(2,128)S(1)}, f32[3,12,2,136]{3,2,1,0:T(2,128)S(1)}, u32[]{:S(2)}, u32[]{:S(2)}) collective-permute-start(f32[3,12,2,136]{3,2,1,0:T(2,128)S(1)} %get-tuple-element.29), channel_id=1, source_target_pairs={{0,2},{2,4},{4,6},{6,0},{1,3},{3,5},{5,7},{7,1},{8,10},{10,12},{12... | collective-permute-start | bytes 117512 | tf_op jit(solution)/shard_map/ppermute | solution.py:55
  75.4 5.7 %collective-permute-start.12 = (f32[3,2,16,136]{3,2,1,0:T(8,128)S(1)}, f32[3,2,16,136]{3,2,1,0:T(8,128)S(1)}, u32[]{:S(2)}, u32[]{:S(2)}) collective-permute-start(f32[3,2,16,136]{3,2,1,0:T(8,128)S(1)} %get-tuple-element.28), channel_id=1, source_target_pairs={{1,0},{0,1},{3,2},{2,3},{5,4},{4,5},{7,6},{6,7},{9,8},{8,9},{11,10... | collective-permute-start | bytes 156680 | tf_op jit(solution)/shard_map/ppermute | solution.py:57
  77.1 5.4 %collective-permute-start.11 = (f32[3,2,16,136]{3,2,1,0:T(8,128)S(1)}, f32[3,2,16,136]{3,2,1,0:T(8,128)S(1)}, u32[]{:S(2)}, u32[]{:S(2)}) collective-permute-start(f32[3,2,16,136]{3,2,1,0:T(8,128)S(1)} %get-tuple-element.27), channel_id=1, source_target_pairs={{0,1},{1,0},{2,3},{3,2},{4,5},{5,4},{6,7},{7,6},{8,9},{9,8},{10,11... | collective-permute-start | bytes 156680 | tf_op jit(solution)/shard_map/ppermute | solution.py:55
  78.0 5.4 %collective-permute-start.16 = (f32[6,3,1,5,2,128]{5,0,4,3,2,1:T(8,128)S(1)}, f32[6,3,1,5,2,128]{5,0,4,3,2,1:T(8,128)S(1)}, u32[]{:S(2)}, u32[]{:S(2)}) collective-permute-start(f32[6,3,1,5,2,128]{5,0,4,3,2,1:T(8,128)S(1)} %get-tuple-element.36), channel_id=1, source_target_pairs={{2,0},{4,2},{6,4},{0,6},{3,1},{5,3},{7,5},{1,7},{10,8},{12,10},{14... | collective-permute-start | bytes 276488 | tf_op jit(solution)/shard_map/ppermute | solution.py:57
  78.0 5.3 %collective-permute-start.15 = (f32[6,3,1,5,2,128]{5,0,4,3,2,1:T(8,128)S(1)}, f32[6,3,1,5,2,128]{5,0,4,3,2,1:T(8,128)S(1)}, u32[]{:S(2)}, u32[]{:S(2)}) collective-permute-start(f32[6,3,1,5,2,128]{5,0,4,3,2,1:T(8,128)S(1)} %get-tuple-element.35), channel_id=1, source_target_pairs={{0,2},{2,4},{4,6},{6,0},{1,3},{3,5},{5,7},{7,1},{8,10},{10,12},{12... | collective-permute-start | bytes 276488 | tf_op jit(solution)/shard_map/ppermute | solution.py:55
  83.4 2.1 %copy-start.12 = (pred[128]{0:T(512)(128)(4,1)S(1)}, pred[128]{0:T(512)(128)(4,1)}, u32[]{:S(2)}) copy-start(pred[128]{0:T(512)(128)(4,1)} %constant.5.clone.1) | copy-start | bytes 388
  83.4 8.0 %collective-permute-start.18 = (f32[6,1,5,5,2,128]{5,0,4,3,2,1:T(8,128)S(1)}, f32[6,1,5,5,2,128]{5,0,4,3,2,1:T(8,128)S(1)}, u32[]{:S(2)}, u32[]{:S(2)}) collective-permute-start(f32[6,1,5,5,2,128]{5,0,4,3,2,1:T(8,128)S(1)} %get-tuple-element.32), channel_id=1, source_target_pairs={{1,0},{0,1},{3,2},{2,3},{5,4},{4,5},{7,6},{6,7},{9,8},{8,9},{11,10... | collective-permute-start | bytes 460808 | tf_op jit(solution)/shard_map/ppermute | solution.py:57
  85.1 9.6 %collective-permute-start.17 = (f32[6,1,5,5,2,128]{5,0,4,3,2,1:T(8,128)S(1)}, f32[6,1,5,5,2,128]{5,0,4,3,2,1:T(8,128)S(1)}, u32[]{:S(2)}, u32[]{:S(2)}) collective-permute-start(f32[6,1,5,5,2,128]{5,0,4,3,2,1:T(8,128)S(1)} %get-tuple-element.31), channel_id=1, source_target_pairs={{0,1},{1,0},{2,3},{3,2},{4,5},{5,4},{6,7},{7,6},{8,9},{9,8},{10,11... | collective-permute-start | bytes 460808 | tf_op jit(solution)/shard_map/ppermute | solution.py:55
  (10 other events, 6.9 us)

commit v3 on v2

--- a/solution.py
+++ b/solution.py
@@ -9,7 +9,6 @@
 from jax.experimental.pallas import tpu as pltpu
 from jax.sharding import PartitionSpec as P
 
-TILE = 8
 CAP = 2
 
 
@@ -41,35 +40,18 @@
 inverse_tau = 0.8
 relax = 0.5
 couple = 8.0
-highest = lax.Precision.HIGHEST
-
-
-def with_halo(cells, sides, width, closed):
-    for axis, dim in sides:
-        count = lax.axis_size(axis)
-        ends = count if closed else count - 1
-        head = lax.slice_in_dim(cells, 0, width, axis=dim)
-        tail = lax.slice_in_dim(cells, cells.shape[dim] - width, cells.shape[dim], axis=dim)
-        cells = jnp.concatenate(
-            [
-                lax.ppermute(tail, axis, [(i, (i + 1) % count) for i in range(ends)]),
-                cells,
-                lax.ppermute(head, axis, [((i + 1) % count, i) for i in range(ends)]),
-            ],
-            axis=dim,
-        )
-    return cells
-
-
-def fold(array, dim, inner):
-    core = lax.slice_in_dim(array, 4, inner + 4, axis=dim)
-    lower = lax.slice_in_dim(array, 0, 2, axis=dim)
-    upper = lax.slice_in_dim(array, inner + 6, inner + 8, axis=dim)
-    low_pad = [(0, 0)] * array.ndim
-    high_pad = [(0, 0)] * array.ndim
-    low_pad[dim] = (0, inner - 2)
-    high_pad[dim] = (inner - 2, 0)
-    return core + jnp.pad(lower, low_pad) + jnp.pad(upper, high_pad)
+
+
+def call(body, outs, ins, scalars=1, scratch=()):
+    vmem = pl.BlockSpec(memory_space=pltpu.VMEM)
+    return pl.pallas_call(
+        body,
+        out_shape=[jax.ShapeDtypeStruct(shape, jnp.float32) for shape in outs],
+        in_specs=[pl.BlockSpec(memory_space=pltpu.SMEM)] * scalars + [vmem] * (len(ins) - scalars),
+        out_specs=[vmem] * len(outs),
+        scratch_shapes=list(scratch),
+        compiler_params=pltpu.CompilerParams(vmem_limit_bytes=56 * 1024 * 1024),
+    )(*ins)
 
 
 ways = [tuple(int(part) for part in lattice[index][::-1]) for index in range(19)] + [(0, 0, 0)]
@@ -280,11 +262,11 @@
         guarded(level_ref[0], receiver, pack)
 
 
-def steps_body(levels, level_ref, posts_ref, low_ref, high_ref, *rest):
+def steps_body(
+    levels, level_ref, posts_ref, low_ref, high_ref, rims, low_rims, high_rims, above_ref, below_ref,
+    pops_ref, vel_ref, ext, strip_low, strip_high, pulled, second,
+):
     depth, height, width = posts_ref.shape[1:]
-    slots = len(rim_sizes(levels))
-    rims, low_rims, high_rims = rest[:slots], rest[slots : 2 * slots], rest[2 * slots : 3 * slots]
-    above_ref, below_ref, pops_ref, vel_ref, ext, strip_low, strip_high, pulled, second = rest[3 * slots :]
     own, own_strips, rim_rows, rim_strips, _ = row_table(depth, levels)
     level = level_ref[0]
     rows, lanes = height + 8, width + 128
@@ -403,45 +385,32 @@
     lax.fori_loop(depth + 1, depth + 3, second_step, 0)
 
 
-def call(body, outs, ins, scratch=()):
-    vmem = pl.BlockSpec(memory_space=pltpu.VMEM)
-    return pl.pallas_call(
-        body,
-        out_shape=[jax.ShapeDtypeStruct(shape, jnp.float32) for shape in outs],
-        in_specs=[pl.BlockSpec(memory_space=pltpu.SMEM)] + [vmem] * (len(ins) - 1),
-        out_specs=[vmem] * len(outs),
-        scratch_shapes=list(scratch),
-        compiler_params=pltpu.CompilerParams(vmem_limit_bytes=56 * 1024 * 1024),
-    )(*ins)
-
-
 def shifted(value, axis, step):
     count = lax.axis_size(axis)
     return lax.ppermute(value, axis, [(i, (i + step) % count) for i in range(count)])
 
 
-def to_level(value, kind, levels, step=0):
-    count = lax.axis_size("gx")
+def to_level(value, kind, levels, side=None, step=0):
     pairs = []
     for at in range(levels):
-        other = 1 - at if levels == 2 else at + 1 if kind == "low" else at - 1
+        other = 1 - at if levels == 2 else at + 1 if kind in ("low", "up") else at - 1
         if 0 <= other < levels:
             pairs.append((at, other))
-    if step == 0:
+    if side is None:
         return lax.ppermute(value, "gz", pairs)
+    count = lax.axis_size(side)
     return lax.ppermute(
         value,
-        ("gx", "gz"),
+        (side, "gz"),
         [
-            (x * levels + at, (x + step) % count * levels + other)
-            for x in range(count)
+            (brick * levels + at, (brick + step) % count * levels + other)
+            for brick in range(count)
             for at, other in pairs
         ],
     )
 
 
-def two_substeps(pops, coarse_pops, interface):
-    level = lax.axis_index("gz").astype(jnp.int32).reshape(1)
+def wide_exchange(level, pops, coarse_pops, interface):
     levels = lax.axis_size("gz")
     depth, height, width = interface.shape
     sizes = rim_sizes(levels)
@@ -459,8 +428,8 @@
     right_rims, left_rims = outs[slots + 3 : 2 * slots + 3], outs[2 * slots + 3 :]
     low = shifted(right, "gx", 1)
     high = shifted(left, "gx", -1)
-    low_rims = [to_level(value, kind, levels, 1) for value, kind in zip(right_rims, kinds)]
-    high_rims = [to_level(value, kind, levels, -1) for value, kind in zip(left_rims, kinds)]
+    low_rims = [to_level(value, kind, levels, "gx", 1) for value, kind in zip(right_rims, kinds)]
+    high_rims = [to_level(value, kind, levels, "gx", -1) for value, kind in zip(left_rims, kinds)]
     rims = [to_level(value, kind, levels) for value, kind in zip(rims, kinds)]
     given = [level, posts, low, high, *rims, *low_rims, *high_rims]
     counts = row_table(depth, levels)[-1]
@@ -469,20 +438,7 @@
     )
     above = shifted(down, "gy", -1)
     below = shifted(up, "gy", 1)
-    rows, lanes = height + 8, width + 128
-    layers = depth + LOW + HIGH
-    return call(
-        functools.partial(steps_body, levels),
-        [pops.shape, (3, depth + 3, rows, lanes)],
-        given + [above, below],
-        [
-            pltpu.VMEM((channels, layers, rows, lanes), jnp.float32),
-            pltpu.VMEM((layers, rows, 128), jnp.float32),
-            pltpu.VMEM((layers, rows, 128), jnp.float32),
-            pltpu.VMEM((19, rows, lanes), jnp.float32),
-            pltpu.VMEM((19, layers - 2, rows, lanes), jnp.float32),
-        ],
-    )
+    return given + [above, below]
 
 
 def phis(frac):
@@ -508,8 +464,10 @@
     return lax.dot_general(left, right, (dims, ((), ())), preferred_element_type=jnp.float32)
 
 
-def droplet_body(size, counts_ref, vel_ref, speed_ref, frac_ref, home_ref, spread_ref, state_ref,
-                 vel_high, vel_low, row_high, row_low, push_high, push_low, plane_ref):
+def droplet_body(
+    size, counts_ref, dest_ref, vel_ref, speed_ref, frac_ref, home_ref, spread_ref, stay_ref, state_ref,
+    vel_high, vel_low, row_high, row_low, push_high, push_low, plane_ref,
+):
     depth, height, width = size
     blocks = home_ref.shape[0]
     layers, rows, lanes = depth + 3, height + 8, width + 128
@@ -565,8 +523,10 @@
                 frac = frac_ref[axis, pl.ds(block, 1), :]
                 moved = speed + relax * (sample - speed)
                 push = jnp.where(live, couple * (moved - sample), 0.0)
-                state_ref[axis, pl.ds(block, 1), :] = jnp.where(live, moved, 0.0)
-                state_ref[3 + axis, pl.ds(block, 1), :] = jnp.where(live, frac + moved, 0.0)
+                stays = live & (dest_ref[block] == 13)
+                for at, value in ((axis, moved), (3 + axis, frac + moved)):
+                    state_ref[block, at : at + 1, :] = jnp.where(live, value, 0.0)
+                    stay_ref[at, pl.ds(block, 1), :] = jnp.where(stays, value, 0.0)
                 high, low = split(
                     (plane[:, :, half * 128 : half * 128 + 128] * push[None]).reshape(layers * rows, 128)
                 )
@@ -589,21 +549,254 @@
     lax.fori_loop(1, blocks // 2, step, 0)
 
 
-def droplets(velocity, drop_vel, drop_frac, home, counts, size):
-    depth, height, width = size
+def force_sides(levels):
+    if levels == 2:
+        return [("up", 0, 1, 0), ("down", 1, 0, 0)]
+    return [("up", None, None, 0), ("down", None, None, 1)]
+
+
+GROUP = 6 * 8
+
+
+def group_at(way_z, way_y):
+    return (way_z + 1) * 3 + way_y + 1
+
+
+def message_rows(depth):
+    return [8 * 8, 2 * 4 * depth, 4 * depth, 2 * 8, 8]
+
+
+def pack_body(
+    levels, level_ref, dest_ref, spread_ref, state_ref, own_ref, side_ref,
+    to_levels, north_ref, south_ref, north_levels, south_levels, outbox, strip, taken,
+):
+    depth, height, width = own_ref.shape[1:]
+    level = level_ref[0]
+    layers, rows = depth + 3, height + 8
+    lane = lax.broadcasted_iota(jnp.int32, (rows, 128), 1)
+    for layer in range(layers):
+        value = jnp.zeros((rows, 128), jnp.float32)
+        for axis in range(3):
+            here = (lane >= 4 * axis) & (lane < 4 * axis + 3)
+            value = jnp.where(here, lane_roll(spread_ref[axis, layer, :, width:], 4 * axis + 1), value)
+        strip[layer] = value
+    for code in range(27):
+        taken[code] = 0
+    outbox[...] = jnp.zeros_like(outbox)
+    for block in range(state_ref.shape[0]):
+        code = dest_ref[block]
+
+        @pl.when(code != 13)
+        def _():
+            rank = taken[code]
+            outbox[code * CAP + rank] = state_ref[block]
+            taken[code] = rank + 1
+
+    def force(part, layer, cut):
+        return spread_ref[part, layer, cut, 0:width] if part < 3 else strip[layer, cut, :]
+
+    def blocks(target, way_z, way_y):
+        base = target.shape[0] - GROUP
+        for slot in range(6):
+            target[base + 8 * slot : base + 8 * slot + 8, :] = outbox[6 * group_at(way_z, way_y) + slot]
+
+    main, north, south = slice(0, height), slice(height, height + 2), slice(rows - 1, rows)
+    for part in range(4):
+        for layer in range(depth):
+            own_ref[part, layer] = force(part, layer + 1, main)
+            at = part * depth + layer
+            north_ref[2 * at : 2 * at + 2, :] = force(part, layer + 1, north)
+            south_ref[at : at + 1, :] = force(part, layer + 1, south)
+    blocks(north_ref, 0, 1)
+    blocks(south_ref, 0, -1)
+    for slot in range(2):
+        side_ref[slot] = outbox[6 * group_at(0, 0) + slot]
+        side_ref[2 + slot] = outbox[6 * group_at(0, 0) + 4 + slot]
+    for kind, sender, _, slot in force_sides(levels):
+
+        def pack(kind=kind, slot=slot):
+            for part in range(4):
+                for step in range(2 if kind == "up" else 1):
+                    layer = depth + 1 + step if kind == "up" else 0
+                    at = 2 * part + step
+                    to_levels[slot][8 * at : 8 * at + 8, :] = force(part, layer, main)
+                    north_levels[slot][2 * at : 2 * at + 2, :] = force(part, layer, north)
+                    south_levels[slot][at : at + 1, :] = force(part, layer, south)
+            way = 1 if kind == "up" else -1
+            blocks(to_levels[slot], way, 0)
+            blocks(north_levels[slot], way, 1)
+            blocks(south_levels[slot], way, -1)
+
+        guarded(level, sender, pack)
+
+
+def main_body(levels, level_ref, counts_ref, dest_ref, *rest):
+    slots = len(rim_sizes(levels))
+    posts_ref, low_ref, high_ref = rest[:3]
+    rims, low_rims, high_rims = (rest[3 + slots * at : 3 + slots * at + slots] for at in range(3))
+    rest = rest[3 + 3 * slots :]
+    above_ref, below_ref, speed_ref, frac_ref, home_ref = rest[:5]
+    pops_ref, own_ref, stay_ref, side_ref, north_ref, south_ref = rest[5:11]
+    to_levels, north_levels, south_levels = (rest[11 + slots * at : 11 + slots * at + slots] for at in range(3))
+    rest = rest[11 + 3 * slots :]
+    vel_ref, spread_ref, state_ref, outbox, strip, taken = rest[:6]
+    steps_body(
+        levels, level_ref, posts_ref, low_ref, high_ref, rims, low_rims, high_rims, above_ref, below_ref,
+        pops_ref, vel_ref, *rest[6:11],
+    )
+    droplet_body(
+        posts_ref.shape[1:], counts_ref, dest_ref, vel_ref, speed_ref, frac_ref, home_ref,
+        spread_ref, stay_ref, state_ref, *rest[11:],
+    )
+    pack_body(
+        levels, level_ref, dest_ref, spread_ref, state_ref, own_ref, side_ref,
+        to_levels, north_ref, south_ref, north_levels, south_levels, outbox, strip, taken,
+    )
+
+
+def gather_body(levels, level_ref, own_ref, side_ref, *rest):
+    depth, height, width = own_ref.shape[1:]
+    slots = len(rim_sizes(levels))
+    north_ref, south_ref = rest[:2]
+    from_levels, north_levels, south_levels = (rest[2 + slots * at : 2 + slots * at + slots] for at in range(3))
+    force_ref, right_ref, left_ref, total = rest[2 + 3 * slots :]
+    base = depth * height
+    total[...] = own_ref[...]
+    right_ref[base:, :] = jnp.zeros((right_ref.shape[0] - base, width), jnp.float32)
+    left_ref[base:, :] = jnp.zeros((left_ref.shape[0] - base, width), jnp.float32)
+    last = slice(height - 1, height)
+    for part in range(4):
+        for layer in range(depth):
+            at = part * depth + layer
+            total[part, layer, 0:2, :] += north_ref[2 * at : 2 * at + 2, :]
+            total[part, layer, last, :] += south_ref[at : at + 1, :]
+
+    def blocks(source, way_z, way_y):
+        at = base + 16 * group_at(way_z, way_y)
+        start = source.shape[0] - GROUP
+        left_ref[at : at + 16, :] = source[start : start + 16, :]
+        right_ref[at : at + 16, :] = source[start + 32 : start + 48, :]
+
+    at = base + 16 * group_at(0, 0)
+    for slot in range(2):
+        left_ref[at + 8 * slot : at + 8 * slot + 8, :] = side_ref[slot]
+        right_ref[at + 8 * slot : at + 8 * slot + 8, :] = side_ref[2 + slot]
+    blocks(north_ref, 0, 1)
+    blocks(south_ref, 0, -1)
+    for kind, _, receiver, slot in force_sides(levels):
+
+        def take(kind=kind, slot=slot):
+            for part in range(4):
+                for step in range(2 if kind == "up" else 1):
+                    layer = step if kind == "up" else depth - 1
+                    at = 2 * part + step
+                    total[part, layer] += from_levels[slot][8 * at : 8 * at + 8, :]
+                    total[part, layer, 0:2, :] += north_levels[slot][2 * at : 2 * at + 2, :]
+                    total[part, layer, last, :] += south_levels[slot][at : at + 1, :]
+            way = 1 if kind == "up" else -1
+            blocks(from_levels[slot], way, 0)
+            blocks(north_levels[slot], way, 1)
+            blocks(south_levels[slot], way, -1)
+
+        guarded(level_ref[0], receiver, take)
+    for layer in range(depth):
+        for axis in range(3):
+            force_ref[axis, layer] = total[axis, layer]
+        for target in (right_ref, left_ref):
+            target[layer * height : layer * height + height, :] = total[3, layer]
+
+
+def last_body(levels, level_ref, part_ref, stay_ref, *rest):
+    depth, height, width = part_ref.shape[1:]
+    slots = len(rim_sizes(levels))
+    north_ref, south_ref = rest[:2]
+    from_levels, north_levels, south_levels = (rest[2 + slots * at : 2 + slots * at + slots] for at in range(3))
+    right_ref, left_ref, force_ref, arrived_ref = rest[2 + 3 * slots :]
+    blocks = stay_ref.shape[1]
+    base = depth * height
+    lane = lax.broadcasted_iota(jnp.int32, (height, 128), 1)
+    for layer in range(depth):
+        rows = slice(layer * height, layer * height + height)
+        before, after = right_ref[rows, :128], left_ref[rows, :128]
+        for axis in range(3):
+            first = jnp.where(lane < 2, lane_roll(before, -4 * axis - 1), 0.0)
+            final = jnp.where(lane == 127, lane_roll(after, 127 - 4 * axis), 0.0)
+            force_ref[axis, layer] = part_ref[axis, layer]
+            force_ref[axis, layer, :, 0:128] += first
+            force_ref[axis, layer, :, width - 128 : width] += final
+    arrived_ref[:, 0:blocks, :] = stay_ref[...]
+
+    def put(source, start, way_z, way_y, way_x):
+        code = group_at(way_z, way_y) * 3 + way_x + 1
+        at = blocks + CAP * (code if code < 13 else code - 1)
+        for slot in range(CAP):
+            for axis in range(6):
+                if source is None:
+                    value = jnp.zeros((1, 128), jnp.float32)
+                else:
+                    value = source[start + 8 * slot + axis : start + 8 * slot + axis + 1, :]
+                arrived_ref[axis, at + slot : at + slot + 1, :] = value
+
+    for way_z in (-1, 0, 1):
+        for way_y in (-1, 0, 1):
+            for way_x, source in ((1, right_ref), (-1, left_ref)):
+                put(source, base + 16 * group_at(way_z, way_y), way_z, way_y, way_x)
+    middle = 16
+
+    def put_group(source, way_z, way_y):
+        put(source, None if source is None else source.shape[0] - GROUP + middle, way_z, way_y, 0)
+
+    put_group(north_ref, 0, 1)
+    put_group(south_ref, 0, -1)
+    for kind, _, receiver, slot in force_sides(levels):
+        way = 1 if kind == "up" else -1
+
+        def take(way=way, slot=slot):
+            put_group(from_levels[slot], way, 0)
+            put_group(north_levels[slot], way, 1)
+            put_group(south_levels[slot], way, -1)
+
+        def clear(way=way):
+            for way_y in (-1, 0, 1):
+                put_group(None, way, way_y)
+
+        guarded(level_ref[0], receiver, take)
+        if receiver is not None:
+            guarded(level_ref[0], 1 - receiver, clear)
+
+
+def local(pops, coarse_pops, interface, drop_vel, drop_frac, home, counts, dest):
+    level = lax.axis_index("gz").astype(jnp.int32).reshape(1)
+    levels = lax.axis_size("gz")
+    depth, height, width = interface.shape
     blocks = home.shape[0]
+    kinds = ["up", "down"][: len(rim_sizes(levels))]
+    slots = len(kinds)
+    given = wide_exchange(level, pops, coarse_pops, interface)
     layers, rows, lanes = depth + 3, height + 8, width + 128
     flat = 3 * layers * rows
-    vmem = pl.BlockSpec(memory_space=pltpu.VMEM)
-    return pl.pallas_call(
-        functools.partial(droplet_body, size),
-        out_shape=(
-            jax.ShapeDtypeStruct((3, layers, rows, lanes), jnp.float32),
-            jax.ShapeDtypeStruct((6, blocks, 128), jnp.float32),
-        ),
-        in_specs=[pl.BlockSpec(memory_space=pltpu.SMEM), vmem, vmem, vmem, vmem],
-        out_specs=(vmem, vmem),
-        scratch_shapes=[
+    deep = depth + LOW + HIGH
+    sizes = [(count + GROUP, width) for count in message_rows(depth)]
+    outs = call(
+        functools.partial(main_body, levels),
+        [pops.shape, (4, depth, height, width), (6, blocks, 128), (4, 8, 128), sizes[1], sizes[2]]
+        + [sizes[0]] * slots
+        + [sizes[3]] * slots
+        + [sizes[4]] * slots,
+        [given[0], counts, dest] + given[1:] + [drop_vel, drop_frac, home],
+        3,
+        [
+            pltpu.VMEM((3, layers, rows, lanes), jnp.float32),
+            pltpu.VMEM((3, layers, rows, lanes), jnp.float32),
+            pltpu.VMEM((blocks, 8, 128), jnp.float32),
+            pltpu.VMEM((27 * CAP, 8, 128), jnp.float32),
+            pltpu.VMEM((layers, rows, 128), jnp.float32),
+            pltpu.SMEM((27,), jnp.int32),
+            pltpu.VMEM((channels, deep, rows, lanes), jnp.float32),
+            pltpu.VMEM((deep, rows, 128), jnp.float32),
+            pltpu.VMEM((deep, rows, 128), jnp.float32),
+            pltpu.VMEM((19, rows, lanes), jnp.float32),
+            pltpu.VMEM((19, deep - 2, rows, lanes), jnp.float32),
             pltpu.VMEM((flat, lanes), jnp.bfloat16),
             pltpu.VMEM((flat, lanes), jnp.bfloat16),
             pltpu.VMEM((lanes, 256), jnp.bfloat16),
@@ -612,46 +805,27 @@
             pltpu.VMEM((flat, 256), jnp.bfloat16),
             pltpu.VMEM((layers, rows, 256), jnp.float32),
         ],
-        compiler_params=pltpu.CompilerParams(vmem_limit_bytes=48 * 1024 * 1024),
-    )(counts, velocity, drop_vel, drop_frac, home)
-
-
-def local(pops, coarse_pops, interface, drop_vel, drop_frac, home, counts, dest):
-    level = lax.axis_index("gz")
-    levels = lax.axis_size("gz")
-    depth, height, width = interface.shape
-    state, circle = two_substeps(pops, coarse_pops, interface)
-    rim_rows = lax.broadcasted_iota(jnp.int32, (1, depth + 4, 1, 1), 1)
-    keep = jnp.logical_not(
-        (level == 0) & (rim_rows < 2) | (level == levels - 1) & (rim_rows >= depth + 2)
-    )
-    blocks = home.shape[0]
-    spread, states = droplets(
-        circle, drop_vel, drop_frac, home, counts, (depth, height, width)
-    )
-    spread = jnp.concatenate(
-        [jnp.zeros_like(spread[..., :1]), spread[..., -1:], spread[..., : width + 2]], axis=3
-    )
-    spread = jnp.concatenate(
-        [jnp.zeros_like(spread[:, :, :1]), spread[:, :, -1:], spread[:, :, : height + 2]], axis=2
-    )
-    spread = jnp.concatenate([jnp.zeros_like(spread[:, :1]), spread], axis=1)
-    spread = jnp.where(keep, spread, 0.0)
-    force_ext = with_halo(spread, (("gx", 3), ("gy", 2), ("gz", 1)), 2, True)
-    force = fold(fold(fold(force_ext, 1, depth), 2, height), 3, width)
-    order = lax.broadcasted_iota(jnp.int32, (blocks,), 0)
-    earlier = (dest[:, None] == dest[None, :]) & (order[None, :] < order[:, None])
-    rank = jnp.sum(earlier.astype(jnp.int32), axis=1)
-    moving = dest != 13
-    slot = jnp.where(moving, dest * CAP + rank, 27 * CAP)
-    outbox = jnp.zeros((6, 27 * CAP, 128), jnp.float32).at[:, slot].set(states, mode="drop")
-    outbox = outbox.reshape(6, 3, 3, 3, CAP, 128)
-    arrived_box = with_halo(outbox, (("gx", 3), ("gy", 2), ("gz", 1)), 1, True)
-    inbox = arrived_box[:, 4::-2, 4::-2, 4::-2].reshape(6, 27 * CAP, 128)
-    incoming = jnp.concatenate([inbox[:, : 13 * CAP], inbox[:, 14 * CAP :]], axis=1)
-    staying = jnp.where(moving[None, :, None], 0.0, states)
-    arrived = jnp.concatenate([staying, incoming], axis=1)
-    return (state, force, arrived)
+    )
+    state, own, stay, side, north, south = outs[:6]
+    to_levels, north_levels, south_levels = (outs[6 + slots * at : 6 + slots * at + slots] for at in range(3))
+    received = [shifted(north, "gy", 1), shifted(south, "gy", -1)]
+    received += [to_level(value, kind, levels) for value, kind in zip(to_levels, kinds)]
+    received += [to_level(value, kind, levels, "gy", 1) for value, kind in zip(north_levels, kinds)]
+    received += [to_level(value, kind, levels, "gy", -1) for value, kind in zip(south_levels, kinds)]
+    side_rows = (depth * height + 9 * 16, width)
+    part, right, left = call(
+        functools.partial(gather_body, levels),
+        [(3, depth, height, width), side_rows, side_rows],
+        [level, own, side] + received,
+        1,
+        [pltpu.VMEM((4, depth, height, width), jnp.float32)],
+    )
+    force, arrived = call(
+        functools.partial(last_body, levels),
+        [(3, depth, height, width), (6, blocks + 26 * CAP, 128)],
+        [level, part, stay] + received + [shifted(right, "gx", 1), shifted(left, "gx", -1)],
+    )
+    return state, force, arrived
 
 
 def solution(mesh):

time: 95.9 us -> 70.5 us (0.74)
  waiting for transfers between devices: 35.7 us -> 16 us
  Pallas kernels: 24.5 us -> 28.1 us
  other arithmetic: 3.55 us -> 0 us
  starting transfers between devices: 24.9 us -> 21.4 us
  local copies, waits for them, and re-layouts: 6.05 us -> 3.46 us
    ppermute x14 -> x4, waiting for transfers between devices: 27.3 us -> 4.08 us  [to_level(): lax.ppermute(value, (side, 'gz'), [(brick * levels + at, (brick + step) %...]
    pallas_call x3 -> x5, Pallas kernels: 14.6 us -> 28.1 us  [call(): pl.pallas_call(body, out_shape=[jax.ShapeDtypeStruct(shape, jnp.float32)...]
    ppermute x14 -> x4, starting transfers between devices: 17.6 us -> 7.37 us  [to_level(): lax.ppermute(value, (side, 'gz'), [(brick * levels + at, (brick + step) %...]
    pallas_call x1 -> x0, Pallas kernels: 9.85 us -> none  [droplets(): pl.pallas_call(functools.partial(droplet_body, size), out_shape=(jax.Shap...]
    ppermute x4 -> x8, starting transfers between devices: 4.38 us -> 10.6 us  [shifted(): lax.ppermute(value, axis, [(i, (i + step) % count) for i in range(count)])]
    ppermute x4 -> x8, waiting for transfers between devices: 8.33 us -> 11.9 us  [shifted(): lax.ppermute(value, axis, [(i, (i + step) % count) for i in range(count)])]
    concatenate x5 -> x0, other arithmetic: 1.74 us -> none  [the longest x1 0.71 us: local(): arrived = jnp.concatenate([staying, incoming], axis=1)]
    unnamed x32 -> x28, local copies, waits for them, and re-layouts: 4.51 us -> 3.46 us
  transfers between devices with their start and end apart: 19 -> 14, of which waited for: 10 -> 4; matrix products, arithmetic and copies ran while one was open for 3% -> 0% of each run, Pallas kernels for 0% -> 0%
where the time goes in v3:
time: 70.5 us; the launch traced here: 69.7 us
  Pallas kernels  28.1 us (40%)
  starting transfers between devices  21.4 us (30%)
  waiting for transfers between devices  16 us (23%)
  local copies, waits for them, and re-layouts  3.46 us (5%)
  between operations  0.75 us (1%)
    pallas_call x5, Pallas kernels, call(): pl.pallas_call(body, out_shape=[jax.ShapeDtypeStruct(shape, jnp.float32)...  28.1 us
    ppermute x8, waiting for transfers between devices, shifted(): lax.ppermute(value, axis, [(i, (i + step) % count) for i in range(count)])  11.9 us
    ppermute x8, starting transfers between devices, shifted(): lax.ppermute(value, axis, [(i, (i + step) % count) for i in range(count)])  10.6 us
    ppermute x4, starting transfers between devices, to_level(): lax.ppermute(value, (side, 'gz'), [(brick * levels + at, (brick + step) %...  7.37 us
    ppermute x4, waiting for transfers between devices, to_level(): lax.ppermute(value, (side, 'gz'), [(brick * levels + at, (brick + step) %...  4.08 us
    unnamed x28, local copies, waits for them, and re-layouts  3.46 us
    ppermute x2, starting transfers between devices, to_level(): return lax.ppermute(value, 'gz', pairs)  3.39 us
  transfers between devices with their start and end apart: 14, of which 4 were waited for; matrix products, arithmetic and copies ran while one was open for 0% of the time, Pallas kernels for 0%

profile of v3, /device:TPU:0, one launch (start us, length us, event | category | flops | bytes accessed | tf_op | source)
XLA Modules:
  0.0 69.7 jit_solution(7868061242454757315)
XLA Ops:
  0.6 3.3 %shard_map.103 = (f32[20,8,8,128]{3,2,1,0:T(8,128)}, f32[60,8,128]{2,1,0:T(8,128)}, f32[8,8,128]{2,1,0:T(8,128)}, f32[8,8,128]{2,1,0:T(8,128)}, f32[4,8,128]{2,1,0:T(8,128)}, /*index=5*/f32[4,8,128]{2,1,0:T(8,128)}) custom-call(s32[1]{0:T(128)} %bitcast.level_ref, f32[19,8,8,128]{3,2,1,0:T(8,128)} %pops_ref.1, bf16[19,8,8,128]{3,2,1,0:T(8,128)(2,1)} %coarse_ref.1, ...), custom_call_target="tpu_custom_call" | custom-call | tf_op jit(solution)/shard_map/pallas_call | solution.py:47
  3.9 3.0 %collective-permute-start.2 = (f32[60,8,128]{2,1,0:T(8,128)}, f32[60,8,128]{2,1,0:T(8,128)S(1)}, u32[]{:S(2)}, u32[]{:S(2)}) collective-permute-start(f32[60,8,128]{2,1,0:T(8,128)} %get-tuple-element.28), channel_id=1, source_target_pairs={{0,1},{1,0},{2,3},{3,2},{4,5},{5,4},{6,7},{7,6},{8,9},{9,8},{10,11... | collective-permute-start | bytes 737288 | tf_op jit(solution)/shard_map/ppermute | solution.py:400
  6.9 1.6 %collective-permute-start = (f32[8,8,128]{2,1,0:T(8,128)}, f32[8,8,128]{2,1,0:T(8,128)S(1)}, u32[]{:S(2)}, u32[]{:S(2)}) collective-permute-start(f32[8,8,128]{2,1,0:T(8,128)} %get-tuple-element.26), channel_id=1, source_target_pairs={{0,8},{8,16},{16,24},{24,0},{1,9},{9,17},{17,25},{25,1},{2,10},{10... | collective-permute-start | bytes 98312 | tf_op jit(solution)/shard_map/ppermute | solution.py:390
  8.5 2.2 %collective-permute-start.1 = (f32[8,8,128]{2,1,0:T(8,128)}, f32[8,8,128]{2,1,0:T(8,128)S(1)}, u32[]{:S(2)}, u32[]{:S(2)}) collective-permute-start(f32[8,8,128]{2,1,0:T(8,128)} %get-tuple-element.27), channel_id=1, source_target_pairs={{0,24},{8,0},{16,8},{24,16},{1,25},{9,1},{17,9},{25,17},{2,26},{10... | collective-permute-start | bytes 98312 | tf_op jit(solution)/shard_map/ppermute | solution.py:390
  10.7 4.7 %collective-permute-start.4 = (f32[4,8,128]{2,1,0:T(8,128)}, f32[4,8,128]{2,1,0:T(8,128)S(1)}, u32[]{:S(2)}, u32[]{:S(2)}) collective-permute-start(f32[4,8,128]{2,1,0:T(8,128)} %get-tuple-element.30), channel_id=1, source_target_pairs={{0,25},{1,24},{8,1},{9,0},{16,9},{17,8},{24,17},{25,16},{2,27},{3,... | collective-permute-start | bytes 49160 | tf_op jit(solution)/shard_map/ppermute | solution.py:402
  15.4 1.9 %collective-permute-done.3.rest_1_.rest_4_ = f32[4,8,128]{2,1,0:T(8,128)S(1)} collective-permute-done((f32[4,8,128]{2,1,0:T(8,128)}, f32[4,8,128]{2,1,0:T(8,128)S(1)}, u32[]{:S(2)}, u32[]{:S(2)}) %collective-permute-start.3) | collective-permute-done | bytes 16416 | tf_op jit(solution)/shard_map/ppermute | solution.py:402
  17.4 0.5 copy-done.12
  18.1 2.3 %shard_map.104 = (f32[760,128]{1,0:T(8,128)}, f32[520,128]{1,0:T(8,128)}) custom-call(s32[1]{0:T(128)} %bitcast.level_ref, f32[20,8,8,128]{3,2,1,0:T(8,128)} %get-tuple-element.25.posts_ref.rest_0_, f32[8,8,128]{2,1,0:T(8,128)} %copy-done.6, f32[8,8,128]{2,1,0:T(8,128)} %copy-done.7, f32[60,8,128]{2,1,0:T(8,128)} %copy-done, f32[4,8,128]{2,1,0:T(8,128)} %copy-done.12, ...), custom_call_target="tpu_custom_call" | custom-call | tf_op jit(solution)/shard_map/pallas_call | solution.py:47
  20.9 8.4 %collective-permute-done.6.rest_7_ = f32[520,128]{1,0:T(8,128)S(1)} collective-permute-done((f32[520,128]{1,0:T(8,128)}, f32[520,128]{1,0:T(8,128)S(1)}, u32[]{:S(2)}, u32[]{:S(2)}) %collective-permute-start.6) | collective-permute-done | bytes 266272 | tf_op jit(solution)/shard_map/ppermute | solution.py:390
  29.3 0.7 %copy-done.2 = f32[520,128]{1,0:T(8,128)} copy-done((f32[520,128]{1,0:T(8,128)}, f32[520,128]{1,0:T(8,128)S(1)}, u32[]{:S(2)}) %copy-start.2) | copy-done | bytes 266264
  30.0 0.8 %copy-done.1 = f32[760,128]{1,0:T(8,128)} copy-done((f32[760,128]{1,0:T(8,128)}, f32[760,128]{1,0:T(8,128)S(1)}, u32[]{:S(2)}) %copy-start.1) | copy-done | bytes 389144
  30.7 18.7 %shard_map.105 = (f32[19,8,8,128]{3,2,1,0:T(8,128)}, f32[4,8,8,128]{3,2,1,0:T(8,128)}, f32[6,16,128]{2,1,0:T(8,128)}, f32[4,8,128]{2,1,0:T(8,128)}, f32[112,128]...) custom-call(s32[1]{0:T(128)} %bitcast.level_ref, ...), custom_call_target="tpu_custom_call" | custom-call | tf_op jit(solution)/shard_map/pallas_call | solution.py:47
  49.4 0.5 collective-permute-start.7
  50.4 0.9 %collective-permute-start.8 = (f32[80,128]{1,0:T(8,128)}, f32[80,128]{1,0:T(8,128)S(1)}, u32[]{:S(2)}, u32[]{:S(2)}) collective-permute-start(f32[80,128]{1,0:T(8,128)} %get-tuple-element.37), channel_id=1, source_target_pairs={{0,6},{2,0},{4,2},{6,4},{1,7},{3,1},{5,3},{7,5},{8,14},{10,8},{12,... | collective-permute-start | bytes 122888 | tf_op jit(solution)/shard_map/ppermute | solution.py:390
  51.2 1.2 %collective-permute-start.10 = (f32[64,128]{1,0:T(8,128)}, f32[64,128]{1,0:T(8,128)S(1)}, u32[]{:S(2)}, u32[]{:S(2)}) collective-permute-start(f32[64,128]{1,0:T(8,128)} %get-tuple-element.39), channel_id=1, source_target_pairs={{0,3},{1,2},{2,5},{3,4},{4,7},{5,6},{6,1},{7,0},{8,11},{9,10},{10,... | collective-permute-start | bytes 98312 | tf_op jit(solution)/shard_map/ppermute | solution.py:402
  52.5 1.4 %collective-permute-start.11 = (f32[56,128]{1,0:T(8,128)}, f32[56,128]{1,0:T(8,128)S(1)}, u32[]{:S(2)}, u32[]{:S(2)}) collective-permute-start(f32[56,128]{1,0:T(8,128)} %get-tuple-element.40), channel_id=1, source_target_pairs={{0,7},{1,6},{2,1},{3,0},{4,3},{5,2},{6,5},{7,4},{8,15},{9,14},{10,... | collective-permute-start | bytes 86024 | tf_op jit(solution)/shard_map/ppermute | solution.py:402
  53.9 2.1 %collective-permute-done.11.rest_4_ = f32[56,128]{1,0:T(8,128)S(1)} collective-permute-done((f32[56,128]{1,0:T(8,128)}, f32[56,128]{1,0:T(8,128)S(1)}, u32[]{:S(2)}, u32[]{:S(2)}) %collective-permute-start.11) | collective-permute-done | bytes 28704 | tf_op jit(solution)/shard_map/ppermute | solution.py:402
  56.1 0.5 copy-done.9
  56.7 1.8 %shard_map.106 = (f32[3,8,8,128]{3,2,1,0:T(8,128)}, f32[208,128]{1,0:T(8,128)}, f32[208,128]{1,0:T(8,128)}) custom-call(s32[1]{0:T(128)} %bitcast.level_ref, f32[4,8,8,128]{3,2,1,0:T(8,128)} %get-tuple-element.34.own_ref, f32[4,8,128]{2,1,0:T(8,128)} %get-tuple-element.35.side_ref, f32[112,128]{1,0:T(8,128)} %copy-done.3, f32[80,128]{1,0:T(8,128)} %copy-done.5, ...), custom_call_target="tpu_custom_call" | custom-call | tf_op jit(solution)/shard_map/pallas_call | solution.py:47
  58.5 0.6 collective-permute-start.12
  59.0 4.4 %collective-permute-start.13 = (f32[208,128]{1,0:T(8,128)}, f32[208,128]{1,0:T(8,128)S(1)}, u32[]{:S(2)}, u32[]{:S(2)}) collective-permute-start(f32[208,128]{1,0:T(8,128)} %get-tuple-element.44), channel_id=1, source_target_pairs={{0,24},{8,0},{16,8},{24,16},{1,25},{9,1},{17,9},{25,17},{2,26},{10... | collective-permute-start | bytes 319496 | tf_op jit(solution)/shard_map/ppermute | solution.py:390
  63.4 3.6 %collective-permute-done.12.rest_5_ = f32[208,128]{1,0:T(8,128)S(1)} collective-permute-done((f32[208,128]{1,0:T(8,128)}, f32[208,128]{1,0:T(8,128)S(1)}, u32[]{:S(2)}, u32[]{:S(2)}) %collective-permute-start.12) | collective-permute-done | bytes 106528 | tf_op jit(solution)/shard_map/ppermute | solution.py:390
  67.0 0.6 copy-done.10
  67.6 2.1 %shard_map.107 = (f32[3,8,8,128]{3,2,1,0:T(8,128)}, f32[6,68,128]{2,1,0:T(8,128)}) custom-call(s32[1]{0:T(128)} %bitcast.level_ref, f32[3,8,8,128]{3,2,1,0:T(8,128)} %get-tuple-element.41.part_ref, f32[6,16,128]{2,1,0:T(8,128)} %get-tuple-element.42.stay_ref, f32[112,128]{1,0:T(8,128)} %copy-done.3, f32[80,128]{1,0:T(8,128)} %copy-done.5, ...), custom_call_target="tpu_custom_call" | custom-call | tf_op jit(solution)/shard_map/pallas_call | solution.py:47
  (37 shorter events, 1.3 us)
Async XLA Ops:
  3.9 13.5 %collective-permute-start.2 = (f32[60,8,128]{2,1,0:T(8,128)}, f32[60,8,128]{2,1,0:T(8,128)S(1)}, u32[]{:S(2)}, u32[]{:S(2)}) collective-permute-start(f32[60,8,128]{2,1,0:T(8,128)} %get-tuple-element.28), channel_id=1, source_target_pairs={{0,1},{1,0},{2,3},{3,2},{4,5},{5,4},{6,7},{7,6},{8,9},{9,8},{10,11... | collective-permute-start | bytes 737288 | tf_op jit(solution)/shard_map/ppermute | solution.py:400
  6.9 10.5 %collective-permute-start = (f32[8,8,128]{2,1,0:T(8,128)}, f32[8,8,128]{2,1,0:T(8,128)S(1)}, u32[]{:S(2)}, u32[]{:S(2)}) collective-permute-start(f32[8,8,128]{2,1,0:T(8,128)} %get-tuple-element.26), channel_id=1, source_target_pairs={{0,8},{8,16},{16,24},{24,0},{1,9},{9,17},{17,25},{25,1},{2,10},{10... | collective-permute-start | bytes 98312 | tf_op jit(solution)/shard_map/ppermute | solution.py:390
  8.5 8.9 %collective-permute-start.1 = (f32[8,8,128]{2,1,0:T(8,128)}, f32[8,8,128]{2,1,0:T(8,128)S(1)}, u32[]{:S(2)}, u32[]{:S(2)}) collective-permute-start(f32[8,8,128]{2,1,0:T(8,128)} %get-tuple-element.27), channel_id=1, source_target_pairs={{0,24},{8,0},{16,8},{24,16},{1,25},{9,1},{17,9},{25,17},{2,26},{10... | collective-permute-start | bytes 98312 | tf_op jit(solution)/shard_map/ppermute | solution.py:390
  10.7 6.6 %collective-permute-start.3 = (f32[4,8,128]{2,1,0:T(8,128)}, f32[4,8,128]{2,1,0:T(8,128)S(1)}, u32[]{:S(2)}, u32[]{:S(2)}) collective-permute-start(f32[4,8,128]{2,1,0:T(8,128)} %get-tuple-element.29), channel_id=1, source_target_pairs={{0,9},{1,8},{8,17},{9,16},{16,25},{17,24},{24,1},{25,0},{2,11},{3,... | collective-permute-start | bytes 49160 | tf_op jit(solution)/shard_map/ppermute | solution.py:402
  10.7 6.6 %collective-permute-start.4 = (f32[4,8,128]{2,1,0:T(8,128)}, f32[4,8,128]{2,1,0:T(8,128)S(1)}, u32[]{:S(2)}, u32[]{:S(2)}) collective-permute-start(f32[4,8,128]{2,1,0:T(8,128)} %get-tuple-element.30), channel_id=1, source_target_pairs={{0,25},{1,24},{8,1},{9,0},{16,9},{17,8},{24,17},{25,16},{2,27},{3,... | collective-permute-start | bytes 49160 | tf_op jit(solution)/shard_map/ppermute | solution.py:402
  17.4 0.6 copy-start.6
  17.4 0.7 %copy-start = (f32[60,8,128]{2,1,0:T(8,128)}, f32[60,8,128]{2,1,0:T(8,128)S(1)}, u32[]{:S(2)}) copy-start(f32[60,8,128]{2,1,0:T(8,128)S(1)} %collective-permute-done.2.rest_0_.rest_3_) | copy-start | bytes 737284
  20.4 8.9 %collective-permute-start.5 = (f32[760,128]{1,0:T(8,128)}, f32[760,128]{1,0:T(8,128)S(1)}, u32[]{:S(2)}, u32[]{:S(2)}) collective-permute-start(f32[760,128]{1,0:T(8,128)} %get-tuple-element.31), channel_id=1, source_target_pairs={{0,6},{2,0},{4,2},{6,4},{1,7},{3,1},{5,3},{7,5},{8,14},{10,8},{12,... | collective-permute-start | bytes 1167368 | tf_op jit(solution)/shard_map/ppermute | solution.py:390
  20.4 8.9 %collective-permute-start.6 = (f32[520,128]{1,0:T(8,128)}, f32[520,128]{1,0:T(8,128)S(1)}, u32[]{:S(2)}, u32[]{:S(2)}) collective-permute-start(f32[520,128]{1,0:T(8,128)} %get-tuple-element.32), channel_id=1, source_target_pairs={{0,2},{2,4},{4,6},{6,0},{1,3},{3,5},{5,7},{7,1},{8,10},{10,12},{12... | collective-permute-start | bytes 798728 | tf_op jit(solution)/shard_map/ppermute | solution.py:390
  29.3 0.7 %copy-start.2 = (f32[520,128]{1,0:T(8,128)}, f32[520,128]{1,0:T(8,128)S(1)}, u32[]{:S(2)}) copy-start(f32[520,128]{1,0:T(8,128)S(1)} %collective-permute-done.6.rest_7_) | copy-start | bytes 798724
  30.0 0.8 %copy-start.1 = (f32[760,128]{1,0:T(8,128)}, f32[760,128]{1,0:T(8,128)S(1)}, u32[]{:S(2)}) copy-start(f32[760,128]{1,0:T(8,128)S(1)} %collective-permute-done.5.rest_6_) | copy-start | bytes 1167364
  49.4 6.6 %collective-permute-start.7 = (f32[112,128]{1,0:T(8,128)}, f32[112,128]{1,0:T(8,128)S(1)}, u32[]{:S(2)}, u32[]{:S(2)}) collective-permute-start(f32[112,128]{1,0:T(8,128)} %get-tuple-element.36), channel_id=1, source_target_pairs={{0,2},{2,4},{4,6},{6,0},{1,3},{3,5},{5,7},{7,1},{8,10},{10,12},{12... | collective-permute-start | bytes 172040 | tf_op jit(solution)/shard_map/ppermute | solution.py:390
  50.0 6.1 %collective-permute-start.9 = (f32[112,128]{1,0:T(8,128)}, f32[112,128]{1,0:T(8,128)S(1)}, u32[]{:S(2)}, u32[]{:S(2)}) collective-permute-start(f32[112,128]{1,0:T(8,128)} %get-tuple-element.38), channel_id=1, source_target_pairs={{0,1},{1,0},{2,3},{3,2},{4,5},{5,4},{6,7},{7,6},{8,9},{9,8},{10,11... | collective-permute-start | bytes 172040 | tf_op jit(solution)/shard_map/ppermute | solution.py:400
  50.4 5.7 %collective-permute-start.8 = (f32[80,128]{1,0:T(8,128)}, f32[80,128]{1,0:T(8,128)S(1)}, u32[]{:S(2)}, u32[]{:S(2)}) collective-permute-start(f32[80,128]{1,0:T(8,128)} %get-tuple-element.37), channel_id=1, source_target_pairs={{0,6},{2,0},{4,2},{6,4},{1,7},{3,1},{5,3},{7,5},{8,14},{10,8},{12,... | collective-permute-start | bytes 122888 | tf_op jit(solution)/shard_map/ppermute | solution.py:390
  51.2 4.8 %collective-permute-start.10 = (f32[64,128]{1,0:T(8,128)}, f32[64,128]{1,0:T(8,128)S(1)}, u32[]{:S(2)}, u32[]{:S(2)}) collective-permute-start(f32[64,128]{1,0:T(8,128)} %get-tuple-element.39), channel_id=1, source_target_pairs={{0,3},{1,2},{2,5},{3,4},{4,7},{5,6},{6,1},{7,0},{8,11},{9,10},{10,... | collective-permute-start | bytes 98312 | tf_op jit(solution)/shard_map/ppermute | solution.py:402
  52.5 3.6 %collective-permute-start.11 = (f32[56,128]{1,0:T(8,128)}, f32[56,128]{1,0:T(8,128)S(1)}, u32[]{:S(2)}, u32[]{:S(2)}) collective-permute-start(f32[56,128]{1,0:T(8,128)} %get-tuple-element.40), channel_id=1, source_target_pairs={{0,7},{1,6},{2,1},{3,0},{4,3},{5,2},{6,5},{7,4},{8,15},{9,14},{10,... | collective-permute-start | bytes 86024 | tf_op jit(solution)/shard_map/ppermute | solution.py:402
  56.0 0.6 copy-start.8
  56.0 0.6 copy-start.5
  56.1 0.6 copy-start.3
  56.1 0.6 copy-start.4
  58.5 8.5 %collective-permute-start.12 = (f32[208,128]{1,0:T(8,128)}, f32[208,128]{1,0:T(8,128)S(1)}, u32[]{:S(2)}, u32[]{:S(2)}) collective-permute-start(f32[208,128]{1,0:T(8,128)} %get-tuple-element.43), channel_id=1, source_target_pairs={{0,8},{8,16},{16,24},{24,0},{1,9},{9,17},{17,25},{25,1},{2,10},{10... | collective-permute-start | bytes 319496 | tf_op jit(solution)/shard_map/ppermute | solution.py:390
  59.0 7.9 %collective-permute-start.13 = (f32[208,128]{1,0:T(8,128)}, f32[208,128]{1,0:T(8,128)S(1)}, u32[]{:S(2)}, u32[]{:S(2)}) collective-permute-start(f32[208,128]{1,0:T(8,128)} %get-tuple-element.44), channel_id=1, source_target_pairs={{0,24},{8,0},{16,8},{24,16},{1,25},{9,1},{17,9},{25,17},{2,26},{10... | collective-permute-start | bytes 319496 | tf_op jit(solution)/shard_map/ppermute | solution.py:390
  67.0 0.6 copy-start.10
  67.0 0.7 copy-start.11
  (4 other events, 2.4 us)

commit v4 on v3

--- a/solution.py
+++ b/solution.py
@@ -42,7 +42,7 @@
 couple = 8.0
 
 
-def call(body, outs, ins, scalars=1, scratch=()):
+def call(body, outs, ins, scalars=1, scratch=(), cost=None):
     vmem = pl.BlockSpec(memory_space=pltpu.VMEM)
     return pl.pallas_call(
         body,
@@ -50,6 +50,7 @@
         in_specs=[pl.BlockSpec(memory_space=pltpu.SMEM)] * scalars + [vmem] * (len(ins) - scalars),
         out_specs=[vmem] * len(outs),
         scratch_shapes=list(scratch),
+        cost_estimate=cost,
         compiler_params=pltpu.CompilerParams(vmem_limit_bytes=56 * 1024 * 1024),
     )(*ins)
 
@@ -89,8 +90,8 @@
 
 
 def rim_sizes(levels):
-    sides = [(len(rim(kind)), rim_count(kind)) for kind, _, _, _ in rim_sides(levels)]
-    return [max(sides)] if levels == 2 else sides
+    sizes = [len(rim(kind)) for kind, _, _, _ in rim_sides(levels)]
+    return [max(sizes)] if levels == 2 else sizes
 
 
 def guarded(level, guard, action):
@@ -100,39 +101,32 @@
         pl.when(level == guard)(action)
 
 
-def row_table(depth, levels):
-    high_at, low_at = 0, 0
-    own, own_strips, rims, strips = [], [], {}, {}
-
-    def entry(channel, bounces=False):
-        nonlocal high_at, low_at
+def row_places(cells):
+    places, high_at, low_at = [], 0, 0
+    for channel, bounces in cells:
         way_z, way, _ = ways[channel]
         above, below = high_reach(way), low_reach(way)
         if bounces and way_z != 0:
             above, below = max(above, HIGH - 1), max(below, LOW - 1)
-        place = (high_at, low_at, above, below)
-        high_at, low_at = high_at + place[2], low_at + place[3]
-        return place
-
-    def strip():
-        nonlocal high_at, low_at
-        place = (high_at, low_at, HIGH, LOW)
-        high_at, low_at = high_at + HIGH, low_at + LOW
-        return place
-
-    for layer in range(depth):
-        for channel in range(channels):
-            own.append((layer, channel, entry(channel, layer in (0, depth - 1))))
-        own_strips.append((strip(), strip()))
-    start = (high_at, low_at)
-    most = start
-    for kind, _, _, _ in rim_sides(levels):
-        if levels == 2:
-            high_at, low_at = start
-        rims[kind] = [(step, channel, entry(channel)) for step, channel in rim(kind)]
-        strips[kind] = [(strip(), strip()) for _ in range(rim_count(kind))]
-        most = (max(most[0], high_at), max(most[1], low_at))
-    return own, own_strips, rims, strips, [-(-count // 8) * 8 for count in most]
+        places.append((high_at, low_at, above, below))
+        high_at, low_at = high_at + above, low_at + below
+    return places, (-(-high_at // 8) * 8, -(-low_at // 8) * 8)
+
+
+def own_rows(depth):
+    cells = [(layer, channel) for layer in range(depth) for channel in range(channels)]
+    places, sizes = row_places([(channel, layer in (0, depth - 1)) for layer, channel in cells])
+    return [(layer, channel, place) for (layer, channel), place in zip(cells, places)], sizes
+
+
+def rim_rows(kind):
+    places, sizes = row_places([(channel, False) for _, channel in rim(kind)])
+    return [(step, channel, place) for (step, channel), place in zip(rim(kind), places)], sizes
+
+
+def rim_row_sizes(levels):
+    sizes = [rim_rows(kind)[1] for kind, _, _, _ in rim_sides(levels)]
+    return [tuple(max(part) for part in zip(*sizes))] if levels == 2 else sizes
 
 
 def moments(cells):
@@ -190,18 +184,12 @@
     return value if shift == 0 else pltpu.roll(value, shift, value.ndim - 1)
 
 
-def first_body(levels, level_ref, pops_ref, coarse_ref, interface_ref, posts_ref, *outs):
+def first_body(levels, level_ref, pops_ref, coarse_ref, interface_ref, posts_ref, down_ref, up_ref, *outs):
     depth, height, width = interface_ref.shape
-    sides = rim_sides(levels)
     slots = len(rim_sizes(levels))
-    rims = outs[:slots]
-    right_ref, left_ref = outs[slots : slots + 2]
-    right_rims = outs[slots + 2 : 2 * slots + 2]
-    left_rims = outs[2 * slots + 2 :]
-    level = level_ref[0]
-    lane = lax.broadcasted_iota(jnp.int32, (height, 128), 1)
-
-    def layer_step(layer, carry):
+    rims, down_rims, up_rims = (outs[slots * at : slots * at + slots] for at in range(3))
+    own = own_rows(depth)[0]
+    for layer in range(depth):
         mask = interface_ref[layer]
         inside = mask == 1
         posts = relaxed([pops_ref[index, layer] for index in range(19)])
@@ -209,119 +197,78 @@
             jnp.where(inside, coarse_ref[index, layer].astype(jnp.float32), posts[index])
             for index in range(19)
         ] + [mask.astype(jnp.float32)]
-        right, left = jnp.zeros((height, 128), jnp.float32), jnp.zeros((height, 128), jnp.float32)
         for channel in range(channels):
             posts_ref[channel, layer] = posts[channel]
-            here = (lane >= 4 * channel) & (lane < 4 * channel + 4)
-            right = jnp.where(here, lane_roll(posts[channel][:, width - 128 :], 4 * channel + 4), right)
-            left = jnp.where(here, lane_roll(posts[channel][:, :128], 4 * channel), left)
-        right_ref[layer] = right
-        left_ref[layer] = left
+            down_at, up_at, down, up = own[layer * channels + channel][2]
+            down_ref[down_at : down_at + down, :] = posts[channel][:down, :]
+            up_ref[up_at : up_at + up, :] = posts[channel][height - up :, :]
+    for kind, _, sender, slot in rim_sides(levels):
+
+        def pack(kind=kind, slot=slot):
+            for at, (step, channel, place) in enumerate(rim_rows(kind)[0]):
+                cells = posts_ref[channel, depth - step if kind == "low" else step - 1]
+                rims[slot][at] = cells
+                down_at, up_at, down, up = place
+                down_rims[slot][down_at : down_at + down, :] = cells[:down, :]
+                up_rims[slot][up_at : up_at + up, :] = cells[height - up :, :]
+
+        guarded(level_ref[0], sender, pack)
+
+
+def unpack(levels, level, posts_ref, above_ref, below_ref, rims, above_rims, below_rims, ext):
+    depth, height = posts_ref.shape[1:3]
+    rows = height + 8
+
+    def put(channel, at, cells, place, above, below):
+        above_at, below_at, above_rows, below_rows = place
+        ext[channel, at, :height, :] = cells
+        ext[channel, at, height : height + above_rows, :] = above[above_at : above_at + above_rows, :]
+        ext[channel, at, rows - below_rows : rows, :] = below[below_at : below_at + below_rows, :]
+
+    for layer, channel, place in own_rows(depth)[0]:
+        put(channel, LOW + layer, posts_ref[channel, layer], place, above_ref, below_ref)
+    for kind, receiver, _, slot in rim_sides(levels):
+
+        def take(kind=kind, slot=slot):
+            for at, (step, channel, place) in enumerate(rim_rows(kind)[0]):
+                layer = LOW - step if kind == "low" else LOW + depth + step - 1
+                put(channel, layer, rims[slot][at], place, above_rims[slot], below_rims[slot])
+
+        guarded(level, receiver, take)
+
+
+def split_given(levels, rest):
+    slots = len(rim_sizes(levels))
+    parts = [rest[3 + slots * at : 3 + slots * at + slots] for at in range(3)]
+    return rest[:3], parts, rest[3 + 3 * slots :]
+
+
+def strip_body(levels, level_ref, *rest):
+    (posts_ref, above_ref, below_ref), parts, (strip_ref, ext) = split_given(levels, rest)
+    unpack(levels, level_ref[0], posts_ref, above_ref, below_ref, *parts, ext)
+    layers, rows, width = ext.shape[1:]
+    lane = lax.broadcasted_iota(jnp.int32, (rows, 128), 1)
+
+    def channel_step(channel, carry):
+        value = jnp.zeros((rows, 128), jnp.float32)
+        for layer in range(layers):
+            cells = ext[channel, layer]
+            if width > 128:
+                cells = jnp.where(lane < 64, cells[:, :128], cells[:, width - 128 :])
+            value = jnp.where(lane // 8 == layer, lane_roll(cells, 8 * layer + 4), value)
+        strip_ref[channel] = value
         return carry
 
-    lax.fori_loop(0, depth, layer_step, 0)
-    for kind, _, sender, slot in sides:
-
-        def pack(kind=kind, slot=slot):
-            for place, (step, channel) in enumerate(rim(kind)):
-                rims[slot][place] = posts_ref[channel, depth - step if kind == "low" else step - 1]
-            for step in range(1, rim_count(kind) + 1):
-                layer = depth - step if kind == "low" else step - 1
-                right_rims[slot][step - 1] = right_ref[layer]
-                left_rims[slot][step - 1] = left_ref[layer]
-
-        guarded(level, sender, pack)
-
-
-def rows_body(levels, level_ref, posts_ref, low_ref, high_ref, *rest):
-    depth, height = posts_ref.shape[1:3]
-    slots = len(rim_sizes(levels))
-    rims, low_rims, high_rims = rest[:slots], rest[slots : 2 * slots], rest[2 * slots : 3 * slots]
-    down_ref, up_ref = rest[3 * slots :]
-    own, own_strips, rim_rows, rim_strips, _ = row_table(depth, levels)
-
-    def put(place, source, *index):
-        down_at, up_at, down_rows, up_rows = place
-        down_ref[down_at : down_at + down_rows, :] = source[(*index, slice(0, down_rows))]
-        up_ref[up_at : up_at + up_rows, :] = source[(*index, slice(height - up_rows, height))]
-
-    for layer, channel, place in own:
-        put(place, posts_ref, channel, layer)
-    for layer in range(depth):
-        put(own_strips[layer][0], low_ref, layer)
-        put(own_strips[layer][1], high_ref, layer)
-    for kind, receiver, _, slot in rim_sides(levels):
-
-        def pack(kind=kind, slot=slot):
-            for at, (_, _, place) in enumerate(rim_rows[kind]):
-                put(place, rims[slot], at)
-            for step, (low, high) in enumerate(rim_strips[kind]):
-                put(low, low_rims[slot], step)
-                put(high, high_rims[slot], step)
-
-        guarded(level_ref[0], receiver, pack)
-
-
-def steps_body(
-    levels, level_ref, posts_ref, low_ref, high_ref, rims, low_rims, high_rims, above_ref, below_ref,
-    pops_ref, vel_ref, ext, strip_low, strip_high, pulled, second,
-):
+    lax.fori_loop(0, channels, channel_step, 0)
+
+
+def inner_body(levels, level_ref, *rest):
+    (posts_ref, above_ref, below_ref), parts, rest = split_given(levels, rest)
+    pops_ref, vel_ref, ext, pulled, second = rest
+    level = level_ref[0]
+    unpack(levels, level, posts_ref, above_ref, below_ref, *parts, ext)
     depth, height, width = posts_ref.shape[1:]
-    own, own_strips, rim_rows, rim_strips, _ = row_table(depth, levels)
-    level = level_ref[0]
-    rows, lanes = height + 8, width + 128
-    main = slice(0, width)
-
-    def place_rows(target, index, place, cols):
-        above_at, below_at, above_rows, below_rows = place
-        target[(*index, slice(height, height + above_rows), cols)] = above_ref[
-            above_at : above_at + above_rows, :
-        ]
-        target[(*index, slice(rows - below_rows, rows), cols)] = below_ref[
-            below_at : below_at + below_rows, :
-        ]
-
-    whole = slice(None)
-    for layer, channel, place in own:
-        ext[channel, LOW + layer, :height, main] = posts_ref[channel, layer]
-        place_rows(ext, (channel, LOW + layer), place, main)
-    for layer in range(depth):
-        for strip, source, place in (
-            (strip_low, low_ref, own_strips[layer][0]),
-            (strip_high, high_ref, own_strips[layer][1]),
-        ):
-            strip[LOW + layer, :height, :] = source[layer]
-            place_rows(strip, (LOW + layer,), place, whole)
-    for kind, receiver, _, slot in rim_sides(levels):
-
-        def unpack(kind=kind, slot=slot):
-            def at_layer(step):
-                return LOW - step if kind == "low" else LOW + depth + step - 1
-
-            for at, (step, channel, place) in enumerate(rim_rows[kind]):
-                ext[channel, at_layer(step), :height, main] = rims[slot][at]
-                place_rows(ext, (channel, at_layer(step)), place, main)
-            for step in range(1, rim_count(kind) + 1):
-                for strip, source, place in (
-                    (strip_low, low_rims[slot], rim_strips[kind][step - 1][0]),
-                    (strip_high, high_rims[slot], rim_strips[kind][step - 1][1]),
-                ):
-                    strip[at_layer(step), :height, :] = source[step - 1]
-                    place_rows(strip, (at_layer(step),), place, whole)
-
-        guarded(level, receiver, unpack)
-
-    lane = lax.broadcasted_iota(jnp.int32, (rows, 128), 1)
-
-    def strip_step(layer, carry):
-        low, high = strip_low[layer], strip_high[layer]
-        for channel in range(channels):
-            ext[channel, layer, :, width:] = jnp.where(
-                lane < 64, lane_roll(high, -4 * channel), lane_roll(low, 124 - 4 * channel)
-            )
-        return carry
-
-    lax.fori_loop(0, LOW + depth + HIGH, strip_step, 0)
+    rows = height + 8
 
     def pull(source, layer, at):
         bottom = (level == 0) & (layer == 0)
@@ -330,7 +277,7 @@
             way_z, way_y, way_x = ways[index]
             value = source[index, at - way_z]
             if way_x != 0:
-                value = pltpu.roll(value, way_x % lanes, 1)
+                value = pltpu.roll(value, way_x % width, 1)
             if way_y != 0:
                 value = pltpu.roll(value, way_y % rows, 0)
             if way_z != 0:
@@ -341,7 +288,7 @@
     tiles = [
         (slice(row, row + 8), slice(col, col + 128))
         for row in range(0, rows, 8)
-        for col in range(0, lanes, 128)
+        for col in range(0, width, 128)
     ]
 
     def first_step(number, carry):
@@ -356,33 +303,100 @@
 
     lax.fori_loop(0, depth + LOW + HIGH - 2, first_step, 0)
 
-    row_at = lax.broadcasted_iota(jnp.int32, (8, 128), 0)
-    lane_at = lax.broadcasted_iota(jnp.int32, (8, 128), 1)
-
     def second_step(number, carry):
-        layer = number - 1
-        pull(second, layer, number + 1)
-        keep = jnp.logical_not((level == 0) & (layer < 0) | (level == levels - 1) & (layer >= depth))
+        pull(second, number - 1, number + 1)
         for tile in tiles:
             density, moment = moments([pulled[(index, *tile)] for index in range(19)])
             inverse = 1.0 / density
-            row = row_at + tile[0].start
-            col = lane_at + tile[1].start
-            valid = ((row < height + 2) | (row == rows - 1)) & ((col < width + 2) | (col == lanes - 1))
             for axis in range(3):
-                vel_ref[(axis, number, *tile)] = jnp.where(valid & keep, moment[axis] * inverse, 0.0)
+                vel_ref[(axis, number, *tile)] = moment[axis] * inverse
         return carry
-
-    lax.fori_loop(0, 1, second_step, 0)
 
     def second_inner(number, carry):
         second_step(number, carry)
         for index in range(19):
-            pops_ref[index, number - 1] = pulled[index, :height, main]
+            pops_ref[index, number - 1] = pulled[index, :height, :]
         return carry
 
+    lax.fori_loop(0, 1, second_step, 0)
     lax.fori_loop(1, depth + 1, second_inner, 0)
     lax.fori_loop(depth + 1, depth + 3, second_step, 0)
+
+
+def edge_body(
+    levels, level_ref, strip_ref, left_ref, right_ref, inner_pops, inner_vel,
+    pops_ref, vel_ref, sides, pulled, second,
+):
+    depth, height, width = pops_ref.shape[1:]
+    rows, lanes = height + 8, width + 128
+    level = level_ref[0]
+    lane = lax.broadcasted_iota(jnp.int32, (rows, 128), 1)
+    before = lane % 8 < 4
+    bottom = (lane // 8 == LOW) & (level == 0)
+    top = (lane // 8 == LOW + depth - 1) & (level == levels - 1)
+    for channel in range(channels):
+        own = strip_ref[channel]
+        sides[0, channel] = jnp.where(before, left_ref[channel], own)
+        sides[1, channel] = jnp.where(before, own, right_ref[channel])
+
+    def pull(source, side, target):
+        for index in range(19):
+            way_z, way_y, way_x = ways[index]
+            value = lane_roll(source[side, index], 8 * way_z + way_x)
+            if way_y != 0:
+                value = pltpu.roll(value, way_y % rows, 0)
+            if way_z != 0:
+                value = jnp.where(bottom if way_z == 1 else top, source[side, opposite[index]], value)
+            target[side, index] = value
+
+    speeds = [[], []]
+    for side in range(2):
+        pull(sides, side, pulled)
+        for row in range(0, rows, 8):
+            cut = slice(row, row + 8)
+            posts = relaxed([pulled[side, index, cut] for index in range(19)])
+            inside = sides[side, 19, cut] > 0.5
+            for index in range(19):
+                second[side, index, cut] = jnp.where(inside, sides[side, index, cut], posts[index])
+        pull(second, side, pulled)
+        density, moment = moments([pulled[side, index] for index in range(19)])
+        inverse = 1.0 / density
+        speeds[side] = [part * inverse for part in moment]
+
+    near = lane[:height]
+    near = (near < 2) | (near >= 126)
+    front = before[:height]
+    for index in range(19):
+        value = jnp.where(front, pulled[1, index, :height], pulled[0, index, :height])
+        for layer in range(depth):
+            turned = lane_roll(value, -(8 * (layer + LOW) + 4))
+            for col in range(0, width, 128):
+                cells = inner_pops[index, layer, :, col : col + 128]
+                if col == 0 or col == width - 128:
+                    mask = near if width == 128 else near & ((lane[:height] < 64) == (col == 0))
+                    cells = jnp.where(mask, turned, cells)
+                pops_ref[index, layer, :, col : col + 128] = cells
+    row = lax.broadcasted_iota(jnp.int32, (rows, 128), 0)
+    valid = (row < height + 2) | (row == rows - 1)
+    beyond = (lane < 2) | (lane == 127)
+    for axis in range(3):
+        main = jnp.where(before, speeds[1][axis], speeds[0][axis])
+        rest = jnp.where(before, speeds[0][axis], speeds[1][axis])
+        for layer in range(depth + 3):
+            keep = valid
+            if layer == 0:
+                keep = valid & (level != 0)
+            if layer > depth:
+                keep = valid & (level != levels - 1)
+            shift = -(8 * (layer - 1 + LOW) + 4)
+            turned = lane_roll(main, shift)
+            for col in range(0, width, 128):
+                cells = inner_vel[axis, layer, :, col : col + 128]
+                if col == 0 or col == width - 128:
+                    mask = (lane < 2) & (col == 0) | (lane >= 126) & (col == width - 128)
+                    cells = jnp.where(mask, turned, cells)
+                vel_ref[axis, layer, :, col : col + 128] = jnp.where(keep, cells, 0.0)
+            vel_ref[axis, layer, :, width:] = jnp.where(keep & beyond, lane_roll(rest, shift), 0.0)
 
 
 def shifted(value, axis, step):
@@ -416,29 +430,38 @@
     sizes = rim_sizes(levels)
     slots = len(sizes)
     kinds = ["low", "high"][:slots]
-    rims_of = [(size, height, width) for size, _ in sizes]
-    strips_of = [(count, height, 128) for _, count in sizes]
+    down_sizes, up_sizes = zip(*rim_row_sizes(levels))
     outs = call(
         functools.partial(first_body, levels),
-        [(channels, depth, height, width)] + rims_of + [(depth, height, 128)] * 2 + strips_of * 2,
+        [(channels, depth, height, width)]
+        + [(size, width) for size in own_rows(depth)[1]]
+        + [(size, height, width) for size in sizes]
+        + [(size, width) for size in down_sizes + up_sizes],
         [level, pops, coarse_pops, interface],
     )
-    posts, rims = outs[0], outs[1 : slots + 1]
-    right, left = outs[slots + 1 : slots + 3]
-    right_rims, left_rims = outs[slots + 3 : 2 * slots + 3], outs[2 * slots + 3 :]
-    low = shifted(right, "gx", 1)
-    high = shifted(left, "gx", -1)
-    low_rims = [to_level(value, kind, levels, "gx", 1) for value, kind in zip(right_rims, kinds)]
-    high_rims = [to_level(value, kind, levels, "gx", -1) for value, kind in zip(left_rims, kinds)]
-    rims = [to_level(value, kind, levels) for value, kind in zip(rims, kinds)]
-    given = [level, posts, low, high, *rims, *low_rims, *high_rims]
-    counts = row_table(depth, levels)[-1]
-    down, up = call(
-        functools.partial(rows_body, levels), [(count, width) for count in counts], given
-    )
-    above = shifted(down, "gy", -1)
-    below = shifted(up, "gy", 1)
-    return given + [above, below]
+    posts, down, up = outs[:3]
+    rims, down_rims, up_rims = (outs[3 + slots * at : 3 + slots * at + slots] for at in range(3))
+    given = [level, posts, shifted(down, "gy", -1), shifted(up, "gy", 1)]
+    given += [to_level(value, kind, levels) for value, kind in zip(rims, kinds)]
+    given += [to_level(value, kind, levels, "gy", -1) for value, kind in zip(down_rims, kinds)]
+    given += [to_level(value, kind, levels, "gy", 1) for value, kind in zip(up_rims, kinds)]
+    deep, rows = depth + LOW + HIGH, height + 8
+    ext = pltpu.VMEM((channels, deep, rows, width), jnp.float32)
+    (strip,) = call(functools.partial(strip_body, levels), [(channels, rows, 128)], given, 1, [ext])
+    left, right = shifted(strip, "gx", 1), shifted(strip, "gx", -1)
+    inner_pops, inner_vel = call(
+        functools.partial(inner_body, levels),
+        [pops.shape, (3, depth + 3, rows, width)],
+        given,
+        1,
+        [
+            ext,
+            pltpu.VMEM((19, rows, width), jnp.float32),
+            pltpu.VMEM((19, deep - 2, rows, width), jnp.float32),
+        ],
+        pl.CostEstimate(flops=10**8, bytes_accessed=1 << 22, transcendentals=0),
+    )
+    return [strip, left, right, inner_pops, inner_vel]
 
 
 def phis(frac):
@@ -630,23 +653,20 @@
         guarded(level, sender, pack)
 
 
-def main_body(levels, level_ref, counts_ref, dest_ref, *rest):
+def main_body(
+    levels, level_ref, counts_ref, dest_ref, strip_ref, left_ref, right_ref, inner_pops, inner_vel,
+    speed_ref, frac_ref, home_ref, pops_ref, own_ref, stay_ref, side_ref, north_ref, south_ref, *rest,
+):
     slots = len(rim_sizes(levels))
-    posts_ref, low_ref, high_ref = rest[:3]
-    rims, low_rims, high_rims = (rest[3 + slots * at : 3 + slots * at + slots] for at in range(3))
-    rest = rest[3 + 3 * slots :]
-    above_ref, below_ref, speed_ref, frac_ref, home_ref = rest[:5]
-    pops_ref, own_ref, stay_ref, side_ref, north_ref, south_ref = rest[5:11]
-    to_levels, north_levels, south_levels = (rest[11 + slots * at : 11 + slots * at + slots] for at in range(3))
-    rest = rest[11 + 3 * slots :]
+    to_levels, north_levels, south_levels = (rest[slots * at : slots * at + slots] for at in range(3))
+    rest = rest[3 * slots :]
     vel_ref, spread_ref, state_ref, outbox, strip, taken = rest[:6]
-    steps_body(
-        levels, level_ref, posts_ref, low_ref, high_ref, rims, low_rims, high_rims, above_ref, below_ref,
-        pops_ref, vel_ref, *rest[6:11],
+    edge_body(
+        levels, level_ref, strip_ref, left_ref, right_ref, inner_pops, inner_vel, pops_ref, vel_ref, *rest[6:9]
     )
     droplet_body(
-        posts_ref.shape[1:], counts_ref, dest_ref, vel_ref, speed_ref, frac_ref, home_ref,
-        spread_ref, stay_ref, state_ref, *rest[11:],
+        pops_ref.shape[1:], counts_ref, dest_ref, vel_ref, speed_ref, frac_ref, home_ref,
+        spread_ref, stay_ref, state_ref, *rest[9:],
     )
     pack_body(
         levels, level_ref, dest_ref, spread_ref, state_ref, own_ref, side_ref,
@@ -775,7 +795,6 @@
     given = wide_exchange(level, pops, coarse_pops, interface)
     layers, rows, lanes = depth + 3, height + 8, width + 128
     flat = 3 * layers * rows
-    deep = depth + LOW + HIGH
     sizes = [(count + GROUP, width) for count in message_rows(depth)]
     outs = call(
         functools.partial(main_body, levels),
@@ -783,7 +802,7 @@
         + [sizes[0]] * slots
         + [sizes[3]] * slots
         + [sizes[4]] * slots,
-        [given[0], counts, dest] + given[1:] + [drop_vel, drop_frac, home],
+        [level, counts, dest] + given + [drop_vel, drop_frac, home],
         3,
         [
             pltpu.VMEM((3, layers, rows, lanes), jnp.float32),
@@ -792,11 +811,9 @@
             pltpu.VMEM((27 * CAP, 8, 128), jnp.float32),
             pltpu.VMEM((layers, rows, 128), jnp.float32),
             pltpu.SMEM((27,), jnp.int32),
-            pltpu.VMEM((channels, deep, rows, lanes), jnp.float32),
-            pltpu.VMEM((deep, rows, 128), jnp.float32),
-            pltpu.VMEM((deep, rows, 128), jnp.float32),
-            pltpu.VMEM((19, rows, lanes), jnp.float32),
-            pltpu.VMEM((19, deep - 2, rows, lanes), jnp.float32),
+            pltpu.VMEM((2, channels, rows, 128), jnp.float32),
+            pltpu.VMEM((2, 19, rows, 128), jnp.float32),
+            pltpu.VMEM((2, 19, rows, 128), jnp.float32),
             pltpu.VMEM((flat, lanes), jnp.bfloat16),
             pltpu.VMEM((flat, lanes), jnp.bfloat16),
             pltpu.VMEM((lanes, 256), jnp.bfloat16),

time: 70.5 us -> 68 us (0.965)
  starting transfers between devices: 21.4 us -> 18.9 us
  waiting for transfers between devices: 16 us -> 17 us
    ppermute x4, waiting for transfers between devices: 4.08 us -> 8.97 us  [to_level(): lax.ppermute(value, (side, 'gz'), [(brick * levels + at, (brick + step) %...]
    ppermute x8, waiting for transfers between devices: 11.9 us -> 8.02 us  [shifted(): lax.ppermute(value, axis, [(i, (i + step) % count) for i in range(count)])]
    ppermute x4, starting transfers between devices: 7.37 us -> 4.39 us  [to_level(): lax.ppermute(value, (side, 'gz'), [(brick * levels + at, (brick + step) %...]
    ppermute x8, starting transfers between devices: 10.6 us -> 11.5 us  [shifted(): lax.ppermute(value, axis, [(i, (i + step) % count) for i in range(count)])]
    pallas_call x5 -> x6, Pallas kernels: 28.1 us -> 28.3 us  [call(): pl.pallas_call(body, out_shape=[jax.ShapeDtypeStruct(shape, jnp.float32)...]
  transfers between devices with their start and end apart: 14 -> 14, of which waited for: 4 -> 5; matrix products, arithmetic and copies ran while one was open for 0% -> 0% of each run, Pallas kernels for 0% -> 8%
where the time goes in v4:
time: 68 us; the launch traced here: 67.8 us
  Pallas kernels  28.3 us (42%)
  starting transfers between devices  18.9 us (28%)
  waiting for transfers between devices  17 us (25%)
  local copies, waits for them, and re-layouts  2.76 us (4%)
  between operations  0.75 us (1%)
    pallas_call x6, Pallas kernels, call(): pl.pallas_call(body, out_shape=[jax.ShapeDtypeStruct(shape, jnp.float32)...  28.3 us
    ppermute x8, starting transfers between devices, shifted(): lax.ppermute(value, axis, [(i, (i + step) % count) for i in range(count)])  11.5 us
    ppermute x4, waiting for transfers between devices, to_level(): lax.ppermute(value, (side, 'gz'), [(brick * levels + at, (brick + step) %...  8.97 us
    ppermute x8, waiting for transfers between devices, shifted(): lax.ppermute(value, axis, [(i, (i + step) % count) for i in range(count)])  8.02 us
    ppermute x4, starting transfers between devices, to_level(): lax.ppermute(value, (side, 'gz'), [(brick * levels + at, (brick + step) %...  4.39 us
    ppermute x2, starting transfers between devices, to_level(): return lax.ppermute(value, 'gz', pairs)  3.09 us
    unnamed x28, local copies, waits for them, and re-layouts  2.76 us
  transfers between devices with their start and end apart: 14, of which 5 were waited for; matrix products, arithmetic and copies ran while one was open for 0% of the time, Pallas kernels for 8%

profile of v4, /device:TPU:0, one launch (start us, length us, event | category | flops | bytes accessed | tf_op | source)
XLA Modules:
  0.0 67.8 jit_solution(10120398319225477963)
XLA Ops:
  0.6 2.6 %shard_map.103 = (f32[20,8,8,128]{3,2,1,0:T(8,128)}, f32[488,128]{1,0:T(8,128)}, f32[328,128]{1,0:T(8,128)}, f32[60,8,128]{2,1,0:T(8,128)}, f32[184,128]{1,0:T(8,128)}, /*index=5*/f32[120,128]{1,0:T(8,128)}) custom-call(s32[1]{0:T(128)} %bitcast.level_ref, f32[19,8,8,128]{3,2,1,0:T(8,128)} %pops_ref.1, bf16[19,8,8,128]{3,2,1,0:T(8,128)(2,1)} %coarse_ref.1, ...), custom_call_target="tpu_custom_call" | custom-call | tf_op jit(solution)/shard_map/pallas_call | solution.py:47
  3.2 2.4 %collective-permute-start = (f32[488,128]{1,0:T(8,128)}, f32[488,128]{1,0:T(8,128)S(1)}, u32[]{:S(2)}, u32[]{:S(2)}) collective-permute-start(f32[488,128]{1,0:T(8,128)} %get-tuple-element.26), channel_id=1, source_target_pairs={{0,6},{2,0},{4,2},{6,4},{1,7},{3,1},{5,3},{7,5},{8,14},{10,8},{12,... | collective-permute-start | bytes 749576 | tf_op jit(solution)/shard_map/ppermute | solution.py:404
  5.6 1.5 %collective-permute-start.2 = (f32[60,8,128]{2,1,0:T(8,128)}, f32[60,8,128]{2,1,0:T(8,128)S(1)}, u32[]{:S(2)}, u32[]{:S(2)}) collective-permute-start(f32[60,8,128]{2,1,0:T(8,128)} %get-tuple-element.28), channel_id=1, source_target_pairs={{0,1},{1,0},{2,3},{3,2},{4,5},{5,4},{6,7},{7,6},{8,9},{9,8},{10,11... | collective-permute-start | bytes 737288 | tf_op jit(solution)/shard_map/ppermute | solution.py:414
  7.1 1.7 %collective-permute-start.3 = (f32[184,128]{1,0:T(8,128)}, f32[184,128]{1,0:T(8,128)S(1)}, u32[]{:S(2)}, u32[]{:S(2)}) collective-permute-start(f32[184,128]{1,0:T(8,128)} %get-tuple-element.29), channel_id=1, source_target_pairs={{0,7},{1,6},{2,1},{3,0},{4,3},{5,2},{6,5},{7,4},{8,15},{9,14},{10,... | collective-permute-start | bytes 282632 | tf_op jit(solution)/shard_map/ppermute | solution.py:416
  8.9 6.9 %collective-permute-done.4.rest_5_ = f32[120,128]{1,0:T(8,128)S(1)} collective-permute-done((f32[120,128]{1,0:T(8,128)}, f32[120,128]{1,0:T(8,128)S(1)}, u32[]{:S(2)}, u32[]{:S(2)}) %collective-permute-start.4) | collective-permute-done | bytes 61472 | tf_op jit(solution)/shard_map/ppermute | solution.py:416
  15.8 0.5 copy-done.4
  16.6 4.2 %shard_map.104.strip_ref = f32[20,16,128]{2,1,0:T(8,128)} custom-call(s32[1]{0:T(128)} %bitcast.level_ref, f32[20,8,8,128]{3,2,1,0:T(8,128)} %get-tuple-element.25.rest_0_, f32[488,128]{1,0:T(8,128)} %copy-done, f32[328,128]{1,0:T(8,128)} %copy-done.2, f32[60,8,128]{2,1,0:T(8,128)} %copy-done.1, f32[184,128]{1,0:T(8,128)} %copy-done.3, f32[120,128]{1,0:T(8,128)} %copy-done.4), custom_call_target="tpu_custom_call" | custom-call | tf_op jit(solution)/shard_map/pallas_call | solution.py:47
  20.9 1.7 %collective-permute-start.5 = (f32[20,16,128]{2,1,0:T(8,128)}, f32[20,16,128]{2,1,0:T(8,128)S(1)}, u32[]{:S(2)}, u32[]{:S(2)}) collective-permute-start(f32[20,16,128]{2,1,0:T(8,128)} %shard_map.104.strip_ref), channel_id=1, source_target_pairs={{0,8},{8,16},{16,24},{24,0},{1,9},{9,17},{17,25},{25,1},{2,10},{10... | collective-permute-start | bytes 491528 | tf_op jit(solution)/shard_map/ppermute | solution.py:404
  22.5 2.2 %collective-permute-start.6 = (f32[20,16,128]{2,1,0:T(8,128)}, f32[20,16,128]{2,1,0:T(8,128)S(1)}, u32[]{:S(2)}, u32[]{:S(2)}) collective-permute-start(f32[20,16,128]{2,1,0:T(8,128)} %shard_map.104.strip_ref), channel_id=1, source_target_pairs={{0,24},{8,0},{16,8},{24,16},{1,25},{9,1},{17,9},{25,17},{2,26},{10... | collective-permute-start | bytes 491528 | tf_op jit(solution)/shard_map/ppermute | solution.py:404
  24.7 5.4 %shard_map.105 = (f32[19,8,8,128]{3,2,1,0:T(8,128)}, f32[3,11,16,128]{3,2,1,0:T(8,128)}) custom-call(s32[1]{0:T(128)} %bitcast.level_ref, f32[20,8,8,128]{3,2,1,0:T(8,128)} %get-tuple-element.25.rest_0_, f32[488,128]{1,0:T(8,128)} %copy-done, f32[328,128]{1,0:T(8,128)} %copy-done.2, f32[60,8,128]{2,1,0:T(8,128)} %copy-done.1, f32[184,128]{1,0:T(8,128)} %copy-done.3, ...), custom_call_target="tpu_custom_call" | custom-call | flops 100000000 | bytes 4194304 | tf_op jit(solution)/shard_map/pallas_call | solution.py:47
  30.1 2.6 %collective-permute-done.6.right_ref = f32[20,16,128]{2,1,0:T(8,128)S(1)} collective-permute-done((f32[20,16,128]{2,1,0:T(8,128)}, f32[20,16,128]{2,1,0:T(8,128)S(1)}, u32[]{:S(2)}, u32[]{:S(2)}) %collective-permute-start.6) | collective-permute-done | bytes 163872 | tf_op jit(solution)/shard_map/ppermute | solution.py:404
  32.7 0.7 copy-done.8
  33.3 12.2 %shard_map.106 = (f32[19,8,8,128]{3,2,1,0:T(8,128)}, f32[4,8,8,128]{3,2,1,0:T(8,128)}, f32[6,16,128]{2,1,0:T(8,128)}, f32[4,8,128]{2,1,0:T(8,128)}, f32[112,128]...) custom-call(s32[1]{0:T(128)} %bitcast.level_ref, ...), custom_call_target="tpu_custom_call" | custom-call | tf_op jit(solution)/shard_map/pallas_call | solution.py:47
  45.6 1.6 %collective-permute-start.9 = (f32[112,128]{1,0:T(8,128)}, f32[112,128]{1,0:T(8,128)S(1)}, u32[]{:S(2)}, u32[]{:S(2)}) collective-permute-start(f32[112,128]{1,0:T(8,128)} %get-tuple-element.38), channel_id=1, source_target_pairs={{0,1},{1,0},{2,3},{3,2},{4,5},{5,4},{6,7},{7,6},{8,9},{9,8},{10,11... | collective-permute-start | bytes 172040 | tf_op jit(solution)/shard_map/ppermute | solution.py:414
  47.2 1.4 %collective-permute-start.8 = (f32[80,128]{1,0:T(8,128)}, f32[80,128]{1,0:T(8,128)S(1)}, u32[]{:S(2)}, u32[]{:S(2)}) collective-permute-start(f32[80,128]{1,0:T(8,128)} %get-tuple-element.37), channel_id=1, source_target_pairs={{0,6},{2,0},{4,2},{6,4},{1,7},{3,1},{5,3},{7,5},{8,14},{10,8},{12,... | collective-permute-start | bytes 122888 | tf_op jit(solution)/shard_map/ppermute | solution.py:404
  48.8 2.4 %collective-permute-start.11 = (f32[56,128]{1,0:T(8,128)}, f32[56,128]{1,0:T(8,128)S(1)}, u32[]{:S(2)}, u32[]{:S(2)}) collective-permute-start(f32[56,128]{1,0:T(8,128)} %get-tuple-element.40), channel_id=1, source_target_pairs={{0,7},{1,6},{2,1},{3,0},{4,3},{5,2},{6,5},{7,4},{8,15},{9,14},{10,... | collective-permute-start | bytes 86024 | tf_op jit(solution)/shard_map/ppermute | solution.py:416
  51.2 2.1 %collective-permute-done.11.rest_4_ = f32[56,128]{1,0:T(8,128)S(1)} collective-permute-done((f32[56,128]{1,0:T(8,128)}, f32[56,128]{1,0:T(8,128)S(1)}, u32[]{:S(2)}, u32[]{:S(2)}) %collective-permute-start.11) | collective-permute-done | bytes 28704 | tf_op jit(solution)/shard_map/ppermute | solution.py:416
  54.0 1.7 %shard_map.107 = (f32[3,8,8,128]{3,2,1,0:T(8,128)}, f32[208,128]{1,0:T(8,128)}, f32[208,128]{1,0:T(8,128)}) custom-call(s32[1]{0:T(128)} %bitcast.level_ref, f32[4,8,8,128]{3,2,1,0:T(8,128)} %get-tuple-element.34.own_ref, f32[4,8,128]{2,1,0:T(8,128)} %get-tuple-element.35.side_ref, f32[112,128]{1,0:T(8,128)} %copy-done.5, f32[80,128]{1,0:T(8,128)} %copy-done.9, ...), custom_call_target="tpu_custom_call" | custom-call | tf_op jit(solution)/shard_map/pallas_call | solution.py:47
  55.7 1.1 %collective-permute-start.12 = (f32[208,128]{1,0:T(8,128)}, f32[208,128]{1,0:T(8,128)S(1)}, u32[]{:S(2)}, u32[]{:S(2)}) collective-permute-start(f32[208,128]{1,0:T(8,128)} %get-tuple-element.43), channel_id=1, source_target_pairs={{0,8},{8,16},{16,24},{24,0},{1,9},{9,17},{17,25},{25,1},{2,10},{10... | collective-permute-start | bytes 319496 | tf_op jit(solution)/shard_map/ppermute | solution.py:404
  56.9 2.7 %collective-permute-start.13 = (f32[208,128]{1,0:T(8,128)}, f32[208,128]{1,0:T(8,128)S(1)}, u32[]{:S(2)}, u32[]{:S(2)}) collective-permute-start(f32[208,128]{1,0:T(8,128)} %get-tuple-element.44), channel_id=1, source_target_pairs={{0,24},{8,0},{16,8},{24,16},{1,25},{9,1},{17,9},{25,17},{2,26},{10... | collective-permute-start | bytes 319496 | tf_op jit(solution)/shard_map/ppermute | solution.py:404
  59.6 3.8 %collective-permute-done.12.rest_5_ = f32[208,128]{1,0:T(8,128)S(1)} collective-permute-done((f32[208,128]{1,0:T(8,128)}, f32[208,128]{1,0:T(8,128)S(1)}, u32[]{:S(2)}, u32[]{:S(2)}) %collective-permute-start.12) | collective-permute-done | bytes 106528 | tf_op jit(solution)/shard_map/ppermute | solution.py:404
  63.4 1.7 %collective-permute-done.13.rest_6_ = f32[208,128]{1,0:T(8,128)S(1)} collective-permute-done((f32[208,128]{1,0:T(8,128)}, f32[208,128]{1,0:T(8,128)S(1)}, u32[]{:S(2)}, u32[]{:S(2)}) %collective-permute-start.13) | collective-permute-done | bytes 106528 | tf_op jit(solution)/shard_map/ppermute | solution.py:404
  65.0 0.6 copy-done.13
  65.7 2.1 %shard_map.108 = (f32[3,8,8,128]{3,2,1,0:T(8,128)}, f32[6,68,128]{2,1,0:T(8,128)}) custom-call(s32[1]{0:T(128)} %bitcast.level_ref, f32[3,8,8,128]{3,2,1,0:T(8,128)} %get-tuple-element.41.part_ref, f32[6,16,128]{2,1,0:T(8,128)} %get-tuple-element.42.stay_ref, f32[112,128]{1,0:T(8,128)} %copy-done.5, f32[80,128]{1,0:T(8,128)} %copy-done.9, ...), custom_call_target="tpu_custom_call" | custom-call | tf_op jit(solution)/shard_map/pallas_call | solution.py:47
  (38 shorter events, 1.3 us)
Async XLA Ops:
  3.2 12.6 %collective-permute-start = (f32[488,128]{1,0:T(8,128)}, f32[488,128]{1,0:T(8,128)S(1)}, u32[]{:S(2)}, u32[]{:S(2)}) collective-permute-start(f32[488,128]{1,0:T(8,128)} %get-tuple-element.26), channel_id=1, source_target_pairs={{0,6},{2,0},{4,2},{6,4},{1,7},{3,1},{5,3},{7,5},{8,14},{10,8},{12,... | collective-permute-start | bytes 749576 | tf_op jit(solution)/shard_map/ppermute | solution.py:404
  5.6 10.2 %collective-permute-start.2 = (f32[60,8,128]{2,1,0:T(8,128)}, f32[60,8,128]{2,1,0:T(8,128)S(1)}, u32[]{:S(2)}, u32[]{:S(2)}) collective-permute-start(f32[60,8,128]{2,1,0:T(8,128)} %get-tuple-element.28), channel_id=1, source_target_pairs={{0,1},{1,0},{2,3},{3,2},{4,5},{5,4},{6,7},{7,6},{8,9},{9,8},{10,11... | collective-permute-start | bytes 737288 | tf_op jit(solution)/shard_map/ppermute | solution.py:414
  7.1 8.6 %collective-permute-start.1 = (f32[328,128]{1,0:T(8,128)}, f32[328,128]{1,0:T(8,128)S(1)}, u32[]{:S(2)}, u32[]{:S(2)}) collective-permute-start(f32[328,128]{1,0:T(8,128)} %get-tuple-element.27), channel_id=1, source_target_pairs={{0,2},{2,4},{4,6},{6,0},{1,3},{3,5},{5,7},{7,1},{8,10},{10,12},{12... | collective-permute-start | bytes 503816 | tf_op jit(solution)/shard_map/ppermute | solution.py:404
  7.1 8.6 %collective-permute-start.3 = (f32[184,128]{1,0:T(8,128)}, f32[184,128]{1,0:T(8,128)S(1)}, u32[]{:S(2)}, u32[]{:S(2)}) collective-permute-start(f32[184,128]{1,0:T(8,128)} %get-tuple-element.29), channel_id=1, source_target_pairs={{0,7},{1,6},{2,1},{3,0},{4,3},{5,2},{6,5},{7,4},{8,15},{9,14},{10,... | collective-permute-start | bytes 282632 | tf_op jit(solution)/shard_map/ppermute | solution.py:416
  8.8 6.9 %collective-permute-start.4 = (f32[120,128]{1,0:T(8,128)}, f32[120,128]{1,0:T(8,128)S(1)}, u32[]{:S(2)}, u32[]{:S(2)}) collective-permute-start(f32[120,128]{1,0:T(8,128)} %get-tuple-element.30), channel_id=1, source_target_pairs={{0,3},{1,2},{2,5},{3,4},{4,7},{5,6},{6,1},{7,0},{8,11},{9,10},{10,... | collective-permute-start | bytes 184328 | tf_op jit(solution)/shard_map/ppermute | solution.py:416
  15.8 0.7 copy-start.3
  15.8 0.7 %copy-start.2 = (f32[328,128]{1,0:T(8,128)}, f32[328,128]{1,0:T(8,128)S(1)}, u32[]{:S(2)}) copy-start(f32[328,128]{1,0:T(8,128)S(1)} %collective-permute-done.1.rest_2_) | copy-start | bytes 503812
  15.8 0.8 %copy-start.1 = (f32[60,8,128]{2,1,0:T(8,128)}, f32[60,8,128]{2,1,0:T(8,128)S(1)}, u32[]{:S(2)}) copy-start(f32[60,8,128]{2,1,0:T(8,128)S(1)} %collective-permute-done.2.rest_3_) | copy-start | bytes 737284
  15.8 0.8 %copy-start = (f32[488,128]{1,0:T(8,128)}, f32[488,128]{1,0:T(8,128)S(1)}, u32[]{:S(2)}) copy-start(f32[488,128]{1,0:T(8,128)S(1)} %collective-permute-done.rest_1_) | copy-start | bytes 749572
  20.9 9.2 %collective-permute-start.5 = (f32[20,16,128]{2,1,0:T(8,128)}, f32[20,16,128]{2,1,0:T(8,128)S(1)}, u32[]{:S(2)}, u32[]{:S(2)}) collective-permute-start(f32[20,16,128]{2,1,0:T(8,128)} %shard_map.104.strip_ref), channel_id=1, source_target_pairs={{0,8},{8,16},{16,24},{24,0},{1,9},{9,17},{17,25},{25,1},{2,10},{10... | collective-permute-start | bytes 491528 | tf_op jit(solution)/shard_map/ppermute | solution.py:404
  22.5 10.1 %collective-permute-start.6 = (f32[20,16,128]{2,1,0:T(8,128)}, f32[20,16,128]{2,1,0:T(8,128)S(1)}, u32[]{:S(2)}, u32[]{:S(2)}) collective-permute-start(f32[20,16,128]{2,1,0:T(8,128)} %shard_map.104.strip_ref), channel_id=1, source_target_pairs={{0,24},{8,0},{16,8},{24,16},{1,25},{9,1},{17,9},{25,17},{2,26},{10... | collective-permute-start | bytes 491528 | tf_op jit(solution)/shard_map/ppermute | solution.py:404
  30.1 2.6 %copy-start.7 = (f32[20,16,128]{2,1,0:T(8,128)}, f32[20,16,128]{2,1,0:T(8,128)S(1)}, u32[]{:S(2)}) copy-start(f32[20,16,128]{2,1,0:T(8,128)S(1)} %collective-permute-done.5.left_ref) | copy-start | bytes 491524
  32.7 0.7 copy-start.8
  45.6 7.8 %collective-permute-start.7 = (f32[112,128]{1,0:T(8,128)}, f32[112,128]{1,0:T(8,128)S(1)}, u32[]{:S(2)}, u32[]{:S(2)}) collective-permute-start(f32[112,128]{1,0:T(8,128)} %get-tuple-element.36), channel_id=1, source_target_pairs={{0,2},{2,4},{4,6},{6,0},{1,3},{3,5},{5,7},{7,1},{8,10},{10,12},{12... | collective-permute-start | bytes 172040 | tf_op jit(solution)/shard_map/ppermute | solution.py:404
  45.6 7.8 %collective-permute-start.9 = (f32[112,128]{1,0:T(8,128)}, f32[112,128]{1,0:T(8,128)S(1)}, u32[]{:S(2)}, u32[]{:S(2)}) collective-permute-start(f32[112,128]{1,0:T(8,128)} %get-tuple-element.38), channel_id=1, source_target_pairs={{0,1},{1,0},{2,3},{3,2},{4,5},{5,4},{6,7},{7,6},{8,9},{9,8},{10,11... | collective-permute-start | bytes 172040 | tf_op jit(solution)/shard_map/ppermute | solution.py:414
  47.2 6.2 %collective-permute-start.8 = (f32[80,128]{1,0:T(8,128)}, f32[80,128]{1,0:T(8,128)S(1)}, u32[]{:S(2)}, u32[]{:S(2)}) collective-permute-start(f32[80,128]{1,0:T(8,128)} %get-tuple-element.37), channel_id=1, source_target_pairs={{0,6},{2,0},{4,2},{6,4},{1,7},{3,1},{5,3},{7,5},{8,14},{10,8},{12,... | collective-permute-start | bytes 122888 | tf_op jit(solution)/shard_map/ppermute | solution.py:404
  48.6 4.8 %collective-permute-start.10 = (f32[64,128]{1,0:T(8,128)}, f32[64,128]{1,0:T(8,128)S(1)}, u32[]{:S(2)}, u32[]{:S(2)}) collective-permute-start(f32[64,128]{1,0:T(8,128)} %get-tuple-element.39), channel_id=1, source_target_pairs={{0,3},{1,2},{2,5},{3,4},{4,7},{5,6},{6,1},{7,0},{8,11},{9,10},{10,... | collective-permute-start | bytes 98312 | tf_op jit(solution)/shard_map/ppermute | solution.py:416
  48.8 4.5 %collective-permute-start.11 = (f32[56,128]{1,0:T(8,128)}, f32[56,128]{1,0:T(8,128)S(1)}, u32[]{:S(2)}, u32[]{:S(2)}) collective-permute-start(f32[56,128]{1,0:T(8,128)} %get-tuple-element.40), channel_id=1, source_target_pairs={{0,7},{1,6},{2,1},{3,0},{4,3},{5,2},{6,5},{7,4},{8,15},{9,14},{10,... | collective-permute-start | bytes 86024 | tf_op jit(solution)/shard_map/ppermute | solution.py:416
  53.3 0.6 copy-start.9
  53.4 0.6 copy-start.6
  55.7 7.6 %collective-permute-start.12 = (f32[208,128]{1,0:T(8,128)}, f32[208,128]{1,0:T(8,128)S(1)}, u32[]{:S(2)}, u32[]{:S(2)}) collective-permute-start(f32[208,128]{1,0:T(8,128)} %get-tuple-element.43), channel_id=1, source_target_pairs={{0,8},{8,16},{16,24},{24,0},{1,9},{9,17},{17,25},{25,1},{2,10},{10... | collective-permute-start | bytes 319496 | tf_op jit(solution)/shard_map/ppermute | solution.py:404
  56.9 8.2 %collective-permute-start.13 = (f32[208,128]{1,0:T(8,128)}, f32[208,128]{1,0:T(8,128)S(1)}, u32[]{:S(2)}, u32[]{:S(2)}) collective-permute-start(f32[208,128]{1,0:T(8,128)} %get-tuple-element.44), channel_id=1, source_target_pairs={{0,24},{8,0},{16,8},{24,16},{1,25},{9,1},{17,9},{25,17},{2,26},{10... | collective-permute-start | bytes 319496 | tf_op jit(solution)/shard_map/ppermute | solution.py:404
  63.4 1.7 %copy-start.12 = (f32[208,128]{1,0:T(8,128)}, f32[208,128]{1,0:T(8,128)S(1)}, u32[]{:S(2)}) copy-start(f32[208,128]{1,0:T(8,128)S(1)} %collective-permute-done.12.rest_5_) | copy-start | bytes 319492
  65.0 0.6 copy-start.13
  (4 other events, 2.5 us)

commit v5 on v4

--- a/solution.py
+++ b/solution.py
@@ -325,10 +325,10 @@
 
 def edge_body(
     levels, level_ref, strip_ref, left_ref, right_ref, inner_pops, inner_vel,
-    pops_ref, vel_ref, sides, pulled, second,
+    pops_ref, vel_ref, beyond_ref, sides, pulled, second,
 ):
     depth, height, width = pops_ref.shape[1:]
-    rows, lanes = height + 8, width + 128
+    rows = height + 8
     level = level_ref[0]
     lane = lax.broadcasted_iota(jnp.int32, (rows, 128), 1)
     before = lane % 8 < 4
@@ -378,7 +378,16 @@
                 pops_ref[index, layer, :, col : col + 128] = cells
     row = lax.broadcasted_iota(jnp.int32, (rows, 128), 0)
     valid = (row < height + 2) | (row == rows - 1)
-    beyond = (lane < 2) | (lane == 127)
+    outside = (lane < 2) | (lane == 127)
+    table = table_rows(depth, height)
+    vel_ref[...] = jnp.zeros_like(vel_ref)
+    beyond_ref[...] = jnp.zeros_like(beyond_ref)
+
+    def put(target, axis, layer, cols, cells):
+        at = axis * table + layer * (height + 3)
+        target[at : at + 1, cols] = cells[rows - 1 :, :]
+        target[at + 1 : at + height + 3, cols] = cells[: height + 2, :]
+
     for axis in range(3):
         main = jnp.where(before, speeds[1][axis], speeds[0][axis])
         rest = jnp.where(before, speeds[0][axis], speeds[1][axis])
@@ -395,8 +404,8 @@
                 if col == 0 or col == width - 128:
                     mask = (lane < 2) & (col == 0) | (lane >= 126) & (col == width - 128)
                     cells = jnp.where(mask, turned, cells)
-                vel_ref[axis, layer, :, col : col + 128] = jnp.where(keep, cells, 0.0)
-            vel_ref[axis, layer, :, width:] = jnp.where(keep & beyond, lane_roll(rest, shift), 0.0)
+                put(vel_ref, axis, layer, slice(col, col + 128), jnp.where(keep, cells, 0.0))
+            put(beyond_ref, axis, layer, slice(0, 128), jnp.where(keep & outside, lane_roll(rest, shift), 0.0))
 
 
 def shifted(value, axis, step):
@@ -487,89 +496,102 @@
     return lax.dot_general(left, right, (dims, ((), ())), preferred_element_type=jnp.float32)
 
 
+def table_rows(depth, height):
+    return -(-(depth + 3) * (height + 3) // 16) * 16
+
+
 def droplet_body(
-    size, counts_ref, dest_ref, vel_ref, speed_ref, frac_ref, home_ref, spread_ref, stay_ref, state_ref,
-    vel_high, vel_low, row_high, row_low, push_high, push_low, plane_ref,
+    size, counts_ref, dest_ref, vel_ref, beyond_ref, speed_ref, frac_ref, home_ref, spread_ref, outer_ref,
+    stay_ref, state_ref, twice, mixed, along, push_high, push_low, plane_ref,
 ):
     depth, height, width = size
     blocks = home_ref.shape[0]
-    layers, rows, lanes = depth + 3, height + 8, width + 128
-    high, low = split(vel_ref[...].reshape(3 * layers * rows, lanes))
-    vel_high[...] = high
-    vel_low[...] = low
-    row_high[...] = jnp.zeros_like(row_high)
-    row_low[...] = jnp.zeros_like(row_low)
-    used = width + 16
-    span_x = lax.broadcasted_iota(jnp.int32, (used, 128), 0) + 1
-    span_y = lax.broadcasted_iota(jnp.int32, (rows, 128), 0)
-    span_y = jnp.where(span_y >= height + 4, span_y - rows, span_y) + 1
-    span_z = lax.broadcasted_iota(jnp.int32, (layers, 128), 0)
-    last = lax.broadcasted_iota(jnp.int32, (16, 128), 0) == 15
+    layers, rows = depth + 3, height + 3
+    table = table_rows(depth, height)
+    high, low = split(vel_ref[...])
+    twice[:, :width] = high
+    twice[:, width:] = high
+    mixed[:, :width] = low
+    high, low = (part.astype(jnp.float32) for part in split(beyond_ref[...]))
+    mixed[:, width:] = (high + lane_roll(low, 32) + lane_roll(high, 64)).astype(jnp.bfloat16)
+    along[2 * width :, :] = jnp.zeros((128, along.shape[1]), jnp.bfloat16)
+    plane_ref[:, layers * rows :, :] = jnp.zeros(
+        (plane_ref.shape[0], table - layers * rows, 256), jnp.float32
+    )
+    span_x = lax.broadcasted_iota(jnp.int32, (width, 128), 0) + 1
+    span_end = lax.broadcasted_iota(jnp.int32, (16, 128), 0)
+    span_y = lax.broadcasted_iota(jnp.int32, (-(-rows // 8) * 8, 128), 0)
+    span_z = lax.broadcasted_iota(jnp.int32, (-(-layers // 8) * 8, 128), 0)
     slots = lax.broadcasted_iota(jnp.int32, (1, 128), 1)
 
-    def pair(number):
+    def weigh(number):
         for half in range(2):
             block = 2 * number + half
-            side = pl.ds(half * 128, 128)
-            cell = home_ref[pl.ds(block, 1), :]
-            cell_x = cell & (width - 1) if width & (width - 1) == 0 else cell % width
+            side = slice(block * 128, block * 128 + 128)
+            cell = home_ref[block : block + 1, :]
+            cell_x = cell % width
             cell_y = cell // width % height
             cell_z = cell // (width * height)
-            part_x = phis(frac_ref[0, pl.ds(block, 1), :])
-            part_y = phis(frac_ref[1, pl.ds(block, 1), :])
-            part_z = phis(frac_ref[2, pl.ds(block, 1), :])
+            part_x = phis(frac_ref[0, block : block + 1, :])
+            part_y = phis(frac_ref[1, block : block + 1, :])
+            part_z = phis(frac_ref[2, block : block + 1, :])
             high, low = split(pick(span_x - cell_x, part_x))
-            row_high[0:used, side] = high
-            row_low[0:used, side] = low
-            high, low = split(jnp.where(last & (cell_x == 0), part_x[0], 0.0))
-            row_high[lanes - 16 : lanes, side] = high
-            row_low[lanes - 16 : lanes, side] = low
-            weight_y = pick(span_y - cell_y, part_y)
+            along[0:width, side] = low
+            along[width : 2 * width, side] = high
+            high, low = split(pick(span_end + (width + 1) - cell_x, part_x))
+            along[2 * width : 2 * width + 16, side] = high
+            along[2 * width + 32 : 2 * width + 48, side] = high
+            along[2 * width + 64 : 2 * width + 80, side] = low
+            high, low = split(jnp.where((span_end == 15) & (cell_x == 0), part_x[0], 0.0))
+            along[2 * width + 112 : 2 * width + 128, side] = high
+            along[2 * width + 16 : 2 * width + 32, side] = high
+            along[2 * width + 48 : 2 * width + 64, side] = low
+            weight_y = pick(span_y - cell_y, part_y)[:rows]
             weight_z = pick(span_z - cell_z, part_z)
             for layer in range(layers):
-                plane_ref[layer, :, side] = weight_y * weight_z[layer : layer + 1, :]
-        along_high = row_high[...]
-        along_low = row_low[...]
-        sums = (
-            dots(vel_high[...], along_high, ((1,), (0,)))
-            + dots(vel_low[...], along_high, ((1,), (0,)))
-            + dots(vel_high[...], along_low, ((1,), (0,)))
-        ).reshape(3, layers, rows, 256)
-        plane = plane_ref[...]
-        sampled = jnp.sum(jnp.sum(sums * plane[None], axis=1), axis=1)
-        for half in range(2):
-            block = 2 * number + half
-            live = slots < counts_ref[block]
-            for axis in range(3):
-                sample = sampled[axis : axis + 1, half * 128 : half * 128 + 128]
-                speed = speed_ref[axis, pl.ds(block, 1), :]
-                frac = frac_ref[axis, pl.ds(block, 1), :]
+                plane_ref[number % 2, layer * rows : layer * rows + rows, half * 128 : half * 128 + 128] = (
+                    weight_y * weight_z[layer : layer + 1, :]
+                )
+
+    def sample(number):
+        pair = slice(number * 256, number * 256 + 256)
+        return dots(twice[...], along[0 : 2 * width, pair], ((1,), (0,))) + dots(
+            mixed[...], along[width:, pair], ((1,), (0,))
+        )
+
+    def move(number, sums):
+        plane = plane_ref[number % 2]
+        for axis in range(3):
+            where = slice(axis * table, axis * table + table)
+            sampled = jnp.sum(sums[where] * plane, axis=0, keepdims=True)
+            for half in range(2):
+                block = 2 * number + half
+                live = slots < counts_ref[block]
+                sample = sampled[:, half * 128 : half * 128 + 128]
+                speed = speed_ref[axis, block : block + 1, :]
+                frac = frac_ref[axis, block : block + 1, :]
                 moved = speed + relax * (sample - speed)
                 push = jnp.where(live, couple * (moved - sample), 0.0)
                 stays = live & (dest_ref[block] == 13)
                 for at, value in ((axis, moved), (3 + axis, frac + moved)):
                     state_ref[block, at : at + 1, :] = jnp.where(live, value, 0.0)
-                    stay_ref[at, pl.ds(block, 1), :] = jnp.where(stays, value, 0.0)
-                high, low = split(
-                    (plane[:, :, half * 128 : half * 128 + 128] * push[None]).reshape(layers * rows, 128)
-                )
-                where = pl.ds(axis * layers * rows, layers * rows)
-                push_high[where, half * 128 : half * 128 + 128] = high
-                push_low[where, half * 128 : half * 128 + 128] = low
-        patch = (
-            dots(push_high[...], along_high, ((1,), (1,)))
-            + dots(push_low[...], along_high, ((1,), (1,)))
-            + dots(push_high[...], along_low, ((1,), (1,)))
-        ).reshape(3, layers, rows, lanes)
-        return patch
-
-    spread_ref[...] = pair(0)
-
-    def step(number, carry):
-        spread_ref[...] += pair(number)
-        return carry
-
-    lax.fori_loop(1, blocks // 2, step, 0)
+                    stay_ref[at, block : block + 1, :] = jnp.where(stays, value, 0.0)
+                high, low = split(plane[:, half * 128 : half * 128 + 128] * push)
+                push_high[where, block * 128 : block * 128 + 128] = high
+                push_low[where, block * 128 : block * 128 + 128] = low
+
+    pairs = blocks // 2
+    weigh(0)
+    for number in range(pairs):
+        sums = sample(number)
+        if number + 1 < pairs:
+            weigh(number + 1)
+        move(number, sums)
+    main = dots(push_high[...], along[0 : 2 * width, :], ((1,), (1,)))
+    rest = dots(push_low[...], along[width:, :], ((1,), (1,)))
+    outer = dots(push_high[...], along[2 * width :, :], ((1,), (1,)))
+    spread_ref[...] = main[:, :width] + main[:, width:] + rest[:, :width]
+    outer_ref[...] = outer + lane_roll(outer, -64) + rest[:, width:]
 
 
 def force_sides(levels):
@@ -590,19 +612,19 @@
 
 
 def pack_body(
-    levels, level_ref, dest_ref, spread_ref, state_ref, own_ref, side_ref,
+    levels, level_ref, dest_ref, spread_ref, outer_ref, state_ref, own_ref, side_ref,
     to_levels, north_ref, south_ref, north_levels, south_levels, outbox, strip, taken,
 ):
     depth, height, width = own_ref.shape[1:]
     level = level_ref[0]
-    layers, rows = depth + 3, height + 8
-    lane = lax.broadcasted_iota(jnp.int32, (rows, 128), 1)
-    for layer in range(layers):
-        value = jnp.zeros((rows, 128), jnp.float32)
-        for axis in range(3):
-            here = (lane >= 4 * axis) & (lane < 4 * axis + 3)
-            value = jnp.where(here, lane_roll(spread_ref[axis, layer, :, width:], 4 * axis + 1), value)
-        strip[layer] = value
+    rows, table = height + 3, table_rows(depth, height)
+    lane = lax.broadcasted_iota(jnp.int32, (table, 128), 1)
+    value = jnp.zeros((table, 128), jnp.float32)
+    for axis in range(3):
+        here = (lane >= 4 * axis) & (lane < 4 * axis + 3)
+        cells = outer_ref[axis * table : axis * table + table, :]
+        value = jnp.where(here, lane_roll(cells, 4 * axis + 1), value)
+    strip[...] = value
     for code in range(27):
         taken[code] = 0
     outbox[...] = jnp.zeros_like(outbox)
@@ -616,14 +638,17 @@
             taken[code] = rank + 1
 
     def force(part, layer, cut):
-        return spread_ref[part, layer, cut, 0:width] if part < 3 else strip[layer, cut, :]
+        at = layer * rows
+        if part < 3:
+            return spread_ref[part * table + at + cut.start : part * table + at + cut.stop, :]
+        return strip[at + cut.start : at + cut.stop, :]
 
     def blocks(target, way_z, way_y):
         base = target.shape[0] - GROUP
         for slot in range(6):
             target[base + 8 * slot : base + 8 * slot + 8, :] = outbox[6 * group_at(way_z, way_y) + slot]
 
-    main, north, south = slice(0, height), slice(height, height + 2), slice(rows - 1, rows)
+    main, north, south = slice(1, height + 1), slice(height + 1, height + 3), slice(0, 1)
     for part in range(4):
         for layer in range(depth):
             own_ref[part, layer] = force(part, layer + 1, main)
@@ -660,16 +685,17 @@
     slots = len(rim_sizes(levels))
     to_levels, north_levels, south_levels = (rest[slots * at : slots * at + slots] for at in range(3))
     rest = rest[3 * slots :]
-    vel_ref, spread_ref, state_ref, outbox, strip, taken = rest[:6]
+    vel_ref, beyond_ref, spread_ref, outer_ref, state_ref, outbox, strip, taken = rest[:8]
     edge_body(
-        levels, level_ref, strip_ref, left_ref, right_ref, inner_pops, inner_vel, pops_ref, vel_ref, *rest[6:9]
+        levels, level_ref, strip_ref, left_ref, right_ref, inner_pops, inner_vel,
+        pops_ref, vel_ref, beyond_ref, *rest[8:11],
     )
     droplet_body(
-        pops_ref.shape[1:], counts_ref, dest_ref, vel_ref, speed_ref, frac_ref, home_ref,
-        spread_ref, stay_ref, state_ref, *rest[9:],
+        pops_ref.shape[1:], counts_ref, dest_ref, vel_ref, beyond_ref, speed_ref, frac_ref, home_ref,
+        spread_ref, outer_ref, stay_ref, state_ref, *rest[11:],
     )
     pack_body(
-        levels, level_ref, dest_ref, spread_ref, state_ref, own_ref, side_ref,
+        levels, level_ref, dest_ref, spread_ref, outer_ref, state_ref, own_ref, side_ref,
         to_levels, north_ref, south_ref, north_levels, south_levels, outbox, strip, taken,
     )
 
@@ -793,8 +819,8 @@
     kinds = ["up", "down"][: len(rim_sizes(levels))]
     slots = len(kinds)
     given = wide_exchange(level, pops, coarse_pops, interface)
-    layers, rows, lanes = depth + 3, height + 8, width + 128
-    flat = 3 * layers * rows
+    rows = height + 8
+    table = table_rows(depth, height)
     sizes = [(count + GROUP, width) for count in message_rows(depth)]
     outs = call(
         functools.partial(main_body, levels),
@@ -805,22 +831,23 @@
         [level, counts, dest] + given + [drop_vel, drop_frac, home],
         3,
         [
-            pltpu.VMEM((3, layers, rows, lanes), jnp.float32),
-            pltpu.VMEM((3, layers, rows, lanes), jnp.float32),
+            pltpu.VMEM((3 * table, width), jnp.float32),
+            pltpu.VMEM((3 * table, 128), jnp.float32),
+            pltpu.VMEM((3 * table, width), jnp.float32),
+            pltpu.VMEM((3 * table, 128), jnp.float32),
             pltpu.VMEM((blocks, 8, 128), jnp.float32),
             pltpu.VMEM((27 * CAP, 8, 128), jnp.float32),
-            pltpu.VMEM((layers, rows, 128), jnp.float32),
+            pltpu.VMEM((table, 128), jnp.float32),
             pltpu.SMEM((27,), jnp.int32),
             pltpu.VMEM((2, channels, rows, 128), jnp.float32),
             pltpu.VMEM((2, 19, rows, 128), jnp.float32),
             pltpu.VMEM((2, 19, rows, 128), jnp.float32),
-            pltpu.VMEM((flat, lanes), jnp.bfloat16),
-            pltpu.VMEM((flat, lanes), jnp.bfloat16),
-            pltpu.VMEM((lanes, 256), jnp.bfloat16),
-            pltpu.VMEM((lanes, 256), jnp.bfloat16),
-            pltpu.VMEM((flat, 256), jnp.bfloat16),
-            pltpu.VMEM((flat, 256), jnp.bfloat16),
-            pltpu.VMEM((layers, rows, 256), jnp.float32),
+            pltpu.VMEM((3 * table, 2 * width), jnp.bfloat16),
+            pltpu.VMEM((3 * table, width + 128), jnp.bfloat16),
+            pltpu.VMEM((2 * width + 128, blocks * 128), jnp.bfloat16),
+            pltpu.VMEM((3 * table, blocks * 128), jnp.bfloat16),
+            pltpu.VMEM((3 * table, blocks * 128), jnp.bfloat16),
+            pltpu.VMEM((2, table, 256), jnp.float32),
         ],
     )
     state, own, stay, side, north, south = outs[:6]

time: 68 us -> 63.2 us (0.929)
  Pallas kernels: 28.3 us -> 23.5 us
    pallas_call x6, Pallas kernels: 28.3 us -> 23.5 us  [call(): pl.pallas_call(body, out_shape=[jax.ShapeDtypeStruct(shape, jnp.float32)...]
  transfers between devices with their start and end apart: 14 -> 14, of which waited for: 5 -> 5; matrix products, arithmetic and copies ran while one was open for 0% -> 0% of each run, Pallas kernels for 8% -> 9%
where the time goes in v5:
time: 63.2 us; the launch traced here: 62.9 us
  Pallas kernels  23.5 us (37%)
  starting transfers between devices  18.9 us (30%)
  waiting for transfers between devices  17 us (27%)
  local copies, waits for them, and re-layouts  2.76 us (4%)
  between operations  0.75 us (1%)
    pallas_call x6, Pallas kernels, call(): pl.pallas_call(body, out_shape=[jax.ShapeDtypeStruct(shape, jnp.float32)...  23.5 us
    ppermute x8, starting transfers between devices, shifted(): lax.ppermute(value, axis, [(i, (i + step) % count) for i in range(count)])  11.5 us
    ppermute x4, waiting for transfers between devices, to_level(): lax.ppermute(value, (side, 'gz'), [(brick * levels + at, (brick + step) %...  8.97 us
    ppermute x8, waiting for transfers between devices, shifted(): lax.ppermute(value, axis, [(i, (i + step) % count) for i in range(count)])  8.02 us
    ppermute x4, starting transfers between devices, to_level(): lax.ppermute(value, (side, 'gz'), [(brick * levels + at, (brick + step) %...  4.39 us
    ppermute x2, starting transfers between devices, to_level(): return lax.ppermute(value, 'gz', pairs)  3.08 us
    unnamed x28, local copies, waits for them, and re-layouts  2.76 us
  transfers between devices with their start and end apart: 14, of which 5 were waited for; matrix products, arithmetic and copies ran while one was open for 0% of the time, Pallas kernels for 9%

profile of v5, /device:TPU:0, one launch (start us, length us, event | category | flops | bytes accessed | tf_op | source)
XLA Modules:
  0.0 62.9 jit_solution(15461110657324151543)
XLA Ops:
  0.6 2.6 %shard_map.103 = (f32[20,8,8,128]{3,2,1,0:T(8,128)}, f32[488,128]{1,0:T(8,128)}, f32[328,128]{1,0:T(8,128)}, f32[60,8,128]{2,1,0:T(8,128)}, f32[184,128]{1,0:T(8,128)}, /*index=5*/f32[120,128]{1,0:T(8,128)}) custom-call(s32[1]{0:T(128)} %bitcast.level_ref, f32[19,8,8,128]{3,2,1,0:T(8,128)} %pops_ref.1, bf16[19,8,8,128]{3,2,1,0:T(8,128)(2,1)} %coarse_ref.1, ...), custom_call_target="tpu_custom_call" | custom-call | tf_op jit(solution)/shard_map/pallas_call | solution.py:47
  3.2 2.4 %collective-permute-start = (f32[488,128]{1,0:T(8,128)}, f32[488,128]{1,0:T(8,128)S(1)}, u32[]{:S(2)}, u32[]{:S(2)}) collective-permute-start(f32[488,128]{1,0:T(8,128)} %get-tuple-element.26), channel_id=1, source_target_pairs={{0,6},{2,0},{4,2},{6,4},{1,7},{3,1},{5,3},{7,5},{8,14},{10,8},{12,... | collective-permute-start | bytes 749576 | tf_op jit(solution)/shard_map/ppermute | solution.py:413
  5.6 1.5 %collective-permute-start.2 = (f32[60,8,128]{2,1,0:T(8,128)}, f32[60,8,128]{2,1,0:T(8,128)S(1)}, u32[]{:S(2)}, u32[]{:S(2)}) collective-permute-start(f32[60,8,128]{2,1,0:T(8,128)} %get-tuple-element.28), channel_id=1, source_target_pairs={{0,1},{1,0},{2,3},{3,2},{4,5},{5,4},{6,7},{7,6},{8,9},{9,8},{10,11... | collective-permute-start | bytes 737288 | tf_op jit(solution)/shard_map/ppermute | solution.py:423
  7.1 1.7 %collective-permute-start.3 = (f32[184,128]{1,0:T(8,128)}, f32[184,128]{1,0:T(8,128)S(1)}, u32[]{:S(2)}, u32[]{:S(2)}) collective-permute-start(f32[184,128]{1,0:T(8,128)} %get-tuple-element.29), channel_id=1, source_target_pairs={{0,7},{1,6},{2,1},{3,0},{4,3},{5,2},{6,5},{7,4},{8,15},{9,14},{10,... | collective-permute-start | bytes 282632 | tf_op jit(solution)/shard_map/ppermute | solution.py:425
  8.9 6.9 %collective-permute-done.4.rest_5_ = f32[120,128]{1,0:T(8,128)S(1)} collective-permute-done((f32[120,128]{1,0:T(8,128)}, f32[120,128]{1,0:T(8,128)S(1)}, u32[]{:S(2)}, u32[]{:S(2)}) %collective-permute-start.4) | collective-permute-done | bytes 61472 | tf_op jit(solution)/shard_map/ppermute | solution.py:425
  15.8 0.5 copy-done.4
  16.6 4.2 %shard_map.104.strip_ref = f32[20,16,128]{2,1,0:T(8,128)} custom-call(s32[1]{0:T(128)} %bitcast.level_ref, f32[20,8,8,128]{3,2,1,0:T(8,128)} %get-tuple-element.25.rest_0_, f32[488,128]{1,0:T(8,128)} %copy-done, f32[328,128]{1,0:T(8,128)} %copy-done.2, f32[60,8,128]{2,1,0:T(8,128)} %copy-done.1, f32[184,128]{1,0:T(8,128)} %copy-done.3, f32[120,128]{1,0:T(8,128)} %copy-done.4), custom_call_target="tpu_custom_call" | custom-call | tf_op jit(solution)/shard_map/pallas_call | solution.py:47
  20.9 1.7 %collective-permute-start.5 = (f32[20,16,128]{2,1,0:T(8,128)}, f32[20,16,128]{2,1,0:T(8,128)S(1)}, u32[]{:S(2)}, u32[]{:S(2)}) collective-permute-start(f32[20,16,128]{2,1,0:T(8,128)} %shard_map.104.strip_ref), channel_id=1, source_target_pairs={{0,8},{8,16},{16,24},{24,0},{1,9},{9,17},{17,25},{25,1},{2,10},{10... | collective-permute-start | bytes 491528 | tf_op jit(solution)/shard_map/ppermute | solution.py:413
  22.5 2.2 %collective-permute-start.6 = (f32[20,16,128]{2,1,0:T(8,128)}, f32[20,16,128]{2,1,0:T(8,128)S(1)}, u32[]{:S(2)}, u32[]{:S(2)}) collective-permute-start(f32[20,16,128]{2,1,0:T(8,128)} %shard_map.104.strip_ref), channel_id=1, source_target_pairs={{0,24},{8,0},{16,8},{24,16},{1,25},{9,1},{17,9},{25,17},{2,26},{10... | collective-permute-start | bytes 491528 | tf_op jit(solution)/shard_map/ppermute | solution.py:413
  24.7 5.4 %shard_map.105 = (f32[19,8,8,128]{3,2,1,0:T(8,128)}, f32[3,11,16,128]{3,2,1,0:T(8,128)}) custom-call(s32[1]{0:T(128)} %bitcast.level_ref, f32[20,8,8,128]{3,2,1,0:T(8,128)} %get-tuple-element.25.rest_0_, f32[488,128]{1,0:T(8,128)} %copy-done, f32[328,128]{1,0:T(8,128)} %copy-done.2, f32[60,8,128]{2,1,0:T(8,128)} %copy-done.1, f32[184,128]{1,0:T(8,128)} %copy-done.3, ...), custom_call_target="tpu_custom_call" | custom-call | flops 100000000 | bytes 4194304 | tf_op jit(solution)/shard_map/pallas_call | solution.py:47
  30.1 2.6 %collective-permute-done.6.right_ref = f32[20,16,128]{2,1,0:T(8,128)S(1)} collective-permute-done((f32[20,16,128]{2,1,0:T(8,128)}, f32[20,16,128]{2,1,0:T(8,128)S(1)}, u32[]{:S(2)}, u32[]{:S(2)}) %collective-permute-start.6) | collective-permute-done | bytes 163872 | tf_op jit(solution)/shard_map/ppermute | solution.py:413
  32.7 0.7 %copy-done.8 = f32[20,16,128]{2,1,0:T(8,128)} copy-done((f32[20,16,128]{2,1,0:T(8,128)}, f32[20,16,128]{2,1,0:T(8,128)S(1)}, u32[]{:S(2)}) %copy-start.8) | copy-done | bytes 163864
  33.3 7.4 %shard_map.106 = (f32[19,8,8,128]{3,2,1,0:T(8,128)}, f32[4,8,8,128]{3,2,1,0:T(8,128)}, f32[6,16,128]{2,1,0:T(8,128)}, f32[4,8,128]{2,1,0:T(8,128)}, f32[112,128]...) custom-call(s32[1]{0:T(128)} %bitcast.level_ref, ...), custom_call_target="tpu_custom_call" | custom-call | tf_op jit(solution)/shard_map/pallas_call | solution.py:47
  40.7 1.6 %collective-permute-start.9 = (f32[112,128]{1,0:T(8,128)}, f32[112,128]{1,0:T(8,128)S(1)}, u32[]{:S(2)}, u32[]{:S(2)}) collective-permute-start(f32[112,128]{1,0:T(8,128)} %get-tuple-element.38), channel_id=1, source_target_pairs={{0,1},{1,0},{2,3},{3,2},{4,5},{5,4},{6,7},{7,6},{8,9},{9,8},{10,11... | collective-permute-start | bytes 172040 | tf_op jit(solution)/shard_map/ppermute | solution.py:423
  42.3 1.4 %collective-permute-start.8 = (f32[80,128]{1,0:T(8,128)}, f32[80,128]{1,0:T(8,128)S(1)}, u32[]{:S(2)}, u32[]{:S(2)}) collective-permute-start(f32[80,128]{1,0:T(8,128)} %get-tuple-element.37), channel_id=1, source_target_pairs={{0,6},{2,0},{4,2},{6,4},{1,7},{3,1},{5,3},{7,5},{8,14},{10,8},{12,... | collective-permute-start | bytes 122888 | tf_op jit(solution)/shard_map/ppermute | solution.py:413
  43.9 2.4 %collective-permute-start.11 = (f32[56,128]{1,0:T(8,128)}, f32[56,128]{1,0:T(8,128)S(1)}, u32[]{:S(2)}, u32[]{:S(2)}) collective-permute-start(f32[56,128]{1,0:T(8,128)} %get-tuple-element.40), channel_id=1, source_target_pairs={{0,7},{1,6},{2,1},{3,0},{4,3},{5,2},{6,5},{7,4},{8,15},{9,14},{10,... | collective-permute-start | bytes 86024 | tf_op jit(solution)/shard_map/ppermute | solution.py:425
  46.3 2.1 %collective-permute-done.11.rest_4_ = f32[56,128]{1,0:T(8,128)S(1)} collective-permute-done((f32[56,128]{1,0:T(8,128)}, f32[56,128]{1,0:T(8,128)S(1)}, u32[]{:S(2)}, u32[]{:S(2)}) %collective-permute-start.11) | collective-permute-done | bytes 28704 | tf_op jit(solution)/shard_map/ppermute | solution.py:425
  49.1 1.7 %shard_map.107 = (f32[3,8,8,128]{3,2,1,0:T(8,128)}, f32[208,128]{1,0:T(8,128)}, f32[208,128]{1,0:T(8,128)}) custom-call(s32[1]{0:T(128)} %bitcast.level_ref, f32[4,8,8,128]{3,2,1,0:T(8,128)} %get-tuple-element.34.own_ref, f32[4,8,128]{2,1,0:T(8,128)} %get-tuple-element.35.side_ref, f32[112,128]{1,0:T(8,128)} %copy-done.5, f32[80,128]{1,0:T(8,128)} %copy-done.9, ...), custom_call_target="tpu_custom_call" | custom-call | tf_op jit(solution)/shard_map/pallas_call | solution.py:47
  50.9 1.1 %collective-permute-start.12 = (f32[208,128]{1,0:T(8,128)}, f32[208,128]{1,0:T(8,128)S(1)}, u32[]{:S(2)}, u32[]{:S(2)}) collective-permute-start(f32[208,128]{1,0:T(8,128)} %get-tuple-element.43), channel_id=1, source_target_pairs={{0,8},{8,16},{16,24},{24,0},{1,9},{9,17},{17,25},{25,1},{2,10},{10... | collective-permute-start | bytes 319496 | tf_op jit(solution)/shard_map/ppermute | solution.py:413
  52.0 2.7 %collective-permute-start.13 = (f32[208,128]{1,0:T(8,128)}, f32[208,128]{1,0:T(8,128)S(1)}, u32[]{:S(2)}, u32[]{:S(2)}) collective-permute-start(f32[208,128]{1,0:T(8,128)} %get-tuple-element.44), channel_id=1, source_target_pairs={{0,24},{8,0},{16,8},{24,16},{1,25},{9,1},{17,9},{25,17},{2,26},{10... | collective-permute-start | bytes 319496 | tf_op jit(solution)/shard_map/ppermute | solution.py:413
  54.7 3.8 %collective-permute-done.12.rest_5_ = f32[208,128]{1,0:T(8,128)S(1)} collective-permute-done((f32[208,128]{1,0:T(8,128)}, f32[208,128]{1,0:T(8,128)S(1)}, u32[]{:S(2)}, u32[]{:S(2)}) %collective-permute-start.12) | collective-permute-done | bytes 106528 | tf_op jit(solution)/shard_map/ppermute | solution.py:413
  58.5 1.7 %collective-permute-done.13.rest_6_ = f32[208,128]{1,0:T(8,128)S(1)} collective-permute-done((f32[208,128]{1,0:T(8,128)}, f32[208,128]{1,0:T(8,128)S(1)}, u32[]{:S(2)}, u32[]{:S(2)}) %collective-permute-start.13) | collective-permute-done | bytes 106528 | tf_op jit(solution)/shard_map/ppermute | solution.py:413
  60.2 0.6 %copy-done.13 = f32[208,128]{1,0:T(8,128)} copy-done((f32[208,128]{1,0:T(8,128)}, f32[208,128]{1,0:T(8,128)S(1)}, u32[]{:S(2)}) %copy-start.13) | copy-done | bytes 106520
  60.8 2.1 %shard_map.108 = (f32[3,8,8,128]{3,2,1,0:T(8,128)}, f32[6,68,128]{2,1,0:T(8,128)}) custom-call(s32[1]{0:T(128)} %bitcast.level_ref, f32[3,8,8,128]{3,2,1,0:T(8,128)} %get-tuple-element.41.part_ref, f32[6,16,128]{2,1,0:T(8,128)} %get-tuple-element.42.stay_ref, f32[112,128]{1,0:T(8,128)} %copy-done.5, f32[80,128]{1,0:T(8,128)} %copy-done.9, ...), custom_call_target="tpu_custom_call" | custom-call | tf_op jit(solution)/shard_map/pallas_call | solution.py:47
  (38 shorter events, 1.3 us)
Async XLA Ops:
  3.2 12.6 %collective-permute-start = (f32[488,128]{1,0:T(8,128)}, f32[488,128]{1,0:T(8,128)S(1)}, u32[]{:S(2)}, u32[]{:S(2)}) collective-permute-start(f32[488,128]{1,0:T(8,128)} %get-tuple-element.26), channel_id=1, source_target_pairs={{0,6},{2,0},{4,2},{6,4},{1,7},{3,1},{5,3},{7,5},{8,14},{10,8},{12,... | collective-permute-start | bytes 749576 | tf_op jit(solution)/shard_map/ppermute | solution.py:413
  5.6 10.2 %collective-permute-start.2 = (f32[60,8,128]{2,1,0:T(8,128)}, f32[60,8,128]{2,1,0:T(8,128)S(1)}, u32[]{:S(2)}, u32[]{:S(2)}) collective-permute-start(f32[60,8,128]{2,1,0:T(8,128)} %get-tuple-element.28), channel_id=1, source_target_pairs={{0,1},{1,0},{2,3},{3,2},{4,5},{5,4},{6,7},{7,6},{8,9},{9,8},{10,11... | collective-permute-start | bytes 737288 | tf_op jit(solution)/shard_map/ppermute | solution.py:423
  7.1 8.6 %collective-permute-start.1 = (f32[328,128]{1,0:T(8,128)}, f32[328,128]{1,0:T(8,128)S(1)}, u32[]{:S(2)}, u32[]{:S(2)}) collective-permute-start(f32[328,128]{1,0:T(8,128)} %get-tuple-element.27), channel_id=1, source_target_pairs={{0,2},{2,4},{4,6},{6,0},{1,3},{3,5},{5,7},{7,1},{8,10},{10,12},{12... | collective-permute-start | bytes 503816 | tf_op jit(solution)/shard_map/ppermute | solution.py:413
  7.1 8.6 %collective-permute-start.3 = (f32[184,128]{1,0:T(8,128)}, f32[184,128]{1,0:T(8,128)S(1)}, u32[]{:S(2)}, u32[]{:S(2)}) collective-permute-start(f32[184,128]{1,0:T(8,128)} %get-tuple-element.29), channel_id=1, source_target_pairs={{0,7},{1,6},{2,1},{3,0},{4,3},{5,2},{6,5},{7,4},{8,15},{9,14},{10,... | collective-permute-start | bytes 282632 | tf_op jit(solution)/shard_map/ppermute | solution.py:425
  8.8 6.9 %collective-permute-start.4 = (f32[120,128]{1,0:T(8,128)}, f32[120,128]{1,0:T(8,128)S(1)}, u32[]{:S(2)}, u32[]{:S(2)}) collective-permute-start(f32[120,128]{1,0:T(8,128)} %get-tuple-element.30), channel_id=1, source_target_pairs={{0,3},{1,2},{2,5},{3,4},{4,7},{5,6},{6,1},{7,0},{8,11},{9,10},{10,... | collective-permute-start | bytes 184328 | tf_op jit(solution)/shard_map/ppermute | solution.py:425
  15.8 0.7 %copy-start.3 = (f32[184,128]{1,0:T(8,128)}, f32[184,128]{1,0:T(8,128)S(1)}, u32[]{:S(2)}) copy-start(f32[184,128]{1,0:T(8,128)S(1)} %collective-permute-done.3.rest_4_) | copy-start | bytes 282628
  15.8 0.7 %copy-start.2 = (f32[328,128]{1,0:T(8,128)}, f32[328,128]{1,0:T(8,128)S(1)}, u32[]{:S(2)}) copy-start(f32[328,128]{1,0:T(8,128)S(1)} %collective-permute-done.1.rest_2_) | copy-start | bytes 503812
  15.8 0.8 %copy-start.1 = (f32[60,8,128]{2,1,0:T(8,128)}, f32[60,8,128]{2,1,0:T(8,128)S(1)}, u32[]{:S(2)}) copy-start(f32[60,8,128]{2,1,0:T(8,128)S(1)} %collective-permute-done.2.rest_3_) | copy-start | bytes 737284
  15.8 0.8 %copy-start = (f32[488,128]{1,0:T(8,128)}, f32[488,128]{1,0:T(8,128)S(1)}, u32[]{:S(2)}) copy-start(f32[488,128]{1,0:T(8,128)S(1)} %collective-permute-done.rest_1_) | copy-start | bytes 749572
  20.9 9.2 %collective-permute-start.5 = (f32[20,16,128]{2,1,0:T(8,128)}, f32[20,16,128]{2,1,0:T(8,128)S(1)}, u32[]{:S(2)}, u32[]{:S(2)}) collective-permute-start(f32[20,16,128]{2,1,0:T(8,128)} %shard_map.104.strip_ref), channel_id=1, source_target_pairs={{0,8},{8,16},{16,24},{24,0},{1,9},{9,17},{17,25},{25,1},{2,10},{10... | collective-permute-start | bytes 491528 | tf_op jit(solution)/shard_map/ppermute | solution.py:413
  22.5 10.1 %collective-permute-start.6 = (f32[20,16,128]{2,1,0:T(8,128)}, f32[20,16,128]{2,1,0:T(8,128)S(1)}, u32[]{:S(2)}, u32[]{:S(2)}) collective-permute-start(f32[20,16,128]{2,1,0:T(8,128)} %shard_map.104.strip_ref), channel_id=1, source_target_pairs={{0,24},{8,0},{16,8},{24,16},{1,25},{9,1},{17,9},{25,17},{2,26},{10... | collective-permute-start | bytes 491528 | tf_op jit(solution)/shard_map/ppermute | solution.py:413
  30.1 2.6 %copy-start.7 = (f32[20,16,128]{2,1,0:T(8,128)}, f32[20,16,128]{2,1,0:T(8,128)S(1)}, u32[]{:S(2)}) copy-start(f32[20,16,128]{2,1,0:T(8,128)S(1)} %collective-permute-done.5.left_ref) | copy-start | bytes 491524
  32.7 0.7 %copy-start.8 = (f32[20,16,128]{2,1,0:T(8,128)}, f32[20,16,128]{2,1,0:T(8,128)S(1)}, u32[]{:S(2)}) copy-start(f32[20,16,128]{2,1,0:T(8,128)S(1)} %collective-permute-done.6.right_ref) | copy-start | bytes 491524
  40.7 7.8 %collective-permute-start.7 = (f32[112,128]{1,0:T(8,128)}, f32[112,128]{1,0:T(8,128)S(1)}, u32[]{:S(2)}, u32[]{:S(2)}) collective-permute-start(f32[112,128]{1,0:T(8,128)} %get-tuple-element.36), channel_id=1, source_target_pairs={{0,2},{2,4},{4,6},{6,0},{1,3},{3,5},{5,7},{7,1},{8,10},{10,12},{12... | collective-permute-start | bytes 172040 | tf_op jit(solution)/shard_map/ppermute | solution.py:413
  40.7 7.8 %collective-permute-start.9 = (f32[112,128]{1,0:T(8,128)}, f32[112,128]{1,0:T(8,128)S(1)}, u32[]{:S(2)}, u32[]{:S(2)}) collective-permute-start(f32[112,128]{1,0:T(8,128)} %get-tuple-element.38), channel_id=1, source_target_pairs={{0,1},{1,0},{2,3},{3,2},{4,5},{5,4},{6,7},{7,6},{8,9},{9,8},{10,11... | collective-permute-start | bytes 172040 | tf_op jit(solution)/shard_map/ppermute | solution.py:423
  42.3 6.2 %collective-permute-start.8 = (f32[80,128]{1,0:T(8,128)}, f32[80,128]{1,0:T(8,128)S(1)}, u32[]{:S(2)}, u32[]{:S(2)}) collective-permute-start(f32[80,128]{1,0:T(8,128)} %get-tuple-element.37), channel_id=1, source_target_pairs={{0,6},{2,0},{4,2},{6,4},{1,7},{3,1},{5,3},{7,5},{8,14},{10,8},{12,... | collective-permute-start | bytes 122888 | tf_op jit(solution)/shard_map/ppermute | solution.py:413
  43.7 4.8 %collective-permute-start.10 = (f32[64,128]{1,0:T(8,128)}, f32[64,128]{1,0:T(8,128)S(1)}, u32[]{:S(2)}, u32[]{:S(2)}) collective-permute-start(f32[64,128]{1,0:T(8,128)} %get-tuple-element.39), channel_id=1, source_target_pairs={{0,3},{1,2},{2,5},{3,4},{4,7},{5,6},{6,1},{7,0},{8,11},{9,10},{10,... | collective-permute-start | bytes 98312 | tf_op jit(solution)/shard_map/ppermute | solution.py:425
  43.9 4.5 %collective-permute-start.11 = (f32[56,128]{1,0:T(8,128)}, f32[56,128]{1,0:T(8,128)S(1)}, u32[]{:S(2)}, u32[]{:S(2)}) collective-permute-start(f32[56,128]{1,0:T(8,128)} %get-tuple-element.40), channel_id=1, source_target_pairs={{0,7},{1,6},{2,1},{3,0},{4,3},{5,2},{6,5},{7,4},{8,15},{9,14},{10,... | collective-permute-start | bytes 86024 | tf_op jit(solution)/shard_map/ppermute | solution.py:425
  48.5 0.6 %copy-start.9 = (f32[80,128]{1,0:T(8,128)}, f32[80,128]{1,0:T(8,128)S(1)}, u32[]{:S(2)}) copy-start(f32[80,128]{1,0:T(8,128)S(1)} %collective-permute-done.8.rest_1_) | copy-start | bytes 122884
  48.5 0.6 %copy-start.6 = (f32[112,128]{1,0:T(8,128)}, f32[112,128]{1,0:T(8,128)S(1)}, u32[]{:S(2)}) copy-start(f32[112,128]{1,0:T(8,128)S(1)} %collective-permute-done.9.rest_2_) | copy-start | bytes 172036
  50.9 7.6 %collective-permute-start.12 = (f32[208,128]{1,0:T(8,128)}, f32[208,128]{1,0:T(8,128)S(1)}, u32[]{:S(2)}, u32[]{:S(2)}) collective-permute-start(f32[208,128]{1,0:T(8,128)} %get-tuple-element.43), channel_id=1, source_target_pairs={{0,8},{8,16},{16,24},{24,0},{1,9},{9,17},{17,25},{25,1},{2,10},{10... | collective-permute-start | bytes 319496 | tf_op jit(solution)/shard_map/ppermute | solution.py:413
  52.0 8.2 %collective-permute-start.13 = (f32[208,128]{1,0:T(8,128)}, f32[208,128]{1,0:T(8,128)S(1)}, u32[]{:S(2)}, u32[]{:S(2)}) collective-permute-start(f32[208,128]{1,0:T(8,128)} %get-tuple-element.44), channel_id=1, source_target_pairs={{0,24},{8,0},{16,8},{24,16},{1,25},{9,1},{17,9},{25,17},{2,26},{10... | collective-permute-start | bytes 319496 | tf_op jit(solution)/shard_map/ppermute | solution.py:413
  58.5 1.7 %copy-start.12 = (f32[208,128]{1,0:T(8,128)}, f32[208,128]{1,0:T(8,128)S(1)}, u32[]{:S(2)}) copy-start(f32[208,128]{1,0:T(8,128)S(1)} %collective-permute-done.12.rest_5_) | copy-start | bytes 319492
  60.2 0.6 %copy-start.13 = (f32[208,128]{1,0:T(8,128)}, f32[208,128]{1,0:T(8,128)S(1)}, u32[]{:S(2)}) copy-start(f32[208,128]{1,0:T(8,128)S(1)} %collective-permute-done.13.rest_6_) | copy-start | bytes 319492
  (4 other events, 2.5 us)

commit v6 on v5

--- a/solution.py
+++ b/solution.py
@@ -42,16 +42,40 @@
 couple = 8.0
 
 
-def call(body, outs, ins, scalars=1, scratch=(), cost=None):
+def call(body, outs, ins, scalars=1, scratch=(), cost=None, heads=()):
+    heads = dict(heads)
+    arrays = ins[scalars:]
+    landing = []
+    for at, value in enumerate(arrays):
+        count = heads.get(at, value.shape[0])
+        landing.append(pltpu.VMEM((count,) + value.shape[1:], value.dtype))
+
+    def whole(*refs):
+        given = refs[scalars : len(ins)]
+        made = refs[len(ins) : len(ins) + len(outs)]
+        rest = refs[len(ins) + len(outs) :]
+        landed, done, rest = rest[: len(arrays)], rest[len(arrays)], rest[len(arrays) + 1 :]
+        copies = []
+        for at, (source, target) in enumerate(zip(given, landed)):
+            if at in heads:
+                source = source.at[pl.ds(0, heads[at])]
+            copies.append(pltpu.make_async_copy(source, target, done.at[at]))
+        for copy in copies:
+            copy.start()
+        for copy in copies:
+            copy.wait()
+        body(*refs[:scalars], *landed, *made, *rest)
+
     vmem = pl.BlockSpec(memory_space=pltpu.VMEM)
+    hbm = pl.BlockSpec(memory_space=pltpu.HBM)
     return pl.pallas_call(
-        body,
+        whole,
         out_shape=[jax.ShapeDtypeStruct(shape, jnp.float32) for shape in outs],
-        in_specs=[pl.BlockSpec(memory_space=pltpu.SMEM)] * scalars + [vmem] * (len(ins) - scalars),
+        in_specs=[pl.BlockSpec(memory_space=pltpu.SMEM)] * scalars + [hbm] * len(arrays),
         out_specs=[vmem] * len(outs),
-        scratch_shapes=list(scratch),
+        scratch_shapes=landing + [pltpu.SemaphoreType.DMA((len(arrays),))] + list(scratch),
         cost_estimate=cost,
-        compiler_params=pltpu.CompilerParams(vmem_limit_bytes=56 * 1024 * 1024),
+        compiler_params=pltpu.CompilerParams(vmem_limit_bytes=64 * 1024 * 1024),
     )(*ins)
 
 
@@ -90,7 +114,7 @@
 
 
 def rim_sizes(levels):
-    sizes = [len(rim(kind)) for kind, _, _, _ in rim_sides(levels)]
+    sizes = [FOUR + len(rim(kind)) for kind, _, _, _ in rim_sides(levels)]
     return [max(sizes)] if levels == 2 else sizes
 
 
@@ -101,32 +125,71 @@
         pl.when(level == guard)(action)
 
 
-def row_places(cells):
-    places, high_at, low_at = [], 0, 0
-    for channel, bounces in cells:
-        way_z, way, _ = ways[channel]
-        above, below = high_reach(way), low_reach(way)
-        if bounces and way_z != 0:
-            above, below = max(above, HIGH - 1), max(below, LOW - 1)
+def padded(count):
+    return -(-count // 8) * 8
+
+
+def reaches(channel, bounces):
+    way_z, way, _ = ways[channel]
+    above, below = high_reach(way), low_reach(way)
+    if bounces and way_z != 0:
+        above, below = max(above, HIGH - 1), max(below, LOW - 1)
+    return above, below
+
+
+def row_places(cells, start=(0, 0)):
+    places, (high_at, low_at) = [], start
+    for above, below in cells:
         places.append((high_at, low_at, above, below))
         high_at, low_at = high_at + above, low_at + below
-    return places, (-(-high_at // 8) * 8, -(-low_at // 8) * 8)
+    return places, (padded(high_at), padded(low_at))
+
+
+def strip_rows():
+    return row_places([reaches(channel, True) for channel in range(channels)])
 
 
 def own_rows(depth):
     cells = [(layer, channel) for layer in range(depth) for channel in range(channels)]
-    places, sizes = row_places([(channel, layer in (0, depth - 1)) for layer, channel in cells])
+    places, sizes = row_places(
+        [reaches(channel, layer in (0, depth - 1)) for layer, channel in cells], strip_rows()[1]
+    )
     return [(layer, channel, place) for (layer, channel), place in zip(cells, places)], sizes
 
 
+FOUR = -(-channels // 4)
+
+
+def rim_strip_rows():
+    return row_places([(HIGH, LOW)] * FOUR)
+
+
 def rim_rows(kind):
-    places, sizes = row_places([(channel, False) for _, channel in rim(kind)])
+    places, sizes = row_places([reaches(channel, False) for _, channel in rim(kind)], rim_strip_rows()[1])
     return [(step, channel, place) for (step, channel), place in zip(rim(kind), places)], sizes
 
 
 def rim_row_sizes(levels):
     sizes = [rim_rows(kind)[1] for kind, _, _, _ in rim_sides(levels)]
     return [tuple(max(part) for part in zip(*sizes))] if levels == 2 else sizes
+
+
+def face_table(high):
+    wants = []
+    for channel in range(channels):
+        way_z, _, way = ways[channel]
+        count = high_reach(way) if high else low_reach(way)
+        if way_z != 0:
+            count = max(count, (HIGH if high else LOW) - 1)
+        wants.append((-count, channel))
+    free, table = [], []
+    for count, channel in sorted(wants):
+        tile = next((at for at, room in enumerate(free) if room >= -count), len(free))
+        if tile == len(free):
+            free.append(8)
+        table.append((channel, tile, 8 - free[tile], -count))
+        free[tile] += count
+    return table, len(free)
 
 
 def moments(cells):
@@ -184,10 +247,20 @@
     return value if shift == 0 else pltpu.roll(value, shift, value.ndim - 1)
 
 
-def first_body(levels, level_ref, pops_ref, coarse_ref, interface_ref, posts_ref, down_ref, up_ref, *outs):
+def first_body(
+    levels, level_ref, pops_ref, coarse_ref, interface_ref, posts_ref, strip_ref, down_ref, up_ref, *outs
+):
     depth, height, width = interface_ref.shape
     slots = len(rim_sizes(levels))
     rims, down_rims, up_rims = (outs[slots * at : slots * at + slots] for at in range(3))
+    lane = lax.broadcasted_iota(jnp.int32, (height, 128), 1)
+
+    def put_rows(down, up, place, cells):
+        down_at, up_at, down_rows, up_rows = place
+        cols = slice(0, cells.shape[1])
+        down[down_at : down_at + down_rows, cols] = cells[:down_rows, :]
+        up[up_at : up_at + up_rows, cols] = cells[height - up_rows :, :]
+
     own = own_rows(depth)[0]
     for layer in range(depth):
         mask = interface_ref[layer]
@@ -199,18 +272,31 @@
         ] + [mask.astype(jnp.float32)]
         for channel in range(channels):
             posts_ref[channel, layer] = posts[channel]
-            down_at, up_at, down, up = own[layer * channels + channel][2]
-            down_ref[down_at : down_at + down, :] = posts[channel][:down, :]
-            up_ref[up_at : up_at + up, :] = posts[channel][height - up :, :]
+            put_rows(down_ref, up_ref, own[layer * channels + channel][2], posts[channel])
+    for channel in range(channels):
+        value = jnp.zeros((height, 128), jnp.float32)
+        for layer in range(depth):
+            cells = posts_ref[channel, layer]
+            if width > 128:
+                cells = jnp.where(lane < 64, cells[:, :128], cells[:, width - 128 :])
+            value = jnp.where(lane // 8 == LOW + layer, lane_roll(cells, 8 * (LOW + layer) + 4), value)
+        strip_ref[channel] = value
+        put_rows(down_ref, up_ref, strip_rows()[0][channel], value)
     for kind, _, sender, slot in rim_sides(levels):
 
         def pack(kind=kind, slot=slot):
+            for tile in range(FOUR):
+                value = jnp.zeros((height, 128), jnp.float32)
+                for part in range(min(4, channels - 4 * tile)):
+                    first = LOW + depth - 4 if kind == "low" else LOW
+                    turned = lane_roll(strip_ref[4 * tile + part], 32 * part - 8 * first)
+                    value = jnp.where(lane // 32 == part, turned, value)
+                rims[slot][tile, :, 0:128] = value
+                put_rows(down_rims[slot], up_rims[slot], rim_strip_rows()[0][tile], value)
             for at, (step, channel, place) in enumerate(rim_rows(kind)[0]):
                 cells = posts_ref[channel, depth - step if kind == "low" else step - 1]
-                rims[slot][at] = cells
-                down_at, up_at, down, up = place
-                down_rims[slot][down_at : down_at + down, :] = cells[:down, :]
-                up_rims[slot][up_at : up_at + up, :] = cells[height - up :, :]
+                rims[slot][FOUR + at] = cells
+                put_rows(down_rims[slot], up_rims[slot], place, cells)
 
         guarded(level_ref[0], sender, pack)
 
@@ -232,7 +318,7 @@
         def take(kind=kind, slot=slot):
             for at, (step, channel, place) in enumerate(rim_rows(kind)[0]):
                 layer = LOW - step if kind == "low" else LOW + depth + step - 1
-                put(channel, layer, rims[slot][at], place, above_rims[slot], below_rims[slot])
+                put(channel, layer, rims[slot][FOUR + at], place, above_rims[slot], below_rims[slot])
 
         guarded(level, receiver, take)
 
@@ -243,23 +329,47 @@
     return rest[:3], parts, rest[3 + 3 * slots :]
 
 
-def strip_body(levels, level_ref, *rest):
-    (posts_ref, above_ref, below_ref), parts, (strip_ref, ext) = split_given(levels, rest)
-    unpack(levels, level_ref[0], posts_ref, above_ref, below_ref, *parts, ext)
-    layers, rows, width = ext.shape[1:]
+def strip_body(levels, depth, level_ref, *rest):
+    (own_ref, above_ref, below_ref), parts, rest = split_given(levels, rest)
+    strip_ref, right_ref, left_ref, tiles = rest
+    rows = strip_ref.shape[1]
+    height = rows - 8
     lane = lax.broadcasted_iota(jnp.int32, (rows, 128), 1)
-
-    def channel_step(channel, carry):
-        value = jnp.zeros((rows, 128), jnp.float32)
-        for layer in range(layers):
-            cells = ext[channel, layer]
-            if width > 128:
-                cells = jnp.where(lane < 64, cells[:, :128], cells[:, width - 128 :])
-            value = jnp.where(lane // 8 == layer, lane_roll(cells, 8 * layer + 4), value)
-        strip_ref[channel] = value
-        return carry
-
-    lax.fori_loop(0, channels, channel_step, 0)
+    layer_at = lane // 8
+
+    def put(target, index, place, above, below):
+        above_at, below_at, above_rows, below_rows = place
+        target[index, height : height + above_rows, :] = above[above_at : above_at + above_rows, 0:128]
+        target[index, rows - below_rows :, :] = below[below_at : below_at + below_rows, 0:128]
+
+    for channel in range(channels):
+        strip_ref[channel, 0:height, :] = own_ref[channel]
+        put(strip_ref, channel, strip_rows()[0][channel], above_ref, below_ref)
+    for kind, receiver, _, slot in rim_sides(levels):
+
+        def take(kind=kind, slot=slot):
+            rims, above_rims, below_rims = (part[slot] for part in parts)
+            first = -1 if kind == "low" else LOW + depth
+            here = layer_at < LOW if kind == "low" else layer_at >= LOW + depth
+            for tile in range(FOUR):
+                tiles[tile, 0:height, :] = rims[tile, :, 0:128]
+                put(tiles, tile, rim_strip_rows()[0][tile], above_rims, below_rims)
+                value = tiles[tile]
+                for part in range(min(4, channels - 4 * tile)):
+                    turned = lane_roll(value, 8 * first - 32 * part)
+                    strip_ref[4 * tile + part] = jnp.where(here, turned, strip_ref[4 * tile + part])
+
+        guarded(level_ref[0], receiver, take)
+    spot = lane % 8
+    for target, high in ((right_ref, False), (left_ref, True)):
+        table, count = face_table(high)
+        for tile in range(count):
+            value = jnp.zeros((rows, 128), jnp.float32)
+            for channel, at, first, cols in table:
+                if at == tile:
+                    turned = lane_roll(strip_ref[channel], first - (4 if high else 4 - cols))
+                    value = jnp.where((spot >= first) & (spot < first + cols), turned, value)
+            target[tile] = value
 
 
 def inner_body(levels, level_ref, *rest):
@@ -334,10 +444,12 @@
     before = lane % 8 < 4
     bottom = (lane // 8 == LOW) & (level == 0)
     top = (lane // 8 == LOW + depth - 1) & (level == levels - 1)
-    for channel in range(channels):
-        own = strip_ref[channel]
-        sides[0, channel] = jnp.where(before, left_ref[channel], own)
-        sides[1, channel] = jnp.where(before, own, right_ref[channel])
+    for channel, tile, first, cols in face_table(False)[0]:
+        turned = lane_roll(left_ref[tile], 4 - cols - first)
+        sides[0, channel] = jnp.where(before, turned, strip_ref[channel])
+    for channel, tile, first, _ in face_table(True)[0]:
+        turned = lane_roll(right_ref[tile], 4 - first)
+        sides[1, channel] = jnp.where(before, strip_ref[channel], turned)
 
     def pull(source, side, target):
         for index in range(19):
@@ -442,26 +554,36 @@
     down_sizes, up_sizes = zip(*rim_row_sizes(levels))
     outs = call(
         functools.partial(first_body, levels),
-        [(channels, depth, height, width)]
+        [(channels, depth, height, width), (channels, height, 128)]
         + [(size, width) for size in own_rows(depth)[1]]
         + [(size, height, width) for size in sizes]
         + [(size, width) for size in down_sizes + up_sizes],
         [level, pops, coarse_pops, interface],
     )
-    posts, down, up = outs[:3]
-    rims, down_rims, up_rims = (outs[3 + slots * at : 3 + slots * at + slots] for at in range(3))
-    given = [level, posts, shifted(down, "gy", -1), shifted(up, "gy", 1)]
+    posts, own, down, up = outs[:4]
+    rims, down_rims, up_rims = (outs[4 + slots * at : 4 + slots * at + slots] for at in range(3))
+    given = [shifted(down, "gy", -1), shifted(up, "gy", 1)]
     given += [to_level(value, kind, levels) for value, kind in zip(rims, kinds)]
     given += [to_level(value, kind, levels, "gy", -1) for value, kind in zip(down_rims, kinds)]
     given += [to_level(value, kind, levels, "gy", 1) for value, kind in zip(up_rims, kinds)]
     deep, rows = depth + LOW + HIGH, height + 8
     ext = pltpu.VMEM((channels, deep, rows, width), jnp.float32)
-    (strip,) = call(functools.partial(strip_body, levels), [(channels, rows, 128)], given, 1, [ext])
-    left, right = shifted(strip, "gx", 1), shifted(strip, "gx", -1)
+    strip, right, left = call(
+        functools.partial(strip_body, levels, depth),
+        [(channels, rows, 128)] + [(face_table(high)[1], rows, 128) for high in (False, True)],
+        [level, own] + given,
+        1,
+        [pltpu.VMEM((FOUR, rows, 128), jnp.float32)],
+        heads=[(1, strip_rows()[1][0]), (2, strip_rows()[1][1])]
+        + [(3 + at, FOUR) for at in range(slots)]
+        + [(3 + slots + at, rim_strip_rows()[1][0]) for at in range(slots)]
+        + [(3 + 2 * slots + at, rim_strip_rows()[1][1]) for at in range(slots)],
+    )
+    left, right = shifted(right, "gx", 1), shifted(left, "gx", -1)
     inner_pops, inner_vel = call(
         functools.partial(inner_body, levels),
         [pops.shape, (3, depth + 3, rows, width)],
-        given,
+        [level, posts] + given,
         1,
         [
             ext,
@@ -607,6 +729,10 @@
     return (way_z + 1) * 3 + way_y + 1
 
 
+def face_rows(depth, height):
+    return -(-depth // 8) * height
+
+
 def message_rows(depth):
     return [8 * 8, 2 * 4 * depth, 4 * depth, 2 * 8, 8]
 
@@ -706,7 +832,7 @@
     north_ref, south_ref = rest[:2]
     from_levels, north_levels, south_levels = (rest[2 + slots * at : 2 + slots * at + slots] for at in range(3))
     force_ref, right_ref, left_ref, total = rest[2 + 3 * slots :]
-    base = depth * height
+    base = face_rows(depth, height)
     total[...] = own_ref[...]
     right_ref[base:, :] = jnp.zeros((right_ref.shape[0] - base, width), jnp.float32)
     left_ref[base:, :] = jnp.zeros((left_ref.shape[0] - base, width), jnp.float32)
@@ -718,15 +844,17 @@
             total[part, layer, last, :] += south_ref[at : at + 1, :]
 
     def blocks(source, way_z, way_y):
-        at = base + 16 * group_at(way_z, way_y)
+        at = base + 12 * group_at(way_z, way_y)
         start = source.shape[0] - GROUP
-        left_ref[at : at + 16, :] = source[start : start + 16, :]
-        right_ref[at : at + 16, :] = source[start + 32 : start + 48, :]
-
-    at = base + 16 * group_at(0, 0)
-    for slot in range(2):
-        left_ref[at + 8 * slot : at + 8 * slot + 8, :] = side_ref[slot]
-        right_ref[at + 8 * slot : at + 8 * slot + 8, :] = side_ref[2 + slot]
+        for slot in range(CAP):
+            rows = slice(at + 6 * slot, at + 6 * slot + 6)
+            left_ref[rows, :] = source[start + 8 * slot : start + 8 * slot + 6, :]
+            right_ref[rows, :] = source[start + 32 + 8 * slot : start + 38 + 8 * slot, :]
+
+    at = base + 12 * group_at(0, 0)
+    for slot in range(CAP):
+        left_ref[at + 6 * slot : at + 6 * slot + 6, :] = side_ref[slot, 0:6, :]
+        right_ref[at + 6 * slot : at + 6 * slot + 6, :] = side_ref[2 + slot, 0:6, :]
     blocks(north_ref, 0, 1)
     blocks(south_ref, 0, -1)
     for kind, _, receiver, slot in force_sides(levels):
@@ -748,8 +876,14 @@
     for layer in range(depth):
         for axis in range(3):
             force_ref[axis, layer] = total[axis, layer]
+    lane = lax.broadcasted_iota(jnp.int32, (height, 128), 1)
+    for tile in range(base // height):
+        value = jnp.zeros((height, 128), jnp.float32)
+        for layer in range(8 * tile, min(8 * tile + 8, depth)):
+            part = layer - 8 * tile
+            value = jnp.where(lane // 16 == part, lane_roll(total[3, layer, :, 0:128], 16 * part), value)
         for target in (right_ref, left_ref):
-            target[layer * height : layer * height + height, :] = total[3, layer]
+            target[tile * height : tile * height + height, 0:128] = value
 
 
 def last_body(levels, level_ref, part_ref, stay_ref, *rest):
@@ -759,20 +893,21 @@
     from_levels, north_levels, south_levels = (rest[2 + slots * at : 2 + slots * at + slots] for at in range(3))
     right_ref, left_ref, force_ref, arrived_ref = rest[2 + 3 * slots :]
     blocks = stay_ref.shape[1]
-    base = depth * height
+    base = face_rows(depth, height)
     lane = lax.broadcasted_iota(jnp.int32, (height, 128), 1)
     for layer in range(depth):
-        rows = slice(layer * height, layer * height + height)
+        rows = slice(layer // 8 * height, layer // 8 * height + height)
         before, after = right_ref[rows, :128], left_ref[rows, :128]
         for axis in range(3):
-            first = jnp.where(lane < 2, lane_roll(before, -4 * axis - 1), 0.0)
-            final = jnp.where(lane == 127, lane_roll(after, 127 - 4 * axis), 0.0)
+            at = 16 * (layer % 8) + 4 * axis
+            first = jnp.where(lane < 2, lane_roll(before, -at - 1), 0.0)
+            final = jnp.where(lane == 127, lane_roll(after, 127 - at), 0.0)
             force_ref[axis, layer] = part_ref[axis, layer]
             force_ref[axis, layer, :, 0:128] += first
             force_ref[axis, layer, :, width - 128 : width] += final
     arrived_ref[:, 0:blocks, :] = stay_ref[...]
 
-    def put(source, start, way_z, way_y, way_x):
+    def put(source, start, stride, way_z, way_y, way_x):
         code = group_at(way_z, way_y) * 3 + way_x + 1
         at = blocks + CAP * (code if code < 13 else code - 1)
         for slot in range(CAP):
@@ -780,17 +915,17 @@
                 if source is None:
                     value = jnp.zeros((1, 128), jnp.float32)
                 else:
-                    value = source[start + 8 * slot + axis : start + 8 * slot + axis + 1, :]
+                    value = source[start + stride * slot + axis : start + stride * slot + axis + 1, :]
                 arrived_ref[axis, at + slot : at + slot + 1, :] = value
 
     for way_z in (-1, 0, 1):
         for way_y in (-1, 0, 1):
             for way_x, source in ((1, right_ref), (-1, left_ref)):
-                put(source, base + 16 * group_at(way_z, way_y), way_z, way_y, way_x)
+                put(source, base + 12 * group_at(way_z, way_y), 6, way_z, way_y, way_x)
     middle = 16
 
     def put_group(source, way_z, way_y):
-        put(source, None if source is None else source.shape[0] - GROUP + middle, way_z, way_y, 0)
+        put(source, None if source is None else source.shape[0] - GROUP + middle, 8, way_z, way_y, 0)
 
     put_group(north_ref, 0, 1)
     put_group(south_ref, 0, -1)
@@ -856,7 +991,7 @@
     received += [to_level(value, kind, levels) for value, kind in zip(to_levels, kinds)]
     received += [to_level(value, kind, levels, "gy", 1) for value, kind in zip(north_levels, kinds)]
     received += [to_level(value, kind, levels, "gy", -1) for value, kind in zip(south_levels, kinds)]
-    side_rows = (depth * height + 9 * 16, width)
+    side_rows = (padded(face_rows(depth, height) + 9 * 6 * CAP), width)
     part, right, left = call(
         functools.partial(gather_body, levels),
         [(3, depth, height, width), side_rows, side_rows],

time: 63.2 us -> 56.1 us (0.89)
  waiting for transfers between devices: 17 us -> 14 us
  local copies, waits for them, and re-layouts: 2.76 us -> 0 us
  Pallas kernels: 23.5 us -> 22 us
    ppermute x8, waiting for transfers between devices: 8.02 us -> 3.61 us  [shifted(): lax.ppermute(value, axis, [(i, (i + step) % count) for i in range(count)])]
    unnamed x28 -> x0, local copies, waits for them, and re-layouts: 2.76 us -> none
    pallas_call x6, Pallas kernels: 23.5 us -> 22 us  [call(): pl.pallas_call(whole, out_shape=[jax.ShapeDtypeStruct(shape, jnp.float32)...]
    ppermute x4, waiting for transfers between devices: 8.97 us -> 10.4 us  [to_level(): lax.ppermute(value, (side, 'gz'), [(brick * levels + at, (brick + step) %...]
  transfers between devices with their start and end apart: 14 -> 14, of which waited for: 5 -> 4; matrix products, arithmetic and copies ran while one was open for 0% -> 0% of each run, Pallas kernels for 9% -> 10%
where the time goes in v6:
time: 56.1 us; the launch traced here: 55.8 us
  Pallas kernels  22 us (39%)
  starting transfers between devices  19.1 us (34%)
  waiting for transfers between devices  14 us (25%)
  between operations  0.72 us (1%)
    pallas_call x6, Pallas kernels, call(): pl.pallas_call(whole, out_shape=[jax.ShapeDtypeStruct(shape, jnp.float32)...  22 us
    ppermute x8, starting transfers between devices, shifted(): lax.ppermute(value, axis, [(i, (i + step) % count) for i in range(count)])  11.6 us
    ppermute x4, waiting for transfers between devices, to_level(): lax.ppermute(value, (side, 'gz'), [(brick * levels + at, (brick + step) %...  10.4 us
    ppermute x4, starting transfers between devices, to_level(): lax.ppermute(value, (side, 'gz'), [(brick * levels + at, (brick + step) %...  4.39 us
    ppermute x8, waiting for transfers between devices, shifted(): lax.ppermute(value, axis, [(i, (i + step) % count) for i in range(count)])  3.61 us
    ppermute x2, starting transfers between devices, to_level(): return lax.ppermute(value, 'gz', pairs)  3.08 us
  transfers between devices with their start and end apart: 14, of which 4 were waited for; matrix products, arithmetic and copies ran while one was open for 0% of the time, Pallas kernels for 10%

profile of v6, /device:TPU:0, one launch (start us, length us, event | category | flops | bytes accessed | tf_op | source)
XLA Modules:
  0.0 55.8 jit_solution(415556541255399415)
XLA Ops:
  0.6 2.8 %shard_map.103 = (f32[20,8,8,128]{3,2,1,0:T(8,128)}, f32[20,8,128]{2,1,0:T(8,128)}, f32[552,128]{1,0:T(8,128)}, f32[376,128]{1,0:T(8,128)}, f32[65,8,128]{2,1,0:...) custom-call(s32[1]{0:T(128)} %bitcast.refs_0_, f32[19,8,8,128]{3,2,1,0:T(8,128)} %refs_1_.2, ...), custom_call_target="tpu_custom_call" | custom-call | tf_op jit(solution)/shard_map/pallas_call | solution.py:71
  3.4 2.4 %collective-permute-start = (f32[552,128]{1,0:T(8,128)}, f32[552,128]{1,0:T(8,128)}, u32[]{:S(2)}, u32[]{:S(2)}) collective-permute-start(f32[552,128]{1,0:T(8,128)} %get-tuple-element.30), channel_id=1, source_target_pairs={{0,6},{2,0},{4,2},{6,4},{1,7},{3,1},{5,3},{7,5},{8,14},{10,8},{12,... | collective-permute-start | bytes 847880 | tf_op jit(solution)/shard_map/ppermute | solution.py:525
  5.8 1.5 %collective-permute-start.2 = (f32[65,8,128]{2,1,0:T(8,128)}, f32[65,8,128]{2,1,0:T(8,128)}, u32[]{:S(2)}, u32[]{:S(2)}) collective-permute-start(f32[65,8,128]{2,1,0:T(8,128)} %get-tuple-element.32), channel_id=1, source_target_pairs={{0,1},{1,0},{2,3},{3,2},{4,5},{5,4},{6,7},{7,6},{8,9},{9,8},{10,11... | collective-permute-start | bytes 798728 | tf_op jit(solution)/shard_map/ppermute | solution.py:535
  7.4 1.7 %collective-permute-start.3 = (f32[208,128]{1,0:T(8,128)}, f32[208,128]{1,0:T(8,128)}, u32[]{:S(2)}, u32[]{:S(2)}) collective-permute-start(f32[208,128]{1,0:T(8,128)} %get-tuple-element.33), channel_id=1, source_target_pairs={{0,7},{1,6},{2,1},{3,0},{4,3},{5,2},{6,5},{7,4},{8,15},{9,14},{10,... | collective-permute-start | bytes 319496 | tf_op jit(solution)/shard_map/ppermute | solution.py:537
  9.1 0.1 collective-permute-start.4
  9.1 7.7 %collective-permute-done.4.refs_6_ = f32[136,128]{1,0:T(8,128)} collective-permute-done((f32[136,128]{1,0:T(8,128)}, f32[136,128]{1,0:T(8,128)}, u32[]{:S(2)}, u32[]{:S(2)}) %collective-permute-start.4) | collective-permute-done | bytes 69664 | tf_op jit(solution)/shard_map/ppermute | solution.py:537
  16.8 0.0 collective-permute-done.3.refs_5_
  16.9 0.0 collective-permute-done.1.refs_3_
  16.9 1.9 %shard_map.104 = (f32[20,16,128]{2,1,0:T(8,128)}, f32[6,16,128]{2,1,0:T(8,128)}, f32[9,16,128]{2,1,0:T(8,128)}) custom-call(s32[1]{0:T(128)} %bitcast.refs_0_, f32[20,8,128]{2,1,0:T(8,128)} %get-tuple-element.29.refs_1_, f32[552,128]{1,0:T(8,128)} %collective-permute-done.refs_2_, f32[376,128]{1,0:T(8,128)} %collective-permute-done.1.refs_3_, ...), custom_call_target="tpu_custom_call" | custom-call | tf_op jit(solution)/shard_map/pallas_call | solution.py:71
  18.7 3.9 %collective-permute-start.6 = (f32[9,16,128]{2,1,0:T(8,128)}, f32[9,16,128]{2,1,0:T(8,128)}, u32[]{:S(2)}, u32[]{:S(2)}) collective-permute-start(f32[9,16,128]{2,1,0:T(8,128)} %get-tuple-element.37), channel_id=1, source_target_pairs={{0,24},{8,0},{16,8},{24,16},{1,25},{9,1},{17,9},{25,17},{2,26},{10... | collective-permute-start | bytes 221192 | tf_op jit(solution)/shard_map/ppermute | solution.py:525
  22.6 5.4 %shard_map.105 = (f32[19,8,8,128]{3,2,1,0:T(8,128)}, f32[3,11,16,128]{3,2,1,0:T(8,128)}) custom-call(s32[1]{0:T(128)} %bitcast.refs_0_, f32[20,8,8,128]{3,2,1,0:T(8,128)} %get-tuple-element.38.refs_1_, f32[552,128]{1,0:T(8,128)} %collective-permute-done.refs_2_, f32[376,128]{1,0:T(8,128)} %collective-permute-done.1.refs_3_, ...), custom_call_target="tpu_custom_call" | custom-call | flops 100000000 | bytes 4194304 | tf_op jit(solution)/shard_map/pallas_call | solution.py:71
  28.0 0.8 %collective-permute-done.5.refs_4_ = f32[6,16,128]{2,1,0:T(8,128)} collective-permute-done((f32[6,16,128]{2,1,0:T(8,128)}, f32[6,16,128]{2,1,0:T(8,128)}, u32[]{:S(2)}, u32[]{:S(2)}) %collective-permute-start.5) | collective-permute-done | bytes 49184 | tf_op jit(solution)/shard_map/ppermute | solution.py:525
  28.8 8.1 %shard_map.106 = (f32[19,8,8,128]{3,2,1,0:T(8,128)}, f32[4,8,8,128]{3,2,1,0:T(8,128)}, f32[6,16,128]{2,1,0:T(8,128)}, f32[4,8,128]{2,1,0:T(8,128)}, f32[112,128]...) custom-call(s32[1]{0:T(128)} %bitcast.refs_0_, s32[16]{0:T(128)} %refs_1_.3, ...), custom_call_target="tpu_custom_call" | custom-call | tf_op jit(solution)/shard_map/pallas_call | solution.py:71
  36.9 0.1 collective-permute-start.7
  37.0 1.6 %collective-permute-start.9 = (f32[112,128]{1,0:T(8,128)}, f32[112,128]{1,0:T(8,128)}, u32[]{:S(2)}, u32[]{:S(2)}) collective-permute-start(f32[112,128]{1,0:T(8,128)} %get-tuple-element.46), channel_id=1, source_target_pairs={{0,1},{1,0},{2,3},{3,2},{4,5},{5,4},{6,7},{7,6},{8,9},{9,8},{10,11... | collective-permute-start | bytes 172040 | tf_op jit(solution)/shard_map/ppermute | solution.py:535
  38.6 1.4 %collective-permute-start.8 = (f32[80,128]{1,0:T(8,128)}, f32[80,128]{1,0:T(8,128)}, u32[]{:S(2)}, u32[]{:S(2)}) collective-permute-start(f32[80,128]{1,0:T(8,128)} %get-tuple-element.45), channel_id=1, source_target_pairs={{0,6},{2,0},{4,2},{6,4},{1,7},{3,1},{5,3},{7,5},{8,14},{10,8},{12,... | collective-permute-start | bytes 122888 | tf_op jit(solution)/shard_map/ppermute | solution.py:525
  40.0 0.7 %collective-permute-start.10 = (f32[64,128]{1,0:T(8,128)}, f32[64,128]{1,0:T(8,128)}, u32[]{:S(2)}, u32[]{:S(2)}) collective-permute-start(f32[64,128]{1,0:T(8,128)} %get-tuple-element.47), channel_id=1, source_target_pairs={{0,3},{1,2},{2,5},{3,4},{4,7},{5,6},{6,1},{7,0},{8,11},{9,10},{10,... | collective-permute-start | bytes 98312 | tf_op jit(solution)/shard_map/ppermute | solution.py:537
  40.7 1.9 %collective-permute-start.11 = (f32[56,128]{1,0:T(8,128)}, f32[56,128]{1,0:T(8,128)}, u32[]{:S(2)}, u32[]{:S(2)}) collective-permute-start(f32[56,128]{1,0:T(8,128)} %get-tuple-element.48), channel_id=1, source_target_pairs={{0,7},{1,6},{2,1},{3,0},{4,3},{5,2},{6,5},{7,4},{8,15},{9,14},{10,... | collective-permute-start | bytes 86024 | tf_op jit(solution)/shard_map/ppermute | solution.py:537
  42.6 2.6 %collective-permute-done.11.refs_7_ = f32[56,128]{1,0:T(8,128)} collective-permute-done((f32[56,128]{1,0:T(8,128)}, f32[56,128]{1,0:T(8,128)}, u32[]{:S(2)}, u32[]{:S(2)}) %collective-permute-start.11) | collective-permute-done | bytes 28704 | tf_op jit(solution)/shard_map/ppermute | solution.py:537
  45.2 1.8 %shard_map.107 = (f32[3,8,8,128]{3,2,1,0:T(8,128)}, f32[120,128]{1,0:T(8,128)}, f32[120,128]{1,0:T(8,128)}) custom-call(s32[1]{0:T(128)} %bitcast.refs_0_, f32[4,8,8,128]{3,2,1,0:T(8,128)} %get-tuple-element.42.refs_1_, f32[4,8,128]{2,1,0:T(8,128)} %get-tuple-element.43.refs_2_, f32[112,128]{1,0:T(8,128)} %collective-permute-done.7.refs_3_, ...), custom_call_target="tpu_custom_call" | custom-call | tf_op jit(solution)/shard_map/pallas_call | solution.py:71
  47.1 0.1 collective-permute-start.12
  47.1 3.8 %collective-permute-start.13 = (f32[120,128]{1,0:T(8,128)}, f32[120,128]{1,0:T(8,128)}, u32[]{:S(2)}, u32[]{:S(2)}) collective-permute-start(f32[120,128]{1,0:T(8,128)} %get-tuple-element.52), channel_id=1, source_target_pairs={{0,24},{8,0},{16,8},{24,16},{1,25},{9,1},{17,9},{25,17},{2,26},{10... | collective-permute-start | bytes 184328 | tf_op jit(solution)/shard_map/ppermute | solution.py:525
  50.9 2.8 %collective-permute-done.12.refs_8_ = f32[120,128]{1,0:T(8,128)} collective-permute-done((f32[120,128]{1,0:T(8,128)}, f32[120,128]{1,0:T(8,128)}, u32[]{:S(2)}, u32[]{:S(2)}) %collective-permute-start.12) | collective-permute-done | bytes 61472 | tf_op jit(solution)/shard_map/ppermute | solution.py:525
  53.7 2.1 %shard_map.108 = (f32[3,8,8,128]{3,2,1,0:T(8,128)}, f32[6,68,128]{2,1,0:T(8,128)}) custom-call(s32[1]{0:T(128)} %bitcast.refs_0_, f32[3,8,8,128]{3,2,1,0:T(8,128)} %get-tuple-element.49.refs_1_, f32[6,16,128]{2,1,0:T(8,128)} %get-tuple-element.50.refs_2_, f32[112,128]{1,0:T(8,128)} %collective-permute-done.7.refs_3_, ...), custom_call_target="tpu_custom_call" | custom-call | tf_op jit(solution)/shard_map/pallas_call | solution.py:71
  (10 shorter events, 0.0 us)
Async XLA Ops:
  3.4 13.4 %collective-permute-start = (f32[552,128]{1,0:T(8,128)}, f32[552,128]{1,0:T(8,128)}, u32[]{:S(2)}, u32[]{:S(2)}) collective-permute-start(f32[552,128]{1,0:T(8,128)} %get-tuple-element.30), channel_id=1, source_target_pairs={{0,6},{2,0},{4,2},{6,4},{1,7},{3,1},{5,3},{7,5},{8,14},{10,8},{12,... | collective-permute-start | bytes 847880 | tf_op jit(solution)/shard_map/ppermute | solution.py:525
  5.8 11.0 %collective-permute-start.2 = (f32[65,8,128]{2,1,0:T(8,128)}, f32[65,8,128]{2,1,0:T(8,128)}, u32[]{:S(2)}, u32[]{:S(2)}) collective-permute-start(f32[65,8,128]{2,1,0:T(8,128)} %get-tuple-element.32), channel_id=1, source_target_pairs={{0,1},{1,0},{2,3},{3,2},{4,5},{5,4},{6,7},{7,6},{8,9},{9,8},{10,11... | collective-permute-start | bytes 798728 | tf_op jit(solution)/shard_map/ppermute | solution.py:535
  7.4 9.5 %collective-permute-start.1 = (f32[376,128]{1,0:T(8,128)}, f32[376,128]{1,0:T(8,128)}, u32[]{:S(2)}, u32[]{:S(2)}) collective-permute-start(f32[376,128]{1,0:T(8,128)} %get-tuple-element.31), channel_id=1, source_target_pairs={{0,2},{2,4},{4,6},{6,0},{1,3},{3,5},{5,7},{7,1},{8,10},{10,12},{12... | collective-permute-start | bytes 577544 | tf_op jit(solution)/shard_map/ppermute | solution.py:525
  7.4 9.5 %collective-permute-start.3 = (f32[208,128]{1,0:T(8,128)}, f32[208,128]{1,0:T(8,128)}, u32[]{:S(2)}, u32[]{:S(2)}) collective-permute-start(f32[208,128]{1,0:T(8,128)} %get-tuple-element.33), channel_id=1, source_target_pairs={{0,7},{1,6},{2,1},{3,0},{4,3},{5,2},{6,5},{7,4},{8,15},{9,14},{10,... | collective-permute-start | bytes 319496 | tf_op jit(solution)/shard_map/ppermute | solution.py:537
  9.1 7.8 %collective-permute-start.4 = (f32[136,128]{1,0:T(8,128)}, f32[136,128]{1,0:T(8,128)}, u32[]{:S(2)}, u32[]{:S(2)}) collective-permute-start(f32[136,128]{1,0:T(8,128)} %get-tuple-element.34), channel_id=1, source_target_pairs={{0,3},{1,2},{2,5},{3,4},{4,7},{5,6},{6,1},{7,0},{8,11},{9,10},{10,... | collective-permute-start | bytes 208904 | tf_op jit(solution)/shard_map/ppermute | solution.py:537
  18.7 10.1 %collective-permute-start.6 = (f32[9,16,128]{2,1,0:T(8,128)}, f32[9,16,128]{2,1,0:T(8,128)}, u32[]{:S(2)}, u32[]{:S(2)}) collective-permute-start(f32[9,16,128]{2,1,0:T(8,128)} %get-tuple-element.37), channel_id=1, source_target_pairs={{0,24},{8,0},{16,8},{24,16},{1,25},{9,1},{17,9},{25,17},{2,26},{10... | collective-permute-start | bytes 221192 | tf_op jit(solution)/shard_map/ppermute | solution.py:525
  22.6 6.2 %collective-permute-start.5 = (f32[6,16,128]{2,1,0:T(8,128)}, f32[6,16,128]{2,1,0:T(8,128)}, u32[]{:S(2)}, u32[]{:S(2)}) collective-permute-start(f32[6,16,128]{2,1,0:T(8,128)} %get-tuple-element.36), channel_id=1, source_target_pairs={{0,8},{8,16},{16,24},{24,0},{1,9},{9,17},{17,25},{25,1},{2,10},{10... | collective-permute-start | bytes 147464 | tf_op jit(solution)/shard_map/ppermute | solution.py:525
  36.9 8.3 %collective-permute-start.7 = (f32[112,128]{1,0:T(8,128)}, f32[112,128]{1,0:T(8,128)}, u32[]{:S(2)}, u32[]{:S(2)}) collective-permute-start(f32[112,128]{1,0:T(8,128)} %get-tuple-element.44), channel_id=1, source_target_pairs={{0,2},{2,4},{4,6},{6,0},{1,3},{3,5},{5,7},{7,1},{8,10},{10,12},{12... | collective-permute-start | bytes 172040 | tf_op jit(solution)/shard_map/ppermute | solution.py:525
  37.0 8.2 %collective-permute-start.9 = (f32[112,128]{1,0:T(8,128)}, f32[112,128]{1,0:T(8,128)}, u32[]{:S(2)}, u32[]{:S(2)}) collective-permute-start(f32[112,128]{1,0:T(8,128)} %get-tuple-element.46), channel_id=1, source_target_pairs={{0,1},{1,0},{2,3},{3,2},{4,5},{5,4},{6,7},{7,6},{8,9},{9,8},{10,11... | collective-permute-start | bytes 172040 | tf_op jit(solution)/shard_map/ppermute | solution.py:535
  38.6 6.6 %collective-permute-start.8 = (f32[80,128]{1,0:T(8,128)}, f32[80,128]{1,0:T(8,128)}, u32[]{:S(2)}, u32[]{:S(2)}) collective-permute-start(f32[80,128]{1,0:T(8,128)} %get-tuple-element.45), channel_id=1, source_target_pairs={{0,6},{2,0},{4,2},{6,4},{1,7},{3,1},{5,3},{7,5},{8,14},{10,8},{12,... | collective-permute-start | bytes 122888 | tf_op jit(solution)/shard_map/ppermute | solution.py:525
  40.0 5.3 %collective-permute-start.10 = (f32[64,128]{1,0:T(8,128)}, f32[64,128]{1,0:T(8,128)}, u32[]{:S(2)}, u32[]{:S(2)}) collective-permute-start(f32[64,128]{1,0:T(8,128)} %get-tuple-element.47), channel_id=1, source_target_pairs={{0,3},{1,2},{2,5},{3,4},{4,7},{5,6},{6,1},{7,0},{8,11},{9,10},{10,... | collective-permute-start | bytes 98312 | tf_op jit(solution)/shard_map/ppermute | solution.py:537
  40.7 4.6 %collective-permute-start.11 = (f32[56,128]{1,0:T(8,128)}, f32[56,128]{1,0:T(8,128)}, u32[]{:S(2)}, u32[]{:S(2)}) collective-permute-start(f32[56,128]{1,0:T(8,128)} %get-tuple-element.48), channel_id=1, source_target_pairs={{0,7},{1,6},{2,1},{3,0},{4,3},{5,2},{6,5},{7,4},{8,15},{9,14},{10,... | collective-permute-start | bytes 86024 | tf_op jit(solution)/shard_map/ppermute | solution.py:537
  47.1 6.6 %collective-permute-start.12 = (f32[120,128]{1,0:T(8,128)}, f32[120,128]{1,0:T(8,128)}, u32[]{:S(2)}, u32[]{:S(2)}) collective-permute-start(f32[120,128]{1,0:T(8,128)} %get-tuple-element.51), channel_id=1, source_target_pairs={{0,8},{8,16},{16,24},{24,0},{1,9},{9,17},{17,25},{25,1},{2,10},{10... | collective-permute-start | bytes 184328 | tf_op jit(solution)/shard_map/ppermute | solution.py:525
  47.1 6.6 %collective-permute-start.13 = (f32[120,128]{1,0:T(8,128)}, f32[120,128]{1,0:T(8,128)}, u32[]{:S(2)}, u32[]{:S(2)}) collective-permute-start(f32[120,128]{1,0:T(8,128)} %get-tuple-element.52), channel_id=1, source_target_pairs={{0,24},{8,0},{16,8},{24,16},{1,25},{9,1},{17,9},{25,17},{2,26},{10... | collective-permute-start | bytes 184328 | tf_op jit(solution)/shard_map/ppermute | solution.py:525

commit v7 on v6

--- a/solution.py
+++ b/solution.py
@@ -42,19 +42,33 @@
 couple = 8.0
 
 
-def call(body, outs, ins, scalars=1, scratch=(), cost=None, heads=()):
+class Level:
+    def __getitem__(self, _):
+        return lax.axis_index("gz").astype(jnp.int32)
+
+
+class Moving:
+    def __init__(self, buffer, copy):
+        self.buffer = buffer
+        self.copy = copy
+
+    def take(self):
+        self.copy.wait()
+        return self.buffer
+
+
+def call(body, outs, arrays, scratch=(), cost=None, heads=(), late=(), kind=jnp.float32):
     heads = dict(heads)
-    arrays = ins[scalars:]
     landing = []
     for at, value in enumerate(arrays):
-        count = heads.get(at, value.shape[0])
-        landing.append(pltpu.VMEM((count,) + value.shape[1:], value.dtype))
+        space = pltpu.SMEM if value.ndim == 1 else pltpu.VMEM
+        landing.append(space((heads.get(at, value.shape[0]),) + value.shape[1:], value.dtype))
 
     def whole(*refs):
-        given = refs[scalars : len(ins)]
-        made = refs[len(ins) : len(ins) + len(outs)]
-        rest = refs[len(ins) + len(outs) :]
-        landed, done, rest = rest[: len(arrays)], rest[len(arrays)], rest[len(arrays) + 1 :]
+        given = refs[: len(arrays)]
+        made = list(refs[len(arrays) : len(arrays) + len(outs)])
+        rest = refs[len(arrays) + len(outs) :]
+        landed, done, rest = list(rest[: len(arrays)]), rest[len(arrays)], rest[len(arrays) + 1 :]
         copies = []
         for at, (source, target) in enumerate(zip(given, landed)):
             if at in heads:
@@ -62,21 +76,29 @@
             copies.append(pltpu.make_async_copy(source, target, done.at[at]))
         for copy in copies:
             copy.start()
-        for copy in copies:
-            copy.wait()
-        body(*refs[:scalars], *landed, *made, *rest)
+        for at, copy in enumerate(copies):
+            if at in late:
+                landed[at] = Moving(landed[at], copy)
+            else:
+                copy.wait()
+        body(Level(), *landed, *made, *rest)
 
     vmem = pl.BlockSpec(memory_space=pltpu.VMEM)
     hbm = pl.BlockSpec(memory_space=pltpu.HBM)
     return pl.pallas_call(
         whole,
-        out_shape=[jax.ShapeDtypeStruct(shape, jnp.float32) for shape in outs],
-        in_specs=[pl.BlockSpec(memory_space=pltpu.SMEM)] * scalars + [hbm] * len(arrays),
+        out_shape=[
+            jax.ShapeDtypeStruct(shape, kind[at] if isinstance(kind, list) else kind)
+            for at, shape in enumerate(outs)
+        ],
+        in_specs=[hbm] * len(arrays),
         out_specs=[vmem] * len(outs),
-        scratch_shapes=landing + [pltpu.SemaphoreType.DMA((len(arrays),))] + list(scratch),
+        scratch_shapes=landing
+        + [pltpu.SemaphoreType.DMA((len(arrays),))]
+        + list(scratch),
         cost_estimate=cost,
         compiler_params=pltpu.CompilerParams(vmem_limit_bytes=64 * 1024 * 1024),
-    )(*ins)
+    )(*arrays)
 
 
 ways = [tuple(int(part) for part in lattice[index][::-1]) for index in range(19)] + [(0, 0, 0)]
@@ -331,7 +353,7 @@
 
 def strip_body(levels, depth, level_ref, *rest):
     (own_ref, above_ref, below_ref), parts, rest = split_given(levels, rest)
-    strip_ref, right_ref, left_ref, tiles = rest
+    _, strip_ref, right_ref, left_ref, tiles = rest
     rows = strip_ref.shape[1]
     height = rows - 8
     lane = lax.broadcasted_iota(jnp.int32, (rows, 128), 1)
@@ -411,7 +433,9 @@
                 second[(index, number, *tile)] = jnp.where(inside, ext[(index, at, *tile)], posts[index])
         return carry
 
-    lax.fori_loop(0, depth + LOW + HIGH - 2, first_step, 0)
+    first = jnp.where(level == 0, LOW - 1, 0)
+    final = jnp.where(level == levels - 1, depth + LOW - 1, depth + LOW + HIGH - 2)
+    lax.fori_loop(first, final, first_step, 0)
 
     def second_step(number, carry):
         pull(second, number - 1, number + 1)
@@ -428,16 +452,16 @@
             pops_ref[index, number - 1] = pulled[index, :height, :]
         return carry
 
-    lax.fori_loop(0, 1, second_step, 0)
+    lax.fori_loop(jnp.where(level == 0, 1, 0), 1, second_step, 0)
     lax.fori_loop(1, depth + 1, second_inner, 0)
-    lax.fori_loop(depth + 1, depth + 3, second_step, 0)
+    lax.fori_loop(depth + 1, jnp.where(level == levels - 1, depth + 1, depth + 3), second_step, 0)
 
 
 def edge_body(
-    levels, level_ref, strip_ref, left_ref, right_ref, inner_pops, inner_vel,
-    pops_ref, vel_ref, beyond_ref, sides, pulled, second,
+    size, levels, level_ref, strip_ref, left_ref, right_ref, inner_vel,
+    edge_ref, vel_ref, beyond_ref, sides, pulled, second,
 ):
-    depth, height, width = pops_ref.shape[1:]
+    depth, height, width = size
     rows = height + 8
     level = level_ref[0]
     lane = lax.broadcasted_iota(jnp.int32, (rows, 128), 1)
@@ -475,22 +499,10 @@
         inverse = 1.0 / density
         speeds[side] = [part * inverse for part in moment]
 
-    near = lane[:height]
-    near = (near < 2) | (near >= 126)
-    front = before[:height]
-    for index in range(19):
-        value = jnp.where(front, pulled[1, index, :height], pulled[0, index, :height])
-        for layer in range(depth):
-            turned = lane_roll(value, -(8 * (layer + LOW) + 4))
-            for col in range(0, width, 128):
-                cells = inner_pops[index, layer, :, col : col + 128]
-                if col == 0 or col == width - 128:
-                    mask = near if width == 128 else near & ((lane[:height] < 64) == (col == 0))
-                    cells = jnp.where(mask, turned, cells)
-                pops_ref[index, layer, :, col : col + 128] = cells
     row = lax.broadcasted_iota(jnp.int32, (rows, 128), 0)
     valid = (row < height + 2) | (row == rows - 1)
     outside = (lane < 2) | (lane == 127)
+    vel_in = inner_vel.take()
     table = table_rows(depth, height)
     vel_ref[...] = jnp.zeros_like(vel_ref)
     beyond_ref[...] = jnp.zeros_like(beyond_ref)
@@ -512,12 +524,33 @@
             shift = -(8 * (layer - 1 + LOW) + 4)
             turned = lane_roll(main, shift)
             for col in range(0, width, 128):
-                cells = inner_vel[axis, layer, :, col : col + 128]
+                cells = vel_in[axis, layer, :, col : col + 128]
                 if col == 0 or col == width - 128:
                     mask = (lane < 2) & (col == 0) | (lane >= 126) & (col == width - 128)
                     cells = jnp.where(mask, turned, cells)
                 put(vel_ref, axis, layer, slice(col, col + 128), jnp.where(keep, cells, 0.0))
             put(beyond_ref, axis, layer, slice(0, 128), jnp.where(keep & outside, lane_roll(rest, shift), 0.0))
+    for index in range(19):
+        edge_ref[index] = jnp.where(before, pulled[1, index], pulled[0, index])[:height]
+
+
+def patch_body(_, pops_in, edge_ref, pops_ref):
+    depth, height, width = pops_ref.shape[1:]
+    lane = lax.broadcasted_iota(jnp.int32, (height, 128), 1)
+    for index in range(19):
+        value = edge_ref[index]
+        for layer in range(depth):
+            turned = lane_roll(value, -(8 * (layer + LOW) + 4))
+            for col in range(0, width, 128):
+                cells = pops_in[index, layer, :, col : col + 128]
+                if col == 0 or col == width - 128:
+                    mask = (lane < 2) & (col == 0) | (lane >= 126) & (col == width - 128)
+                    cells = jnp.where(mask, turned, cells)
+                pops_ref[index, layer, :, col : col + 128] = cells
+
+
+def long_cost():
+    return pl.CostEstimate(flops=10**8, bytes_accessed=1 << 22, transcendentals=0)
 
 
 def shifted(value, axis, step):
@@ -545,7 +578,7 @@
     )
 
 
-def wide_exchange(level, pops, coarse_pops, interface):
+def wide_exchange(pops, coarse_pops, interface, ready):
     levels = lax.axis_size("gz")
     depth, height, width = interface.shape
     sizes = rim_sizes(levels)
@@ -558,7 +591,7 @@
         + [(size, width) for size in own_rows(depth)[1]]
         + [(size, height, width) for size in sizes]
         + [(size, width) for size in down_sizes + up_sizes],
-        [level, pops, coarse_pops, interface],
+        [pops, coarse_pops, interface],
     )
     posts, own, down, up = outs[:4]
     rims, down_rims, up_rims = (outs[4 + slots * at : 4 + slots * at + slots] for at in range(3))
@@ -571,8 +604,7 @@
     strip, right, left = call(
         functools.partial(strip_body, levels, depth),
         [(channels, rows, 128)] + [(face_table(high)[1], rows, 128) for high in (False, True)],
-        [level, own] + given,
-        1,
+        [own] + given + [ready],
         [pltpu.VMEM((FOUR, rows, 128), jnp.float32)],
         heads=[(1, strip_rows()[1][0]), (2, strip_rows()[1][1])]
         + [(3 + at, FOUR) for at in range(slots)]
@@ -583,14 +615,13 @@
     inner_pops, inner_vel = call(
         functools.partial(inner_body, levels),
         [pops.shape, (3, depth + 3, rows, width)],
-        [level, posts] + given,
-        1,
+        [posts] + given,
         [
             ext,
             pltpu.VMEM((19, rows, width), jnp.float32),
             pltpu.VMEM((19, deep - 2, rows, width), jnp.float32),
         ],
-        pl.CostEstimate(flops=10**8, bytes_accessed=1 << 22, transcendentals=0),
+        long_cost(),
     )
     return [strip, left, right, inner_pops, inner_vel]
 
@@ -622,13 +653,55 @@
     return -(-(depth + 3) * (height + 3) // 16) * 16
 
 
-def droplet_body(
-    size, counts_ref, dest_ref, vel_ref, beyond_ref, speed_ref, frac_ref, home_ref, spread_ref, outer_ref,
-    stay_ref, state_ref, twice, mixed, along, push_high, push_low, plane_ref,
-):
+def weigh_body(size, _, frac_ref, home_ref, along, plane_ref, ready_ref):
     depth, height, width = size
     blocks = home_ref.shape[0]
     layers, rows = depth + 3, height + 3
+    table = table_rows(depth, height)
+    ready_ref[...] = jnp.zeros_like(ready_ref)
+    along[2 * width :, :] = jnp.zeros((128, along.shape[1]), jnp.bfloat16)
+    plane_ref[:, layers * rows :, :] = jnp.zeros(
+        (plane_ref.shape[0], table - layers * rows, 256), jnp.float32
+    )
+    span_x = lax.broadcasted_iota(jnp.int32, (width, 128), 0) + 1
+    span_end = lax.broadcasted_iota(jnp.int32, (16, 128), 0)
+    span_y = lax.broadcasted_iota(jnp.int32, (padded(rows), 128), 0)
+    span_z = lax.broadcasted_iota(jnp.int32, (padded(layers), 128), 0)
+    for block in range(blocks):
+        side = slice(block * 128, block * 128 + 128)
+        cell = home_ref[block : block + 1, :]
+        cell_x = cell % width
+        cell_y = cell // width % height
+        cell_z = cell // (width * height)
+        part_x = phis(frac_ref[0, block : block + 1, :])
+        part_y = phis(frac_ref[1, block : block + 1, :])
+        part_z = phis(frac_ref[2, block : block + 1, :])
+        high, low = split(pick(span_x - cell_x, part_x))
+        along[0:width, side] = low
+        along[width : 2 * width, side] = high
+        high, low = split(pick(span_end + (width + 1) - cell_x, part_x))
+        along[2 * width : 2 * width + 16, side] = high
+        along[2 * width + 32 : 2 * width + 48, side] = high
+        along[2 * width + 64 : 2 * width + 80, side] = low
+        high, low = split(jnp.where((span_end == 15) & (cell_x == 0), part_x[0], 0.0))
+        along[2 * width + 112 : 2 * width + 128, side] = high
+        along[2 * width + 16 : 2 * width + 32, side] = high
+        along[2 * width + 48 : 2 * width + 64, side] = low
+        weight_y = pick(span_y - cell_y, part_y)[:rows]
+        weight_z = pick(span_z - cell_z, part_z)
+        half = block % 2 * 128
+        for layer in range(layers):
+            plane_ref[block // 2, layer * rows : layer * rows + rows, half : half + 128] = (
+                weight_y * weight_z[layer : layer + 1, :]
+            )
+
+
+def droplet_body(
+    size, counts_ref, dest_ref, vel_ref, beyond_ref, speed_ref, frac_ref, along_in, plane_in,
+    spread_ref, outer_ref, stay_ref, state_ref, twice, mixed, push_high, push_low, meanwhile,
+):
+    depth, height, width = size
+    blocks = state_ref.shape[0]
     table = table_rows(depth, height)
     high, low = split(vel_ref[...])
     twice[:, :width] = high
@@ -636,44 +709,8 @@
     mixed[:, :width] = low
     high, low = (part.astype(jnp.float32) for part in split(beyond_ref[...]))
     mixed[:, width:] = (high + lane_roll(low, 32) + lane_roll(high, 64)).astype(jnp.bfloat16)
-    along[2 * width :, :] = jnp.zeros((128, along.shape[1]), jnp.bfloat16)
-    plane_ref[:, layers * rows :, :] = jnp.zeros(
-        (plane_ref.shape[0], table - layers * rows, 256), jnp.float32
-    )
-    span_x = lax.broadcasted_iota(jnp.int32, (width, 128), 0) + 1
-    span_end = lax.broadcasted_iota(jnp.int32, (16, 128), 0)
-    span_y = lax.broadcasted_iota(jnp.int32, (-(-rows // 8) * 8, 128), 0)
-    span_z = lax.broadcasted_iota(jnp.int32, (-(-layers // 8) * 8, 128), 0)
     slots = lax.broadcasted_iota(jnp.int32, (1, 128), 1)
-
-    def weigh(number):
-        for half in range(2):
-            block = 2 * number + half
-            side = slice(block * 128, block * 128 + 128)
-            cell = home_ref[block : block + 1, :]
-            cell_x = cell % width
-            cell_y = cell // width % height
-            cell_z = cell // (width * height)
-            part_x = phis(frac_ref[0, block : block + 1, :])
-            part_y = phis(frac_ref[1, block : block + 1, :])
-            part_z = phis(frac_ref[2, block : block + 1, :])
-            high, low = split(pick(span_x - cell_x, part_x))
-            along[0:width, side] = low
-            along[width : 2 * width, side] = high
-            high, low = split(pick(span_end + (width + 1) - cell_x, part_x))
-            along[2 * width : 2 * width + 16, side] = high
-            along[2 * width + 32 : 2 * width + 48, side] = high
-            along[2 * width + 64 : 2 * width + 80, side] = low
-            high, low = split(jnp.where((span_end == 15) & (cell_x == 0), part_x[0], 0.0))
-            along[2 * width + 112 : 2 * width + 128, side] = high
-            along[2 * width + 16 : 2 * width + 32, side] = high
-            along[2 * width + 48 : 2 * width + 64, side] = low
-            weight_y = pick(span_y - cell_y, part_y)[:rows]
-            weight_z = pick(span_z - cell_z, part_z)
-            for layer in range(layers):
-                plane_ref[number % 2, layer * rows : layer * rows + rows, half * 128 : half * 128 + 128] = (
-                    weight_y * weight_z[layer : layer + 1, :]
-                )
+    along, plane_ref = along_in.take(), plane_in.take()
 
     def sample(number):
         pair = slice(number * 256, number * 256 + 256)
@@ -682,7 +719,7 @@
         )
 
     def move(number, sums):
-        plane = plane_ref[number % 2]
+        plane = plane_ref[number]
         for axis in range(3):
             where = slice(axis * table, axis * table + table)
             sampled = jnp.sum(sums[where] * plane, axis=0, keepdims=True)
@@ -703,13 +740,11 @@
                 push_low[where, block * 128 : block * 128 + 128] = low
 
     pairs = blocks // 2
-    weigh(0)
     for number in range(pairs):
-        sums = sample(number)
-        if number + 1 < pairs:
-            weigh(number + 1)
-        move(number, sums)
+        move(number, sample(number))
     main = dots(push_high[...], along[0 : 2 * width, :], ((1,), (1,)))
+    for action in meanwhile:
+        action()
     rest = dots(push_low[...], along[width:, :], ((1,), (1,)))
     outer = dots(push_high[...], along[2 * width :, :], ((1,), (1,)))
     spread_ref[...] = main[:, :width] + main[:, width:] + rest[:, :width]
@@ -737,12 +772,43 @@
     return [8 * 8, 2 * 4 * depth, 4 * depth, 2 * 8, 8]
 
 
-def pack_body(
-    levels, level_ref, dest_ref, spread_ref, outer_ref, state_ref, own_ref, side_ref,
-    to_levels, north_ref, south_ref, north_levels, south_levels, outbox, strip, taken,
+def pack_blocks(
+    levels, level_ref, dest_ref, state_ref, side_ref,
+    to_levels, north_ref, south_ref, north_levels, south_levels, outbox,
+):
+    level = level_ref[0]
+    blocks = state_ref.shape[0]
+    codes = [dest_ref[block] for block in range(blocks)]
+    outbox[...] = jnp.zeros_like(outbox)
+    for block in range(blocks):
+        rank = jnp.int32(0)
+        for earlier in range(block):
+            rank = rank + (codes[earlier] == codes[block]).astype(jnp.int32)
+        slot = jnp.where(codes[block] == 13, 27 * CAP, codes[block] * CAP + jnp.minimum(rank, CAP - 1))
+        outbox[slot] = state_ref[block]
+
+    def put(target, way_z, way_y):
+        base = target.shape[0] - GROUP
+        for slot in range(6):
+            target[base + 8 * slot : base + 8 * slot + 8, :] = outbox[6 * group_at(way_z, way_y) + slot]
+
+    put(north_ref, 0, 1)
+    put(south_ref, 0, -1)
+    for slot in range(CAP):
+        side_ref[slot] = outbox[6 * group_at(0, 0) + slot]
+        side_ref[CAP + slot] = outbox[6 * group_at(0, 0) + 4 + slot]
+    ways_z = [(1 - 2 * level, 0)] if levels == 2 else [(1, 0), (-1, 1)]
+    for way_z, slot in ways_z:
+        put(to_levels[slot], way_z, 0)
+        put(north_levels[slot], way_z, 1)
+        put(south_levels[slot], way_z, -1)
+
+
+def pack_force(
+    levels, level_ref, spread_ref, outer_ref, own_ref,
+    to_levels, north_ref, south_ref, north_levels, south_levels, strip,
 ):
     depth, height, width = own_ref.shape[1:]
-    level = level_ref[0]
     rows, table = height + 3, table_rows(depth, height)
     lane = lax.broadcasted_iota(jnp.int32, (table, 128), 1)
     value = jnp.zeros((table, 128), jnp.float32)
@@ -751,28 +817,12 @@
         cells = outer_ref[axis * table : axis * table + table, :]
         value = jnp.where(here, lane_roll(cells, 4 * axis + 1), value)
     strip[...] = value
-    for code in range(27):
-        taken[code] = 0
-    outbox[...] = jnp.zeros_like(outbox)
-    for block in range(state_ref.shape[0]):
-        code = dest_ref[block]
-
-        @pl.when(code != 13)
-        def _():
-            rank = taken[code]
-            outbox[code * CAP + rank] = state_ref[block]
-            taken[code] = rank + 1
 
     def force(part, layer, cut):
         at = layer * rows
         if part < 3:
             return spread_ref[part * table + at + cut.start : part * table + at + cut.stop, :]
         return strip[at + cut.start : at + cut.stop, :]
-
-    def blocks(target, way_z, way_y):
-        base = target.shape[0] - GROUP
-        for slot in range(6):
-            target[base + 8 * slot : base + 8 * slot + 8, :] = outbox[6 * group_at(way_z, way_y) + slot]
 
     main, north, south = slice(1, height + 1), slice(height + 1, height + 3), slice(0, 1)
     for part in range(4):
@@ -781,11 +831,6 @@
             at = part * depth + layer
             north_ref[2 * at : 2 * at + 2, :] = force(part, layer + 1, north)
             south_ref[at : at + 1, :] = force(part, layer + 1, south)
-    blocks(north_ref, 0, 1)
-    blocks(south_ref, 0, -1)
-    for slot in range(2):
-        side_ref[slot] = outbox[6 * group_at(0, 0) + slot]
-        side_ref[2 + slot] = outbox[6 * group_at(0, 0) + 4 + slot]
     for kind, sender, _, slot in force_sides(levels):
 
         def pack(kind=kind, slot=slot):
@@ -796,33 +841,37 @@
                     to_levels[slot][8 * at : 8 * at + 8, :] = force(part, layer, main)
                     north_levels[slot][2 * at : 2 * at + 2, :] = force(part, layer, north)
                     south_levels[slot][at : at + 1, :] = force(part, layer, south)
-            way = 1 if kind == "up" else -1
-            blocks(to_levels[slot], way, 0)
-            blocks(north_levels[slot], way, 1)
-            blocks(south_levels[slot], way, -1)
-
-        guarded(level, sender, pack)
+
+        guarded(level_ref[0], sender, pack)
 
 
 def main_body(
-    levels, level_ref, counts_ref, dest_ref, strip_ref, left_ref, right_ref, inner_pops, inner_vel,
-    speed_ref, frac_ref, home_ref, pops_ref, own_ref, stay_ref, side_ref, north_ref, south_ref, *rest,
+    size, levels, level_ref, counts, dest, strip_ref, left_ref, right_ref, inner_vel,
+    speed, frac, along, plane, edge_ref, own_ref, stay_ref, side_ref, north_ref, south_ref, *rest,
 ):
     slots = len(rim_sizes(levels))
     to_levels, north_levels, south_levels = (rest[slots * at : slots * at + slots] for at in range(3))
     rest = rest[3 * slots :]
-    vel_ref, beyond_ref, spread_ref, outer_ref, state_ref, outbox, strip, taken = rest[:8]
+    vel_ref, beyond_ref, spread_ref, outer_ref, state_ref, outbox, strip = rest[:7]
+    counts_ref, dest_ref = counts.take(), dest.take()
     edge_body(
-        levels, level_ref, strip_ref, left_ref, right_ref, inner_pops, inner_vel,
-        pops_ref, vel_ref, beyond_ref, *rest[8:11],
-    )
+        size, levels, level_ref, strip_ref, left_ref, right_ref, inner_vel,
+        edge_ref, vel_ref, beyond_ref, *rest[7:10],
+    )
+
+    def move_out():
+        pack_blocks(
+            levels, level_ref, dest_ref, state_ref, side_ref,
+            to_levels, north_ref, south_ref, north_levels, south_levels, outbox,
+        )
+
     droplet_body(
-        pops_ref.shape[1:], counts_ref, dest_ref, vel_ref, beyond_ref, speed_ref, frac_ref, home_ref,
-        spread_ref, outer_ref, stay_ref, state_ref, *rest[11:],
-    )
-    pack_body(
-        levels, level_ref, dest_ref, spread_ref, outer_ref, state_ref, own_ref, side_ref,
-        to_levels, north_ref, south_ref, north_levels, south_levels, outbox, strip, taken,
+        size, counts_ref, dest_ref, vel_ref, beyond_ref, speed.take(), frac.take(), along, plane,
+        spread_ref, outer_ref, stay_ref, state_ref, *rest[10:], [move_out],
+    )
+    pack_force(
+        levels, level_ref, spread_ref, outer_ref, own_ref,
+        to_levels, north_ref, south_ref, north_levels, south_levels, strip,
     )
 
 
@@ -947,62 +996,66 @@
 
 
 def local(pops, coarse_pops, interface, drop_vel, drop_frac, home, counts, dest):
-    level = lax.axis_index("gz").astype(jnp.int32).reshape(1)
     levels = lax.axis_size("gz")
     depth, height, width = interface.shape
     blocks = home.shape[0]
     kinds = ["up", "down"][: len(rim_sizes(levels))]
     slots = len(kinds)
-    given = wide_exchange(level, pops, coarse_pops, interface)
+    size = (depth, height, width)
     rows = height + 8
     table = table_rows(depth, height)
+    along, plane, ready = call(
+        functools.partial(weigh_body, size),
+        [(2 * width + 128, blocks * 128), (blocks // 2, table, 256), (8, 128)],
+        [drop_frac, home],
+        cost=long_cost(),
+        kind=[jnp.bfloat16, jnp.float32, jnp.float32],
+    )
+    strip, left, right, inner_pops, inner_vel = wide_exchange(pops, coarse_pops, interface, ready)
     sizes = [(count + GROUP, width) for count in message_rows(depth)]
     outs = call(
-        functools.partial(main_body, levels),
-        [pops.shape, (4, depth, height, width), (6, blocks, 128), (4, 8, 128), sizes[1], sizes[2]]
+        functools.partial(main_body, size, levels),
+        [(19, height, 128), (4, depth, height, width), (6, blocks, 128), (4, 8, 128), sizes[1], sizes[2]]
         + [sizes[0]] * slots
         + [sizes[3]] * slots
         + [sizes[4]] * slots,
-        [level, counts, dest] + given + [drop_vel, drop_frac, home],
-        3,
+        [counts, dest, strip, left, right, inner_vel, drop_vel, drop_frac, along, plane],
         [
             pltpu.VMEM((3 * table, width), jnp.float32),
             pltpu.VMEM((3 * table, 128), jnp.float32),
             pltpu.VMEM((3 * table, width), jnp.float32),
             pltpu.VMEM((3 * table, 128), jnp.float32),
             pltpu.VMEM((blocks, 8, 128), jnp.float32),
-            pltpu.VMEM((27 * CAP, 8, 128), jnp.float32),
+            pltpu.VMEM((27 * CAP + 1, 8, 128), jnp.float32),
             pltpu.VMEM((table, 128), jnp.float32),
-            pltpu.SMEM((27,), jnp.int32),
             pltpu.VMEM((2, channels, rows, 128), jnp.float32),
             pltpu.VMEM((2, 19, rows, 128), jnp.float32),
             pltpu.VMEM((2, 19, rows, 128), jnp.float32),
             pltpu.VMEM((3 * table, 2 * width), jnp.bfloat16),
             pltpu.VMEM((3 * table, width + 128), jnp.bfloat16),
-            pltpu.VMEM((2 * width + 128, blocks * 128), jnp.bfloat16),
             pltpu.VMEM((3 * table, blocks * 128), jnp.bfloat16),
             pltpu.VMEM((3 * table, blocks * 128), jnp.bfloat16),
-            pltpu.VMEM((2, table, 256), jnp.float32),
         ],
-    )
-    state, own, stay, side, north, south = outs[:6]
+        late=(0, 1, 5, 6, 7, 8, 9),
+    )
+    edge, own, stay, side, north, south = outs[:6]
     to_levels, north_levels, south_levels = (outs[6 + slots * at : 6 + slots * at + slots] for at in range(3))
     received = [shifted(north, "gy", 1), shifted(south, "gy", -1)]
     received += [to_level(value, kind, levels) for value, kind in zip(to_levels, kinds)]
     received += [to_level(value, kind, levels, "gy", 1) for value, kind in zip(north_levels, kinds)]
     received += [to_level(value, kind, levels, "gy", -1) for value, kind in zip(south_levels, kinds)]
+    (state,) = call(patch_body, [pops.shape], [inner_pops, edge], cost=long_cost())
     side_rows = (padded(face_rows(depth, height) + 9 * 6 * CAP), width)
     part, right, left = call(
         functools.partial(gather_body, levels),
         [(3, depth, height, width), side_rows, side_rows],
-        [level, own, side] + received,
-        1,
+        [own, side] + received,
         [pltpu.VMEM((4, depth, height, width), jnp.float32)],
     )
     force, arrived = call(
         functools.partial(last_body, levels),
         [(3, depth, height, width), (6, blocks + 26 * CAP, 128)],
-        [level, part, stay] + received + [shifted(right, "gx", 1), shifted(left, "gx", -1)],
+        [part, stay] + received + [shifted(right, "gx", 1), shifted(left, "gx", -1)],
     )
     return state, force, arrived
 

time: 56.1 us -> 53.8 us (0.959)
  waiting for transfers between devices: 14 us -> 8.35 us
  Pallas kernels: 22 us -> 25.1 us
    ppermute x4, waiting for transfers between devices: 10.4 us -> 6.55 us  [to_level(): lax.ppermute(value, (side, 'gz'), [(brick * levels + at, (brick + step) %...]
    pallas_call x6 -> x8, Pallas kernels: 22 us -> 25.1 us  [call(): pl.pallas_call(whole, out_shape=[jax.ShapeDtypeStruct(shape, kind[at] if...]
    ppermute x8, waiting for transfers between devices: 3.61 us -> 1.8 us  [shifted(): lax.ppermute(value, axis, [(i, (i + step) % count) for i in range(count)])]
  transfers between devices with their start and end apart: 14 -> 14, of which waited for: 4 -> 4; matrix products, arithmetic and copies ran while one was open for 0% -> 0% of each run, Pallas kernels for 10% -> 21%
where the time goes in v7:
time: 53.8 us; the launch traced here: 53.2 us
  Pallas kernels  25.1 us (47%)
  starting transfers between devices  19.1 us (36%)
  waiting for transfers between devices  8.35 us (16%)
  between operations  0.74 us (1%)
    pallas_call x8, Pallas kernels, call(): pl.pallas_call(whole, out_shape=[jax.ShapeDtypeStruct(shape, kind[at] if...  25.1 us
    ppermute x8, starting transfers between devices, shifted(): lax.ppermute(value, axis, [(i, (i + step) % count) for i in range(count)])  11.6 us
    ppermute x4, waiting for transfers between devices, to_level(): lax.ppermute(value, (side, 'gz'), [(brick * levels + at, (brick + step) %...  6.55 us
    ppermute x4, starting transfers between devices, to_level(): lax.ppermute(value, (side, 'gz'), [(brick * levels + at, (brick + step) %...  4.39 us
    ppermute x2, starting transfers between devices, to_level(): return lax.ppermute(value, 'gz', pairs)  3.1 us
    ppermute x8, waiting for transfers between devices, shifted(): lax.ppermute(value, axis, [(i, (i + step) % count) for i in range(count)])  1.8 us
  transfers between devices with their start and end apart: 14, of which 4 were waited for; matrix products, arithmetic and copies ran while one was open for 0% of the time, Pallas kernels for 21%

profile of v7, /device:TPU:0, one launch (start us, length us, event | category | flops | bytes accessed | tf_op | source)
XLA Modules:
  0.0 53.2 jit_solution(9096324595053038064)
XLA Ops:
  0.6 2.8 %shard_map.103 = (f32[20,8,8,128]{3,2,1,0:T(8,128)}, f32[20,8,128]{2,1,0:T(8,128)}, f32[552,128]{1,0:T(8,128)}, f32[376,128]{1,0:T(8,128)}, f32[65,8,128]{2,1,0:...) custom-call(f32[19,8,8,128]{3,2,1,0:T(8,128)} %refs_0_.3, bf16[19,8,8,128]{3,2,1,0:T(8,128)(2,1)} %refs_1_.3, ...), custom_call_target="tpu_custom_call" | custom-call | tf_op jit(solution)/shard_map/pallas_call | solution.py:88
  3.4 2.4 %collective-permute-start = (f32[552,128]{1,0:T(8,128)}, f32[552,128]{1,0:T(8,128)}, u32[]{:S(2)}, u32[]{:S(2)}) collective-permute-start(f32[552,128]{1,0:T(8,128)} %get-tuple-element.33), channel_id=1, source_target_pairs={{0,6},{2,0},{4,2},{6,4},{1,7},{3,1},{5,3},{7,5},{8,14},{10,8},{12,... | collective-permute-start | bytes 847880 | tf_op jit(solution)/shard_map/ppermute | solution.py:558
  5.8 1.5 %collective-permute-start.2 = (f32[65,8,128]{2,1,0:T(8,128)}, f32[65,8,128]{2,1,0:T(8,128)}, u32[]{:S(2)}, u32[]{:S(2)}) collective-permute-start(f32[65,8,128]{2,1,0:T(8,128)} %get-tuple-element.35), channel_id=1, source_target_pairs={{0,1},{1,0},{2,3},{3,2},{4,5},{5,4},{6,7},{7,6},{8,9},{9,8},{10,11... | collective-permute-start | bytes 798728 | tf_op jit(solution)/shard_map/ppermute | solution.py:568
  7.3 1.7 %collective-permute-start.3 = (f32[208,128]{1,0:T(8,128)}, f32[208,128]{1,0:T(8,128)}, u32[]{:S(2)}, u32[]{:S(2)}) collective-permute-start(f32[208,128]{1,0:T(8,128)} %get-tuple-element.36), channel_id=1, source_target_pairs={{0,7},{1,6},{2,1},{3,0},{4,3},{5,2},{6,5},{7,4},{8,15},{9,14},{10,... | collective-permute-start | bytes 319496 | tf_op jit(solution)/shard_map/ppermute | solution.py:570
  9.0 0.1 collective-permute-start.4
  9.1 3.8 %shard_map.105 = (bf16[384,2048]{1,0:T(8,128)(2,1)}, f32[8,128,256]{2,1,0:T(8,128)}, f32[8,128]{1,0:T(8,128)}) custom-call(f32[3,16,128]{2,1,0:T(8,128)} %refs_7_.1, s32[16,128]{1,0:T(8,128)} %refs_1_.4), custom_call_target="tpu_custom_call" | custom-call | flops 100000000 | bytes 4194304 | tf_op jit(solution)/shard_map/pallas_call | solution.py:88
  12.9 3.9 %collective-permute-done.4.refs_5_ = f32[136,128]{1,0:T(8,128)} collective-permute-done((f32[136,128]{1,0:T(8,128)}, f32[136,128]{1,0:T(8,128)}, u32[]{:S(2)}, u32[]{:S(2)}) %collective-permute-start.4) | collective-permute-done | bytes 69664 | tf_op jit(solution)/shard_map/ppermute | solution.py:570
  16.9 1.9 %shard_map.106 = (f32[20,16,128]{2,1,0:T(8,128)}, f32[6,16,128]{2,1,0:T(8,128)}, f32[9,16,128]{2,1,0:T(8,128)}) custom-call(f32[20,8,128]{2,1,0:T(8,128)} %get-tuple-element.39.refs_0_, f32[552,128]{1,0:T(8,128)} %collective-permute-done.refs_1_, f32[376,128]{1,0:T(8,128)} %collective-permute-done.1.refs_2_, f32[65,8,128]{2,1,0:T(8,128)} %collective-permute-done.2.refs_3_, ...), custom_call_target="tpu_custom_call" | custom-call | tf_op jit(solution)/shard_map/pallas_call | solution.py:88
  18.7 3.9 %collective-permute-start.6 = (f32[9,16,128]{2,1,0:T(8,128)}, f32[9,16,128]{2,1,0:T(8,128)}, u32[]{:S(2)}, u32[]{:S(2)}) collective-permute-start(f32[9,16,128]{2,1,0:T(8,128)} %get-tuple-element.43), channel_id=1, source_target_pairs={{0,24},{8,0},{16,8},{24,16},{1,25},{9,1},{17,9},{25,17},{2,26},{10... | collective-permute-start | bytes 221192 | tf_op jit(solution)/shard_map/ppermute | solution.py:558
  22.6 5.0 %shard_map.104 = (f32[19,8,8,128]{3,2,1,0:T(8,128)}, f32[3,11,16,128]{3,2,1,0:T(8,128)}) custom-call(f32[20,8,8,128]{3,2,1,0:T(8,128)} %get-tuple-element.32.refs_0_, f32[552,128]{1,0:T(8,128)} %collective-permute-done.refs_1_, f32[376,128]{1,0:T(8,128)} %collective-permute-done.1.refs_2_, f32[65,8,128]{2,1,0:T(8,128)} %collective-permute-done.2.refs_3_, ...), custom_call_target="tpu_custom_call" | custom-call | flops 100000000 | bytes 4194304 | tf_op jit(solution)/shard_map/pallas_call | solution.py:88
  27.6 1.2 %collective-permute-done.5.refs_3_ = f32[6,16,128]{2,1,0:T(8,128)} collective-permute-done((f32[6,16,128]{2,1,0:T(8,128)}, f32[6,16,128]{2,1,0:T(8,128)}, u32[]{:S(2)}, u32[]{:S(2)}) %collective-permute-start.5) | collective-permute-done | bytes 49184 | tf_op jit(solution)/shard_map/ppermute | solution.py:558
  28.8 5.6 %shard_map.107 = (f32[19,8,128]{2,1,0:T(8,128)}, f32[4,8,8,128]{3,2,1,0:T(8,128)}, f32[6,16,128]{2,1,0:T(8,128)}, f32[4,8,128]{2,1,0:T(8,128)}, f32[112,128]{1,0...) custom-call(s32[16]{0:T(128)} %refs_0_.5, s32[16]{0:T(128)} %refs_1_.5, ...), custom_call_target="tpu_custom_call" | custom-call | tf_op jit(solution)/shard_map/pallas_call | solution.py:88
  34.4 0.1 collective-permute-start.7
  34.5 1.6 %collective-permute-start.9 = (f32[112,128]{1,0:T(8,128)}, f32[112,128]{1,0:T(8,128)}, u32[]{:S(2)}, u32[]{:S(2)}) collective-permute-start(f32[112,128]{1,0:T(8,128)} %get-tuple-element.52), channel_id=1, source_target_pairs={{0,1},{1,0},{2,3},{3,2},{4,5},{5,4},{6,7},{7,6},{8,9},{9,8},{10,11... | collective-permute-start | bytes 172040 | tf_op jit(solution)/shard_map/ppermute | solution.py:568
  36.1 1.4 %collective-permute-start.8 = (f32[80,128]{1,0:T(8,128)}, f32[80,128]{1,0:T(8,128)}, u32[]{:S(2)}, u32[]{:S(2)}) collective-permute-start(f32[80,128]{1,0:T(8,128)} %get-tuple-element.51), channel_id=1, source_target_pairs={{0,6},{2,0},{4,2},{6,4},{1,7},{3,1},{5,3},{7,5},{8,14},{10,8},{12,... | collective-permute-start | bytes 122888 | tf_op jit(solution)/shard_map/ppermute | solution.py:558
  37.4 0.7 %collective-permute-start.10 = (f32[64,128]{1,0:T(8,128)}, f32[64,128]{1,0:T(8,128)}, u32[]{:S(2)}, u32[]{:S(2)}) collective-permute-start(f32[64,128]{1,0:T(8,128)} %get-tuple-element.53), channel_id=1, source_target_pairs={{0,3},{1,2},{2,5},{3,4},{4,7},{5,6},{6,1},{7,0},{8,11},{9,10},{10,... | collective-permute-start | bytes 98312 | tf_op jit(solution)/shard_map/ppermute | solution.py:570
  38.1 2.0 %collective-permute-start.11 = (f32[56,128]{1,0:T(8,128)}, f32[56,128]{1,0:T(8,128)}, u32[]{:S(2)}, u32[]{:S(2)}) collective-permute-start(f32[56,128]{1,0:T(8,128)} %get-tuple-element.54), channel_id=1, source_target_pairs={{0,7},{1,6},{2,1},{3,0},{4,3},{5,2},{6,5},{7,4},{8,15},{9,14},{10,... | collective-permute-start | bytes 86024 | tf_op jit(solution)/shard_map/ppermute | solution.py:570
  40.1 2.6 %collective-permute-done.11.refs_6_ = f32[56,128]{1,0:T(8,128)} collective-permute-done((f32[56,128]{1,0:T(8,128)}, f32[56,128]{1,0:T(8,128)}, u32[]{:S(2)}, u32[]{:S(2)}) %collective-permute-start.11) | collective-permute-done | bytes 28704 | tf_op jit(solution)/shard_map/ppermute | solution.py:570
  42.7 1.8 %shard_map.109 = (f32[3,8,8,128]{3,2,1,0:T(8,128)}, f32[120,128]{1,0:T(8,128)}, f32[120,128]{1,0:T(8,128)}) custom-call(f32[4,8,8,128]{3,2,1,0:T(8,128)} %get-tuple-element.48.refs_0_, f32[4,8,128]{2,1,0:T(8,128)} %get-tuple-element.49.refs_1_, f32[112,128]{1,0:T(8,128)} %collective-permute-done.7.refs_2_, f32[80,128]{1,0:T(8,128)} %collective-permute-done.8.refs_3_, ...), custom_call_target="tpu_custom_call" | custom-call | tf_op jit(solution)/shard_map/pallas_call | solution.py:88
  44.5 0.1 collective-permute-start.12
  44.6 3.8 %collective-permute-start.13 = (f32[120,128]{1,0:T(8,128)}, f32[120,128]{1,0:T(8,128)}, u32[]{:S(2)}, u32[]{:S(2)}) collective-permute-start(f32[120,128]{1,0:T(8,128)} %get-tuple-element.58), channel_id=1, source_target_pairs={{0,24},{8,0},{16,8},{24,16},{1,25},{9,1},{17,9},{25,17},{2,26},{10... | collective-permute-start | bytes 184328 | tf_op jit(solution)/shard_map/ppermute | solution.py:558
  48.4 2.1 %shard_map.108 = f32[19,8,8,128]{3,2,1,0:T(8,128)} custom-call(f32[19,8,8,128]{3,2,1,0:T(8,128)} %get-tuple-element.38.refs_0_, f32[19,8,128]{2,1,0:T(8,128)} %get-tuple-element.47.refs_1_), custom_call_target="tpu_custom_call" | custom-call | flops 100000000 | bytes 4194304 | tf_op jit(solution)/shard_map/pallas_call | solution.py:88
  50.5 0.6 %collective-permute-done.12.refs_7_ = f32[120,128]{1,0:T(8,128)} collective-permute-done((f32[120,128]{1,0:T(8,128)}, f32[120,128]{1,0:T(8,128)}, u32[]{:S(2)}, u32[]{:S(2)}) %collective-permute-start.12) | collective-permute-done | bytes 61472 | tf_op jit(solution)/shard_map/ppermute | solution.py:558
  51.2 2.1 %shard_map.110 = (f32[3,8,8,128]{3,2,1,0:T(8,128)}, f32[6,68,128]{2,1,0:T(8,128)}) custom-call(f32[3,8,8,128]{3,2,1,0:T(8,128)} %get-tuple-element.55.refs_0_, f32[6,16,128]{2,1,0:T(8,128)} %get-tuple-element.56.refs_1_, f32[112,128]{1,0:T(8,128)} %collective-permute-done.7.refs_2_, f32[80,128]{1,0:T(8,128)} %collective-permute-done.8.refs_3_, ...), custom_call_target="tpu_custom_call" | custom-call | tf_op jit(solution)/shard_map/pallas_call | solution.py:88
  (12 shorter events, 0.0 us)
Async XLA Ops:
  3.4 13.4 %collective-permute-start = (f32[552,128]{1,0:T(8,128)}, f32[552,128]{1,0:T(8,128)}, u32[]{:S(2)}, u32[]{:S(2)}) collective-permute-start(f32[552,128]{1,0:T(8,128)} %get-tuple-element.33), channel_id=1, source_target_pairs={{0,6},{2,0},{4,2},{6,4},{1,7},{3,1},{5,3},{7,5},{8,14},{10,8},{12,... | collective-permute-start | bytes 847880 | tf_op jit(solution)/shard_map/ppermute | solution.py:558
  5.8 11.0 %collective-permute-start.2 = (f32[65,8,128]{2,1,0:T(8,128)}, f32[65,8,128]{2,1,0:T(8,128)}, u32[]{:S(2)}, u32[]{:S(2)}) collective-permute-start(f32[65,8,128]{2,1,0:T(8,128)} %get-tuple-element.35), channel_id=1, source_target_pairs={{0,1},{1,0},{2,3},{3,2},{4,5},{5,4},{6,7},{7,6},{8,9},{9,8},{10,11... | collective-permute-start | bytes 798728 | tf_op jit(solution)/shard_map/ppermute | solution.py:568
  7.3 9.5 %collective-permute-start.1 = (f32[376,128]{1,0:T(8,128)}, f32[376,128]{1,0:T(8,128)}, u32[]{:S(2)}, u32[]{:S(2)}) collective-permute-start(f32[376,128]{1,0:T(8,128)} %get-tuple-element.34), channel_id=1, source_target_pairs={{0,2},{2,4},{4,6},{6,0},{1,3},{3,5},{5,7},{7,1},{8,10},{10,12},{12... | collective-permute-start | bytes 577544 | tf_op jit(solution)/shard_map/ppermute | solution.py:558
  7.3 9.5 %collective-permute-start.3 = (f32[208,128]{1,0:T(8,128)}, f32[208,128]{1,0:T(8,128)}, u32[]{:S(2)}, u32[]{:S(2)}) collective-permute-start(f32[208,128]{1,0:T(8,128)} %get-tuple-element.36), channel_id=1, source_target_pairs={{0,7},{1,6},{2,1},{3,0},{4,3},{5,2},{6,5},{7,4},{8,15},{9,14},{10,... | collective-permute-start | bytes 319496 | tf_op jit(solution)/shard_map/ppermute | solution.py:570
  9.0 7.8 %collective-permute-start.4 = (f32[136,128]{1,0:T(8,128)}, f32[136,128]{1,0:T(8,128)}, u32[]{:S(2)}, u32[]{:S(2)}) collective-permute-start(f32[136,128]{1,0:T(8,128)} %get-tuple-element.37), channel_id=1, source_target_pairs={{0,3},{1,2},{2,5},{3,4},{4,7},{5,6},{6,1},{7,0},{8,11},{9,10},{10,... | collective-permute-start | bytes 208904 | tf_op jit(solution)/shard_map/ppermute | solution.py:570
  18.7 10.1 %collective-permute-start.6 = (f32[9,16,128]{2,1,0:T(8,128)}, f32[9,16,128]{2,1,0:T(8,128)}, u32[]{:S(2)}, u32[]{:S(2)}) collective-permute-start(f32[9,16,128]{2,1,0:T(8,128)} %get-tuple-element.43), channel_id=1, source_target_pairs={{0,24},{8,0},{16,8},{24,16},{1,25},{9,1},{17,9},{25,17},{2,26},{10... | collective-permute-start | bytes 221192 | tf_op jit(solution)/shard_map/ppermute | solution.py:558
  22.6 6.2 %collective-permute-start.5 = (f32[6,16,128]{2,1,0:T(8,128)}, f32[6,16,128]{2,1,0:T(8,128)}, u32[]{:S(2)}, u32[]{:S(2)}) collective-permute-start(f32[6,16,128]{2,1,0:T(8,128)} %get-tuple-element.42), channel_id=1, source_target_pairs={{0,8},{8,16},{16,24},{24,0},{1,9},{9,17},{17,25},{25,1},{2,10},{10... | collective-permute-start | bytes 147464 | tf_op jit(solution)/shard_map/ppermute | solution.py:558
  34.4 8.3 %collective-permute-start.7 = (f32[112,128]{1,0:T(8,128)}, f32[112,128]{1,0:T(8,128)}, u32[]{:S(2)}, u32[]{:S(2)}) collective-permute-start(f32[112,128]{1,0:T(8,128)} %get-tuple-element.50), channel_id=1, source_target_pairs={{0,2},{2,4},{4,6},{6,0},{1,3},{3,5},{5,7},{7,1},{8,10},{10,12},{12... | collective-permute-start | bytes 172040 | tf_op jit(solution)/shard_map/ppermute | solution.py:558
  34.5 8.2 %collective-permute-start.9 = (f32[112,128]{1,0:T(8,128)}, f32[112,128]{1,0:T(8,128)}, u32[]{:S(2)}, u32[]{:S(2)}) collective-permute-start(f32[112,128]{1,0:T(8,128)} %get-tuple-element.52), channel_id=1, source_target_pairs={{0,1},{1,0},{2,3},{3,2},{4,5},{5,4},{6,7},{7,6},{8,9},{9,8},{10,11... | collective-permute-start | bytes 172040 | tf_op jit(solution)/shard_map/ppermute | solution.py:568
  36.1 6.7 %collective-permute-start.8 = (f32[80,128]{1,0:T(8,128)}, f32[80,128]{1,0:T(8,128)}, u32[]{:S(2)}, u32[]{:S(2)}) collective-permute-start(f32[80,128]{1,0:T(8,128)} %get-tuple-element.51), channel_id=1, source_target_pairs={{0,6},{2,0},{4,2},{6,4},{1,7},{3,1},{5,3},{7,5},{8,14},{10,8},{12,... | collective-permute-start | bytes 122888 | tf_op jit(solution)/shard_map/ppermute | solution.py:558
  37.4 5.3 %collective-permute-start.10 = (f32[64,128]{1,0:T(8,128)}, f32[64,128]{1,0:T(8,128)}, u32[]{:S(2)}, u32[]{:S(2)}) collective-permute-start(f32[64,128]{1,0:T(8,128)} %get-tuple-element.53), channel_id=1, source_target_pairs={{0,3},{1,2},{2,5},{3,4},{4,7},{5,6},{6,1},{7,0},{8,11},{9,10},{10,... | collective-permute-start | bytes 98312 | tf_op jit(solution)/shard_map/ppermute | solution.py:570
  38.1 4.6 %collective-permute-start.11 = (f32[56,128]{1,0:T(8,128)}, f32[56,128]{1,0:T(8,128)}, u32[]{:S(2)}, u32[]{:S(2)}) collective-permute-start(f32[56,128]{1,0:T(8,128)} %get-tuple-element.54), channel_id=1, source_target_pairs={{0,7},{1,6},{2,1},{3,0},{4,3},{5,2},{6,5},{7,4},{8,15},{9,14},{10,... | collective-permute-start | bytes 86024 | tf_op jit(solution)/shard_map/ppermute | solution.py:570
  44.5 6.7 %collective-permute-start.12 = (f32[120,128]{1,0:T(8,128)}, f32[120,128]{1,0:T(8,128)}, u32[]{:S(2)}, u32[]{:S(2)}) collective-permute-start(f32[120,128]{1,0:T(8,128)} %get-tuple-element.57), channel_id=1, source_target_pairs={{0,8},{8,16},{16,24},{24,0},{1,9},{9,17},{17,25},{25,1},{2,10},{10... | collective-permute-start | bytes 184328 | tf_op jit(solution)/shard_map/ppermute | solution.py:558
  44.6 6.6 %collective-permute-start.13 = (f32[120,128]{1,0:T(8,128)}, f32[120,128]{1,0:T(8,128)}, u32[]{:S(2)}, u32[]{:S(2)}) collective-permute-start(f32[120,128]{1,0:T(8,128)} %get-tuple-element.58), channel_id=1, source_target_pairs={{0,24},{8,0},{16,8},{24,16},{1,25},{9,1},{17,9},{25,17},{2,26},{10... | collective-permute-start | bytes 184328 | tf_op jit(solution)/shard_map/ppermute | solution.py:558

commit v8 on v7

--- a/solution.py
+++ b/solution.py
@@ -116,17 +116,13 @@
 
 
 def rim(kind):
-    count, reach = (LOW, low_reach) if kind == "low" else (HIGH, high_reach)
+    side = 1 if kind == "low" else -1
     return [
         (step, channel)
-        for step in range(1, count + 1)
+        for step in (1, 2)
         for channel in range(channels)
-        if step <= reach(ways[channel][0])
+        if step <= 1 + side * ways[channel][0]
     ]
-
-
-def rim_count(kind):
-    return LOW if kind == "low" else HIGH
 
 
 def rim_sides(levels):
@@ -211,7 +207,7 @@
             free.append(8)
         table.append((channel, tile, 8 - free[tile], -count))
         free[tile] += count
-    return table, len(free)
+    return table, max(len(free), 9)
 
 
 def moments(cells):
@@ -394,17 +390,11 @@
             target[tile] = value
 
 
-def inner_body(levels, level_ref, *rest):
-    (posts_ref, above_ref, below_ref), parts, rest = split_given(levels, rest)
-    pops_ref, vel_ref, ext, pulled, second = rest
-    level = level_ref[0]
-    unpack(levels, level, posts_ref, above_ref, below_ref, *parts, ext)
-    depth, height, width = posts_ref.shape[1:]
+def substeps(levels, level, size, ext, pulled, second):
+    depth, height, width = size
     rows = height + 8
 
-    def pull(source, layer, at):
-        bottom = (level == 0) & (layer == 0)
-        top = (level == levels - 1) & (layer == depth - 1)
+    def pull(source, layer, at, target):
         for index in range(19):
             way_z, way_y, way_x = ways[index]
             value = source[index, at - way_z]
@@ -412,10 +402,11 @@
                 value = pltpu.roll(value, way_x % width, 1)
             if way_y != 0:
                 value = pltpu.roll(value, way_y % rows, 0)
-            if way_z != 0:
-                wall = bottom if way_z == 1 else top
-                value = jnp.where(wall, source[opposite[index], at], value)
-            pulled[index] = value
+            if way_z == 1 and layer == 0:
+                value = jnp.where(level == 0, source[opposite[index], at], value)
+            if way_z == -1 and layer == depth - 1:
+                value = jnp.where(level == levels - 1, source[opposite[index], at], value)
+            target[index] = value
 
     tiles = [
         (slice(row, row + 8), slice(col, col + 128))
@@ -423,42 +414,78 @@
         for col in range(0, width, 128)
     ]
 
-    def first_step(number, carry):
-        at = number + 1
-        pull(ext, at - LOW, at)
-        for tile in tiles:
-            posts = relaxed([pulled[(index, *tile)] for index in range(19)])
-            inside = ext[(19, at, *tile)] > 0.5
-            for index in range(19):
-                second[(index, number, *tile)] = jnp.where(inside, ext[(index, at, *tile)], posts[index])
-        return carry
-
-    first = jnp.where(level == 0, LOW - 1, 0)
-    final = jnp.where(level == levels - 1, depth + LOW - 1, depth + LOW + HIGH - 2)
-    lax.fori_loop(first, final, first_step, 0)
-
-    def second_step(number, carry):
-        pull(second, number - 1, number + 1)
-        for tile in tiles:
-            density, moment = moments([pulled[(index, *tile)] for index in range(19)])
-            inverse = 1.0 / density
-            for axis in range(3):
-                vel_ref[(axis, number, *tile)] = moment[axis] * inverse
-        return carry
-
-    def second_inner(number, carry):
-        second_step(number, carry)
+    def first_steps(layers):
+        for layer in layers:
+            at = LOW + layer
+            cells = pulled.at[at % pulled.shape[0]]
+            pull(ext, layer, at, cells)
+            for tile in tiles:
+                posts = relaxed([cells[(index, *tile)] for index in range(19)])
+                inside = ext[(19, at, *tile)] > 0.5
+                for index in range(19):
+                    second[(index, at - 1, *tile)] = jnp.where(
+                        inside, ext[(index, at, *tile)], posts[index]
+                    )
+
+    def second_steps(layers, put):
+        for layer in layers:
+            at = LOW - 1 + layer
+            cells = pulled.at[at % pulled.shape[0]]
+            pull(second, layer, at, cells)
+            for tile in tiles:
+                density, moment = moments([cells[(index, *tile)] for index in range(19)])
+                inverse = 1.0 / density
+                for axis in range(3):
+                    put(axis, layer, tile, moment[axis] * inverse)
+            yield layer, cells
+
+    return first_steps, second_steps
+
+
+def inner_body(levels, level_ref, *rest):
+    (posts_ref, above_ref, below_ref), parts, rest = split_given(levels, rest)
+    pops_ref, vel_ref, ext, pulled, second = rest
+    level = level_ref[0]
+    unpack(levels, level, posts_ref, above_ref, below_ref, *parts, ext)
+    depth, height, _ = size = posts_ref.shape[1:]
+    first_steps, second_steps = substeps(levels, level, size, ext, pulled, second)
+
+    def put(axis, layer, tile, value):
+        vel_ref[(axis, layer, *tile)] = value
+
+    pl.when(level != 0)(lambda: first_steps([-1]))
+    pl.when(level != levels - 1)(lambda: first_steps([depth]))
+    first_steps(range(depth))
+    for layer, cells in second_steps(range(depth), put):
         for index in range(19):
-            pops_ref[index, number - 1] = pulled[index, :height, :]
-        return carry
-
-    lax.fori_loop(jnp.where(level == 0, 1, 0), 1, second_step, 0)
-    lax.fori_loop(1, depth + 1, second_inner, 0)
-    lax.fori_loop(depth + 1, jnp.where(level == levels - 1, depth + 1, depth + 3), second_step, 0)
+            pops_ref[index, layer] = cells[index, :height, :]
+
+
+def face_body(levels, level_ref, *rest):
+    (posts_ref, above_ref, below_ref), parts, rest = split_given(levels, rest)
+    slots = len(rim_sizes(levels))
+    faces, (ext, pulled, second) = rest[:slots], rest[slots:]
+    level = level_ref[0]
+    unpack(levels, level, posts_ref, above_ref, below_ref, *parts, ext)
+    size = posts_ref.shape[1:]
+    depth = size[0]
+    first_steps, second_steps = substeps(levels, level, size, ext, pulled, second)
+    for kind, sender, _, slot in force_sides(levels):
+        wanted = [depth - 1] if kind == "up" else [0, 1]
+
+        def work(wanted=wanted, slot=slot):
+            def put(axis, layer, tile, value):
+                faces[slot][(axis, layer - wanted[0], *tile)] = value
+
+            first_steps(range(wanted[0] - 1, wanted[-1] + 2))
+            for _ in second_steps(wanted, put):
+                pass
+
+        guarded(level, sender, work)
 
 
 def edge_body(
-    size, levels, level_ref, strip_ref, left_ref, right_ref, inner_vel,
+    size, levels, level_ref, strip_ref, left_ref, right_ref, inner_vel, faces,
     edge_ref, vel_ref, beyond_ref, sides, pulled, second,
 ):
     depth, height, width = size
@@ -503,6 +530,15 @@
     valid = (row < height + 2) | (row == rows - 1)
     outside = (lane < 2) | (lane == 127)
     vel_in = inner_vel.take()
+    faces = [face.take() for face in faces]
+
+    def inner(axis, layer, cols):
+        if layer == 0:
+            return faces[0][axis, 0, :, cols]
+        if layer > depth:
+            return faces[-1][axis, layer - depth - 1, :, cols]
+        return vel_in[axis, layer - 1, :, cols]
+
     table = table_rows(depth, height)
     vel_ref[...] = jnp.zeros_like(vel_ref)
     beyond_ref[...] = jnp.zeros_like(beyond_ref)
@@ -524,7 +560,7 @@
             shift = -(8 * (layer - 1 + LOW) + 4)
             turned = lane_roll(main, shift)
             for col in range(0, width, 128):
-                cells = vel_in[axis, layer, :, col : col + 128]
+                cells = inner(axis, layer, slice(col, col + 128))
                 if col == 0 or col == width - 128:
                     mask = (lane < 2) & (col == 0) | (lane >= 126) & (col == width - 128)
                     cells = jnp.where(mask, turned, cells)
@@ -612,18 +648,23 @@
         + [(3 + 2 * slots + at, rim_strip_rows()[1][1]) for at in range(slots)],
     )
     left, right = shifted(right, "gx", 1), shifted(left, "gx", -1)
+    scratch = [
+        ext,
+        pltpu.VMEM((4, 19, rows, width), jnp.float32),
+        pltpu.VMEM((19, deep - 2, rows, width), jnp.float32),
+    ]
+    faces = call(
+        functools.partial(face_body, levels), [(3, 2, rows, width)] * slots, [posts] + given, scratch
+    )
+    faces = [to_level(value, kind, levels) for value, kind in zip(faces, ["up", "down"])]
     inner_pops, inner_vel = call(
         functools.partial(inner_body, levels),
-        [pops.shape, (3, depth + 3, rows, width)],
+        [pops.shape, (3, depth, rows, width)],
         [posts] + given,
-        [
-            ext,
-            pltpu.VMEM((19, rows, width), jnp.float32),
-            pltpu.VMEM((19, deep - 2, rows, width), jnp.float32),
-        ],
+        scratch,
         long_cost(),
     )
-    return [strip, left, right, inner_pops, inner_vel]
+    return strip, left, right, inner_pops, inner_vel, faces
 
 
 def phis(frac):
@@ -847,15 +888,18 @@
 
 def main_body(
     size, levels, level_ref, counts, dest, strip_ref, left_ref, right_ref, inner_vel,
-    speed, frac, along, plane, edge_ref, own_ref, stay_ref, side_ref, north_ref, south_ref, *rest,
+    speed, frac, along, plane, *rest,
 ):
     slots = len(rim_sizes(levels))
+    faces, rest = rest[:slots], rest[slots:]
+    edge_ref, own_ref, stay_ref, side_ref, north_ref, south_ref = rest[:6]
+    rest = rest[6:]
     to_levels, north_levels, south_levels = (rest[slots * at : slots * at + slots] for at in range(3))
     rest = rest[3 * slots :]
     vel_ref, beyond_ref, spread_ref, outer_ref, state_ref, outbox, strip = rest[:7]
     counts_ref, dest_ref = counts.take(), dest.take()
     edge_body(
-        size, levels, level_ref, strip_ref, left_ref, right_ref, inner_vel,
+        size, levels, level_ref, strip_ref, left_ref, right_ref, inner_vel, faces,
         edge_ref, vel_ref, beyond_ref, *rest[7:10],
     )
 
@@ -1011,7 +1055,7 @@
         cost=long_cost(),
         kind=[jnp.bfloat16, jnp.float32, jnp.float32],
     )
-    strip, left, right, inner_pops, inner_vel = wide_exchange(pops, coarse_pops, interface, ready)
+    strip, left, right, inner_pops, inner_vel, faces = wide_exchange(pops, coarse_pops, interface, ready)
     sizes = [(count + GROUP, width) for count in message_rows(depth)]
     outs = call(
         functools.partial(main_body, size, levels),
@@ -1019,7 +1063,7 @@
         + [sizes[0]] * slots
         + [sizes[3]] * slots
         + [sizes[4]] * slots,
-        [counts, dest, strip, left, right, inner_vel, drop_vel, drop_frac, along, plane],
+        [counts, dest, strip, left, right, inner_vel, drop_vel, drop_frac, along, plane] + faces,
         [
             pltpu.VMEM((3 * table, width), jnp.float32),
             pltpu.VMEM((3 * table, 128), jnp.float32),
@@ -1036,7 +1080,7 @@
             pltpu.VMEM((3 * table, blocks * 128), jnp.bfloat16),
             pltpu.VMEM((3 * table, blocks * 128), jnp.bfloat16),
         ],
-        late=(0, 1, 5, 6, 7, 8, 9),
+        late=(0, 1, *range(5, 10 + slots)),
     )
     edge, own, stay, side, north, south = outs[:6]
     to_levels, north_levels, south_levels = (outs[6 + slots * at : 6 + slots * at + slots] for at in range(3))

time: 53.8 us -> 51.3 us (0.954)
  waiting for transfers between devices: 8.35 us -> 5.29 us
  Pallas kernels: 25.1 us -> 25.8 us
    ppermute x4, waiting for transfers between devices: 6.55 us -> 3.82 us  [to_level(): lax.ppermute(value, (side, 'gz'), [(brick * levels + at, (brick + step) %...]
    ppermute x8, waiting for transfers between devices: 1.8 us -> 0.87 us  [shifted(): lax.ppermute(value, axis, [(i, (i + step) % count) for i in range(count)])]
    pallas_call x8 -> x9, Pallas kernels: 25.1 us -> 25.8 us  [call(): pl.pallas_call(whole, out_shape=[jax.ShapeDtypeStruct(shape, kind[at] if...]
    ppermute x2 -> x3, waiting for transfers between devices: 0.01 us -> 0.6 us  [to_level(): return lax.ppermute(value, 'gz', pairs)]
    ppermute x2 -> x3, starting transfers between devices: 3.1 us -> 3.12 us  [to_level(): return lax.ppermute(value, 'gz', pairs)]
  transfers between devices with their start and end apart: 14 -> 15, of which waited for: 4 -> 5; matrix products, arithmetic and copies ran while one was open for 0% -> 0% of each run, Pallas kernels for 21% -> 22%
where the time goes in v8:
time: 51.3 us; the launch traced here: 51 us
  Pallas kernels  25.8 us (50%)
  starting transfers between devices  19.1 us (37%)
  waiting for transfers between devices  5.29 us (10%)
  between operations  0.74 us (1%)
    pallas_call x9, Pallas kernels, call(): pl.pallas_call(whole, out_shape=[jax.ShapeDtypeStruct(shape, kind[at] if...  25.8 us
    ppermute x8, starting transfers between devices, shifted(): lax.ppermute(value, axis, [(i, (i + step) % count) for i in range(count)])  11.6 us
    ppermute x4, starting transfers between devices, to_level(): lax.ppermute(value, (side, 'gz'), [(brick * levels + at, (brick + step) %...  4.39 us
    ppermute x4, waiting for transfers between devices, to_level(): lax.ppermute(value, (side, 'gz'), [(brick * levels + at, (brick + step) %...  3.82 us
    ppermute x3, starting transfers between devices, to_level(): return lax.ppermute(value, 'gz', pairs)  3.12 us
  transfers between devices with their start and end apart: 15, of which 5 were waited for; matrix products, arithmetic and copies ran while one was open for 0% of the time, Pallas kernels for 22%

profile of v8, /device:TPU:0, one launch (start us, length us, event | category | flops | bytes accessed | tf_op | source)
XLA Modules:
  0.0 51.0 jit_solution(4182446559667001305)
XLA Ops:
  0.6 2.7 %shard_map.103 = (f32[20,8,8,128]{3,2,1,0:T(8,128)}, f32[20,8,128]{2,1,0:T(8,128)}, f32[552,128]{1,0:T(8,128)}, f32[376,128]{1,0:T(8,128)}, f32[25,8,128]{2,1,0:...) custom-call(f32[19,8,8,128]{3,2,1,0:T(8,128)} %refs_0_.3, bf16[19,8,8,128]{3,2,1,0:T(8,128)(2,1)} %refs_1_.3, ...), custom_call_target="tpu_custom_call" | custom-call | tf_op jit(solution)/shard_map/pallas_call | solution.py:88
  3.3 2.4 %collective-permute-start = (f32[552,128]{1,0:T(8,128)}, f32[552,128]{1,0:T(8,128)}, u32[]{:S(2)}, u32[]{:S(2)}) collective-permute-start(f32[552,128]{1,0:T(8,128)} %get-tuple-element.33), channel_id=1, source_target_pairs={{0,6},{2,0},{4,2},{6,4},{1,7},{3,1},{5,3},{7,5},{8,14},{10,8},{12,... | collective-permute-start | bytes 847880 | tf_op jit(solution)/shard_map/ppermute | solution.py:594
  5.8 1.5 %collective-permute-start.2 = (f32[25,8,128]{2,1,0:T(8,128)}, f32[25,8,128]{2,1,0:T(8,128)}, u32[]{:S(2)}, u32[]{:S(2)}) collective-permute-start(f32[25,8,128]{2,1,0:T(8,128)} %get-tuple-element.35), channel_id=1, source_target_pairs={{0,1},{1,0},{2,3},{3,2},{4,5},{5,4},{6,7},{7,6},{8,9},{9,8},{10,11... | collective-permute-start | bytes 307208 | tf_op jit(solution)/shard_map/ppermute | solution.py:604
  7.3 1.4 %collective-permute-start.3 = (f32[88,128]{1,0:T(8,128)}, f32[88,128]{1,0:T(8,128)}, u32[]{:S(2)}, u32[]{:S(2)}) collective-permute-start(f32[88,128]{1,0:T(8,128)} %get-tuple-element.36), channel_id=1, source_target_pairs={{0,7},{1,6},{2,1},{3,0},{4,3},{5,2},{6,5},{7,4},{8,15},{9,14},{10,... | collective-permute-start | bytes 135176 | tf_op jit(solution)/shard_map/ppermute | solution.py:606
  8.7 0.3 collective-permute-start.4
  9.0 3.8 %shard_map.105 = (bf16[384,2048]{1,0:T(8,128)(2,1)}, f32[8,128,256]{2,1,0:T(8,128)}, f32[8,128]{1,0:T(8,128)}) custom-call(f32[3,16,128]{2,1,0:T(8,128)} %refs_7_.1, s32[16,128]{1,0:T(8,128)} %refs_1_.4), custom_call_target="tpu_custom_call" | custom-call | flops 100000000 | bytes 4194304 | tf_op jit(solution)/shard_map/pallas_call | solution.py:88
  12.8 1.9 %collective-permute-done.4.refs_5_ = f32[56,128]{1,0:T(8,128)} collective-permute-done((f32[56,128]{1,0:T(8,128)}, f32[56,128]{1,0:T(8,128)}, u32[]{:S(2)}, u32[]{:S(2)}) %collective-permute-start.4) | collective-permute-done | bytes 28704 | tf_op jit(solution)/shard_map/ppermute | solution.py:606
  14.8 1.9 %shard_map.106 = (f32[20,16,128]{2,1,0:T(8,128)}, f32[9,16,128]{2,1,0:T(8,128)}, f32[9,16,128]{2,1,0:T(8,128)}) custom-call(f32[20,8,128]{2,1,0:T(8,128)} %get-tuple-element.39.refs_0_, f32[552,128]{1,0:T(8,128)} %collective-permute-done.refs_1_, f32[376,128]{1,0:T(8,128)} %collective-permute-done.1.refs_2_, f32[25,8,128]{2,1,0:T(8,128)} %collective-permute-done.2.refs_3_, ...), custom_call_target="tpu_custom_call" | custom-call | tf_op jit(solution)/shard_map/pallas_call | solution.py:88
  16.6 1.6 %collective-permute-start.5 = (f32[9,16,128]{2,1,0:T(8,128)}, f32[9,16,128]{2,1,0:T(8,128)}, u32[]{:S(2)}, u32[]{:S(2)}) collective-permute-start(f32[9,16,128]{2,1,0:T(8,128)} %get-tuple-element.42), channel_id=1, source_target_pairs={{0,8},{8,16},{16,24},{24,0},{1,9},{9,17},{17,25},{25,1},{2,10},{10... | collective-permute-start | bytes 221192 | tf_op jit(solution)/shard_map/ppermute | solution.py:594
  18.3 2.2 %collective-permute-start.6 = (f32[9,16,128]{2,1,0:T(8,128)}, f32[9,16,128]{2,1,0:T(8,128)}, u32[]{:S(2)}, u32[]{:S(2)}) collective-permute-start(f32[9,16,128]{2,1,0:T(8,128)} %get-tuple-element.43), channel_id=1, source_target_pairs={{0,24},{8,0},{16,8},{24,16},{1,25},{9,1},{17,9},{25,17},{2,26},{10... | collective-permute-start | bytes 221192 | tf_op jit(solution)/shard_map/ppermute | solution.py:594
  20.5 2.3 %shard_map.107 = f32[3,2,16,128]{3,2,1,0:T(8,128)} custom-call(f32[20,8,8,128]{3,2,1,0:T(8,128)} %get-tuple-element.32.refs_0_, f32[552,128]{1,0:T(8,128)} %collective-permute-done.refs_1_, f32[376,128]{1,0:T(8,128)} %collective-permute-done.1.refs_2_, f32[25,8,128]{2,1,0:T(8,128)} %collective-permute-done.2.refs_3_, ...), custom_call_target="tpu_custom_call" | custom-call | tf_op jit(solution)/shard_map/pallas_call | solution.py:88
  22.8 0.7 %collective-permute-start.7 = (f32[3,2,16,128]{3,2,1,0:T(8,128)}, f32[3,2,16,128]{3,2,1,0:T(8,128)}, u32[]{:S(2)}, u32[]{:S(2)}) collective-permute-start(f32[3,2,16,128]{3,2,1,0:T(8,128)} %shard_map.107), channel_id=1, source_target_pairs={{0,1},{1,0},{2,3},{3,2},{4,5},{5,4},{6,7},{7,6},{8,9},{9,8},{10,11... | collective-permute-start | bytes 147464 | tf_op jit(solution)/shard_map/ppermute | solution.py:604
  23.5 3.2 %shard_map.104 = (f32[19,8,8,128]{3,2,1,0:T(8,128)}, f32[3,8,16,128]{3,2,1,0:T(8,128)}) custom-call(f32[20,8,8,128]{3,2,1,0:T(8,128)} %get-tuple-element.32.refs_0_, f32[552,128]{1,0:T(8,128)} %collective-permute-done.refs_1_, f32[376,128]{1,0:T(8,128)} %collective-permute-done.1.refs_2_, f32[25,8,128]{2,1,0:T(8,128)} %collective-permute-done.2.refs_3_, ...), custom_call_target="tpu_custom_call" | custom-call | flops 100000000 | bytes 4194304 | tf_op jit(solution)/shard_map/pallas_call | solution.py:88
  26.7 0.6 %collective-permute-done.7.refs_10_ = f32[3,2,16,128]{3,2,1,0:T(8,128)} collective-permute-done((f32[3,2,16,128]{3,2,1,0:T(8,128)}, f32[3,2,16,128]{3,2,1,0:T(8,128)}, u32[]{:S(2)}, u32[]{:S(2)}) %collective-permute-start.7) | collective-permute-done | bytes 49184 | tf_op jit(solution)/shard_map/ppermute | solution.py:604
  27.3 5.9 %shard_map.108 = (f32[19,8,128]{2,1,0:T(8,128)}, f32[4,8,8,128]{3,2,1,0:T(8,128)}, f32[6,16,128]{2,1,0:T(8,128)}, f32[4,8,128]{2,1,0:T(8,128)}, f32[112,128]{1,0...) custom-call(s32[16]{0:T(128)} %refs_0_.5, s32[16]{0:T(128)} %refs_1_.5, ...), custom_call_target="tpu_custom_call" | custom-call | tf_op jit(solution)/shard_map/pallas_call | solution.py:88
  33.3 1.0 %collective-permute-start.10 = (f32[112,128]{1,0:T(8,128)}, f32[112,128]{1,0:T(8,128)}, u32[]{:S(2)}, u32[]{:S(2)}) collective-permute-start(f32[112,128]{1,0:T(8,128)} %get-tuple-element.52), channel_id=1, source_target_pairs={{0,1},{1,0},{2,3},{3,2},{4,5},{5,4},{6,7},{7,6},{8,9},{9,8},{10,11... | collective-permute-start | bytes 172040 | tf_op jit(solution)/shard_map/ppermute | solution.py:604
  34.3 1.4 %collective-permute-start.9 = (f32[80,128]{1,0:T(8,128)}, f32[80,128]{1,0:T(8,128)}, u32[]{:S(2)}, u32[]{:S(2)}) collective-permute-start(f32[80,128]{1,0:T(8,128)} %get-tuple-element.51), channel_id=1, source_target_pairs={{0,6},{2,0},{4,2},{6,4},{1,7},{3,1},{5,3},{7,5},{8,14},{10,8},{12,... | collective-permute-start | bytes 122888 | tf_op jit(solution)/shard_map/ppermute | solution.py:594
  35.6 2.6 %collective-permute-start.12 = (f32[56,128]{1,0:T(8,128)}, f32[56,128]{1,0:T(8,128)}, u32[]{:S(2)}, u32[]{:S(2)}) collective-permute-start(f32[56,128]{1,0:T(8,128)} %get-tuple-element.54), channel_id=1, source_target_pairs={{0,7},{1,6},{2,1},{3,0},{4,3},{5,2},{6,5},{7,4},{8,15},{9,14},{10,... | collective-permute-start | bytes 86024 | tf_op jit(solution)/shard_map/ppermute | solution.py:606
  38.3 1.8 %collective-permute-done.12.refs_6_ = f32[56,128]{1,0:T(8,128)} collective-permute-done((f32[56,128]{1,0:T(8,128)}, f32[56,128]{1,0:T(8,128)}, u32[]{:S(2)}, u32[]{:S(2)}) %collective-permute-start.12) | collective-permute-done | bytes 28704 | tf_op jit(solution)/shard_map/ppermute | solution.py:606
  40.2 1.8 %shard_map.110 = (f32[3,8,8,128]{3,2,1,0:T(8,128)}, f32[120,128]{1,0:T(8,128)}, f32[120,128]{1,0:T(8,128)}) custom-call(f32[4,8,8,128]{3,2,1,0:T(8,128)} %get-tuple-element.48.refs_0_, f32[4,8,128]{2,1,0:T(8,128)} %get-tuple-element.49.refs_1_, f32[112,128]{1,0:T(8,128)} %collective-permute-done.8.refs_2_, f32[80,128]{1,0:T(8,128)} %collective-permute-done.9.refs_3_, ...), custom_call_target="tpu_custom_call" | custom-call | tf_op jit(solution)/shard_map/pallas_call | solution.py:88
  42.1 3.8 %collective-permute-start.14 = (f32[120,128]{1,0:T(8,128)}, f32[120,128]{1,0:T(8,128)}, u32[]{:S(2)}, u32[]{:S(2)}) collective-permute-start(f32[120,128]{1,0:T(8,128)} %get-tuple-element.58), channel_id=1, source_target_pairs={{0,24},{8,0},{16,8},{24,16},{1,25},{9,1},{17,9},{25,17},{2,26},{10... | collective-permute-start | bytes 184328 | tf_op jit(solution)/shard_map/ppermute | solution.py:594
  45.9 2.1 %shard_map.109 = f32[19,8,8,128]{3,2,1,0:T(8,128)} custom-call(f32[19,8,8,128]{3,2,1,0:T(8,128)} %get-tuple-element.38.refs_0_, f32[19,8,128]{2,1,0:T(8,128)} %get-tuple-element.47.refs_1_), custom_call_target="tpu_custom_call" | custom-call | flops 100000000 | bytes 4194304 | tf_op jit(solution)/shard_map/pallas_call | solution.py:88
  48.0 0.9 %collective-permute-done.13.refs_7_ = f32[120,128]{1,0:T(8,128)} collective-permute-done((f32[120,128]{1,0:T(8,128)}, f32[120,128]{1,0:T(8,128)}, u32[]{:S(2)}, u32[]{:S(2)}) %collective-permute-start.13) | collective-permute-done | bytes 61472 | tf_op jit(solution)/shard_map/ppermute | solution.py:594
  48.9 2.1 %shard_map.111 = (f32[3,8,8,128]{3,2,1,0:T(8,128)}, f32[6,68,128]{2,1,0:T(8,128)}) custom-call(f32[3,8,8,128]{3,2,1,0:T(8,128)} %get-tuple-element.55.refs_0_, f32[6,16,128]{2,1,0:T(8,128)} %get-tuple-element.56.refs_1_, f32[112,128]{1,0:T(8,128)} %collective-permute-done.8.refs_2_, f32[80,128]{1,0:T(8,128)} %collective-permute-done.9.refs_3_, ...), custom_call_target="tpu_custom_call" | custom-call | tf_op jit(solution)/shard_map/pallas_call | solution.py:88
  (15 shorter events, 0.3 us)
Async XLA Ops:
  3.3 11.4 %collective-permute-start = (f32[552,128]{1,0:T(8,128)}, f32[552,128]{1,0:T(8,128)}, u32[]{:S(2)}, u32[]{:S(2)}) collective-permute-start(f32[552,128]{1,0:T(8,128)} %get-tuple-element.33), channel_id=1, source_target_pairs={{0,6},{2,0},{4,2},{6,4},{1,7},{3,1},{5,3},{7,5},{8,14},{10,8},{12,... | collective-permute-start | bytes 847880 | tf_op jit(solution)/shard_map/ppermute | solution.py:594
  5.8 9.0 %collective-permute-start.1 = (f32[376,128]{1,0:T(8,128)}, f32[376,128]{1,0:T(8,128)}, u32[]{:S(2)}, u32[]{:S(2)}) collective-permute-start(f32[376,128]{1,0:T(8,128)} %get-tuple-element.34), channel_id=1, source_target_pairs={{0,2},{2,4},{4,6},{6,0},{1,3},{3,5},{5,7},{7,1},{8,10},{10,12},{12... | collective-permute-start | bytes 577544 | tf_op jit(solution)/shard_map/ppermute | solution.py:594
  5.8 9.0 %collective-permute-start.2 = (f32[25,8,128]{2,1,0:T(8,128)}, f32[25,8,128]{2,1,0:T(8,128)}, u32[]{:S(2)}, u32[]{:S(2)}) collective-permute-start(f32[25,8,128]{2,1,0:T(8,128)} %get-tuple-element.35), channel_id=1, source_target_pairs={{0,1},{1,0},{2,3},{3,2},{4,5},{5,4},{6,7},{7,6},{8,9},{9,8},{10,11... | collective-permute-start | bytes 307208 | tf_op jit(solution)/shard_map/ppermute | solution.py:604
  7.3 7.5 %collective-permute-start.3 = (f32[88,128]{1,0:T(8,128)}, f32[88,128]{1,0:T(8,128)}, u32[]{:S(2)}, u32[]{:S(2)}) collective-permute-start(f32[88,128]{1,0:T(8,128)} %get-tuple-element.36), channel_id=1, source_target_pairs={{0,7},{1,6},{2,1},{3,0},{4,3},{5,2},{6,5},{7,4},{8,15},{9,14},{10,... | collective-permute-start | bytes 135176 | tf_op jit(solution)/shard_map/ppermute | solution.py:606
  8.7 6.1 %collective-permute-start.4 = (f32[56,128]{1,0:T(8,128)}, f32[56,128]{1,0:T(8,128)}, u32[]{:S(2)}, u32[]{:S(2)}) collective-permute-start(f32[56,128]{1,0:T(8,128)} %get-tuple-element.37), channel_id=1, source_target_pairs={{0,3},{1,2},{2,5},{3,4},{4,7},{5,6},{6,1},{7,0},{8,11},{9,10},{10,... | collective-permute-start | bytes 86024 | tf_op jit(solution)/shard_map/ppermute | solution.py:606
  16.6 10.7 %collective-permute-start.5 = (f32[9,16,128]{2,1,0:T(8,128)}, f32[9,16,128]{2,1,0:T(8,128)}, u32[]{:S(2)}, u32[]{:S(2)}) collective-permute-start(f32[9,16,128]{2,1,0:T(8,128)} %get-tuple-element.42), channel_id=1, source_target_pairs={{0,8},{8,16},{16,24},{24,0},{1,9},{9,17},{17,25},{25,1},{2,10},{10... | collective-permute-start | bytes 221192 | tf_op jit(solution)/shard_map/ppermute | solution.py:594
  18.3 9.0 %collective-permute-start.6 = (f32[9,16,128]{2,1,0:T(8,128)}, f32[9,16,128]{2,1,0:T(8,128)}, u32[]{:S(2)}, u32[]{:S(2)}) collective-permute-start(f32[9,16,128]{2,1,0:T(8,128)} %get-tuple-element.43), channel_id=1, source_target_pairs={{0,24},{8,0},{16,8},{24,16},{1,25},{9,1},{17,9},{25,17},{2,26},{10... | collective-permute-start | bytes 221192 | tf_op jit(solution)/shard_map/ppermute | solution.py:594
  22.8 4.5 %collective-permute-start.7 = (f32[3,2,16,128]{3,2,1,0:T(8,128)}, f32[3,2,16,128]{3,2,1,0:T(8,128)}, u32[]{:S(2)}, u32[]{:S(2)}) collective-permute-start(f32[3,2,16,128]{3,2,1,0:T(8,128)} %shard_map.107), channel_id=1, source_target_pairs={{0,1},{1,0},{2,3},{3,2},{4,5},{5,4},{6,7},{7,6},{8,9},{9,8},{10,11... | collective-permute-start | bytes 147464 | tf_op jit(solution)/shard_map/ppermute | solution.py:604
  33.2 7.0 %collective-permute-start.8 = (f32[112,128]{1,0:T(8,128)}, f32[112,128]{1,0:T(8,128)}, u32[]{:S(2)}, u32[]{:S(2)}) collective-permute-start(f32[112,128]{1,0:T(8,128)} %get-tuple-element.50), channel_id=1, source_target_pairs={{0,2},{2,4},{4,6},{6,0},{1,3},{3,5},{5,7},{7,1},{8,10},{10,12},{12... | collective-permute-start | bytes 172040 | tf_op jit(solution)/shard_map/ppermute | solution.py:594
  33.3 6.9 %collective-permute-start.10 = (f32[112,128]{1,0:T(8,128)}, f32[112,128]{1,0:T(8,128)}, u32[]{:S(2)}, u32[]{:S(2)}) collective-permute-start(f32[112,128]{1,0:T(8,128)} %get-tuple-element.52), channel_id=1, source_target_pairs={{0,1},{1,0},{2,3},{3,2},{4,5},{5,4},{6,7},{7,6},{8,9},{9,8},{10,11... | collective-permute-start | bytes 172040 | tf_op jit(solution)/shard_map/ppermute | solution.py:604
  34.3 5.9 %collective-permute-start.9 = (f32[80,128]{1,0:T(8,128)}, f32[80,128]{1,0:T(8,128)}, u32[]{:S(2)}, u32[]{:S(2)}) collective-permute-start(f32[80,128]{1,0:T(8,128)} %get-tuple-element.51), channel_id=1, source_target_pairs={{0,6},{2,0},{4,2},{6,4},{1,7},{3,1},{5,3},{7,5},{8,14},{10,8},{12,... | collective-permute-start | bytes 122888 | tf_op jit(solution)/shard_map/ppermute | solution.py:594
  35.6 4.6 %collective-permute-start.11 = (f32[64,128]{1,0:T(8,128)}, f32[64,128]{1,0:T(8,128)}, u32[]{:S(2)}, u32[]{:S(2)}) collective-permute-start(f32[64,128]{1,0:T(8,128)} %get-tuple-element.53), channel_id=1, source_target_pairs={{0,3},{1,2},{2,5},{3,4},{4,7},{5,6},{6,1},{7,0},{8,11},{9,10},{10,... | collective-permute-start | bytes 98312 | tf_op jit(solution)/shard_map/ppermute | solution.py:606
  35.6 4.4 %collective-permute-start.12 = (f32[56,128]{1,0:T(8,128)}, f32[56,128]{1,0:T(8,128)}, u32[]{:S(2)}, u32[]{:S(2)}) collective-permute-start(f32[56,128]{1,0:T(8,128)} %get-tuple-element.54), channel_id=1, source_target_pairs={{0,7},{1,6},{2,1},{3,0},{4,3},{5,2},{6,5},{7,4},{8,15},{9,14},{10,... | collective-permute-start | bytes 86024 | tf_op jit(solution)/shard_map/ppermute | solution.py:606
  42.0 6.9 %collective-permute-start.13 = (f32[120,128]{1,0:T(8,128)}, f32[120,128]{1,0:T(8,128)}, u32[]{:S(2)}, u32[]{:S(2)}) collective-permute-start(f32[120,128]{1,0:T(8,128)} %get-tuple-element.57), channel_id=1, source_target_pairs={{0,8},{8,16},{16,24},{24,0},{1,9},{9,17},{17,25},{25,1},{2,10},{10... | collective-permute-start | bytes 184328 | tf_op jit(solution)/shard_map/ppermute | solution.py:594
  42.1 6.8 %collective-permute-start.14 = (f32[120,128]{1,0:T(8,128)}, f32[120,128]{1,0:T(8,128)}, u32[]{:S(2)}, u32[]{:S(2)}) collective-permute-start(f32[120,128]{1,0:T(8,128)} %get-tuple-element.58), channel_id=1, source_target_pairs={{0,24},{8,0},{16,8},{24,16},{1,25},{9,1},{17,9},{25,17},{2,26},{10... | collective-permute-start | bytes 184328 | tf_op jit(solution)/shard_map/ppermute | solution.py:594

commit v9 on v8

--- a/solution.py
+++ b/solution.py
@@ -207,7 +207,7 @@
             free.append(8)
         table.append((channel, tile, 8 - free[tile], -count))
         free[tile] += count
-    return table, max(len(free), 9)
+    return table, len(free)
 
 
 def moments(cells):
@@ -467,15 +467,20 @@
     faces, (ext, pulled, second) = rest[:slots], rest[slots:]
     level = level_ref[0]
     unpack(levels, level, posts_ref, above_ref, below_ref, *parts, ext)
-    size = posts_ref.shape[1:]
-    depth = size[0]
+    depth, height, _ = size = posts_ref.shape[1:]
     first_steps, second_steps = substeps(levels, level, size, ext, pulled, second)
     for kind, sender, _, slot in force_sides(levels):
         wanted = [depth - 1] if kind == "up" else [0, 1]
 
         def work(wanted=wanted, slot=slot):
             def put(axis, layer, tile, value):
-                faces[slot][(axis, layer - wanted[0], *tile)] = value
+                at = (2 * axis + layer - wanted[0]) * (height + 3)
+                row, cols = tile[0].start, tile[1]
+                if row < height:
+                    faces[slot][at + 1 + row : at + 9 + row, cols] = value
+                else:
+                    faces[slot][at + 1 + height : at + 3 + height, cols] = value[:2, :]
+                    faces[slot][at : at + 1, cols] = value[7:, :]
 
             first_steps(range(wanted[0] - 1, wanted[-1] + 2))
             for _ in second_steps(wanted, put):
@@ -533,11 +538,19 @@
     faces = [face.take() for face in faces]
 
     def inner(axis, layer, cols):
-        if layer == 0:
-            return faces[0][axis, 0, :, cols]
-        if layer > depth:
-            return faces[-1][axis, layer - depth - 1, :, cols]
-        return vel_in[axis, layer - 1, :, cols]
+        if 0 < layer <= depth:
+            return vel_in[axis, layer - 1, :, cols]
+        at = 2 * axis * (height + 3) if layer == 0 else (2 * axis + layer - depth - 1) * (height + 3)
+        face = faces[0 if layer == 0 else -1]
+        return jnp.concatenate(
+            [
+                face[at + 1 : at + height + 1, cols],
+                face[at + height + 1 : at + height + 3, cols],
+                jnp.zeros((5, 128), jnp.float32),
+                face[at : at + 1, cols],
+            ],
+            axis=0,
+        )
 
     table = table_rows(depth, height)
     vel_ref[...] = jnp.zeros_like(vel_ref)
@@ -654,7 +667,7 @@
         pltpu.VMEM((19, deep - 2, rows, width), jnp.float32),
     ]
     faces = call(
-        functools.partial(face_body, levels), [(3, 2, rows, width)] * slots, [posts] + given, scratch
+        functools.partial(face_body, levels), [(padded(6 * (height + 3)), width)] * slots, [posts] + given, scratch
     )
     faces = [to_level(value, kind, levels) for value, kind in zip(faces, ["up", "down"])]
     inner_pops, inner_vel = call(
@@ -887,11 +900,10 @@
 
 
 def main_body(
-    size, levels, level_ref, counts, dest, strip_ref, left_ref, right_ref, inner_vel,
-    speed, frac, along, plane, *rest,
+    size, levels, level_ref, counts, dest, strip_ref, left_ref, right_ref, inner_vel, *rest,
 ):
     slots = len(rim_sizes(levels))
-    faces, rest = rest[:slots], rest[slots:]
+    faces, (speed, frac, along, plane), rest = rest[:slots], rest[slots : slots + 4], rest[slots + 4 :]
     edge_ref, own_ref, stay_ref, side_ref, north_ref, south_ref = rest[:6]
     rest = rest[6:]
     to_levels, north_levels, south_levels = (rest[slots * at : slots * at + slots] for at in range(3))
@@ -1063,7 +1075,7 @@
         + [sizes[0]] * slots
         + [sizes[3]] * slots
         + [sizes[4]] * slots,
-        [counts, dest, strip, left, right, inner_vel, drop_vel, drop_frac, along, plane] + faces,
+        [counts, dest, strip, left, right, inner_vel, *faces, drop_vel, drop_frac, along, plane],
         [
             pltpu.VMEM((3 * table, width), jnp.float32),
             pltpu.VMEM((3 * table, 128), jnp.float32),

time: 51.3 us -> 50.6 us (0.986)
  transfers between devices with their start and end apart: 15 -> 15, of which waited for: 5 -> 5; matrix products, arithmetic and copies ran while one was open for 0% -> 0% of each run, Pallas kernels for 22% -> 23%
where the time goes in v9:
time: 50.6 us; the launch traced here: 50.2 us
  Pallas kernels  25.5 us (50%)
  starting transfers between devices  19.1 us (38%)
  waiting for transfers between devices  4.89 us (10%)
  between operations  0.74 us (1%)
    pallas_call x9, Pallas kernels, call(): pl.pallas_call(whole, out_shape=[jax.ShapeDtypeStruct(shape, kind[at] if...  25.5 us
    ppermute x8, starting transfers between devices, shifted(): lax.ppermute(value, axis, [(i, (i + step) % count) for i in range(count)])  11.5 us
    ppermute x4, starting transfers between devices, to_level(): lax.ppermute(value, (side, 'gz'), [(brick * levels + at, (brick + step) %...  4.39 us
    ppermute x4, waiting for transfers between devices, to_level(): lax.ppermute(value, (side, 'gz'), [(brick * levels + at, (brick + step) %...  3.82 us
    ppermute x3, starting transfers between devices, to_level(): return lax.ppermute(value, 'gz', pairs)  3.25 us
  transfers between devices with their start and end apart: 15, of which 5 were waited for; matrix products, arithmetic and copies ran while one was open for 0% of the time, Pallas kernels for 23%

profile of v9, /device:TPU:0, one launch (start us, length us, event | category | flops | bytes accessed | tf_op | source)
XLA Modules:
  0.0 50.2 jit_solution(2443983888448251609)
XLA Ops:
  0.6 2.7 %shard_map.103 = (f32[20,8,8,128]{3,2,1,0:T(8,128)}, f32[20,8,128]{2,1,0:T(8,128)}, f32[552,128]{1,0:T(8,128)}, f32[376,128]{1,0:T(8,128)}, f32[25,8,128]{2,1,0:...) custom-call(f32[19,8,8,128]{3,2,1,0:T(8,128)} %refs_0_.3, bf16[19,8,8,128]{3,2,1,0:T(8,128)(2,1)} %refs_1_.3, ...), custom_call_target="tpu_custom_call" | custom-call | tf_op jit(solution)/shard_map/pallas_call | solution.py:88
  3.3 2.4 %collective-permute-start = (f32[552,128]{1,0:T(8,128)}, f32[552,128]{1,0:T(8,128)}, u32[]{:S(2)}, u32[]{:S(2)}) collective-permute-start(f32[552,128]{1,0:T(8,128)} %get-tuple-element.33), channel_id=1, source_target_pairs={{0,6},{2,0},{4,2},{6,4},{1,7},{3,1},{5,3},{7,5},{8,14},{10,8},{12,... | collective-permute-start | bytes 847880 | tf_op jit(solution)/shard_map/ppermute | solution.py:607
  5.7 1.5 %collective-permute-start.2 = (f32[25,8,128]{2,1,0:T(8,128)}, f32[25,8,128]{2,1,0:T(8,128)}, u32[]{:S(2)}, u32[]{:S(2)}) collective-permute-start(f32[25,8,128]{2,1,0:T(8,128)} %get-tuple-element.35), channel_id=1, source_target_pairs={{0,1},{1,0},{2,3},{3,2},{4,5},{5,4},{6,7},{7,6},{8,9},{9,8},{10,11... | collective-permute-start | bytes 307208 | tf_op jit(solution)/shard_map/ppermute | solution.py:617
  7.3 1.4 %collective-permute-start.3 = (f32[88,128]{1,0:T(8,128)}, f32[88,128]{1,0:T(8,128)}, u32[]{:S(2)}, u32[]{:S(2)}) collective-permute-start(f32[88,128]{1,0:T(8,128)} %get-tuple-element.36), channel_id=1, source_target_pairs={{0,7},{1,6},{2,1},{3,0},{4,3},{5,2},{6,5},{7,4},{8,15},{9,14},{10,... | collective-permute-start | bytes 135176 | tf_op jit(solution)/shard_map/ppermute | solution.py:619
  8.7 0.3 collective-permute-start.4
  9.0 3.8 %shard_map.105 = (bf16[384,2048]{1,0:T(8,128)(2,1)}, f32[8,128,256]{2,1,0:T(8,128)}, f32[8,128]{1,0:T(8,128)}) custom-call(f32[3,16,128]{2,1,0:T(8,128)} %refs_8_.1, s32[16,128]{1,0:T(8,128)} %refs_1_.4), custom_call_target="tpu_custom_call" | custom-call | flops 100000000 | bytes 4194304 | tf_op jit(solution)/shard_map/pallas_call | solution.py:88
  12.8 1.9 %collective-permute-done.4.refs_5_ = f32[56,128]{1,0:T(8,128)} collective-permute-done((f32[56,128]{1,0:T(8,128)}, f32[56,128]{1,0:T(8,128)}, u32[]{:S(2)}, u32[]{:S(2)}) %collective-permute-start.4) | collective-permute-done | bytes 28704 | tf_op jit(solution)/shard_map/ppermute | solution.py:619
  14.7 1.9 %shard_map.106 = (f32[20,16,128]{2,1,0:T(8,128)}, f32[6,16,128]{2,1,0:T(8,128)}, f32[9,16,128]{2,1,0:T(8,128)}) custom-call(f32[20,8,128]{2,1,0:T(8,128)} %get-tuple-element.39.refs_0_, f32[552,128]{1,0:T(8,128)} %collective-permute-done.refs_1_, f32[376,128]{1,0:T(8,128)} %collective-permute-done.1.refs_2_, f32[25,8,128]{2,1,0:T(8,128)} %collective-permute-done.2.refs_3_, ...), custom_call_target="tpu_custom_call" | custom-call | tf_op jit(solution)/shard_map/pallas_call | solution.py:88
  16.6 3.7 %collective-permute-start.6 = (f32[9,16,128]{2,1,0:T(8,128)}, f32[9,16,128]{2,1,0:T(8,128)}, u32[]{:S(2)}, u32[]{:S(2)}) collective-permute-start(f32[9,16,128]{2,1,0:T(8,128)} %get-tuple-element.43), channel_id=1, source_target_pairs={{0,24},{8,0},{16,8},{24,16},{1,25},{9,1},{17,9},{25,17},{2,26},{10... | collective-permute-start | bytes 221192 | tf_op jit(solution)/shard_map/ppermute | solution.py:607
  20.3 2.3 %shard_map.107 = f32[72,128]{1,0:T(8,128)} custom-call(f32[20,8,8,128]{3,2,1,0:T(8,128)} %get-tuple-element.32.refs_0_, f32[552,128]{1,0:T(8,128)} %collective-permute-done.refs_1_, f32[376,128]{1,0:T(8,128)} %collective-permute-done.1.refs_2_, f32[25,8,128]{2,1,0:T(8,128)} %collective-permute-done.2.refs_3_, f32[88,128]{1,0:T(8,128)} %collective-permute-done.3.refs_4_, ...), custom_call_target="tpu_custom_call" | custom-call | tf_op jit(solution)/shard_map/pallas_call | solution.py:88
  22.6 0.7 %collective-permute-start.7 = (f32[72,128]{1,0:T(8,128)}, f32[72,128]{1,0:T(8,128)}, u32[]{:S(2)}, u32[]{:S(2)}) collective-permute-start(f32[72,128]{1,0:T(8,128)} %shard_map.107), channel_id=1, source_target_pairs={{0,1},{1,0},{2,3},{3,2},{4,5},{5,4},{6,7},{7,6},{8,9},{9,8},{10,11... | collective-permute-start | bytes 110600 | tf_op jit(solution)/shard_map/ppermute | solution.py:617
  23.2 3.2 %shard_map.104 = (f32[19,8,8,128]{3,2,1,0:T(8,128)}, f32[3,8,16,128]{3,2,1,0:T(8,128)}) custom-call(f32[20,8,8,128]{3,2,1,0:T(8,128)} %get-tuple-element.32.refs_0_, f32[552,128]{1,0:T(8,128)} %collective-permute-done.refs_1_, f32[376,128]{1,0:T(8,128)} %collective-permute-done.1.refs_2_, f32[25,8,128]{2,1,0:T(8,128)} %collective-permute-done.2.refs_3_, ...), custom_call_target="tpu_custom_call" | custom-call | flops 100000000 | bytes 4194304 | tf_op jit(solution)/shard_map/pallas_call | solution.py:88
  26.5 0.5 collective-permute-done.7.refs_6_
  26.9 5.7 %shard_map.108 = (f32[19,8,128]{2,1,0:T(8,128)}, f32[4,8,8,128]{3,2,1,0:T(8,128)}, f32[6,16,128]{2,1,0:T(8,128)}, f32[4,8,128]{2,1,0:T(8,128)}, f32[112,128]{1,0...) custom-call(s32[16]{0:T(128)} %refs_0_.5, s32[16]{0:T(128)} %refs_1_.5, ...), custom_call_target="tpu_custom_call" | custom-call | tf_op jit(solution)/shard_map/pallas_call | solution.py:88
  32.7 1.1 %collective-permute-start.10 = (f32[112,128]{1,0:T(8,128)}, f32[112,128]{1,0:T(8,128)}, u32[]{:S(2)}, u32[]{:S(2)}) collective-permute-start(f32[112,128]{1,0:T(8,128)} %get-tuple-element.52), channel_id=1, source_target_pairs={{0,1},{1,0},{2,3},{3,2},{4,5},{5,4},{6,7},{7,6},{8,9},{9,8},{10,11... | collective-permute-start | bytes 172040 | tf_op jit(solution)/shard_map/ppermute | solution.py:617
  33.7 1.4 %collective-permute-start.9 = (f32[80,128]{1,0:T(8,128)}, f32[80,128]{1,0:T(8,128)}, u32[]{:S(2)}, u32[]{:S(2)}) collective-permute-start(f32[80,128]{1,0:T(8,128)} %get-tuple-element.51), channel_id=1, source_target_pairs={{0,6},{2,0},{4,2},{6,4},{1,7},{3,1},{5,3},{7,5},{8,14},{10,8},{12,... | collective-permute-start | bytes 122888 | tf_op jit(solution)/shard_map/ppermute | solution.py:607
  35.1 2.6 %collective-permute-start.12 = (f32[56,128]{1,0:T(8,128)}, f32[56,128]{1,0:T(8,128)}, u32[]{:S(2)}, u32[]{:S(2)}) collective-permute-start(f32[56,128]{1,0:T(8,128)} %get-tuple-element.54), channel_id=1, source_target_pairs={{0,7},{1,6},{2,1},{3,0},{4,3},{5,2},{6,5},{7,4},{8,15},{9,14},{10,... | collective-permute-start | bytes 86024 | tf_op jit(solution)/shard_map/ppermute | solution.py:619
  37.8 1.8 %collective-permute-done.12.refs_6_ = f32[56,128]{1,0:T(8,128)} collective-permute-done((f32[56,128]{1,0:T(8,128)}, f32[56,128]{1,0:T(8,128)}, u32[]{:S(2)}, u32[]{:S(2)}) %collective-permute-start.12) | collective-permute-done | bytes 28704 | tf_op jit(solution)/shard_map/ppermute | solution.py:619
  39.5 0.1 collective-permute-done.11.refs_5_
  39.7 1.8 %shard_map.110 = (f32[3,8,8,128]{3,2,1,0:T(8,128)}, f32[120,128]{1,0:T(8,128)}, f32[120,128]{1,0:T(8,128)}) custom-call(f32[4,8,8,128]{3,2,1,0:T(8,128)} %get-tuple-element.48.refs_0_, f32[4,8,128]{2,1,0:T(8,128)} %get-tuple-element.49.refs_1_, f32[112,128]{1,0:T(8,128)} %collective-permute-done.8.refs_2_, f32[80,128]{1,0:T(8,128)} %collective-permute-done.9.refs_3_, ...), custom_call_target="tpu_custom_call" | custom-call | tf_op jit(solution)/shard_map/pallas_call | solution.py:88
  41.6 3.9 %collective-permute-start.14 = (f32[120,128]{1,0:T(8,128)}, f32[120,128]{1,0:T(8,128)}, u32[]{:S(2)}, u32[]{:S(2)}) collective-permute-start(f32[120,128]{1,0:T(8,128)} %get-tuple-element.58), channel_id=1, source_target_pairs={{0,24},{8,0},{16,8},{24,16},{1,25},{9,1},{17,9},{25,17},{2,26},{10... | collective-permute-start | bytes 184328 | tf_op jit(solution)/shard_map/ppermute | solution.py:607
  45.4 2.1 %shard_map.109 = f32[19,8,8,128]{3,2,1,0:T(8,128)} custom-call(f32[19,8,8,128]{3,2,1,0:T(8,128)} %get-tuple-element.38.refs_0_, f32[19,8,128]{2,1,0:T(8,128)} %get-tuple-element.47.refs_1_), custom_call_target="tpu_custom_call" | custom-call | flops 100000000 | bytes 4194304 | tf_op jit(solution)/shard_map/pallas_call | solution.py:88
  47.6 0.6 %collective-permute-done.13.refs_7_ = f32[120,128]{1,0:T(8,128)} collective-permute-done((f32[120,128]{1,0:T(8,128)}, f32[120,128]{1,0:T(8,128)}, u32[]{:S(2)}, u32[]{:S(2)}) %collective-permute-start.13) | collective-permute-done | bytes 61472 | tf_op jit(solution)/shard_map/ppermute | solution.py:607
  48.2 2.1 %shard_map.111 = (f32[3,8,8,128]{3,2,1,0:T(8,128)}, f32[6,68,128]{2,1,0:T(8,128)}) custom-call(f32[3,8,8,128]{3,2,1,0:T(8,128)} %get-tuple-element.55.refs_0_, f32[6,16,128]{2,1,0:T(8,128)} %get-tuple-element.56.refs_1_, f32[112,128]{1,0:T(8,128)} %collective-permute-done.8.refs_2_, f32[80,128]{1,0:T(8,128)} %collective-permute-done.9.refs_3_, ...), custom_call_target="tpu_custom_call" | custom-call | tf_op jit(solution)/shard_map/pallas_call | solution.py:88
  (15 shorter events, 0.2 us)
Async XLA Ops:
  3.3 11.4 %collective-permute-start = (f32[552,128]{1,0:T(8,128)}, f32[552,128]{1,0:T(8,128)}, u32[]{:S(2)}, u32[]{:S(2)}) collective-permute-start(f32[552,128]{1,0:T(8,128)} %get-tuple-element.33), channel_id=1, source_target_pairs={{0,6},{2,0},{4,2},{6,4},{1,7},{3,1},{5,3},{7,5},{8,14},{10,8},{12,... | collective-permute-start | bytes 847880 | tf_op jit(solution)/shard_map/ppermute | solution.py:607
  5.7 9.0 %collective-permute-start.1 = (f32[376,128]{1,0:T(8,128)}, f32[376,128]{1,0:T(8,128)}, u32[]{:S(2)}, u32[]{:S(2)}) collective-permute-start(f32[376,128]{1,0:T(8,128)} %get-tuple-element.34), channel_id=1, source_target_pairs={{0,2},{2,4},{4,6},{6,0},{1,3},{3,5},{5,7},{7,1},{8,10},{10,12},{12... | collective-permute-start | bytes 577544 | tf_op jit(solution)/shard_map/ppermute | solution.py:607
  5.7 9.0 %collective-permute-start.2 = (f32[25,8,128]{2,1,0:T(8,128)}, f32[25,8,128]{2,1,0:T(8,128)}, u32[]{:S(2)}, u32[]{:S(2)}) collective-permute-start(f32[25,8,128]{2,1,0:T(8,128)} %get-tuple-element.35), channel_id=1, source_target_pairs={{0,1},{1,0},{2,3},{3,2},{4,5},{5,4},{6,7},{7,6},{8,9},{9,8},{10,11... | collective-permute-start | bytes 307208 | tf_op jit(solution)/shard_map/ppermute | solution.py:617
  7.3 7.5 %collective-permute-start.3 = (f32[88,128]{1,0:T(8,128)}, f32[88,128]{1,0:T(8,128)}, u32[]{:S(2)}, u32[]{:S(2)}) collective-permute-start(f32[88,128]{1,0:T(8,128)} %get-tuple-element.36), channel_id=1, source_target_pairs={{0,7},{1,6},{2,1},{3,0},{4,3},{5,2},{6,5},{7,4},{8,15},{9,14},{10,... | collective-permute-start | bytes 135176 | tf_op jit(solution)/shard_map/ppermute | solution.py:619
  8.7 6.1 %collective-permute-start.4 = (f32[56,128]{1,0:T(8,128)}, f32[56,128]{1,0:T(8,128)}, u32[]{:S(2)}, u32[]{:S(2)}) collective-permute-start(f32[56,128]{1,0:T(8,128)} %get-tuple-element.37), channel_id=1, source_target_pairs={{0,3},{1,2},{2,5},{3,4},{4,7},{5,6},{6,1},{7,0},{8,11},{9,10},{10,... | collective-permute-start | bytes 86024 | tf_op jit(solution)/shard_map/ppermute | solution.py:619
  16.6 10.3 %collective-permute-start.6 = (f32[9,16,128]{2,1,0:T(8,128)}, f32[9,16,128]{2,1,0:T(8,128)}, u32[]{:S(2)}, u32[]{:S(2)}) collective-permute-start(f32[9,16,128]{2,1,0:T(8,128)} %get-tuple-element.43), channel_id=1, source_target_pairs={{0,24},{8,0},{16,8},{24,16},{1,25},{9,1},{17,9},{25,17},{2,26},{10... | collective-permute-start | bytes 221192 | tf_op jit(solution)/shard_map/ppermute | solution.py:607
  20.3 6.7 %collective-permute-start.5 = (f32[6,16,128]{2,1,0:T(8,128)}, f32[6,16,128]{2,1,0:T(8,128)}, u32[]{:S(2)}, u32[]{:S(2)}) collective-permute-start(f32[6,16,128]{2,1,0:T(8,128)} %get-tuple-element.42), channel_id=1, source_target_pairs={{0,8},{8,16},{16,24},{24,0},{1,9},{9,17},{17,25},{25,1},{2,10},{10... | collective-permute-start | bytes 147464 | tf_op jit(solution)/shard_map/ppermute | solution.py:607
  22.6 4.3 %collective-permute-start.7 = (f32[72,128]{1,0:T(8,128)}, f32[72,128]{1,0:T(8,128)}, u32[]{:S(2)}, u32[]{:S(2)}) collective-permute-start(f32[72,128]{1,0:T(8,128)} %shard_map.107), channel_id=1, source_target_pairs={{0,1},{1,0},{2,3},{3,2},{4,5},{5,4},{6,7},{7,6},{8,9},{9,8},{10,11... | collective-permute-start | bytes 110600 | tf_op jit(solution)/shard_map/ppermute | solution.py:617
  32.6 7.1 %collective-permute-start.8 = (f32[112,128]{1,0:T(8,128)}, f32[112,128]{1,0:T(8,128)}, u32[]{:S(2)}, u32[]{:S(2)}) collective-permute-start(f32[112,128]{1,0:T(8,128)} %get-tuple-element.50), channel_id=1, source_target_pairs={{0,2},{2,4},{4,6},{6,0},{1,3},{3,5},{5,7},{7,1},{8,10},{10,12},{12... | collective-permute-start | bytes 172040 | tf_op jit(solution)/shard_map/ppermute | solution.py:607
  32.7 7.0 %collective-permute-start.10 = (f32[112,128]{1,0:T(8,128)}, f32[112,128]{1,0:T(8,128)}, u32[]{:S(2)}, u32[]{:S(2)}) collective-permute-start(f32[112,128]{1,0:T(8,128)} %get-tuple-element.52), channel_id=1, source_target_pairs={{0,1},{1,0},{2,3},{3,2},{4,5},{5,4},{6,7},{7,6},{8,9},{9,8},{10,11... | collective-permute-start | bytes 172040 | tf_op jit(solution)/shard_map/ppermute | solution.py:617
  33.7 5.9 %collective-permute-start.9 = (f32[80,128]{1,0:T(8,128)}, f32[80,128]{1,0:T(8,128)}, u32[]{:S(2)}, u32[]{:S(2)}) collective-permute-start(f32[80,128]{1,0:T(8,128)} %get-tuple-element.51), channel_id=1, source_target_pairs={{0,6},{2,0},{4,2},{6,4},{1,7},{3,1},{5,3},{7,5},{8,14},{10,8},{12,... | collective-permute-start | bytes 122888 | tf_op jit(solution)/shard_map/ppermute | solution.py:607
  35.1 4.6 %collective-permute-start.11 = (f32[64,128]{1,0:T(8,128)}, f32[64,128]{1,0:T(8,128)}, u32[]{:S(2)}, u32[]{:S(2)}) collective-permute-start(f32[64,128]{1,0:T(8,128)} %get-tuple-element.53), channel_id=1, source_target_pairs={{0,3},{1,2},{2,5},{3,4},{4,7},{5,6},{6,1},{7,0},{8,11},{9,10},{10,... | collective-permute-start | bytes 98312 | tf_op jit(solution)/shard_map/ppermute | solution.py:619
  35.1 4.4 %collective-permute-start.12 = (f32[56,128]{1,0:T(8,128)}, f32[56,128]{1,0:T(8,128)}, u32[]{:S(2)}, u32[]{:S(2)}) collective-permute-start(f32[56,128]{1,0:T(8,128)} %get-tuple-element.54), channel_id=1, source_target_pairs={{0,7},{1,6},{2,1},{3,0},{4,3},{5,2},{6,5},{7,4},{8,15},{9,14},{10,... | collective-permute-start | bytes 86024 | tf_op jit(solution)/shard_map/ppermute | solution.py:619
  41.5 6.7 %collective-permute-start.13 = (f32[120,128]{1,0:T(8,128)}, f32[120,128]{1,0:T(8,128)}, u32[]{:S(2)}, u32[]{:S(2)}) collective-permute-start(f32[120,128]{1,0:T(8,128)} %get-tuple-element.57), channel_id=1, source_target_pairs={{0,8},{8,16},{16,24},{24,0},{1,9},{9,17},{17,25},{25,1},{2,10},{10... | collective-permute-start | bytes 184328 | tf_op jit(solution)/shard_map/ppermute | solution.py:607
  41.6 6.6 %collective-permute-start.14 = (f32[120,128]{1,0:T(8,128)}, f32[120,128]{1,0:T(8,128)}, u32[]{:S(2)}, u32[]{:S(2)}) collective-permute-start(f32[120,128]{1,0:T(8,128)} %get-tuple-element.58), channel_id=1, source_target_pairs={{0,24},{8,0},{16,8},{24,16},{1,25},{9,1},{17,9},{25,17},{2,26},{10... | collective-permute-start | bytes 184328 | tf_op jit(solution)/shard_map/ppermute | solution.py:607

commit v10 on v9

--- a/solution.py
+++ b/solution.py
@@ -796,13 +796,14 @@
     pairs = blocks // 2
     for number in range(pairs):
         move(number, sample(number))
-    main = dots(push_high[...], along[0 : 2 * width, :], ((1,), (1,)))
+    outer = dots(push_high[...], along[2 * width :, :], ((1,), (1,)))
+    rest = dots(push_low[...], along[width:, :], ((1,), (1,)))
+    outer_ref[...] = outer + lane_roll(outer, -64) + rest[:, width:]
+    spread_ref[...] = rest[:, :width]
     for action in meanwhile:
         action()
-    rest = dots(push_low[...], along[width:, :], ((1,), (1,)))
-    outer = dots(push_high[...], along[2 * width :, :], ((1,), (1,)))
-    spread_ref[...] = main[:, :width] + main[:, width:] + rest[:, :width]
-    outer_ref[...] = outer + lane_roll(outer, -64) + rest[:, width:]
+    main = dots(push_high[...], along[0 : 2 * width, :], ((1,), (1,)))
+    spread_ref[...] += main[:, :width] + main[:, width:]
 
 
 def force_sides(levels):

time: 50.6 us -> 50.5 us (level)
  no operation moved by 1% of the time
where the time goes in v10:
time: 50.5 us; the launch traced here: 50.1 us
  Pallas kernels  25.3 us (50%)
  starting transfers between devices  19.1 us (38%)
  waiting for transfers between devices  4.89 us (10%)
  between operations  0.74 us (1%)
    pallas_call x9, Pallas kernels, call(): pl.pallas_call(whole, out_shape=[jax.ShapeDtypeStruct(shape, kind[at] if...  25.3 us
    ppermute x8, starting transfers between devices, shifted(): lax.ppermute(value, axis, [(i, (i + step) % count) for i in range(count)])  11.5 us
    ppermute x4, starting transfers between devices, to_level(): lax.ppermute(value, (side, 'gz'), [(brick * levels + at, (brick + step) %...  4.39 us
    ppermute x4, waiting for transfers between devices, to_level(): lax.ppermute(value, (side, 'gz'), [(brick * levels + at, (brick + step) %...  3.82 us
    ppermute x3, starting transfers between devices, to_level(): return lax.ppermute(value, 'gz', pairs)  3.24 us
  transfers between devices with their start and end apart: 15, of which 5 were waited for; matrix products, arithmetic and copies ran while one was open for 0% of the time, Pallas kernels for 23%

profile of v10, /device:TPU:0, one launch (start us, length us, event | category | flops | bytes accessed | tf_op | source)
XLA Modules:
  0.0 50.1 jit_solution(6105884807556930964)
XLA Ops:
  0.6 2.7 %shard_map.103 = (f32[20,8,8,128]{3,2,1,0:T(8,128)}, f32[20,8,128]{2,1,0:T(8,128)}, f32[552,128]{1,0:T(8,128)}, f32[376,128]{1,0:T(8,128)}, f32[25,8,128]{2,1,0:...) custom-call(f32[19,8,8,128]{3,2,1,0:T(8,128)} %refs_0_.3, bf16[19,8,8,128]{3,2,1,0:T(8,128)(2,1)} %refs_1_.3, ...), custom_call_target="tpu_custom_call" | custom-call | tf_op jit(solution)/shard_map/pallas_call | solution.py:88
  3.3 2.4 %collective-permute-start = (f32[552,128]{1,0:T(8,128)}, f32[552,128]{1,0:T(8,128)}, u32[]{:S(2)}, u32[]{:S(2)}) collective-permute-start(f32[552,128]{1,0:T(8,128)} %get-tuple-element.33), channel_id=1, source_target_pairs={{0,6},{2,0},{4,2},{6,4},{1,7},{3,1},{5,3},{7,5},{8,14},{10,8},{12,... | collective-permute-start | bytes 847880 | tf_op jit(solution)/shard_map/ppermute | solution.py:607
  5.7 1.5 %collective-permute-start.2 = (f32[25,8,128]{2,1,0:T(8,128)}, f32[25,8,128]{2,1,0:T(8,128)}, u32[]{:S(2)}, u32[]{:S(2)}) collective-permute-start(f32[25,8,128]{2,1,0:T(8,128)} %get-tuple-element.35), channel_id=1, source_target_pairs={{0,1},{1,0},{2,3},{3,2},{4,5},{5,4},{6,7},{7,6},{8,9},{9,8},{10,11... | collective-permute-start | bytes 307208 | tf_op jit(solution)/shard_map/ppermute | solution.py:617
  7.3 1.4 %collective-permute-start.3 = (f32[88,128]{1,0:T(8,128)}, f32[88,128]{1,0:T(8,128)}, u32[]{:S(2)}, u32[]{:S(2)}) collective-permute-start(f32[88,128]{1,0:T(8,128)} %get-tuple-element.36), channel_id=1, source_target_pairs={{0,7},{1,6},{2,1},{3,0},{4,3},{5,2},{6,5},{7,4},{8,15},{9,14},{10,... | collective-permute-start | bytes 135176 | tf_op jit(solution)/shard_map/ppermute | solution.py:619
  8.7 0.3 collective-permute-start.4
  9.0 3.8 %shard_map.105 = (bf16[384,2048]{1,0:T(8,128)(2,1)}, f32[8,128,256]{2,1,0:T(8,128)}, f32[8,128]{1,0:T(8,128)}) custom-call(f32[3,16,128]{2,1,0:T(8,128)} %refs_8_.1, s32[16,128]{1,0:T(8,128)} %refs_1_.4), custom_call_target="tpu_custom_call" | custom-call | flops 100000000 | bytes 4194304 | tf_op jit(solution)/shard_map/pallas_call | solution.py:88
  12.8 1.9 %collective-permute-done.4.refs_5_ = f32[56,128]{1,0:T(8,128)} collective-permute-done((f32[56,128]{1,0:T(8,128)}, f32[56,128]{1,0:T(8,128)}, u32[]{:S(2)}, u32[]{:S(2)}) %collective-permute-start.4) | collective-permute-done | bytes 28704 | tf_op jit(solution)/shard_map/ppermute | solution.py:619
  14.7 1.9 %shard_map.106 = (f32[20,16,128]{2,1,0:T(8,128)}, f32[6,16,128]{2,1,0:T(8,128)}, f32[9,16,128]{2,1,0:T(8,128)}) custom-call(f32[20,8,128]{2,1,0:T(8,128)} %get-tuple-element.39.refs_0_, f32[552,128]{1,0:T(8,128)} %collective-permute-done.refs_1_, f32[376,128]{1,0:T(8,128)} %collective-permute-done.1.refs_2_, f32[25,8,128]{2,1,0:T(8,128)} %collective-permute-done.2.refs_3_, ...), custom_call_target="tpu_custom_call" | custom-call | tf_op jit(solution)/shard_map/pallas_call | solution.py:88
  16.6 3.7 %collective-permute-start.6 = (f32[9,16,128]{2,1,0:T(8,128)}, f32[9,16,128]{2,1,0:T(8,128)}, u32[]{:S(2)}, u32[]{:S(2)}) collective-permute-start(f32[9,16,128]{2,1,0:T(8,128)} %get-tuple-element.43), channel_id=1, source_target_pairs={{0,24},{8,0},{16,8},{24,16},{1,25},{9,1},{17,9},{25,17},{2,26},{10... | collective-permute-start | bytes 221192 | tf_op jit(solution)/shard_map/ppermute | solution.py:607
  20.3 2.3 %shard_map.107 = f32[72,128]{1,0:T(8,128)} custom-call(f32[20,8,8,128]{3,2,1,0:T(8,128)} %get-tuple-element.32.refs_0_, f32[552,128]{1,0:T(8,128)} %collective-permute-done.refs_1_, f32[376,128]{1,0:T(8,128)} %collective-permute-done.1.refs_2_, f32[25,8,128]{2,1,0:T(8,128)} %collective-permute-done.2.refs_3_, f32[88,128]{1,0:T(8,128)} %collective-permute-done.3.refs_4_, ...), custom_call_target="tpu_custom_call" | custom-call | tf_op jit(solution)/shard_map/pallas_call | solution.py:88
  22.6 0.7 %collective-permute-start.7 = (f32[72,128]{1,0:T(8,128)}, f32[72,128]{1,0:T(8,128)}, u32[]{:S(2)}, u32[]{:S(2)}) collective-permute-start(f32[72,128]{1,0:T(8,128)} %shard_map.107), channel_id=1, source_target_pairs={{0,1},{1,0},{2,3},{3,2},{4,5},{5,4},{6,7},{7,6},{8,9},{9,8},{10,11... | collective-permute-start | bytes 110600 | tf_op jit(solution)/shard_map/ppermute | solution.py:617
  23.2 3.2 %shard_map.104 = (f32[19,8,8,128]{3,2,1,0:T(8,128)}, f32[3,8,16,128]{3,2,1,0:T(8,128)}) custom-call(f32[20,8,8,128]{3,2,1,0:T(8,128)} %get-tuple-element.32.refs_0_, f32[552,128]{1,0:T(8,128)} %collective-permute-done.refs_1_, f32[376,128]{1,0:T(8,128)} %collective-permute-done.1.refs_2_, f32[25,8,128]{2,1,0:T(8,128)} %collective-permute-done.2.refs_3_, ...), custom_call_target="tpu_custom_call" | custom-call | flops 100000000 | bytes 4194304 | tf_op jit(solution)/shard_map/pallas_call | solution.py:88
  26.5 0.5 collective-permute-done.7.refs_6_
  26.9 5.5 %shard_map.108 = (f32[19,8,128]{2,1,0:T(8,128)}, f32[4,8,8,128]{3,2,1,0:T(8,128)}, f32[6,16,128]{2,1,0:T(8,128)}, f32[4,8,128]{2,1,0:T(8,128)}, f32[112,128]{1,0...) custom-call(s32[16]{0:T(128)} %refs_0_.5, s32[16]{0:T(128)} %refs_1_.5, ...), custom_call_target="tpu_custom_call" | custom-call | tf_op jit(solution)/shard_map/pallas_call | solution.py:88
  32.5 1.1 %collective-permute-start.10 = (f32[112,128]{1,0:T(8,128)}, f32[112,128]{1,0:T(8,128)}, u32[]{:S(2)}, u32[]{:S(2)}) collective-permute-start(f32[112,128]{1,0:T(8,128)} %get-tuple-element.52), channel_id=1, source_target_pairs={{0,1},{1,0},{2,3},{3,2},{4,5},{5,4},{6,7},{7,6},{8,9},{9,8},{10,11... | collective-permute-start | bytes 172040 | tf_op jit(solution)/shard_map/ppermute | solution.py:617
  33.6 1.4 %collective-permute-start.9 = (f32[80,128]{1,0:T(8,128)}, f32[80,128]{1,0:T(8,128)}, u32[]{:S(2)}, u32[]{:S(2)}) collective-permute-start(f32[80,128]{1,0:T(8,128)} %get-tuple-element.51), channel_id=1, source_target_pairs={{0,6},{2,0},{4,2},{6,4},{1,7},{3,1},{5,3},{7,5},{8,14},{10,8},{12,... | collective-permute-start | bytes 122888 | tf_op jit(solution)/shard_map/ppermute | solution.py:607
  35.0 2.6 %collective-permute-start.12 = (f32[56,128]{1,0:T(8,128)}, f32[56,128]{1,0:T(8,128)}, u32[]{:S(2)}, u32[]{:S(2)}) collective-permute-start(f32[56,128]{1,0:T(8,128)} %get-tuple-element.54), channel_id=1, source_target_pairs={{0,7},{1,6},{2,1},{3,0},{4,3},{5,2},{6,5},{7,4},{8,15},{9,14},{10,... | collective-permute-start | bytes 86024 | tf_op jit(solution)/shard_map/ppermute | solution.py:619
  37.6 1.8 %collective-permute-done.12.refs_6_ = f32[56,128]{1,0:T(8,128)} collective-permute-done((f32[56,128]{1,0:T(8,128)}, f32[56,128]{1,0:T(8,128)}, u32[]{:S(2)}, u32[]{:S(2)}) %collective-permute-start.12) | collective-permute-done | bytes 28704 | tf_op jit(solution)/shard_map/ppermute | solution.py:619
  39.4 0.1 collective-permute-done.11.refs_5_
  39.5 1.8 %shard_map.110 = (f32[3,8,8,128]{3,2,1,0:T(8,128)}, f32[120,128]{1,0:T(8,128)}, f32[120,128]{1,0:T(8,128)}) custom-call(f32[4,8,8,128]{3,2,1,0:T(8,128)} %get-tuple-element.48.refs_0_, f32[4,8,128]{2,1,0:T(8,128)} %get-tuple-element.49.refs_1_, f32[112,128]{1,0:T(8,128)} %collective-permute-done.8.refs_2_, f32[80,128]{1,0:T(8,128)} %collective-permute-done.9.refs_3_, ...), custom_call_target="tpu_custom_call" | custom-call | tf_op jit(solution)/shard_map/pallas_call | solution.py:88
  41.4 3.9 %collective-permute-start.14 = (f32[120,128]{1,0:T(8,128)}, f32[120,128]{1,0:T(8,128)}, u32[]{:S(2)}, u32[]{:S(2)}) collective-permute-start(f32[120,128]{1,0:T(8,128)} %get-tuple-element.58), channel_id=1, source_target_pairs={{0,24},{8,0},{16,8},{24,16},{1,25},{9,1},{17,9},{25,17},{2,26},{10... | collective-permute-start | bytes 184328 | tf_op jit(solution)/shard_map/ppermute | solution.py:607
  45.3 2.1 %shard_map.109 = f32[19,8,8,128]{3,2,1,0:T(8,128)} custom-call(f32[19,8,8,128]{3,2,1,0:T(8,128)} %get-tuple-element.38.refs_0_, f32[19,8,128]{2,1,0:T(8,128)} %get-tuple-element.47.refs_1_), custom_call_target="tpu_custom_call" | custom-call | flops 100000000 | bytes 4194304 | tf_op jit(solution)/shard_map/pallas_call | solution.py:88
  47.4 0.6 %collective-permute-done.13.refs_7_ = f32[120,128]{1,0:T(8,128)} collective-permute-done((f32[120,128]{1,0:T(8,128)}, f32[120,128]{1,0:T(8,128)}, u32[]{:S(2)}, u32[]{:S(2)}) %collective-permute-start.13) | collective-permute-done | bytes 61472 | tf_op jit(solution)/shard_map/ppermute | solution.py:607
  48.0 2.1 %shard_map.111 = (f32[3,8,8,128]{3,2,1,0:T(8,128)}, f32[6,68,128]{2,1,0:T(8,128)}) custom-call(f32[3,8,8,128]{3,2,1,0:T(8,128)} %get-tuple-element.55.refs_0_, f32[6,16,128]{2,1,0:T(8,128)} %get-tuple-element.56.refs_1_, f32[112,128]{1,0:T(8,128)} %collective-permute-done.8.refs_2_, f32[80,128]{1,0:T(8,128)} %collective-permute-done.9.refs_3_, ...), custom_call_target="tpu_custom_call" | custom-call | tf_op jit(solution)/shard_map/pallas_call | solution.py:88
  (15 shorter events, 0.2 us)
Async XLA Ops:
  3.3 11.4 %collective-permute-start = (f32[552,128]{1,0:T(8,128)}, f32[552,128]{1,0:T(8,128)}, u32[]{:S(2)}, u32[]{:S(2)}) collective-permute-start(f32[552,128]{1,0:T(8,128)} %get-tuple-element.33), channel_id=1, source_target_pairs={{0,6},{2,0},{4,2},{6,4},{1,7},{3,1},{5,3},{7,5},{8,14},{10,8},{12,... | collective-permute-start | bytes 847880 | tf_op jit(solution)/shard_map/ppermute | solution.py:607
  5.7 9.0 %collective-permute-start.1 = (f32[376,128]{1,0:T(8,128)}, f32[376,128]{1,0:T(8,128)}, u32[]{:S(2)}, u32[]{:S(2)}) collective-permute-start(f32[376,128]{1,0:T(8,128)} %get-tuple-element.34), channel_id=1, source_target_pairs={{0,2},{2,4},{4,6},{6,0},{1,3},{3,5},{5,7},{7,1},{8,10},{10,12},{12... | collective-permute-start | bytes 577544 | tf_op jit(solution)/shard_map/ppermute | solution.py:607
  5.7 9.0 %collective-permute-start.2 = (f32[25,8,128]{2,1,0:T(8,128)}, f32[25,8,128]{2,1,0:T(8,128)}, u32[]{:S(2)}, u32[]{:S(2)}) collective-permute-start(f32[25,8,128]{2,1,0:T(8,128)} %get-tuple-element.35), channel_id=1, source_target_pairs={{0,1},{1,0},{2,3},{3,2},{4,5},{5,4},{6,7},{7,6},{8,9},{9,8},{10,11... | collective-permute-start | bytes 307208 | tf_op jit(solution)/shard_map/ppermute | solution.py:617
  7.3 7.5 %collective-permute-start.3 = (f32[88,128]{1,0:T(8,128)}, f32[88,128]{1,0:T(8,128)}, u32[]{:S(2)}, u32[]{:S(2)}) collective-permute-start(f32[88,128]{1,0:T(8,128)} %get-tuple-element.36), channel_id=1, source_target_pairs={{0,7},{1,6},{2,1},{3,0},{4,3},{5,2},{6,5},{7,4},{8,15},{9,14},{10,... | collective-permute-start | bytes 135176 | tf_op jit(solution)/shard_map/ppermute | solution.py:619
  8.7 6.1 %collective-permute-start.4 = (f32[56,128]{1,0:T(8,128)}, f32[56,128]{1,0:T(8,128)}, u32[]{:S(2)}, u32[]{:S(2)}) collective-permute-start(f32[56,128]{1,0:T(8,128)} %get-tuple-element.37), channel_id=1, source_target_pairs={{0,3},{1,2},{2,5},{3,4},{4,7},{5,6},{6,1},{7,0},{8,11},{9,10},{10,... | collective-permute-start | bytes 86024 | tf_op jit(solution)/shard_map/ppermute | solution.py:619
  16.6 10.3 %collective-permute-start.6 = (f32[9,16,128]{2,1,0:T(8,128)}, f32[9,16,128]{2,1,0:T(8,128)}, u32[]{:S(2)}, u32[]{:S(2)}) collective-permute-start(f32[9,16,128]{2,1,0:T(8,128)} %get-tuple-element.43), channel_id=1, source_target_pairs={{0,24},{8,0},{16,8},{24,16},{1,25},{9,1},{17,9},{25,17},{2,26},{10... | collective-permute-start | bytes 221192 | tf_op jit(solution)/shard_map/ppermute | solution.py:607
  20.3 6.7 %collective-permute-start.5 = (f32[6,16,128]{2,1,0:T(8,128)}, f32[6,16,128]{2,1,0:T(8,128)}, u32[]{:S(2)}, u32[]{:S(2)}) collective-permute-start(f32[6,16,128]{2,1,0:T(8,128)} %get-tuple-element.42), channel_id=1, source_target_pairs={{0,8},{8,16},{16,24},{24,0},{1,9},{9,17},{17,25},{25,1},{2,10},{10... | collective-permute-start | bytes 147464 | tf_op jit(solution)/shard_map/ppermute | solution.py:607
  22.6 4.3 %collective-permute-start.7 = (f32[72,128]{1,0:T(8,128)}, f32[72,128]{1,0:T(8,128)}, u32[]{:S(2)}, u32[]{:S(2)}) collective-permute-start(f32[72,128]{1,0:T(8,128)} %shard_map.107), channel_id=1, source_target_pairs={{0,1},{1,0},{2,3},{3,2},{4,5},{5,4},{6,7},{7,6},{8,9},{9,8},{10,11... | collective-permute-start | bytes 110600 | tf_op jit(solution)/shard_map/ppermute | solution.py:617
  32.4 7.1 %collective-permute-start.8 = (f32[112,128]{1,0:T(8,128)}, f32[112,128]{1,0:T(8,128)}, u32[]{:S(2)}, u32[]{:S(2)}) collective-permute-start(f32[112,128]{1,0:T(8,128)} %get-tuple-element.50), channel_id=1, source_target_pairs={{0,2},{2,4},{4,6},{6,0},{1,3},{3,5},{5,7},{7,1},{8,10},{10,12},{12... | collective-permute-start | bytes 172040 | tf_op jit(solution)/shard_map/ppermute | solution.py:607
  32.5 7.0 %collective-permute-start.10 = (f32[112,128]{1,0:T(8,128)}, f32[112,128]{1,0:T(8,128)}, u32[]{:S(2)}, u32[]{:S(2)}) collective-permute-start(f32[112,128]{1,0:T(8,128)} %get-tuple-element.52), channel_id=1, source_target_pairs={{0,1},{1,0},{2,3},{3,2},{4,5},{5,4},{6,7},{7,6},{8,9},{9,8},{10,11... | collective-permute-start | bytes 172040 | tf_op jit(solution)/shard_map/ppermute | solution.py:617
  33.6 5.9 %collective-permute-start.9 = (f32[80,128]{1,0:T(8,128)}, f32[80,128]{1,0:T(8,128)}, u32[]{:S(2)}, u32[]{:S(2)}) collective-permute-start(f32[80,128]{1,0:T(8,128)} %get-tuple-element.51), channel_id=1, source_target_pairs={{0,6},{2,0},{4,2},{6,4},{1,7},{3,1},{5,3},{7,5},{8,14},{10,8},{12,... | collective-permute-start | bytes 122888 | tf_op jit(solution)/shard_map/ppermute | solution.py:607
  35.0 4.6 %collective-permute-start.11 = (f32[64,128]{1,0:T(8,128)}, f32[64,128]{1,0:T(8,128)}, u32[]{:S(2)}, u32[]{:S(2)}) collective-permute-start(f32[64,128]{1,0:T(8,128)} %get-tuple-element.53), channel_id=1, source_target_pairs={{0,3},{1,2},{2,5},{3,4},{4,7},{5,6},{6,1},{7,0},{8,11},{9,10},{10,... | collective-permute-start | bytes 98312 | tf_op jit(solution)/shard_map/ppermute | solution.py:619
  35.0 4.4 %collective-permute-start.12 = (f32[56,128]{1,0:T(8,128)}, f32[56,128]{1,0:T(8,128)}, u32[]{:S(2)}, u32[]{:S(2)}) collective-permute-start(f32[56,128]{1,0:T(8,128)} %get-tuple-element.54), channel_id=1, source_target_pairs={{0,7},{1,6},{2,1},{3,0},{4,3},{5,2},{6,5},{7,4},{8,15},{9,14},{10,... | collective-permute-start | bytes 86024 | tf_op jit(solution)/shard_map/ppermute | solution.py:619
  41.3 6.7 %collective-permute-start.13 = (f32[120,128]{1,0:T(8,128)}, f32[120,128]{1,0:T(8,128)}, u32[]{:S(2)}, u32[]{:S(2)}) collective-permute-start(f32[120,128]{1,0:T(8,128)} %get-tuple-element.57), channel_id=1, source_target_pairs={{0,8},{8,16},{16,24},{24,0},{1,9},{9,17},{17,25},{25,1},{2,10},{10... | collective-permute-start | bytes 184328 | tf_op jit(solution)/shard_map/ppermute | solution.py:607
  41.4 6.6 %collective-permute-start.14 = (f32[120,128]{1,0:T(8,128)}, f32[120,128]{1,0:T(8,128)}, u32[]{:S(2)}, u32[]{:S(2)}) collective-permute-start(f32[120,128]{1,0:T(8,128)} %get-tuple-element.58), channel_id=1, source_target_pairs={{0,24},{8,0},{16,8},{24,16},{1,25},{9,1},{17,9},{25,17},{2,26},{10... | collective-permute-start | bytes 184328 | tf_op jit(solution)/shard_map/ppermute | solution.py:607

commit v11 on v10

--- a/solution.py
+++ b/solution.py
@@ -43,6 +43,8 @@
 
 
 class Level:
+    later = ()
+
     def __getitem__(self, _):
         return lax.axis_index("gz").astype(jnp.int32)
 
@@ -57,7 +59,7 @@
         return self.buffer
 
 
-def call(body, outs, arrays, scratch=(), cost=None, heads=(), late=(), kind=jnp.float32):
+def call(body, outs, arrays, scratch=(), cost=None, heads=(), late=(), kind=jnp.float32, halves=()):
     heads = dict(heads)
     landing = []
     for at, value in enumerate(arrays):
@@ -69,19 +71,27 @@
         made = list(refs[len(arrays) : len(arrays) + len(outs)])
         rest = refs[len(arrays) + len(outs) :]
         landed, done, rest = list(rest[: len(arrays)]), rest[len(arrays)], rest[len(arrays) + 1 :]
-        copies = []
+        copies, level = [], Level()
         for at, (source, target) in enumerate(zip(given, landed)):
             if at in heads:
                 source = source.at[pl.ds(0, heads[at])]
-            copies.append(pltpu.make_async_copy(source, target, done.at[at]))
-        for copy in copies:
+            copies.append(pltpu.make_async_copy(source, target, done.at[at, 0]))
+        if halves:
+            cuts = []
+            for at, (source, target, dim) in enumerate(zip(given, landed, halves)):
+                half = source.shape[dim] // 2
+                for part, size in ((0, half), (1, source.shape[dim] - half)):
+                    where = (slice(None),) * dim + (pl.ds(part * half, size),)
+                    cuts.append(pltpu.make_async_copy(source.at[where], target.at[where], done.at[at, part]))
+            copies, level.later = cuts[::2], cuts[1::2]
+        for copy in [*copies, *level.later]:
             copy.start()
         for at, copy in enumerate(copies):
             if at in late:
                 landed[at] = Moving(landed[at], copy)
             else:
                 copy.wait()
-        body(Level(), *landed, *made, *rest)
+        body(level, *landed, *made, *rest)
 
     vmem = pl.BlockSpec(memory_space=pltpu.VMEM)
     hbm = pl.BlockSpec(memory_space=pltpu.HBM)
@@ -94,7 +104,7 @@
         in_specs=[hbm] * len(arrays),
         out_specs=[vmem] * len(outs),
         scratch_shapes=landing
-        + [pltpu.SemaphoreType.DMA((len(arrays),))]
+        + [pltpu.SemaphoreType.DMA((len(arrays), 2))]
         + list(scratch),
         cost_estimate=cost,
         compiler_params=pltpu.CompilerParams(vmem_limit_bytes=64 * 1024 * 1024),
@@ -281,6 +291,9 @@
 
     own = own_rows(depth)[0]
     for layer in range(depth):
+        if layer == depth // 2:
+            for copy in level_ref.later:
+                copy.wait()
         mask = interface_ref[layer]
         inside = mask == 1
         posts = relaxed([pops_ref[index, layer] for index in range(19)])
@@ -641,6 +654,7 @@
         + [(size, height, width) for size in sizes]
         + [(size, width) for size in down_sizes + up_sizes],
         [pops, coarse_pops, interface],
+        halves=(1, 1, 0),
     )
     posts, own, down, up = outs[:4]
     rims, down_rims, up_rims = (outs[4 + slots * at : 4 + slots * at + slots] for at in range(3))

time: 50.5 us -> 50.9 us (level)
  no operation moved by 1% of the time
where the time goes in v11:
time: 50.9 us; the launch traced here: 50.5 us
  Pallas kernels  25.8 us (51%)
  starting transfers between devices  19.1 us (38%)
  waiting for transfers between devices  4.86 us (10%)
  between operations  0.74 us (1%)
    pallas_call x9, Pallas kernels, call(): pl.pallas_call(whole, out_shape=[jax.ShapeDtypeStruct(shape, kind[at] if...  25.8 us
    ppermute x8, starting transfers between devices, shifted(): lax.ppermute(value, axis, [(i, (i + step) % count) for i in range(count)])  11.5 us
    ppermute x4, starting transfers between devices, to_level(): lax.ppermute(value, (side, 'gz'), [(brick * levels + at, (brick + step) %...  4.39 us
    ppermute x4, waiting for transfers between devices, to_level(): lax.ppermute(value, (side, 'gz'), [(brick * levels + at, (brick + step) %...  3.8 us
    ppermute x3, starting transfers between devices, to_level(): return lax.ppermute(value, 'gz', pairs)  3.3 us
  transfers between devices with their start and end apart: 15, of which 5 were waited for; matrix products, arithmetic and copies ran while one was open for 0% of the time, Pallas kernels for 23%

profile of v11, /device:TPU:0, one launch (start us, length us, event | category | flops | bytes accessed | tf_op | source)
XLA Modules:
  0.0 50.5 jit_solution(12998155373915579526)
XLA Ops:
  0.6 2.7 %shard_map.103 = (f32[20,8,8,128]{3,2,1,0:T(8,128)}, f32[20,8,128]{2,1,0:T(8,128)}, f32[552,128]{1,0:T(8,128)}, f32[376,128]{1,0:T(8,128)}, f32[25,8,128]{2,1,0:...) custom-call(f32[19,8,8,128]{3,2,1,0:T(8,128)} %refs_0_.3, bf16[19,8,8,128]{3,2,1,0:T(8,128)(2,1)} %refs_1_.3, ...), custom_call_target="tpu_custom_call" | custom-call | tf_op jit(solution)/shard_map/pallas_call | solution.py:98
  3.3 2.4 %collective-permute-start = (f32[552,128]{1,0:T(8,128)}, f32[552,128]{1,0:T(8,128)}, u32[]{:S(2)}, u32[]{:S(2)}) collective-permute-start(f32[552,128]{1,0:T(8,128)} %get-tuple-element.33), channel_id=1, source_target_pairs={{0,6},{2,0},{4,2},{6,4},{1,7},{3,1},{5,3},{7,5},{8,14},{10,8},{12,... | collective-permute-start | bytes 847880 | tf_op jit(solution)/shard_map/ppermute | solution.py:620
  5.7 1.5 %collective-permute-start.2 = (f32[25,8,128]{2,1,0:T(8,128)}, f32[25,8,128]{2,1,0:T(8,128)}, u32[]{:S(2)}, u32[]{:S(2)}) collective-permute-start(f32[25,8,128]{2,1,0:T(8,128)} %get-tuple-element.35), channel_id=1, source_target_pairs={{0,1},{1,0},{2,3},{3,2},{4,5},{5,4},{6,7},{7,6},{8,9},{9,8},{10,11... | collective-permute-start | bytes 307208 | tf_op jit(solution)/shard_map/ppermute | solution.py:630
  7.2 1.4 %collective-permute-start.3 = (f32[88,128]{1,0:T(8,128)}, f32[88,128]{1,0:T(8,128)}, u32[]{:S(2)}, u32[]{:S(2)}) collective-permute-start(f32[88,128]{1,0:T(8,128)} %get-tuple-element.36), channel_id=1, source_target_pairs={{0,7},{1,6},{2,1},{3,0},{4,3},{5,2},{6,5},{7,4},{8,15},{9,14},{10,... | collective-permute-start | bytes 135176 | tf_op jit(solution)/shard_map/ppermute | solution.py:632
  8.7 0.3 collective-permute-start.4
  9.0 3.8 %shard_map.105 = (bf16[384,2048]{1,0:T(8,128)(2,1)}, f32[8,128,256]{2,1,0:T(8,128)}, f32[8,128]{1,0:T(8,128)}) custom-call(f32[3,16,128]{2,1,0:T(8,128)} %refs_8_.1, s32[16,128]{1,0:T(8,128)} %refs_1_.4), custom_call_target="tpu_custom_call" | custom-call | flops 100000000 | bytes 4194304 | tf_op jit(solution)/shard_map/pallas_call | solution.py:98
  12.8 1.9 %collective-permute-done.4.refs_5_ = f32[56,128]{1,0:T(8,128)} collective-permute-done((f32[56,128]{1,0:T(8,128)}, f32[56,128]{1,0:T(8,128)}, u32[]{:S(2)}, u32[]{:S(2)}) %collective-permute-start.4) | collective-permute-done | bytes 28704 | tf_op jit(solution)/shard_map/ppermute | solution.py:632
  14.7 1.9 %shard_map.106 = (f32[20,16,128]{2,1,0:T(8,128)}, f32[6,16,128]{2,1,0:T(8,128)}, f32[9,16,128]{2,1,0:T(8,128)}) custom-call(f32[20,8,128]{2,1,0:T(8,128)} %get-tuple-element.39.refs_0_, f32[552,128]{1,0:T(8,128)} %collective-permute-done.refs_1_, f32[376,128]{1,0:T(8,128)} %collective-permute-done.1.refs_2_, f32[25,8,128]{2,1,0:T(8,128)} %collective-permute-done.2.refs_3_, ...), custom_call_target="tpu_custom_call" | custom-call | tf_op jit(solution)/shard_map/pallas_call | solution.py:98
  16.7 3.7 %collective-permute-start.6 = (f32[9,16,128]{2,1,0:T(8,128)}, f32[9,16,128]{2,1,0:T(8,128)}, u32[]{:S(2)}, u32[]{:S(2)}) collective-permute-start(f32[9,16,128]{2,1,0:T(8,128)} %get-tuple-element.43), channel_id=1, source_target_pairs={{0,24},{8,0},{16,8},{24,16},{1,25},{9,1},{17,9},{25,17},{2,26},{10... | collective-permute-start | bytes 221192 | tf_op jit(solution)/shard_map/ppermute | solution.py:620
  20.3 2.4 %shard_map.107 = f32[72,128]{1,0:T(8,128)} custom-call(f32[20,8,8,128]{3,2,1,0:T(8,128)} %get-tuple-element.32.refs_0_, f32[552,128]{1,0:T(8,128)} %collective-permute-done.refs_1_, f32[376,128]{1,0:T(8,128)} %collective-permute-done.1.refs_2_, f32[25,8,128]{2,1,0:T(8,128)} %collective-permute-done.2.refs_3_, f32[88,128]{1,0:T(8,128)} %collective-permute-done.3.refs_4_, ...), custom_call_target="tpu_custom_call" | custom-call | tf_op jit(solution)/shard_map/pallas_call | solution.py:98
  22.7 0.7 %collective-permute-start.7 = (f32[72,128]{1,0:T(8,128)}, f32[72,128]{1,0:T(8,128)}, u32[]{:S(2)}, u32[]{:S(2)}) collective-permute-start(f32[72,128]{1,0:T(8,128)} %shard_map.107), channel_id=1, source_target_pairs={{0,1},{1,0},{2,3},{3,2},{4,5},{5,4},{6,7},{7,6},{8,9},{9,8},{10,11... | collective-permute-start | bytes 110600 | tf_op jit(solution)/shard_map/ppermute | solution.py:630
  23.3 3.3 %shard_map.104 = (f32[19,8,8,128]{3,2,1,0:T(8,128)}, f32[3,8,16,128]{3,2,1,0:T(8,128)}) custom-call(f32[20,8,8,128]{3,2,1,0:T(8,128)} %get-tuple-element.32.refs_0_, f32[552,128]{1,0:T(8,128)} %collective-permute-done.refs_1_, f32[376,128]{1,0:T(8,128)} %collective-permute-done.1.refs_2_, f32[25,8,128]{2,1,0:T(8,128)} %collective-permute-done.2.refs_3_, ...), custom_call_target="tpu_custom_call" | custom-call | flops 100000000 | bytes 4194304 | tf_op jit(solution)/shard_map/pallas_call | solution.py:98
  26.6 0.4 collective-permute-done.7.refs_6_
  27.0 5.6 %shard_map.108 = (f32[19,8,128]{2,1,0:T(8,128)}, f32[4,8,8,128]{3,2,1,0:T(8,128)}, f32[6,16,128]{2,1,0:T(8,128)}, f32[4,8,128]{2,1,0:T(8,128)}, f32[112,128]{1,0...) custom-call(s32[16]{0:T(128)} %refs_0_.5, s32[16]{0:T(128)} %refs_1_.5, ...), custom_call_target="tpu_custom_call" | custom-call | tf_op jit(solution)/shard_map/pallas_call | solution.py:98
  32.7 1.1 %collective-permute-start.10 = (f32[112,128]{1,0:T(8,128)}, f32[112,128]{1,0:T(8,128)}, u32[]{:S(2)}, u32[]{:S(2)}) collective-permute-start(f32[112,128]{1,0:T(8,128)} %get-tuple-element.52), channel_id=1, source_target_pairs={{0,1},{1,0},{2,3},{3,2},{4,5},{5,4},{6,7},{7,6},{8,9},{9,8},{10,11... | collective-permute-start | bytes 172040 | tf_op jit(solution)/shard_map/ppermute | solution.py:630
  33.8 1.4 %collective-permute-start.9 = (f32[80,128]{1,0:T(8,128)}, f32[80,128]{1,0:T(8,128)}, u32[]{:S(2)}, u32[]{:S(2)}) collective-permute-start(f32[80,128]{1,0:T(8,128)} %get-tuple-element.51), channel_id=1, source_target_pairs={{0,6},{2,0},{4,2},{6,4},{1,7},{3,1},{5,3},{7,5},{8,14},{10,8},{12,... | collective-permute-start | bytes 122888 | tf_op jit(solution)/shard_map/ppermute | solution.py:620
  35.2 2.6 %collective-permute-start.12 = (f32[56,128]{1,0:T(8,128)}, f32[56,128]{1,0:T(8,128)}, u32[]{:S(2)}, u32[]{:S(2)}) collective-permute-start(f32[56,128]{1,0:T(8,128)} %get-tuple-element.54), channel_id=1, source_target_pairs={{0,7},{1,6},{2,1},{3,0},{4,3},{5,2},{6,5},{7,4},{8,15},{9,14},{10,... | collective-permute-start | bytes 86024 | tf_op jit(solution)/shard_map/ppermute | solution.py:632
  37.9 1.8 %collective-permute-done.12.refs_6_ = f32[56,128]{1,0:T(8,128)} collective-permute-done((f32[56,128]{1,0:T(8,128)}, f32[56,128]{1,0:T(8,128)}, u32[]{:S(2)}, u32[]{:S(2)}) %collective-permute-start.12) | collective-permute-done | bytes 28704 | tf_op jit(solution)/shard_map/ppermute | solution.py:632
  39.6 0.1 collective-permute-done.11.refs_5_
  39.8 1.9 %shard_map.110 = (f32[3,8,8,128]{3,2,1,0:T(8,128)}, f32[120,128]{1,0:T(8,128)}, f32[120,128]{1,0:T(8,128)}) custom-call(f32[4,8,8,128]{3,2,1,0:T(8,128)} %get-tuple-element.48.refs_0_, f32[4,8,128]{2,1,0:T(8,128)} %get-tuple-element.49.refs_1_, f32[112,128]{1,0:T(8,128)} %collective-permute-done.8.refs_2_, f32[80,128]{1,0:T(8,128)} %collective-permute-done.9.refs_3_, ...), custom_call_target="tpu_custom_call" | custom-call | tf_op jit(solution)/shard_map/pallas_call | solution.py:98
  41.7 3.9 %collective-permute-start.14 = (f32[120,128]{1,0:T(8,128)}, f32[120,128]{1,0:T(8,128)}, u32[]{:S(2)}, u32[]{:S(2)}) collective-permute-start(f32[120,128]{1,0:T(8,128)} %get-tuple-element.58), channel_id=1, source_target_pairs={{0,24},{8,0},{16,8},{24,16},{1,25},{9,1},{17,9},{25,17},{2,26},{10... | collective-permute-start | bytes 184328 | tf_op jit(solution)/shard_map/ppermute | solution.py:620
  45.6 2.2 %shard_map.109 = f32[19,8,8,128]{3,2,1,0:T(8,128)} custom-call(f32[19,8,8,128]{3,2,1,0:T(8,128)} %get-tuple-element.38.refs_0_, f32[19,8,128]{2,1,0:T(8,128)} %get-tuple-element.47.refs_1_), custom_call_target="tpu_custom_call" | custom-call | flops 100000000 | bytes 4194304 | tf_op jit(solution)/shard_map/pallas_call | solution.py:98
  47.8 0.6 %collective-permute-done.13.refs_7_ = f32[120,128]{1,0:T(8,128)} collective-permute-done((f32[120,128]{1,0:T(8,128)}, f32[120,128]{1,0:T(8,128)}, u32[]{:S(2)}, u32[]{:S(2)}) %collective-permute-start.13) | collective-permute-done | bytes 61472 | tf_op jit(solution)/shard_map/ppermute | solution.py:620
  48.4 2.1 %shard_map.111 = (f32[3,8,8,128]{3,2,1,0:T(8,128)}, f32[6,68,128]{2,1,0:T(8,128)}) custom-call(f32[3,8,8,128]{3,2,1,0:T(8,128)} %get-tuple-element.55.refs_0_, f32[6,16,128]{2,1,0:T(8,128)} %get-tuple-element.56.refs_1_, f32[112,128]{1,0:T(8,128)} %collective-permute-done.8.refs_2_, f32[80,128]{1,0:T(8,128)} %collective-permute-done.9.refs_3_, ...), custom_call_target="tpu_custom_call" | custom-call | tf_op jit(solution)/shard_map/pallas_call | solution.py:98
  (15 shorter events, 0.2 us)
Async XLA Ops:
  3.3 11.4 %collective-permute-start = (f32[552,128]{1,0:T(8,128)}, f32[552,128]{1,0:T(8,128)}, u32[]{:S(2)}, u32[]{:S(2)}) collective-permute-start(f32[552,128]{1,0:T(8,128)} %get-tuple-element.33), channel_id=1, source_target_pairs={{0,6},{2,0},{4,2},{6,4},{1,7},{3,1},{5,3},{7,5},{8,14},{10,8},{12,... | collective-permute-start | bytes 847880 | tf_op jit(solution)/shard_map/ppermute | solution.py:620
  5.7 9.0 %collective-permute-start.1 = (f32[376,128]{1,0:T(8,128)}, f32[376,128]{1,0:T(8,128)}, u32[]{:S(2)}, u32[]{:S(2)}) collective-permute-start(f32[376,128]{1,0:T(8,128)} %get-tuple-element.34), channel_id=1, source_target_pairs={{0,2},{2,4},{4,6},{6,0},{1,3},{3,5},{5,7},{7,1},{8,10},{10,12},{12... | collective-permute-start | bytes 577544 | tf_op jit(solution)/shard_map/ppermute | solution.py:620
  5.7 9.0 %collective-permute-start.2 = (f32[25,8,128]{2,1,0:T(8,128)}, f32[25,8,128]{2,1,0:T(8,128)}, u32[]{:S(2)}, u32[]{:S(2)}) collective-permute-start(f32[25,8,128]{2,1,0:T(8,128)} %get-tuple-element.35), channel_id=1, source_target_pairs={{0,1},{1,0},{2,3},{3,2},{4,5},{5,4},{6,7},{7,6},{8,9},{9,8},{10,11... | collective-permute-start | bytes 307208 | tf_op jit(solution)/shard_map/ppermute | solution.py:630
  7.2 7.5 %collective-permute-start.3 = (f32[88,128]{1,0:T(8,128)}, f32[88,128]{1,0:T(8,128)}, u32[]{:S(2)}, u32[]{:S(2)}) collective-permute-start(f32[88,128]{1,0:T(8,128)} %get-tuple-element.36), channel_id=1, source_target_pairs={{0,7},{1,6},{2,1},{3,0},{4,3},{5,2},{6,5},{7,4},{8,15},{9,14},{10,... | collective-permute-start | bytes 135176 | tf_op jit(solution)/shard_map/ppermute | solution.py:632
  8.7 6.1 %collective-permute-start.4 = (f32[56,128]{1,0:T(8,128)}, f32[56,128]{1,0:T(8,128)}, u32[]{:S(2)}, u32[]{:S(2)}) collective-permute-start(f32[56,128]{1,0:T(8,128)} %get-tuple-element.37), channel_id=1, source_target_pairs={{0,3},{1,2},{2,5},{3,4},{4,7},{5,6},{6,1},{7,0},{8,11},{9,10},{10,... | collective-permute-start | bytes 86024 | tf_op jit(solution)/shard_map/ppermute | solution.py:632
  16.7 10.4 %collective-permute-start.6 = (f32[9,16,128]{2,1,0:T(8,128)}, f32[9,16,128]{2,1,0:T(8,128)}, u32[]{:S(2)}, u32[]{:S(2)}) collective-permute-start(f32[9,16,128]{2,1,0:T(8,128)} %get-tuple-element.43), channel_id=1, source_target_pairs={{0,24},{8,0},{16,8},{24,16},{1,25},{9,1},{17,9},{25,17},{2,26},{10... | collective-permute-start | bytes 221192 | tf_op jit(solution)/shard_map/ppermute | solution.py:620
  20.3 6.7 %collective-permute-start.5 = (f32[6,16,128]{2,1,0:T(8,128)}, f32[6,16,128]{2,1,0:T(8,128)}, u32[]{:S(2)}, u32[]{:S(2)}) collective-permute-start(f32[6,16,128]{2,1,0:T(8,128)} %get-tuple-element.42), channel_id=1, source_target_pairs={{0,8},{8,16},{16,24},{24,0},{1,9},{9,17},{17,25},{25,1},{2,10},{10... | collective-permute-start | bytes 147464 | tf_op jit(solution)/shard_map/ppermute | solution.py:620
  22.7 4.3 %collective-permute-start.7 = (f32[72,128]{1,0:T(8,128)}, f32[72,128]{1,0:T(8,128)}, u32[]{:S(2)}, u32[]{:S(2)}) collective-permute-start(f32[72,128]{1,0:T(8,128)} %shard_map.107), channel_id=1, source_target_pairs={{0,1},{1,0},{2,3},{3,2},{4,5},{5,4},{6,7},{7,6},{8,9},{9,8},{10,11... | collective-permute-start | bytes 110600 | tf_op jit(solution)/shard_map/ppermute | solution.py:630
  32.6 7.1 %collective-permute-start.8 = (f32[112,128]{1,0:T(8,128)}, f32[112,128]{1,0:T(8,128)}, u32[]{:S(2)}, u32[]{:S(2)}) collective-permute-start(f32[112,128]{1,0:T(8,128)} %get-tuple-element.50), channel_id=1, source_target_pairs={{0,2},{2,4},{4,6},{6,0},{1,3},{3,5},{5,7},{7,1},{8,10},{10,12},{12... | collective-permute-start | bytes 172040 | tf_op jit(solution)/shard_map/ppermute | solution.py:620
  32.7 7.1 %collective-permute-start.10 = (f32[112,128]{1,0:T(8,128)}, f32[112,128]{1,0:T(8,128)}, u32[]{:S(2)}, u32[]{:S(2)}) collective-permute-start(f32[112,128]{1,0:T(8,128)} %get-tuple-element.52), channel_id=1, source_target_pairs={{0,1},{1,0},{2,3},{3,2},{4,5},{5,4},{6,7},{7,6},{8,9},{9,8},{10,11... | collective-permute-start | bytes 172040 | tf_op jit(solution)/shard_map/ppermute | solution.py:630
  33.8 5.9 %collective-permute-start.9 = (f32[80,128]{1,0:T(8,128)}, f32[80,128]{1,0:T(8,128)}, u32[]{:S(2)}, u32[]{:S(2)}) collective-permute-start(f32[80,128]{1,0:T(8,128)} %get-tuple-element.51), channel_id=1, source_target_pairs={{0,6},{2,0},{4,2},{6,4},{1,7},{3,1},{5,3},{7,5},{8,14},{10,8},{12,... | collective-permute-start | bytes 122888 | tf_op jit(solution)/shard_map/ppermute | solution.py:620
  35.2 4.6 %collective-permute-start.11 = (f32[64,128]{1,0:T(8,128)}, f32[64,128]{1,0:T(8,128)}, u32[]{:S(2)}, u32[]{:S(2)}) collective-permute-start(f32[64,128]{1,0:T(8,128)} %get-tuple-element.53), channel_id=1, source_target_pairs={{0,3},{1,2},{2,5},{3,4},{4,7},{5,6},{6,1},{7,0},{8,11},{9,10},{10,... | collective-permute-start | bytes 98312 | tf_op jit(solution)/shard_map/ppermute | solution.py:632
  35.2 4.4 %collective-permute-start.12 = (f32[56,128]{1,0:T(8,128)}, f32[56,128]{1,0:T(8,128)}, u32[]{:S(2)}, u32[]{:S(2)}) collective-permute-start(f32[56,128]{1,0:T(8,128)} %get-tuple-element.54), channel_id=1, source_target_pairs={{0,7},{1,6},{2,1},{3,0},{4,3},{5,2},{6,5},{7,4},{8,15},{9,14},{10,... | collective-permute-start | bytes 86024 | tf_op jit(solution)/shard_map/ppermute | solution.py:632
  41.7 6.7 %collective-permute-start.13 = (f32[120,128]{1,0:T(8,128)}, f32[120,128]{1,0:T(8,128)}, u32[]{:S(2)}, u32[]{:S(2)}) collective-permute-start(f32[120,128]{1,0:T(8,128)} %get-tuple-element.57), channel_id=1, source_target_pairs={{0,8},{8,16},{16,24},{24,0},{1,9},{9,17},{17,25},{25,1},{2,10},{10... | collective-permute-start | bytes 184328 | tf_op jit(solution)/shard_map/ppermute | solution.py:620
  41.7 6.7 %collective-permute-start.14 = (f32[120,128]{1,0:T(8,128)}, f32[120,128]{1,0:T(8,128)}, u32[]{:S(2)}, u32[]{:S(2)}) collective-permute-start(f32[120,128]{1,0:T(8,128)} %get-tuple-element.58), channel_id=1, source_target_pairs={{0,24},{8,0},{16,8},{24,16},{1,25},{9,1},{17,9},{25,17},{2,26},{10... | collective-permute-start | bytes 184328 | tf_op jit(solution)/shard_map/ppermute | solution.py:620
